TPU v7x, 32 devices: a whole 2x2x4 slice. The times are simulated.
32 devices in a mesh: ctx: 16 (over z, y, core), tp: 2 (over x).
Axes of the slice: x: 2, y: 2, z: 4, core: 2. Of those that a mesh axis runs over, the one named last changes fastest.
Arguments:
- query_heads: bfloat16 [2048, 8192], P('ctx', 'tp'), may hold values from -32 to 32
- key_heads: bfloat16 [2048, 8192], P('ctx', 'tp'), may hold values from -6 to 6
- value_heads: bfloat16 [2048, 8192], P('ctx', 'tp'), may hold values from -6 to 6
- hyena_query: bfloat16 [2048, 8192], P('ctx', 'tp'), may hold values from -6 to 6
- hyena_key: bfloat16 [2048, 8192], P('ctx', 'tp'), may hold values from -6 to 6
- hyena_value: bfloat16 [2048, 8192], P('ctx', 'tp'), may hold values from -6 to 6
- short_filter: float32 [3, 7, 8192], P(None, None, 'tp'), may hold values from -2 to 2
- long_filter: float32 [2048, 512], P('ctx', 'tp'), may hold values from -0.125 to 0.125
- output_grad: bfloat16 [2048, 8192], P('ctx', 'tp'), may hold values from -70 to 70
Outputs:
- attention: bfloat16 [2048, 8192], P('ctx', 'tp')
- query_grad: bfloat16 [2048, 8192], P('ctx', 'tp')
- key_grad: bfloat16 [2048, 8192], P('ctx', 'tp')
- value_grad: bfloat16 [2048, 8192], P('ctx', 'tp')
- filter_grad: float32 [2048, 512], P('ctx', 'tp')
All inputs are finite; a program needn't handle non-finite values.
Results may differ from a plain program's by a relative error of at most 0.0049.
Values may be sent and summed in bfloat16 or wider, within the bound.
No kernel may reach another device: no remote copies, remote signals or barrier semaphores. Data moves between devices by JAX's collectives and lax.ppermute only.
A program may use at most 128 MiB of HBM per device.

v0:
```python
import math

import jax
import jax.numpy as jnp
from jax import lax
from jax.sharding import PartitionSpec as P

HEAD_DIM = 128
GROUPS = 512


HIGHEST = lax.Precision.HIGHEST
FULL_TURN = 2.0 * math.pi


def shifted(block, axis, distance):
    devices = range(lax.axis_size(axis))
    route = [(i - distance, i) for i in devices if i - distance in devices]
    return lax.ppermute(block, axis, route)


def angle_table(left, right, period):
    product = left * right % period
    angle = product.astype(jnp.float32) * (FULL_TURN / period)
    return (jnp.cos(angle), jnp.sin(angle))


def attend(query_block, key_own, value_own, key_prev, value_prev, position):
    row_count = query_block.shape[0]
    head_count = query_block.shape[1] // HEAD_DIM
    queries = query_block.reshape(row_count, head_count, HEAD_DIM)
    all_keys = jnp.concatenate([key_prev, key_own], 0).reshape(2 * row_count, head_count, HEAD_DIM)
    all_values = jnp.concatenate([value_prev, value_own], 0).reshape(
        2 * row_count, head_count, HEAD_DIM
    )
    scores = jnp.einsum("qhd,khd->hqk", queries, all_keys, preferred_element_type=jnp.float32) * (
        1.0 / math.sqrt(HEAD_DIM)
    )
    query_pos = jnp.arange(row_count)[:, None]
    key_pos = jnp.arange(2 * row_count)[None, :] - row_count
    allowed = (key_pos <= query_pos) & ((key_pos >= 0) | (position > 0))
    masked = jnp.where(allowed[None], scores, -jnp.inf)
    largest = jnp.max(masked, axis=2, keepdims=True)
    raised = jnp.exp(masked - largest)
    weights = (raised / jnp.sum(raised, axis=2, keepdims=True)).astype(jnp.bfloat16)
    mixed = jnp.einsum("hqk,khd->qhd", weights, all_values, preferred_element_type=jnp.float32)
    return mixed.astype(jnp.bfloat16).reshape(row_count, head_count * HEAD_DIM)


def causal_short(signal, before, filter_taps):
    tap_count = filter_taps.shape[0]
    row_count = signal.shape[0]
    extended = jnp.concatenate([before, signal], 0)
    total = jnp.zeros_like(signal)
    for offset in range(tap_count):
        total = (
            total
            + filter_taps[offset]
            * extended[tap_count - 1 - offset : tap_count - 1 - offset + row_count]
        )
    return total


def anti_short(signal, after, filter_taps):
    tap_count = filter_taps.shape[0]
    row_count = signal.shape[0]
    extended = jnp.concatenate([signal, after], 0)
    total = jnp.zeros_like(signal)
    for offset in range(tap_count):
        total = total + filter_taps[offset] * extended[offset : offset + row_count]
    return total


def spectral_products(real_part, imag_part):
    mixed_real, filter_real, delta_real = (real_part[0], real_part[1], real_part[2])
    mixed_imag, filter_imag, delta_imag = (imag_part[0], imag_part[1], imag_part[2])
    out_real = jnp.stack(
        [
            filter_real * mixed_real - filter_imag * mixed_imag,
            filter_real * delta_real + filter_imag * delta_imag,
            mixed_real * delta_real + mixed_imag * delta_imag,
        ]
    )
    out_imag = jnp.stack(
        [
            filter_real * mixed_imag + filter_imag * mixed_real,
            filter_real * delta_imag - filter_imag * delta_real,
            mixed_real * delta_imag - mixed_imag * delta_real,
        ]
    )
    return (out_real, out_imag)


def channel_conv(stacked):
    groups = lax.axis_size("ctx")
    stack_count, row_count, channels = stacked.shape
    period = 2 * groups * row_count
    flipped = jnp.swapaxes(stacked, 1, 2)
    spread = lax.all_to_all(flipped, "ctx", split_axis=1, concat_axis=2, tiled=True)
    narrow = spread.shape[1]
    whole = spread.reshape(stack_count, narrow, groups, row_count)
    freq_first = jnp.arange(2 * groups)
    cos_first, sin_first = angle_table(freq_first[:, None], jnp.arange(groups)[None, :], 2 * groups)
    real_part = jnp.einsum("ka,scab->sckb", cos_first, whole, precision=HIGHEST)
    imag_part = -jnp.einsum("ka,scab->sckb", sin_first, whole, precision=HIGHEST)
    cos_twist, sin_twist = angle_table(freq_first[:, None], jnp.arange(row_count)[None, :], period)
    twist_real = real_part * cos_twist + imag_part * sin_twist
    twist_imag = imag_part * cos_twist - real_part * sin_twist
    cos_rows, sin_rows = angle_table(
        jnp.arange(row_count)[:, None], jnp.arange(row_count)[None, :], row_count
    )
    spec_real = jnp.einsum("kb,scjb->scjk", cos_rows, twist_real, precision=HIGHEST) + jnp.einsum(
        "kb,scjb->scjk", sin_rows, twist_imag, precision=HIGHEST
    )
    spec_imag = jnp.einsum("kb,scjb->scjk", cos_rows, twist_imag, precision=HIGHEST) - jnp.einsum(
        "kb,scjb->scjk", sin_rows, twist_real, precision=HIGHEST
    )
    prod_real, prod_imag = spectral_products(spec_real, spec_imag)
    back_real = jnp.einsum("kb,scjk->scjb", cos_rows, prod_real, precision=HIGHEST) - jnp.einsum(
        "kb,scjk->scjb", sin_rows, prod_imag, precision=HIGHEST
    )
    back_imag = jnp.einsum("kb,scjk->scjb", cos_rows, prod_imag, precision=HIGHEST) + jnp.einsum(
        "kb,scjk->scjb", sin_rows, prod_real, precision=HIGHEST
    )
    turn_real = back_real * cos_twist - back_imag * sin_twist
    turn_imag = back_imag * cos_twist + back_real * sin_twist
    cos_last, sin_last = angle_table(jnp.arange(groups)[:, None], freq_first[None, :], 2 * groups)
    signal = (
        jnp.einsum("ak,sckb->scab", cos_last, turn_real, precision=HIGHEST)
        - jnp.einsum("ak,sckb->scab", sin_last, turn_imag, precision=HIGHEST)
    ) * (1.0 / period)
    signal = signal.reshape(stack_count, narrow, groups * row_count)
    returned = lax.all_to_all(signal, "ctx", split_axis=2, concat_axis=1, tiled=True)
    return jnp.swapaxes(returned, 1, 2)


def on_device(
    query_heads,
    key_heads,
    value_heads,
    hyena_query,
    hyena_key,
    hyena_value,
    short_filter,
    long_filter,
    output_grad,
):
    row_count = query_heads.shape[0]
    channels = query_heads.shape[1]
    group_count = long_filter.shape[1]
    group_width = channels // group_count
    rim_rows = short_filter.shape[1] - 1
    position = lax.axis_index("ctx")
    tail = jnp.concatenate(
        [
            key_heads,
            value_heads,
            hyena_query[row_count - rim_rows :],
            hyena_key[row_count - rim_rows :],
            hyena_value[row_count - rim_rows :],
        ],
        0,
    )
    before = shifted(tail, "ctx", 1)
    attention = attend(
        query_heads,
        key_heads,
        value_heads,
        before[:row_count],
        before[row_count : 2 * row_count],
        position,
    )
    leading = before[2 * row_count :].astype(jnp.float32)
    short_q = causal_short(hyena_query.astype(jnp.float32), leading[0:rim_rows], short_filter[0])
    short_k = causal_short(
        hyena_key.astype(jnp.float32), leading[rim_rows : 2 * rim_rows], short_filter[1]
    )
    short_v = causal_short(
        hyena_value.astype(jnp.float32), leading[2 * rim_rows : 3 * rim_rows], short_filter[2]
    )
    mixed = short_k * short_v
    upstream = output_grad.astype(jnp.float32)
    grad_conv = upstream * short_q
    channel_filter = jnp.repeat(long_filter, group_width, axis=1)
    stacked = jnp.stack([mixed, channel_filter, grad_conv])
    results = channel_conv(stacked)
    conv, grad_mixed, channel_grad = (results[0], results[1], results[2])
    raw_grad = jnp.sum(channel_grad.reshape(row_count, group_count, group_width), axis=2)
    grad_short_q = upstream * conv
    grad_short_k = grad_mixed * short_v
    grad_short_v = grad_mixed * short_k
    heads_first = jnp.stack(
        [grad_short_q[:rim_rows], grad_short_k[:rim_rows], grad_short_v[:rim_rows]]
    )
    after = shifted(heads_first.astype(jnp.bfloat16), "ctx", -1).astype(heads_first.dtype)
    query_grad = anti_short(grad_short_q, after[0], short_filter[0]).astype(jnp.bfloat16)
    key_grad = anti_short(grad_short_k, after[1], short_filter[1]).astype(jnp.bfloat16)
    value_grad = anti_short(grad_short_v, after[2], short_filter[2]).astype(jnp.bfloat16)
    squares = lax.psum(jnp.sum(raw_grad * raw_grad), ("ctx", "tp"))
    grad_norm = jnp.sqrt(squares)
    bound = math.sqrt(row_count * lax.axis_size("ctx") * GROUPS)
    factor = jnp.minimum(1.0, bound / grad_norm)
    filter_grad = raw_grad * factor
    return (attention, query_grad, key_grad, value_grad, filter_grad)


def solution(mesh):
    in_specs = (
        P("ctx", "tp"),
        P("ctx", "tp"),
        P("ctx", "tp"),
        P("ctx", "tp"),
        P("ctx", "tp"),
        P("ctx", "tp"),
        P(None, None, "tp"),
        P("ctx", "tp"),
        P("ctx", "tp"),
    )
    out_specs = (P("ctx", "tp"), P("ctx", "tp"), P("ctx", "tp"), P("ctx", "tp"), P("ctx", "tp"))
    return jax.shard_map(
        on_device, mesh=mesh, in_specs=in_specs, out_specs=out_specs, check_vma=False
    )
```

profile of v0, /device:TPU:16, one launch (start us, length us, event | category | flops | bytes accessed | tf_op | source)
XLA Modules:
  0.0 921.2 jit_solution(11700356448302633328)
XLA Ops:
  3.3 14.3 %concatenate.27 = bf16[274,4096]{1,0:T(8,128)(2,1)} concatenate(bf16[128,4096]{1,0:T(8,128)(2,1)} %param.10, bf16[128,4096]{1,0:T(8,128)(2,1)} %param.11, bf16[6,4096]{1,0:T(8,128)(2,1)S(1)} %slice.315, bf16[6,4096]{1,0:T(8,128)(2,1)S(1)} %slice.316, bf16[6,4096]{1,0:T(8,128)(2,1)S(1)} %slice.317), dimensions={0} | concatenate | bytes 4489216 | tf_op jit(solution)/shard_map/concatenate | solution.py:154
  33.4 15.0 %collective-permute-done = bf16[274,4096]{1,0:T(8,128)(2,1)} collective-permute-done((bf16[274,4096]{1,0:T(8,128)(2,1)}, bf16[274,4096]{1,0:T(8,128)(2,1)}, u32[]{:S(2)}, u32[]{:S(2)}) %collective-permute-start) | collective-permute-done | bytes 2244640 | tf_op jit(solution)/shard_map/ppermute | solution.py:19
  51.6 10.5 %fusion.50 = f32[1,128,4096]{1,2,0:T(8,128)S(1)} fusion(bf16[128,4096]{0,1:T(8,128)(2,1)S(1)} %copy.62, f32[6,4096]{0,1:T(8,128)S(1)} %get-tuple-element.40, f32[128,4096]{0,1:T(8,128)S(1)} %copy-done.9, f32[4096]{0:T(1024)S(1)} %bitcast.203, f32[4096]{0:T(1024)S(1)} %bitcast.201, f32[4096]{0:T(1024)S(1)} %bitcast.191, f32[4096]{0:T(1024)S(1)} %bitcast.193, ...), kind=kLoop, calls=%fused_computation.123 | loop fusion | flops 11010048 | bytes 5455872 | tf_op jit(solution)/shard_map/stack | solution.py:185
  62.2 23.1 %multiply_bitcast_fusion.1 = (f32[1,128,4096]{1,2,0:T(8,128)S(1)}, f32[128,4096]{0,1:T(8,128)}, f32[128,4096]{0,1:T(8,128)}) fusion(f32[128,4096]{0,1:T(8,128)S(1)} %copy-done.8, f32[6,4096]{0,1:T(8,128)S(1)} %get-tuple-element.41, f32[4096]{0:T(1024)S(1)} %bitcast.177, f32[4096]{0:T(1024)S(1)} %bitcast.179, f32[4096]{0:T(1024)S(1)} %bitcast.181, ...), kind=kLoop, calls=%fused_computation.245 | loop fusion | flops 20447232 | bytes 10911744 | tf_op jit(solution)/shard_map/stack | solution.py:185
  86.0 18.7 %copy.68 = f32[3,4096,128]{2,0,1:T(4,128)} copy(f32[3,4096,128]{2,1,0:T(8,128)S(1)} %maximum_bitcast_fusion) | data formatting | bytes 12582912 | tf_op jit(solution)/shard_map/transpose | solution.py:98
  104.7 5.6 all-to-all-start
  110.5 182.3 %all-to-all-done = f32[3,4096,128]{2,0,1:T(4,128)} async-done(((f32[3,4096,128]{2,0,1:T(4,128)}), f32[3,4096,128]{2,0,1:T(4,128)}, u32[]{:S(2)}, u32[]{:S(2)}) %all-to-all-start) | async-done | bytes 6291488 | tf_op jit(solution)/shard_map/all_to_all | solution.py:99
  292.8 18.7 %fusion.27 = f32[3,256,128,32]{2,3,1,0:T(8,128)} fusion(f32[3,16,256,128]{3,0,2,1:T(4,128)} %bitcast.30), kind=kOutput, calls=%fused_computation.94 | convolution fusion | flops 603986944 | bytes 18874368 | tf_op jit(solution)/shard_map/ka,scab->sckb/dot_general | solution.py:105
  311.5 25.2 %fusion.1 = (f32[3,256,32,128]{3,2,1,0:T(8,128)}, f32[3,256,32,128]{3,2,1,0:T(8,128)}) fusion(f32[3,256,128,32]{2,3,1,0:T(8,128)} %fusion.27, f32[32,128]{1,0:T(8,128)S(1)} %get-tuple-element.65, f32[32,128]{1,0:T(8,128)S(1)} %get-tuple-element.66, f32[3,16,256,128]{3,0,2,1:T(4,128)} %bitcast.30), kind=kOutput, calls=%fused_computation.5 | convolution fusion | flops 626007040 | bytes 44072960 | tf_op jit(solution)/shard_map/ka,scab->sckb/dot_general | solution.py:104
  336.7 24.0 %fusion.19 = f32[3,256,32,128]{3,1,2,0:T(8,128)} fusion(f32[3,256,32,128]{3,2,1,0:T(8,128)} %get-tuple-element.24), kind=kOutput, calls=%fused_computation.25 | convolution fusion | flops 4832067584 | bytes 25165824 | tf_op jit(solution)/shard_map/kb,scjb->scjk/dot_general | solution.py:115
  360.7 22.4 %fusion.21 = f32[3,256,32,128]{3,1,2,0:T(8,128)} fusion(f32[3,256,32,128]{3,2,1,0:T(8,128)S(1)} %copy-done.3), kind=kOutput, calls=%fused_computation.27 | convolution fusion | flops 4832067584 | bytes 25165824 | tf_op jit(solution)/shard_map/kb,scjb->scjk/dot_general | solution.py:112
  383.1 22.5 %fusion.44 = f32[3,256,32,128]{3,1,2,0:T(8,128)S(1)} fusion(f32[3,256,32,128]{3,1,2,0:T(8,128)} %fusion.19, f32[3,256,32,128]{3,2,1,0:T(8,128)S(1)} %bitcast.152), kind=kOutput, calls=%fused_computation.119 | convolution fusion | flops 4835213312 | bytes 37748736 | tf_op jit(solution)/shard_map/kb,scjb->scjk/dot_general | solution.py:115
  405.6 23.4 %fusion.41 = f32[3,256,32,128]{3,1,2,0:T(8,128)} fusion(f32[3,256,32,128]{3,1,2,0:T(8,128)} %fusion.21, f32[3,256,32,128]{3,2,1,0:T(8,128)S(1)} %bitcast.152), kind=kOutput, calls=%fused_computation.118 | convolution fusion | flops 4835213312 | bytes 37748736 | tf_op jit(solution)/shard_map/kb,scjb->scjk/dot_general | solution.py:112
  429.0 7.8 multiply_add_fusion.2
  436.8 9.9 %multiply_subtract_fusion.2 = (f32[1,256,32,128]{3,1,2,0:T(8,128)}, f32[1,256,32,128]{3,1,2,0:T(8,128)}, f32[1,256,32,128]{3,1,2,0:T(8,128)}, f32[1,256,32,128]{3,1,2,0:T(8,128)}) fusion(f32[3,256,32,128]{3,1,2,0:T(8,128)S(1)} %fusion.44, f32[3,256,32,128]{3,1,2,0:T(8,128)} %fusion.41), kind=kLoop, calls=%fused_computation.115 | loop fusion | flops 12582912 | bytes 41943040 | tf_op jit(solution)/shard_map/sub | solution.py:79
  446.7 10.8 %pad_maximum_fusion.1 = f32[3,256,32,128]{3,1,2,0:T(8,128)} fusion(f32[1,256,32,128]{3,1,2,0:T(8,128)} %get-tuple-element.28, f32[1,256,32,128]{3,1,2,0:T(8,128)} %get-tuple-element.27, f32[1,256,32,128]{3,1,2,0:T(8,128)} %get-tuple-element.30), kind=kLoop, calls=%fused_computation.2 | loop fusion | flops 6291456 | bytes 25165824 | tf_op jit(solution)/shard_map/stack | solution.py:84
  457.5 22.8 %fusion.11 = f32[3,256,32,128]{3,2,1,0:T(8,128)} fusion(f32[3,256,32,128]{3,1,2,0:T(8,128)} %pad_maximum_fusion.1), kind=kOutput, calls=%fused_computation.17 | convolution fusion | flops 4832067584 | bytes 25165824 | tf_op jit(solution)/shard_map/kb,scjk->scjb/dot_general | solution.py:122
  480.3 18.4 %fusion.13 = f32[3,256,32,128]{3,2,1,0:T(8,128)} fusion(f32[3,256,32,128]{3,1,2,0:T(8,128)S(1)} %copy-done.1), kind=kOutput, calls=%fused_computation.19 | convolution fusion | flops 4832067584 | bytes 25165824 | tf_op jit(solution)/shard_map/kb,scjk->scjb/dot_general | solution.py:119
  498.8 9.3 %pad_maximum_fusion = f32[3,256,32,128]{3,1,2,0:T(8,128)} fusion(f32[1,256,32,128]{3,1,2,0:T(8,128)} %get-tuple-element.26, f32[1,256,32,128]{3,1,2,0:T(8,128)} %get-tuple-element.29, f32[1,256,32,128]{3,1,2,0:T(8,128)S(1)} %copy-done.4), kind=kLoop, calls=%fused_computation.1 | loop fusion | flops 6291456 | bytes 25165824 | tf_op jit(solution)/shard_map/stack | solution.py:77
  508.1 22.7 %fusion.15 = f32[3,256,32,128]{3,2,1,0:T(8,128)} fusion(f32[3,256,32,128]{3,1,2,0:T(8,128)} %pad_maximum_fusion), kind=kOutput, calls=%fused_computation.21 | convolution fusion | flops 4832067584 | bytes 25165824 | tf_op jit(solution)/shard_map/kb,scjk->scjb/dot_general | solution.py:122
  530.8 18.3 %fusion.17 = f32[3,256,32,128]{3,2,1,0:T(8,128)} fusion(f32[3,256,32,128]{3,1,2,0:T(8,128)S(1)} %copy-done.2), kind=kOutput, calls=%fused_computation.23 | convolution fusion | flops 4832067584 | bytes 25165824 | tf_op jit(solution)/shard_map/kb,scjk->scjb/dot_general | solution.py:119
  549.1 18.4 %fusion.3 = f32[3,256,128,16]{2,3,1,0:T(8,128)} fusion(f32[32,128]{1,0:T(8,128)S(1)} %get-tuple-element.65, f32[32,128]{1,0:T(8,128)S(1)} %get-tuple-element.66, f32[3,256,32,128]{3,2,1,0:T(8,128)S(1)} %bitcast.154, f32[3,256,32,128]{3,2,1,0:T(8,128)} %fusion.15, f32[3,256,32,128]{3,2,1,0:T(8,128)} %fusion.17, f32[3,256,32,128]{3,2,1,0:T(8,128)} %fusion.13), kind=kOutput, calls=%fused_computation.9 | convolution fusion | flops 619715584 | bytes 56655872 | tf_op jit(solution)/shard_map/ak,sckb->scab/dot_general | solution.py:130
  567.6 23.2 %multiply_bitcast_fusion = f32[3,256,16,128]{3,2,1,0:T(8,128)} fusion(f32[3,256,128,16]{2,3,1,0:T(8,128)} %fusion.3, f32[32,128]{1,0:T(8,128)S(1)} %get-tuple-element.65, f32[32,128]{1,0:T(8,128)S(1)} %get-tuple-element.66, f32[3,256,32,128]{3,2,1,0:T(8,128)} %fusion.11, f32[3,256,32,128]{3,2,1,0:T(8,128)} %fusion.15, f32[3,256,32,128]{3,2,1,0:T(8,128)} %fusion.17, ...), kind=kOutput, calls=%fused_computation.98 | convolution fusion | flops 622861312 | bytes 62947328 | tf_op jit(solution)/shard_map/ak,sckb->scab/dot_general | solution.py:129
  590.8 7.6 copy.106
  598.4 5.2 all-to-all-start.1
  619.1 166.9 %all-to-all-done.1 = f32[3,256,2048]{1,0,2:T(4,128)} async-done(((f32[3,256,2048]{1,0,2:T(4,128)}), f32[3,256,2048]{1,0,2:T(4,128)}, u32[]{:S(2)}, u32[]{:S(2)}) %all-to-all-start.1) | async-done | bytes 6291488 | tf_op jit(solution)/shard_map/all_to_all | solution.py:133
  786.0 9.0 copy.80
  800.0 38.9 %psum.7 = f32[]{:T(128)} all-reduce(f32[]{:T(128)} %multiply_reduce_fusion), channel_id=1, replica_groups=mesh['ctx'=16,'tp'=2] {'ctx','tp'}, use_global_device_ids=true, to_apply=%region_4.5 | all-reduce | flops 1 | bytes 8 | tf_op jit(solution)/shard_map/psum | solution.py:199
  839.6 6.2 fusion.161
  872.2 11.9 %fusion.89 = bf16[128,4096]{0,1:T(8,128)(2,1)} fusion(f32[128,4096]{0,1:T(8,128)S(1)} %copy-done.5, f32[6,4096]{0,1:T(8,128)S(1)} %get-tuple-element.33, f32[4096]{0:T(1024)S(1)} %bitcast.204, f32[4096]{0:T(1024)S(1)} %bitcast.202, f32[4096]{0:T(1024)S(1)} %bitcast.192, f32[4096]{0:T(1024)S(1)} %bitcast.194, f32[4096]{0:T(1024)S(1)} %bitcast.196, ...), kind=kLoop, calls=%fused_computation.162 | loop fusion | flops 10485760 | bytes 3358720 | tf_op jit(solution)/shard_map/convert_element_type | solution.py:196
  886.6 18.5 %fusion.55 = bf16[128,4096]{0,1:T(8,128)(2,1)} fusion(f32[128,4096]{0,1:T(8,128)} %get-tuple-element.35, f32[6,4096]{0,1:T(8,128)} %get-tuple-element.31, f32[4096]{0:T(1024)S(1)} %bitcast.178, f32[4096]{0:T(1024)S(1)} %bitcast.180, f32[4096]{0:T(1024)S(1)} %bitcast.182, f32[4096]{0:T(1024)S(1)} %bitcast.184, f32[4096]{0:T(1024)S(1)} %bitcast.186, ...), kind=kLoop, calls=%fused_computation.128 | loop fusion | flops 10485760 | bytes 3358720 | tf_op jit(solution)/shard_map/convert_element_type | solution.py:198
  905.1 11.9 %fusion.72 = bf16[128,4096]{0,1:T(8,128)(2,1)} fusion(f32[128,4096]{0,1:T(8,128)S(1)} %get-tuple-element.34, f32[6,4096]{0,1:T(8,128)S(1)} %copy-done.10, f32[4096]{0:T(1024)S(1)} %bitcast.166, f32[4096]{0:T(1024)S(1)} %bitcast.168, f32[4096]{0:T(1024)S(1)} %bitcast.170, f32[4096]{0:T(1024)S(1)} %bitcast.172, f32[4096]{0:T(1024)S(1)} %bitcast.174, ...), kind=kLoop, calls=%fused_computation.145 | loop fusion | flops 10485760 | bytes 3358720 | tf_op jit(solution)/shard_map/convert_element_type | solution.py:197
  (189 shorter events, 74.9 us)
Async XLA Ops:
  0.6 614.4 %copy-start = (bf16[128,4096]{1,0:T(8,128)(2,1)S(1)}, bf16[128,4096]{1,0:T(8,128)(2,1)}, u32[]{:S(2)}) copy-start(bf16[128,4096]{1,0:T(8,128)(2,1)} %param.9) | copy-start | bytes 3145732
  3.3 16.3 %copy-start.15 = (bf16[128,4096]{1,0:T(8,128)(2,1)S(1)}, bf16[128,4096]{1,0:T(8,128)(2,1)}, u32[]{:S(2)}) copy-start(bf16[128,4096]{1,0:T(8,128)(2,1)} %param.12) | copy-start | bytes 3145732
  17.6 30.8 %collective-permute-start = (bf16[274,4096]{1,0:T(8,128)(2,1)}, bf16[274,4096]{1,0:T(8,128)(2,1)}, u32[]{:S(2)}, u32[]{:S(2)}) collective-permute-start(bf16[274,4096]{1,0:T(8,128)(2,1)} %concatenate.27), channel_id=1, source_target_pairs={{0,2},{2,4},{4,6},{6,8},{8,10},{10,12},{12,14},{14,16},{16,18},{18... | collective-permute-start | bytes 6733832 | tf_op jit(solution)/shard_map/ppermute | solution.py:19
  25.6 25.0 %copy-start.6 = (bf16[128,4096]{0,1:T(8,128)(2,1)}, bf16[128,4096]{0,1:T(8,128)(2,1)S(1)}, u32[]{:S(2)}) copy-start(bf16[128,4096]{0,1:T(8,128)(2,1)S(1)} %copy.62) | copy-start | bytes 3145732
  33.4 28.7 %copy-start.18 = (f32[1,1,4096]{2,1,0:T(1,128)}, f32[1,1,4096]{2,1,0:T(1,128)S(1)}, u32[]{:S(2)}) copy-start(f32[1,1,4096]{2,1,0:T(1,128)S(1)} %get-tuple-element.42) | copy-start | bytes 49156
  33.4 28.7 %copy-start.20 = (f32[1,1,4096]{2,1,0:T(1,128)}, f32[1,1,4096]{2,1,0:T(1,128)S(1)}, u32[]{:S(2)}) copy-start(f32[1,1,4096]{2,1,0:T(1,128)S(1)} %get-tuple-element.54) | copy-start | bytes 49156
  33.4 28.8 %copy-start.22 = (f32[1,1,4096]{2,1,0:T(1,128)}, f32[1,1,4096]{2,1,0:T(1,128)S(1)}, u32[]{:S(2)}) copy-start(f32[1,1,4096]{2,1,0:T(1,128)S(1)} %get-tuple-element.55) | copy-start | bytes 49156
  33.4 28.8 %copy-start.24 = (f32[1,1,4096]{2,1,0:T(1,128)}, f32[1,1,4096]{2,1,0:T(1,128)S(1)}, u32[]{:S(2)}) copy-start(f32[1,1,4096]{2,1,0:T(1,128)S(1)} %get-tuple-element.56) | copy-start | bytes 49156
  33.4 28.8 %copy-start.26 = (f32[1,1,4096]{2,1,0:T(1,128)}, f32[1,1,4096]{2,1,0:T(1,128)S(1)}, u32[]{:S(2)}) copy-start(f32[1,1,4096]{2,1,0:T(1,128)S(1)} %get-tuple-element.57) | copy-start | bytes 49156
  51.5 10.7 %copy-start.7 = (f32[128,4096]{0,1:T(8,128)S(1)}, f32[128,4096]{0,1:T(8,128)}, u32[]{:S(2)}) copy-start(f32[128,4096]{0,1:T(8,128)} %convert_element_type.92) | copy-start | bytes 6291460
  51.5 10.7 %copy-start.8 = (f32[128,4096]{0,1:T(8,128)S(1)}, f32[128,4096]{0,1:T(8,128)}, u32[]{:S(2)}) copy-start(f32[128,4096]{0,1:T(8,128)} %convert_element_type.94) | copy-start | bytes 6291460
  104.7 188.1 %all-to-all-start = ((f32[3,4096,128]{2,0,1:T(4,128)}), f32[3,4096,128]{2,0,1:T(4,128)}, u32[]{:S(2)}, u32[]{:S(2)}) async-start(f32[3,4096,128]{2,0,1:T(4,128)} %copy.68), calls=%async_computation | async-start | bytes 16777216 | tf_op jit(solution)/shard_map/all_to_all | solution.py:99
  336.7 24.0 %copy-start.3 = (f32[3,256,32,128]{3,2,1,0:T(8,128)S(1)}, f32[3,256,32,128]{3,2,1,0:T(8,128)}, u32[]{:S(2)}) copy-start(f32[3,256,32,128]{3,2,1,0:T(8,128)} %get-tuple-element.24) | copy-start | bytes 37748740
  336.7 46.4 %slice-start = ((s8[12582912]{0:T(1024)(128)(4,1)}), s8[4194304]{0:T(1024)(128)(4,1)S(1)}, s32[]{:S(2)}) async-start(s8[12582912]{0:T(1024)(128)(4,1)} %bitcast.151), calls=%async_computation.2 | async-start | bytes 8388608
  336.7 46.4 %slice-start.1 = ((s8[12582912]{0:T(1024)(128)(4,1)}), s8[4194304]{0:T(1024)(128)(4,1)S(1)}, s32[]{:S(2)}) async-start(s8[12582912]{0:T(1024)(128)(4,1)} %bitcast.151), calls=%async_computation.3 | async-start | bytes 8388608
  360.7 22.4 %slice-start.2 = ((s8[12582912]{0:T(1024)(128)(4,1)}), s8[4194304]{0:T(1024)(128)(4,1)S(1)}, s32[]{:S(2)}) async-start(s8[12582912]{0:T(1024)(128)(4,1)} %bitcast.151), calls=%async_computation.4 | async-start | bytes 8388608
  457.5 22.9 %copy-start.1 = (f32[3,256,32,128]{3,1,2,0:T(8,128)S(1)}, f32[3,256,32,128]{3,1,2,0:T(8,128)}, u32[]{:S(2)}) copy-start(f32[3,256,32,128]{3,1,2,0:T(8,128)} %pad_maximum_fusion.1) | copy-start | bytes 37748740
  480.3 18.4 %copy-start.4 = (f32[1,256,32,128]{3,1,2,0:T(8,128)S(1)}, f32[1,256,32,128]{3,1,2,0:T(8,128)}, u32[]{:S(2)}) copy-start(f32[1,256,32,128]{3,1,2,0:T(8,128)} %get-tuple-element.25) | copy-start | bytes 12582916
  508.1 22.7 %copy-start.2 = (f32[3,256,32,128]{3,1,2,0:T(8,128)S(1)}, f32[3,256,32,128]{3,1,2,0:T(8,128)}, u32[]{:S(2)}) copy-start(f32[3,256,32,128]{3,1,2,0:T(8,128)} %pad_maximum_fusion) | copy-start | bytes 37748740
  508.1 41.0 %slice-start.3 = ((s8[12582912]{0:T(1024)(128)(4,1)}), s8[4194304]{0:T(1024)(128)(4,1)S(1)}, s32[]{:S(2)}) async-start(s8[12582912]{0:T(1024)(128)(4,1)} %bitcast.153), calls=%async_computation.5 | async-start | bytes 8388608
  508.1 41.0 %slice-start.4 = ((s8[12582912]{0:T(1024)(128)(4,1)}), s8[4194304]{0:T(1024)(128)(4,1)S(1)}, s32[]{:S(2)}) async-start(s8[12582912]{0:T(1024)(128)(4,1)} %bitcast.153), calls=%async_computation.6 | async-start | bytes 8388608
  530.8 18.4 %slice-start.5 = ((s8[12582912]{0:T(1024)(128)(4,1)}), s8[4194304]{0:T(1024)(128)(4,1)S(1)}, s32[]{:S(2)}) async-start(s8[12582912]{0:T(1024)(128)(4,1)} %bitcast.153), calls=%async_computation.7 | async-start | bytes 8388608
  598.4 187.6 %all-to-all-start.1 = ((f32[3,256,2048]{1,0,2:T(4,128)}), f32[3,256,2048]{1,0,2:T(4,128)}, u32[]{:S(2)}, u32[]{:S(2)}) async-start(f32[3,256,2048]{1,0,2:T(4,128)} %bitcast.155), calls=%async_computation.1 | async-start | bytes 16777216 | tf_op jit(solution)/shard_map/all_to_all | solution.py:133
  857.8 5.7 collective-permute-start.1
  886.5 18.6 %copy-start.10 = (f32[6,4096]{0,1:T(8,128)S(1)}, f32[6,4096]{0,1:T(8,128)}, u32[]{:S(2)}) copy-start(f32[6,4096]{0,1:T(8,128)} %get-tuple-element.32) | copy-start | bytes 294916
  886.5 18.6 %copy-start.19 = (f32[1,1,4096]{2,1,0:T(1,128)S(1)}, f32[1,1,4096]{2,1,0:T(1,128)}, u32[]{:S(2)}) copy-start(f32[1,1,4096]{2,1,0:T(1,128)} %copy-done.18) | copy-start | bytes 49156
  886.5 18.6 %copy-start.21 = (f32[1,1,4096]{2,1,0:T(1,128)S(1)}, f32[1,1,4096]{2,1,0:T(1,128)}, u32[]{:S(2)}) copy-start(f32[1,1,4096]{2,1,0:T(1,128)} %copy-done.20) | copy-start | bytes 49156
  886.5 18.6 %copy-start.23 = (f32[1,1,4096]{2,1,0:T(1,128)S(1)}, f32[1,1,4096]{2,1,0:T(1,128)}, u32[]{:S(2)}) copy-start(f32[1,1,4096]{2,1,0:T(1,128)} %copy-done.22) | copy-start | bytes 49156
  886.5 18.6 %copy-start.25 = (f32[1,1,4096]{2,1,0:T(1,128)S(1)}, f32[1,1,4096]{2,1,0:T(1,128)}, u32[]{:S(2)}) copy-start(f32[1,1,4096]{2,1,0:T(1,128)} %copy-done.24) | copy-start | bytes 49156
  886.5 18.6 %copy-start.27 = (f32[1,1,4096]{2,1,0:T(1,128)S(1)}, f32[1,1,4096]{2,1,0:T(1,128)}, u32[]{:S(2)}) copy-start(f32[1,1,4096]{2,1,0:T(1,128)} %copy-done.26) | copy-start | bytes 49156
  886.5 18.6 %copy-start.29 = (f32[1,1,4096]{2,1,0:T(1,128)S(1)}, f32[1,1,4096]{2,1,0:T(1,128)}, u32[]{:S(2)}) copy-start(f32[1,1,4096]{2,1,0:T(1,128)} %get-tuple-element.58) | copy-start | bytes 49156
  886.5 18.6 %copy-start.31 = (f32[1,1,4096]{2,1,0:T(1,128)S(1)}, f32[1,1,4096]{2,1,0:T(1,128)}, u32[]{:S(2)}) copy-start(f32[1,1,4096]{2,1,0:T(1,128)} %get-tuple-element.59) | copy-start | bytes 49156
  (39 other events, 164.9 us)
where the time goes:
time: 935 us; the launch traced here: 921 us
  waiting for transfers between devices  367 us (39%)
  matrix products  263 us (28%)
  other arithmetic  135 us (14%)
  local copies, waits for them, and re-layouts  99.6 us (11%)
  blocking collectives  38.9 us (4%)
  starting transfers between devices  15.1 us (2%)
    all_to_all x1, waiting for transfers between devices, channel_conv(): lax.all_to_all(flipped, 'ctx', split_axis=1, concat_axis=2, tiled=True)  182 us
    all_to_all x1, waiting for transfers between devices, channel_conv(): lax.all_to_all(signal, 'ctx', split_axis=2, concat_axis=1, tiled=True)  167 us
    psum x1, blocking collectives, on_device(): squares = lax.psum(jnp.sum(raw_grad * raw_grad), ('ctx', 'tp'))  38.9 us
    another operation x2, other arithmetic, on_device(): stacked = jnp.stack([mixed, channel_filter, grad_conv])  33.6 us
    dot_general x1, matrix products, channel_conv(): real_part = jnp.einsum('ka,scab->sckb', cos_first, whole, precision=HIGHEST)  25.2 us
    dot_general x1, matrix products, channel_conv(): jnp.einsum('kb,scjb->scjk', cos_rows, twist_imag, precision=HIGHEST)  24 us
    dot_general x1, matrix products, channel_conv(): jnp.einsum('kb,scjb->scjk', cos_rows, twist_real, precision=HIGHEST)  23.4 us
    dot_general x1, matrix products, channel_conv(): jnp.einsum('ak,sckb->scab', cos_last, turn_real, precision=HIGHEST)  23.2 us
  transfers between devices with their start and end apart: 4, of which 4 were waited for; matrix products, arithmetic and copies ran while one was open for 3% of the time, Pallas kernels for 0%

commit v1 on v0

v1 whole, which is shorter than its diff:
```python
import functools
import math

import jax
import jax.numpy as jnp
from jax import lax
from jax.experimental import pallas as pl
from jax.experimental.pallas import tpu as pltpu
from jax.sharding import PartitionSpec as P

HEAD_DIM = 128
LANES = 128
EDGE = 8
F32 = jnp.float32
BF16 = jnp.bfloat16
VMEM_BYTES = 40 * 1024 * 1024


def params():
    return pltpu.CompilerParams(vmem_limit_bytes=VMEM_BYTES)


def shifted(block, axis, distance):
    devices = range(lax.axis_size(axis))
    route = [(i - distance, i) for i in devices if i - distance in devices]
    return lax.ppermute(block, axis, route)


def round_up(value, step):
    return -(-value // step) * step


def attend_kernel(place_ref, q_ref, k_ref, v_ref, kp_ref, vp_ref, out_ref):
    rows = q_ref.shape[0]
    row = lax.broadcasted_iota(jnp.int32, (rows, rows), 0)
    col = lax.broadcasted_iota(jnp.int32, (rows, rows), 1)
    own_ok = col <= row
    prev_ok = jnp.broadcast_to(place_ref[0], (rows, rows)) > 0
    contract = (((1,), (1,)), ((), ()))
    for head in range(q_ref.shape[1] // HEAD_DIM):
        at = slice(head * HEAD_DIM, (head + 1) * HEAD_DIM)
        scale = 1.0 / math.sqrt(HEAD_DIM)
        query = q_ref[:, at]
        own = lax.dot_general(query, k_ref[:, at], contract, preferred_element_type=F32) * scale
        prev = lax.dot_general(query, kp_ref[:, at], contract, preferred_element_type=F32) * scale
        own = jnp.where(own_ok, own, -jnp.inf)
        prev = jnp.where(prev_ok, prev, -jnp.inf)
        largest = jnp.max(jnp.maximum(own, prev), axis=1, keepdims=True)
        own = jnp.exp(own - largest)
        prev = jnp.exp(prev - largest)
        total = jnp.sum(own + prev, axis=1, keepdims=True)
        inverse = 1.0 / total
        own = (own * inverse).astype(BF16)
        prev = (prev * inverse).astype(BF16)
        mixed = jnp.dot(own, v_ref[:, at], preferred_element_type=F32) + jnp.dot(
            prev, vp_ref[:, at], preferred_element_type=F32
        )
        out_ref[:, at] = mixed.astype(BF16)


def attend(query, key, value, key_prev, value_prev, position):
    rows, channels = query.shape
    tile = min(512, channels)
    block = pl.BlockSpec((rows, tile), lambda i: (0, i))
    heads = channels // HEAD_DIM
    return pl.pallas_call(
        attend_kernel,
        grid=(channels // tile,),
        in_specs=[pl.BlockSpec(memory_space=pltpu.SMEM)] + [block] * 5,
        out_specs=block,
        out_shape=jax.ShapeDtypeStruct((rows, channels), BF16),
        compiler_params=params(),
        cost_estimate=pl.CostEstimate(
            flops=8 * heads * rows * rows * HEAD_DIM,
            bytes_accessed=12 * rows * channels,
            transcendentals=2 * heads * rows * rows,
        ),
        name="attend",
    )(position.astype(jnp.int32).reshape(1), query, key, value, key_prev, value_prev)


def taps_causal(ext_ref, before, signal, filter_taps):
    rows = signal.shape[0]
    ext_ref[0:EDGE, :] = before
    ext_ref[EDGE : EDGE + rows, :] = signal
    total = filter_taps[0:1] * signal
    for s in range(1, filter_taps.shape[0]):
        total = total + filter_taps[s : s + 1] * ext_ref[EDGE - s : EDGE - s + rows, :]
    return total


def before_kernel(
    cpd, gpd, q_ref, k_ref, v_ref, og_ref, tail_ref, taps_ref, long_ref, send_ref, sk_ref, sv_ref,
    long_rows, ext_q, ext_k, ext_v,
):
    step = pl.program_id(0)
    groups = long_ref.shape[1]
    per_tile, _, rows = send_ref.shape

    @pl.when(step == 0)
    def _():
        long_rows[...] = jnp.zeros_like(long_rows)
        long_rows[0:groups, :] = long_ref[...].T

    for j in range(q_ref.shape[1] // LANES):
        at = slice(j * LANES, (j + 1) * LANES)
        tail = tail_ref[:, at].astype(F32)
        short_q = taps_causal(ext_q.at[j], tail[0:EDGE], q_ref[:, at].astype(F32), taps_ref[0, :, at])
        short_k = taps_causal(
            ext_k.at[j], tail[EDGE : 2 * EDGE], k_ref[:, at].astype(F32), taps_ref[1, :, at]
        )
        short_v = taps_causal(
            ext_v.at[j], tail[2 * EDGE : 3 * EDGE], v_ref[:, at].astype(F32), taps_ref[2, :, at]
        )
        sk_ref[:, at] = short_k
        sv_ref[:, at] = short_v
        mixed = (short_k * short_v).T.astype(BF16)
        delta = (og_ref[:, at].astype(F32) * short_q).T.astype(BF16)
        width = min(cpd, LANES)
        for piece in range(LANES // width):
            channel = j * LANES + piece * width
            dest, low = channel // cpd, channel % cpd
            rows_at = slice(piece * width, (piece + 1) * width)
            send_ref[dest, low : low + width, :] = mixed[rows_at]
            send_ref[dest, cpd + low : cpd + low + width, :] = delta[rows_at]
    filter_rows = send_ref.shape[1] - 2 * cpd
    for dest in range(per_tile):
        first = (step * per_tile + dest) * gpd
        send_ref[dest, 2 * cpd :, :] = long_rows[pl.ds(first, filter_rows), :].astype(BF16)


def before_exchange(query, key, value, out_grad, tail, taps, long_filter, n):
    rows, channels = query.shape
    groups = long_filter.shape[1]
    cpd, gpd = channels // n, groups // n
    tile = min(channels, max(512, cpd))
    per_tile = tile // cpd
    filter_rows = round_up(gpd, 16)
    send_rows = 2 * cpd + filter_rows
    block = pl.BlockSpec((rows, tile), lambda i: (0, i))
    ext = pltpu.VMEM((tile // LANES, rows + EDGE, LANES), F32)
    return pl.pallas_call(
        functools.partial(before_kernel, cpd, gpd),
        grid=(channels // tile,),
        in_specs=[block] * 4
        + [
            pl.BlockSpec((3 * EDGE, tile), lambda i: (0, i)),
            pl.BlockSpec((3, taps.shape[1], tile), lambda i: (0, 0, i)),
            pl.BlockSpec((rows, groups), lambda i: (0, 0)),
        ],
        out_specs=[pl.BlockSpec((per_tile, send_rows, rows), lambda i: (i, 0, 0)), block, block],
        out_shape=[
            jax.ShapeDtypeStruct((n, send_rows, rows), BF16),
            jax.ShapeDtypeStruct((rows, channels), F32),
            jax.ShapeDtypeStruct((rows, channels), F32),
        ],
        scratch_shapes=[pltpu.VMEM((round_up(groups, 8) + filter_rows, rows), F32), ext, ext, ext],
        compiler_params=params(),
        cost_estimate=pl.CostEstimate(
            flops=50 * rows * channels, bytes_accessed=20 * rows * channels, transcendentals=0
        ),
        name="before_exchange",
    )(query, key, value, out_grad, tail, taps, long_filter)


def long_kernel(cpd, gpd, in_ref, out_ref, taps, wide, gram, raw):
    n, send_rows, rows = in_ref.shape
    gw = cpd // gpd
    span = n * rows
    filter_rows = send_rows - 2 * cpd
    for a in range(n):
        taps[:, a * rows : (a + 1) * rows] = in_ref[a, 2 * cpd :, :].astype(F32)
    if gpd < filter_rows:
        raw[...] = jnp.zeros_like(raw)
    row8 = lax.broadcasted_iota(jnp.int32, (8, span), 0)
    row_tile = lax.broadcasted_iota(jnp.int32, (8, rows), 0)
    lane_tile = lax.broadcasted_iota(jnp.int32, (8, rows), 1)
    no_rows = jnp.zeros((gw, rows), BF16)

    def keep_upper(block, first):
        head = jnp.where(lane_tile >= row_tile + first, block[:, :rows], 0.0)
        return jnp.concatenate([head, block[:, rows:]], 1)

    def one_group(g, slot):
        base = jnp.broadcast_to(taps[pl.ds(g, 1), :], (8, span))
        for bit in (1, 2, 4):
            base = jnp.where((row8 & bit) != 0, pltpu.roll(base, bit, 1), base)
        for m in range(0, rows // 8, 2):
            low = base if m == 0 else pltpu.roll(base, 8 * m, 1)
            high = pltpu.roll(base, 8 * m + 8, 1)
            pair = jnp.concatenate([keep_upper(low, 8 * m), keep_upper(high, 8 * m + 8)], 0)
            wide[slot, 8 * m : 8 * m + 16, :] = pair.astype(BF16)
        first = pl.multiple_of(g * gw, gw)
        x = in_ref[:, pl.ds(first, gw), :].reshape(n * gw, rows)
        second = pl.multiple_of(cpd + g * gw, gw)
        d = in_ref[:, pl.ds(second, gw), :].reshape(n * gw, rows)
        x_turned = x.astype(F32).T.astype(BF16)
        conv = None
        back = None
        for k in range(0, n, 2):
            count = (n - k) * gw
            at = slice(k * rows, (k + 2) * rows)
            ahead = jnp.concatenate([no_rows, x[: count - gw]], 0)
            stacked = jnp.concatenate(
                [
                    wide[slot, :, k * rows : (k + 1) * rows],
                    wide[slot, :, (k + 1) * rows : (k + 2) * rows],
                ],
                0,
            )
            part = jnp.dot(
                jnp.concatenate([x[:count], ahead], 1), stacked, preferred_element_type=F32
            )
            conv = part if k == 0 else jnp.concatenate([conv[: k * gw], conv[k * gw :] + part], 0)
            later = jnp.concatenate([d[(k + 1) * gw :], no_rows], 0)
            pairs = jnp.concatenate([d[k * gw :], later], 1)
            part = lax.dot_general(
                pairs, wide[slot, :, at], (((1,), (1,)), ((), ())), preferred_element_type=F32
            )
            back = part if k == 0 else jnp.concatenate([back[:count] + part, back[count:]], 0)
            if k > 0:
                pairs = jnp.concatenate([pairs, jnp.zeros((k * gw, 2 * rows), BF16)], 0)
            gram[slot, :, at] = jnp.dot(x_turned, pairs, preferred_element_type=F32)
        out_ref[:, pl.ds(first, gw), :] = conv.astype(BF16).reshape(n, gw, rows)
        out_ref[:, pl.ds(second, gw), :] = back.astype(BF16).reshape(n, gw, rows)
        total = keep_upper(gram[slot, 0:8, :], 0)
        for m in range(1, rows // 8):
            block = keep_upper(gram[slot, 8 * m : 8 * m + 8, :], 8 * m)
            total = total + pltpu.roll(block, span - 8 * m, 1)
        for bit in (1, 2, 4):
            total = jnp.where((row8 & bit) != 0, pltpu.roll(total, span - bit, 1), total)
        line = jnp.sum(total, axis=0, keepdims=True)
        raw[pl.ds(g, 1), :] = line
        return line * line

    def body(i, squares):
        squares = squares + one_group(2 * i, 0)
        return squares + one_group(2 * i + 1, 1)

    squares = lax.fori_loop(0, gpd // 2, body, jnp.zeros((1, span), F32))
    total = jnp.sum(squares, axis=1, keepdims=True)
    upper = total.astype(BF16).astype(F32)
    lower = total - upper
    for a in range(n):
        out_ref[a, 2 * cpd : 2 * cpd + filter_rows, :] = raw[:, a * rows : (a + 1) * rows].astype(BF16)
    halo_at = 2 * cpd + filter_rows
    row = lax.broadcasted_iota(jnp.int32, (2 * EDGE, 2 * rows), 0)
    lane = lax.broadcasted_iota(jnp.int32, (2 * EDGE, 2 * rows), 1)
    wanted = jnp.where(row < EDGE, row, rows - EDGE + row)
    pick = jnp.where(lane == wanted, 1.0, 0.0).astype(BF16)
    row_out = lax.broadcasted_iota(jnp.int32, (2 * EDGE, rows), 0)
    for a in range(n):
        if a + 1 < n:
            results = jnp.concatenate([out_ref[a + 1, 0:cpd, :], out_ref[a + 1, cpd : 2 * cpd, :]], 1)
            halo = lax.dot_general(
                pick, results, (((1,), (1,)), ((), ())), preferred_element_type=F32
            )
            if cpd < LANES:
                halo = jnp.concatenate([halo, jnp.zeros((2 * EDGE, LANES - cpd), F32)], 1)
        else:
            halo = jnp.zeros((2 * EDGE, max(cpd, LANES)), F32)
        for j in range(halo.shape[1] // LANES):
            tile = halo[:, j * LANES : (j + 1) * LANES]
            tile = jnp.where(row_out == EDGE - 2, upper, jnp.where(row_out == EDGE - 1, lower, tile))
            at = halo_at + 2 * EDGE * j
            out_ref[a, at : at + 2 * EDGE, :] = tile.astype(BF16)


def long_products(received, cpd, gpd):
    n, send_rows, rows = received.shape
    filter_rows = send_rows - 2 * cpd
    out_rows = send_rows + 2 * EDGE * max(1, cpd // LANES)
    span = n * rows
    return pl.pallas_call(
        functools.partial(long_kernel, cpd, gpd),
        in_specs=[pl.BlockSpec(memory_space=pltpu.VMEM)],
        out_specs=pl.BlockSpec(memory_space=pltpu.VMEM),
        out_shape=jax.ShapeDtypeStruct((n, out_rows, rows), BF16),
        scratch_shapes=[
            pltpu.VMEM((filter_rows, span), F32),
            pltpu.VMEM((2, rows, span), BF16),
            pltpu.VMEM((2, rows, span), F32),
            pltpu.VMEM((filter_rows, span), F32),
        ],
        compiler_params=params(),
        cost_estimate=pl.CostEstimate(
            flops=6 * cpd * span * span, bytes_accessed=4 * n * out_rows * rows, transcendentals=0
        ),
        name="long_products",
    )(received)


def taps_anti(ext_ref, signal, after, filter_taps):
    rows = signal.shape[0]
    ext_ref[0:rows, :] = signal
    ext_ref[rows : rows + EDGE, :] = after
    total = filter_taps[0:1] * signal
    for s in range(1, filter_taps.shape[0]):
        total = total + filter_taps[s : s + 1] * ext_ref[s : s + rows, :]
    return total


def short_edge(before, signal, filter_taps):
    both = jnp.concatenate([before, signal], 0)
    total = filter_taps[0:1] * signal
    for s in range(1, filter_taps.shape[0]):
        total = total + filter_taps[s : s + 1] * both[EDGE - s : 2 * EDGE - s]
    return total


def after_kernel(
    cpd, gpd, in_ref, og_ref, sk_ref, sv_ref, k_end, v_end, next_ref, taps_ref,
    dq_ref, dk_ref, dv_ref, raw_ref, raw_rows, ext_q, ext_k, ext_v,
):
    step = pl.program_id(0)
    per_tile, in_rows, rows = in_ref.shape
    groups = raw_ref.shape[1]
    halo_rows = 2 * EDGE * max(1, cpd // LANES)
    halo_at = in_rows - halo_rows
    end_rows = k_end.shape[0]
    for j in range(og_ref.shape[1] // LANES):
        at = slice(j * LANES, (j + 1) * LANES)
        if cpd >= LANES:
            dest, low = j * LANES // cpd, j * LANES % cpd
            conv = in_ref[dest, low : low + LANES, :]
            back = in_ref[dest, cpd + low : cpd + low + LANES, :]
            edge = halo_at + 2 * EDGE * (low // LANES)
            halo = in_ref[dest, edge : edge + 2 * EDGE, :].astype(F32)
        else:
            dests = range(j * LANES // cpd, (j + 1) * LANES // cpd)
            conv = jnp.concatenate([in_ref[d, 0:cpd, :] for d in dests], 0)
            back = jnp.concatenate([in_ref[d, cpd : 2 * cpd, :] for d in dests], 0)
            halo = jnp.concatenate(
                [in_ref[d, halo_at:, :].astype(F32)[:, :cpd] for d in dests], 1
            )
        conv = conv.astype(F32).T
        back = back.astype(F32).T
        following = next_ref[:, at].astype(F32)
        taps_k = taps_ref[1, :, at]
        taps_v = taps_ref[2, :, at]
        next_k = short_edge(
            k_end[:, at].astype(F32)[end_rows - EDGE :], following[EDGE : 2 * EDGE], taps_k
        )
        next_v = short_edge(
            v_end[:, at].astype(F32)[end_rows - EDGE :], following[2 * EDGE : 3 * EDGE], taps_v
        )
        grad_q = og_ref[:, at].astype(F32) * conv
        dq_ref[:, at] = taps_anti(
            ext_q.at[j], grad_q, following[0:EDGE] * halo[0:EDGE], taps_ref[0, :, at]
        ).astype(BF16)
        dk_ref[:, at] = taps_anti(
            ext_k.at[j], back * sv_ref[:, at], halo[EDGE:] * next_v, taps_k
        ).astype(BF16)
        dv_ref[:, at] = taps_anti(
            ext_v.at[j], back * sk_ref[:, at], halo[EDGE:] * next_k, taps_v
        ).astype(BF16)
    for dest in range(per_tile):
        lines = in_ref[dest, 2 * cpd : halo_at, :].astype(F32)
        raw_rows[pl.ds((step * per_tile + dest) * gpd, gpd), :] = lines[:gpd]

    @pl.when(step == pl.num_programs(0) - 1)
    def _():
        raw_ref[...] = raw_rows[...].T


def after_exchange(returned, out_grad, short_k, short_v, key, value, following, taps, groups):
    n, in_rows, rows = returned.shape
    channels = out_grad.shape[1]
    cpd, gpd = channels // n, groups // n
    tile = min(channels, max(512, cpd))
    per_tile = tile // cpd
    block = pl.BlockSpec((rows, tile), lambda i: (0, i))
    end = pl.BlockSpec((16, tile), lambda i: (rows // 16 - 1, i))
    ext = pltpu.VMEM((tile // LANES, rows + EDGE, LANES), F32)
    grad = jax.ShapeDtypeStruct((rows, channels), BF16)
    return pl.pallas_call(
        functools.partial(after_kernel, cpd, gpd),
        grid=(channels // tile,),
        in_specs=[
            pl.BlockSpec((per_tile, in_rows, rows), lambda i: (i, 0, 0)),
            block,
            block,
            block,
            end,
            end,
            pl.BlockSpec((3 * EDGE, tile), lambda i: (0, i)),
            pl.BlockSpec((3, taps.shape[1], tile), lambda i: (0, 0, i)),
        ],
        out_specs=[block, block, block, pl.BlockSpec((rows, groups), lambda i: (0, 0))],
        out_shape=[grad, grad, grad, jax.ShapeDtypeStruct((rows, groups), F32)],
        scratch_shapes=[pltpu.VMEM((groups, rows), F32), ext, ext, ext],
        compiler_params=params(),
        cost_estimate=pl.CostEstimate(
            flops=60 * rows * channels, bytes_accessed=22 * rows * channels, transcendentals=0
        ),
        name="after_exchange",
    )(returned, out_grad, short_k, short_v, key, value, following, taps)


def on_device(
    query_heads,
    key_heads,
    value_heads,
    hyena_query,
    hyena_key,
    hyena_value,
    short_filter,
    long_filter,
    output_grad,
):
    rows, channels = query_heads.shape
    groups = long_filter.shape[1]
    n = lax.axis_size("ctx")
    tp = lax.axis_size("tp")
    cpd, gpd = channels // n, groups // n
    position = lax.axis_index("ctx")
    tail = shifted(
        jnp.concatenate([a[rows - EDGE :] for a in (hyena_query, hyena_key, hyena_value)], 0), "ctx", 1
    )
    key_prev = shifted(key_heads, "ctx", 1)
    value_prev = shifted(value_heads, "ctx", 1)
    following = shifted(
        jnp.concatenate([a[:EDGE] for a in (output_grad, hyena_key, hyena_value)], 0), "ctx", -1
    )
    send, short_k, short_v = before_exchange(
        hyena_query, hyena_key, hyena_value, output_grad, tail, short_filter, long_filter, n
    )
    received = lax.all_to_all(send, "ctx", split_axis=0, concat_axis=0, tiled=True)
    attention = attend(query_heads, key_heads, value_heads, key_prev, value_prev, position)
    results = long_products(received, cpd, gpd)
    returned = lax.all_to_all(results, "ctx", split_axis=0, concat_axis=0, tiled=True)
    norm_at = returned.shape[1] - 2 * EDGE * max(1, cpd // LANES) + EDGE - 2
    own_squares = jnp.sum(returned[:, norm_at : norm_at + 2, 0].astype(F32)).reshape(1, 1)
    squares = own_squares
    for distance in range(1, tp):
        route = [(i, (i + distance) % tp) for i in range(tp)]
        squares = squares + lax.ppermute(own_squares, "tp", route)
    query_grad, key_grad, value_grad, raw_grad = after_exchange(
        returned, output_grad, short_k, short_v, hyena_key, hyena_value, following, short_filter, groups
    )
    bound = math.sqrt(rows * n * groups * tp)
    factor = jnp.minimum(1.0, bound / jnp.sqrt(squares))
    return (attention, query_grad, key_grad, value_grad, raw_grad * factor)


def solution(mesh):
    whole = P("ctx", "tp")
    in_specs = (whole,) * 6 + (P(None, None, "tp"), whole, whole)
    return jax.shard_map(
        on_device, mesh=mesh, in_specs=in_specs, out_specs=(whole,) * 5, check_vma=False
    )
```

time: 935 us -> 222 us (0.24); the launches traced: 921 us -> 221 us
  waiting for transfers between devices: 367 us -> 71.2 us
  matrix products: 263 us -> 0 us
  other arithmetic: 135 us -> 1.99 us
  local copies, waits for them, and re-layouts: 99.6 us -> 23.1 us
  Pallas kernels: 0 us -> 50.6 us
  blocking collectives: 38.9 us -> 54.1 us
    all_to_all x2 -> x1, waiting for transfers between devices: 349 us -> 0.01 us  [on_device(): lax.all_to_all(results, 'ctx', split_axis=0, concat_axis=0, tiled=True)]
    dot_general x14 -> x0, matrix products: 263 us -> none  [the longest x1 25.2 us: channel_conv(): real_part = jnp.einsum('ka,scab->sckb', cos_first, whole, precision=HIGHEST)]
    another operation x5 -> x0, other arithmetic: 54.5 us -> none  [the longest x2 33.6 us: on_device(): stacked = jnp.stack([mixed, channel_filter, grad_conv])]
    all_to_all x0 -> x1, blocking collectives: none -> 54.1 us  [on_device(): lax.all_to_all(send, 'ctx', split_axis=0, concat_axis=0, tiled=True)]
    ppermute x2 -> x4, waiting for transfers between devices: 17.7 us -> 71.2 us  [shifted(): return lax.ppermute(block, axis, route)]
    convert_element_type x7 -> x0, other arithmetic: 50.7 us -> none  [the longest x1 18.5 us: on_device(): anti_short(grad_short_v, after[2], short_filter[2]).astype(jnp.bfloat16)]
    pallas_call x0 -> x4, Pallas kernels: none -> 50.6 us  [the longest x1 23 us: long_products(): pl.pallas_call(functools.partial(long_kernel, cpd, gpd), in_specs=[pl.Blo...]
    psum x1 -> x0, blocking collectives: 38.9 us -> none  [on_device(): squares = lax.psum(jnp.sum(raw_grad * raw_grad), ('ctx', 'tp'))]
  transfers between devices with their start and end apart: 4 -> 6, of which waited for: 4 -> 3; matrix products, arithmetic and copies ran while one was open for 3% -> 1% of each run, Pallas kernels for 0% -> 10%
where the time goes in v1:
time: 222 us; the launch traced here: 221 us
  waiting for transfers between devices  71.2 us (32%)
  blocking collectives  54.1 us (24%)
  Pallas kernels  50.6 us (23%)
  local copies, waits for them, and re-layouts  23.1 us (10%)
  starting transfers between devices  17.7 us (8%)
    ppermute x4, waiting for transfers between devices, shifted(): return lax.ppermute(block, axis, route)  71.2 us
    all_to_all x1, blocking collectives, on_device(): lax.all_to_all(send, 'ctx', split_axis=0, concat_axis=0, tiled=True)  54.1 us
    pallas_call x1, Pallas kernels, long_products(): pl.pallas_call(functools.partial(long_kernel, cpd, gpd), in_specs=[pl.Blo...  23 us
    unnamed x38, local copies, waits for them, and re-layouts  21.3 us
    pallas_call x1, Pallas kernels, attend(): pl.pallas_call(attend_kernel, grid=(channels // tile,), in_specs=[pl.Bloc...  14.1 us
    ppermute x4, starting transfers between devices, shifted(): return lax.ppermute(block, axis, route)  10.4 us
    pallas_call x1, Pallas kernels, after_exchange(): pl.pallas_call(functools.partial(after_kernel, cpd, gpd), grid=(channels...  7.47 us
    pallas_call x1, Pallas kernels, before_exchange(): pl.pallas_call(functools.partial(before_kernel, cpd, gpd), grid=(channels...  6.03 us
  transfers between devices with their start and end apart: 6, of which 3 were waited for; matrix products, arithmetic and copies ran while one was open for 1% of the time, Pallas kernels for 10%

profile of v1, /device:TPU:16, one launch (start us, length us, event | category | flops | bytes accessed | tf_op | source)
XLA Modules:
  0.0 220.8 jit_solution(13360026555424701702)
XLA Ops:
  1.5 1.0 fusion
  2.5 1.9 collective-permute-start.2
  4.4 6.0 %collective-permute-done.2.tail_ref = bf16[24,4096]{1,0:T(8,128)(2,1)S(1)} collective-permute-done((bf16[24,4096]{1,0:T(8,128)(2,1)S(1)}, bf16[24,4096]{1,0:T(8,128)(2,1)S(1)}, u32[]{:S(2)}, u32[]{:S(2)}) %collective-permute-start.2) | collective-permute-done | bytes 196640 | tf_op jit(solution)/shard_map/ppermute | solution.py:26
  10.3 1.2 copy-done
  11.6 1.2 copy-done.2
  12.8 1.2 copy-done.4
  14.0 1.0 copy-done.11
  15.0 1.2 copy-done.13
  16.2 0.9 copy-done.18
  17.1 6.0 %before_exchange.1 = (bf16[16,528,128]{2,1,0:T(8,128)(2,1)S(1)}, f32[128,4096]{1,0:T(8,128)S(1)}, f32[128,4096]{1,0:T(8,128)S(1)}) custom-call(bf16[128,4096]{1,0:T(8,128)(2,1)S(1)} %copy-done.13, bf16[128,4096]{1,0:T(8,128)(2,1)S(1)} %copy-done, bf16[128,4096]{1,0:T(8,128)(2,1)S(1)} %copy-done.2, bf16[128,4096]{1,0:T(8,128)(2,1)S(1)} %copy-done.4, ...), custom_call_target="tpu_custom_call" | custom-call | flops 26214400 | bytes 10485760 | tf_op jit(solution)/shard_map/before_exchange/pallas_call | solution.py:142
  23.2 1.3 copy-done.7
  24.5 1.4 copy-done.9
  25.9 54.1 %all_to_all.10.in_ref = bf16[16,528,128]{2,1,0:T(8,128)(2,1)S(1)} all-to-all(bf16[16,528,128]{2,1,0:T(8,128)(2,1)S(1)} %get-tuple-element.12), channel_id=1, replica_groups=mesh['ctx'=16,'tp'=2] {'ctx'}, dimensions={0} | all-to-all | bytes 4325376 | tf_op jit(solution)/shard_map/all_to_all | solution.py:428
  80.0 23.0 %long_products.1 = bf16[16,560,128]{2,1,0:T(8,128)(2,1)S(1)} custom-call(bf16[16,528,128]{2,1,0:T(8,128)(2,1)S(1)} %all_to_all.10.in_ref), custom_call_target="tpu_custom_call" | custom-call | flops 6442450944 | bytes 4587520 | tf_op jit(solution)/shard_map/long_products/pallas_call | solution.py:274
  103.0 1.4 copy-done.6
  104.4 5.8 %all-to-all-start.1 = ((bf16[16,560,128]{2,1,0:T(8,128)(2,1)}), bf16[16,560,128]{2,1,0:T(8,128)(2,1)S(1)}, u32[]{:S(2)}, u32[]{:S(2)}) async-start(bf16[16,560,128]{2,1,0:T(8,128)(2,1)} %copy-done.6), calls=%async_computation.1 | async-start | bytes 4587520 | tf_op jit(solution)/shard_map/all_to_all | solution.py:431
  110.2 2.1 collective-permute-start
  112.3 3.4 %collective-permute-start.1 = (bf16[128,4096]{1,0:T(8,128)(2,1)}, bf16[128,4096]{1,0:T(8,128)(2,1)}, u32[]{:S(2)}, u32[]{:S(2)}) collective-permute-start(bf16[128,4096]{1,0:T(8,128)(2,1)} %v_ref.2), channel_id=1, source_target_pairs={{0,2},{2,4},{4,6},{6,8},{8,10},{10,12},{12,14},{14,16},{16,18},{18... | collective-permute-start | bytes 3145736 | tf_op jit(solution)/shard_map/ppermute | solution.py:26
  116.3 3.1 %collective-permute-start.3 = (bf16[24,4096]{1,0:T(8,128)(2,1)}, bf16[24,4096]{1,0:T(8,128)(2,1)S(1)}, u32[]{:S(2)}, u32[]{:S(2)}) collective-permute-start(bf16[24,4096]{1,0:T(8,128)(2,1)} %pad_maximum_fusion.1), channel_id=1, source_target_pairs={{2,0},{4,2},{6,4},{8,6},{10,8},{12,10},{14,12},{16,14},{18,16},{20... | collective-permute-start | bytes 589832 | tf_op jit(solution)/shard_map/ppermute | solution.py:26
  119.4 54.0 %collective-permute-done.kp_ref = bf16[128,4096]{1,0:T(8,128)(2,1)} collective-permute-done((bf16[128,4096]{1,0:T(8,128)(2,1)S(1)}, bf16[128,4096]{1,0:T(8,128)(2,1)}, u32[]{:S(2)}, u32[]{:S(2)}) %collective-permute-start) | collective-permute-done | bytes 1048608 | tf_op jit(solution)/shard_map/ppermute | solution.py:26
  173.4 11.2 %collective-permute-done.1.vp_ref = bf16[128,4096]{1,0:T(8,128)(2,1)} collective-permute-done((bf16[128,4096]{1,0:T(8,128)(2,1)}, bf16[128,4096]{1,0:T(8,128)(2,1)}, u32[]{:S(2)}, u32[]{:S(2)}) %collective-permute-start.1) | collective-permute-done | bytes 1048608 | tf_op jit(solution)/shard_map/ppermute | solution.py:26
  184.7 1.2 copy-done.14
  185.9 1.2 copy-done.16
  187.1 1.2 copy-done.17
  188.3 14.1 %attend.1 = bf16[128,4096]{1,0:T(8,128)(2,1)} custom-call(s32[1]{0:T(128)} %bitcast.place_ref, bf16[128,4096]{1,0:T(8,128)(2,1)S(1)} %copy-done.14, bf16[128,4096]{1,0:T(8,128)(2,1)S(1)} %copy-done.16, bf16[128,4096]{1,0:T(8,128)(2,1)S(1)} %copy-done.17, bf16[128,4096]{1,0:T(8,128)(2,1)} %collective-permute-done.kp_ref, ...), custom_call_target="tpu_custom_call" | custom-call | flops 536870912 | bytes 6291456 | tf_op jit(solution)/shard_map/attend/pallas_call | solution.py:66
  203.1 1.5 collective-permute-start.4
  204.6 1.2 copy-done.3
  205.8 1.2 copy-done.5
  207.1 1.6 copy-done.8
  208.7 1.6 copy-done.10
  210.2 1.0 copy-done.12
  211.2 7.5 %after_exchange.1 = (bf16[128,4096]{1,0:T(8,128)(2,1)}, bf16[128,4096]{1,0:T(8,128)(2,1)}, bf16[128,4096]{1,0:T(8,128)(2,1)}, f32[128,256]{1,0:T(8,128)S(1)}) custom-call(bf16[16,560,128]{2,1,0:T(8,128)(2,1)S(1)} %all-to-all-done.1.in_ref, bf16[128,4096]{1,0:T(8,128)(2,1)S(1)} %copy-done.5, f32[128,4096]{1,0:T(8,128)S(1)} %copy-done.8, ...), custom_call_target="tpu_custom_call" | custom-call | flops 31457280 | bytes 11534336 | tf_op jit(solution)/shard_map/after_exchange/pallas_call | solution.py:376
  (31 shorter events, 2.9 us)
Async XLA Ops:
  2.5 7.9 %collective-permute-start.2 = (bf16[24,4096]{1,0:T(8,128)(2,1)S(1)}, bf16[24,4096]{1,0:T(8,128)(2,1)S(1)}, u32[]{:S(2)}, u32[]{:S(2)}) collective-permute-start(bf16[24,4096]{1,0:T(8,128)(2,1)S(1)} %pad_maximum_fusion), channel_id=1, source_target_pairs={{0,2},{2,4},{4,6},{6,8},{8,10},{10,12},{12,14},{14,16},{16,18},{18... | collective-permute-start | bytes 589832 | tf_op jit(solution)/shard_map/ppermute | solution.py:26
  10.3 1.2 copy-start
  11.6 1.2 copy-start.2
  12.8 1.2 copy-start.4
  14.0 1.0 copy-start.11
  15.0 1.2 copy-start.13
  16.2 0.9 copy-start.18
  23.2 1.3 copy-start.7
  24.5 1.4 copy-start.9
  103.0 1.4 copy-start.6
  104.4 5.8 %copy-start.15 = (bf16[128,4096]{1,0:T(8,128)(2,1)S(1)}, bf16[128,4096]{1,0:T(8,128)(2,1)}, u32[]{:S(2)}) copy-start(bf16[128,4096]{1,0:T(8,128)(2,1)} %k_ref.2) | copy-start | bytes 3145732
  104.4 11.2 %slice-start = ((bf16[128,4096]{1,0:T(8,128)(2,1)}), bf16[8,4096]{1,0:T(8,128)(2,1)S(1)}, s32[]{:S(2)}) async-start(bf16[128,4096]{1,0:T(8,128)(2,1)} %og_ref.3), calls=%async_computation.2 | async-start | bytes 131072 | tf_op jit(solution)/shard_map/slice | solution.py:423
  104.4 98.1 %all-to-all-start.1 = ((bf16[16,560,128]{2,1,0:T(8,128)(2,1)}), bf16[16,560,128]{2,1,0:T(8,128)(2,1)S(1)}, u32[]{:S(2)}, u32[]{:S(2)}) async-start(bf16[16,560,128]{2,1,0:T(8,128)(2,1)} %copy-done.6), calls=%async_computation.1 | async-start | bytes 4587520 | tf_op jit(solution)/shard_map/all_to_all | solution.py:431
  110.2 63.2 %collective-permute-start = (bf16[128,4096]{1,0:T(8,128)(2,1)S(1)}, bf16[128,4096]{1,0:T(8,128)(2,1)}, u32[]{:S(2)}, u32[]{:S(2)}) collective-permute-start(bf16[128,4096]{1,0:T(8,128)(2,1)S(1)} %copy-done.15), channel_id=1, source_target_pairs={{0,2},{2,4},{4,6},{6,8},{8,10},{10,12},{12,14},{14,16},{16,18},{18... | collective-permute-start | bytes 3145736 | tf_op jit(solution)/shard_map/ppermute | solution.py:26
  112.3 72.4 %collective-permute-start.1 = (bf16[128,4096]{1,0:T(8,128)(2,1)}, bf16[128,4096]{1,0:T(8,128)(2,1)}, u32[]{:S(2)}, u32[]{:S(2)}) collective-permute-start(bf16[128,4096]{1,0:T(8,128)(2,1)} %v_ref.2), channel_id=1, source_target_pairs={{0,2},{2,4},{4,6},{6,8},{8,10},{10,12},{12,14},{14,16},{16,18},{18... | collective-permute-start | bytes 3145736 | tf_op jit(solution)/shard_map/ppermute | solution.py:26
  116.3 88.3 %collective-permute-start.3 = (bf16[24,4096]{1,0:T(8,128)(2,1)}, bf16[24,4096]{1,0:T(8,128)(2,1)S(1)}, u32[]{:S(2)}, u32[]{:S(2)}) collective-permute-start(bf16[24,4096]{1,0:T(8,128)(2,1)} %pad_maximum_fusion.1), channel_id=1, source_target_pairs={{2,0},{4,2},{6,4},{8,6},{10,8},{12,10},{14,12},{16,14},{18,16},{20... | collective-permute-start | bytes 589832 | tf_op jit(solution)/shard_map/ppermute | solution.py:26
  184.7 1.2 copy-start.14
  185.9 1.2 copy-start.16
  187.1 1.2 copy-start.17
  188.3 16.3 %copy-start.1 = (bf16[128,4096]{1,0:T(8,128)(2,1)S(1)}, bf16[128,4096]{1,0:T(8,128)(2,1)}, u32[]{:S(2)}) copy-start(bf16[128,4096]{1,0:T(8,128)(2,1)} %k_end.1) | copy-start | bytes 3145732
  203.1 15.6 %collective-permute-start.4 = (f32[1,1]{1,0:T(1,128)}, f32[1,1]{1,0:T(1,128)}, u32[]{:S(2)}, u32[]{:S(2)}) collective-permute-start(f32[1,1]{1,0:T(1,128)} %bitcast.1), channel_id=1, source_target_pairs={{0,1},{1,0},{2,3},{3,2},{4,5},{5,4},{6,7},{7,6},{8,9},{9,8},{10,11... | collective-permute-start | bytes 20 | tf_op jit(solution)/shard_map/ppermute | solution.py:437
  204.6 1.2 copy-start.3
  205.8 1.2 copy-start.5
  207.1 1.6 copy-start.8
  208.6 1.6 copy-start.10
  210.2 1.0 copy-start.12

commit v2 on v1

--- a/solution.py
+++ b/solution.py
@@ -13,7 +13,7 @@
 EDGE = 8
 F32 = jnp.float32
 BF16 = jnp.bfloat16
-VMEM_BYTES = 40 * 1024 * 1024
+VMEM_BYTES = 60 * 1024 * 1024
 
 
 def params():
@@ -129,26 +129,29 @@
         send_ref[dest, 2 * cpd :, :] = long_rows[pl.ds(first, filter_rows), :].astype(BF16)
 
 
-def before_exchange(query, key, value, out_grad, tail, taps, long_filter, n):
-    rows, channels = query.shape
-    groups = long_filter.shape[1]
+def before_exchange(query, key, value, out_grad, tail, taps, long_filter, n, chunk, chunks):
+    rows = query.shape[0]
+    channels = query.shape[1] // chunks
+    groups = long_filter.shape[1] // chunks
     cpd, gpd = channels // n, groups // n
     tile = min(channels, max(512, cpd))
     per_tile = tile // cpd
     filter_rows = round_up(gpd, 16)
     send_rows = 2 * cpd + filter_rows
-    block = pl.BlockSpec((rows, tile), lambda i: (0, i))
+    first = chunk * channels // tile
+    block = pl.BlockSpec((rows, tile), lambda i: (0, first + i))
+    own = pl.BlockSpec((rows, tile), lambda i: (0, i))
     ext = pltpu.VMEM((tile // LANES, rows + EDGE, LANES), F32)
     return pl.pallas_call(
         functools.partial(before_kernel, cpd, gpd),
         grid=(channels // tile,),
         in_specs=[block] * 4
         + [
-            pl.BlockSpec((3 * EDGE, tile), lambda i: (0, i)),
-            pl.BlockSpec((3, taps.shape[1], tile), lambda i: (0, 0, i)),
-            pl.BlockSpec((rows, groups), lambda i: (0, 0)),
+            pl.BlockSpec((3 * EDGE, tile), lambda i: (0, first + i)),
+            pl.BlockSpec((3, taps.shape[1], tile), lambda i: (0, 0, first + i)),
+            pl.BlockSpec((rows, groups), lambda i: (0, chunk)),
         ],
-        out_specs=[pl.BlockSpec((per_tile, send_rows, rows), lambda i: (i, 0, 0)), block, block],
+        out_specs=[pl.BlockSpec((per_tile, send_rows, rows), lambda i: (i, 0, 0)), own, own],
         out_shape=[
             jax.ShapeDtypeStruct((n, send_rows, rows), BF16),
             jax.ShapeDtypeStruct((rows, channels), F32),
@@ -310,8 +313,9 @@
 
 def after_kernel(
     cpd, gpd, in_ref, og_ref, sk_ref, sv_ref, k_end, v_end, next_ref, taps_ref,
-    dq_ref, dk_ref, dv_ref, raw_ref, raw_rows, ext_q, ext_k, ext_v,
+    *refs,
 ):
+    dq_ref, dk_ref, dv_ref, raw_ref, raw_rows, ext_q, ext_k, ext_v = refs[-8:]
     step = pl.program_id(0)
     per_tile, in_rows, rows = in_ref.shape
     groups = raw_ref.shape[1]
@@ -363,29 +367,36 @@
         raw_ref[...] = raw_rows[...].T
 
 
-def after_exchange(returned, out_grad, short_k, short_v, key, value, following, taps, groups):
+def after_exchange(
+    returned, out_grad, short_k, short_v, key, value, following, taps, groups, chunk, chunks, grads
+):
     n, in_rows, rows = returned.shape
-    channels = out_grad.shape[1]
+    channels = out_grad.shape[1] // chunks
+    groups = groups // chunks
     cpd, gpd = channels // n, groups // n
     tile = min(channels, max(512, cpd))
     per_tile = tile // cpd
-    block = pl.BlockSpec((rows, tile), lambda i: (0, i))
-    end = pl.BlockSpec((16, tile), lambda i: (rows // 16 - 1, i))
+    first = chunk * channels // tile
+    block = pl.BlockSpec((rows, tile), lambda i: (0, first + i))
+    own = pl.BlockSpec((rows, tile), lambda i: (0, i))
+    end = pl.BlockSpec((16, tile), lambda i: (rows // 16 - 1, first + i))
     ext = pltpu.VMEM((tile // LANES, rows + EDGE, LANES), F32)
-    grad = jax.ShapeDtypeStruct((rows, channels), BF16)
+    grad = jax.ShapeDtypeStruct(out_grad.shape, BF16)
     return pl.pallas_call(
         functools.partial(after_kernel, cpd, gpd),
         grid=(channels // tile,),
         in_specs=[
             pl.BlockSpec((per_tile, in_rows, rows), lambda i: (i, 0, 0)),
             block,
-            block,
-            block,
+            own,
+            own,
             end,
             end,
-            pl.BlockSpec((3 * EDGE, tile), lambda i: (0, i)),
-            pl.BlockSpec((3, taps.shape[1], tile), lambda i: (0, 0, i)),
-        ],
+            pl.BlockSpec((3 * EDGE, tile), lambda i: (0, first + i)),
+            pl.BlockSpec((3, taps.shape[1], tile), lambda i: (0, 0, first + i)),
+        ]
+        + [pl.BlockSpec(memory_space=pl.ANY)] * len(grads),
+        input_output_aliases={8 + i: i for i in range(len(grads))},
         out_specs=[block, block, block, pl.BlockSpec((rows, groups), lambda i: (0, 0))],
         out_shape=[grad, grad, grad, jax.ShapeDtypeStruct((rows, groups), F32)],
         scratch_shapes=[pltpu.VMEM((groups, rows), F32), ext, ext, ext],
@@ -394,7 +405,7 @@
             flops=60 * rows * channels, bytes_accessed=22 * rows * channels, transcendentals=0
         ),
         name="after_exchange",
-    )(returned, out_grad, short_k, short_v, key, value, following, taps)
+    )(returned, out_grad, short_k, short_v, key, value, following, taps, *grads)
 
 
 def on_device(
@@ -422,25 +433,40 @@
     following = shifted(
         jnp.concatenate([a[:EDGE] for a in (output_grad, hyena_key, hyena_value)], 0), "ctx", -1
     )
-    send, short_k, short_v = before_exchange(
-        hyena_query, hyena_key, hyena_value, output_grad, tail, short_filter, long_filter, n
-    )
-    received = lax.all_to_all(send, "ctx", split_axis=0, concat_axis=0, tiled=True)
+    chunks = 2 if gpd % 4 == 0 else 1
+    cpd, gpd = cpd // chunks, gpd // chunks
+    received = []
+    shorts = []
+    for chunk in range(chunks):
+        send, short_k, short_v = before_exchange(
+            hyena_query, hyena_key, hyena_value, output_grad, tail, short_filter, long_filter, n, chunk, chunks
+        )
+        shorts.append((short_k, short_v))
+        received.append(lax.all_to_all(send, "ctx", split_axis=0, concat_axis=0, tiled=True))
     attention = attend(query_heads, key_heads, value_heads, key_prev, value_prev, position)
-    results = long_products(received, cpd, gpd)
-    returned = lax.all_to_all(results, "ctx", split_axis=0, concat_axis=0, tiled=True)
-    norm_at = returned.shape[1] - 2 * EDGE * max(1, cpd // LANES) + EDGE - 2
-    own_squares = jnp.sum(returned[:, norm_at : norm_at + 2, 0].astype(F32)).reshape(1, 1)
+    received[0], attention = lax.optimization_barrier((received[0], attention))
+    returned = []
+    for chunk in range(chunks):
+        results = long_products(received[chunk], cpd, gpd)
+        returned.append(lax.all_to_all(results, "ctx", split_axis=0, concat_axis=0, tiled=True))
+    norm_at = returned[0].shape[1] - 2 * EDGE * max(1, cpd // LANES) + EDGE - 2
+    own_squares = sum(jnp.sum(r[:, norm_at : norm_at + 2, 0].astype(F32)) for r in returned).reshape(1, 1)
     squares = own_squares
     for distance in range(1, tp):
         route = [(i, (i + distance) % tp) for i in range(tp)]
         squares = squares + lax.ppermute(own_squares, "tp", route)
-    query_grad, key_grad, value_grad, raw_grad = after_exchange(
-        returned, output_grad, short_k, short_v, hyena_key, hyena_value, following, short_filter, groups
-    )
+    grads = ()
+    raws = []
+    for chunk in range(chunks):
+        *grads, raw = after_exchange(
+            returned[chunk], output_grad, *shorts[chunk], hyena_key, hyena_value, following, short_filter,
+            groups, chunk, chunks, grads,
+        )
+        raws.append(raw)
     bound = math.sqrt(rows * n * groups * tp)
     factor = jnp.minimum(1.0, bound / jnp.sqrt(squares))
-    return (attention, query_grad, key_grad, value_grad, raw_grad * factor)
+    raw_grad = raws[0] if chunks == 1 else jnp.concatenate(raws, 1)
+    return (attention, *grads, raw_grad * factor)
 
 
 def solution(mesh):

time: 222 us -> 217 us (0.977)
  blocking collectives: 54.1 us -> 0 us
  waiting for transfers between devices: 71.2 us -> 109 us
  local copies, waits for them, and re-layouts: 23.1 us -> 4.19 us
  starting transfers between devices: 17.7 us -> 32.2 us
  Pallas kernels: 50.6 us -> 64.4 us
    all_to_all x1 -> x0, blocking collectives: 54.1 us -> none  [on_device(): lax.all_to_all(send, 'ctx', split_axis=0, concat_axis=0, tiled=True)]
    all_to_all x0 -> x2, waiting for transfers between devices: none -> 33.8 us  [on_device(): lax.all_to_all(send, 'ctx', split_axis=0, concat_axis=0, tiled=True)]
    all_to_all x1 -> x2, waiting for transfers between devices: 0.01 us -> 24.2 us  [on_device(): lax.all_to_all(results, 'ctx', split_axis=0, concat_axis=0, tiled=True)]
    ppermute x4, waiting for transfers between devices: 71.2 us -> 51.2 us  [shifted(): return lax.ppermute(block, axis, route)]
    unnamed x38 -> x18, local copies, waits for them, and re-layouts: 21.3 us -> 2.39 us
    all_to_all x0 -> x2, starting transfers between devices: none -> 9.94 us  [on_device(): lax.all_to_all(send, 'ctx', split_axis=0, concat_axis=0, tiled=True)]
    pallas_call x1 -> x2, Pallas kernels: 6.03 us -> 10.9 us  [before_exchange(): pl.pallas_call(functools.partial(before_kernel, cpd, gpd), grid=(channels...]
    pallas_call x1 -> x2, Pallas kernels: 23 us -> 27.7 us  [long_products(): pl.pallas_call(functools.partial(long_kernel, cpd, gpd), in_specs=[pl.Blo...]
  transfers between devices with their start and end apart: 6 -> 9, of which waited for: 3 -> 6; matrix products, arithmetic and copies ran while one was open for 1% -> 1% of each run, Pallas kernels for 10% -> 27%
where the time goes in v2:
time: 217 us; the launch traced here: 216 us
  waiting for transfers between devices  109 us (50%)
  Pallas kernels  64.4 us (30%)
  starting transfers between devices  32.2 us (15%)
  local copies, waits for them, and re-layouts  4.19 us (2%)
  other arithmetic  2.87 us (1%)
  between operations  2.72 us (1%)
    ppermute x4, waiting for transfers between devices, shifted(): return lax.ppermute(block, axis, route)  51.2 us
    all_to_all x2, waiting for transfers between devices, on_device(): lax.all_to_all(send, 'ctx', split_axis=0, concat_axis=0, tiled=True)  33.8 us
    pallas_call x2, Pallas kernels, long_products(): pl.pallas_call(functools.partial(long_kernel, cpd, gpd), in_specs=[pl.Blo...  27.7 us
    all_to_all x2, waiting for transfers between devices, on_device(): lax.all_to_all(results, 'ctx', split_axis=0, concat_axis=0, tiled=True)  24.2 us
    pallas_call x1, Pallas kernels, attend(): pl.pallas_call(attend_kernel, grid=(channels // tile,), in_specs=[pl.Bloc...  14.1 us
    pallas_call x2, Pallas kernels, after_exchange(): pl.pallas_call(functools.partial(after_kernel, cpd, gpd), grid=(channels...  11.7 us
    pallas_call x2, Pallas kernels, before_exchange(): pl.pallas_call(functools.partial(before_kernel, cpd, gpd), grid=(channels...  10.9 us
    ppermute x4, starting transfers between devices, shifted(): return lax.ppermute(block, axis, route)  10.4 us
  transfers between devices with their start and end apart: 9, of which 6 were waited for; matrix products, arithmetic and copies ran while one was open for 1% of the time, Pallas kernels for 27%

profile of v2, /device:TPU:16, one launch (start us, length us, event | category | flops | bytes accessed | tf_op | source)
XLA Modules:
  0.0 215.6 jit_solution(1738829659673819379)
XLA Ops:
  0.6 0.8 slice.24
  1.5 1.0 fusion
  2.5 1.9 collective-permute-start
  4.4 6.0 %collective-permute-done.tail_ref = bf16[24,4096]{1,0:T(8,128)(2,1)S(1)} collective-permute-done((bf16[24,4096]{1,0:T(8,128)(2,1)S(1)}, bf16[24,4096]{1,0:T(8,128)(2,1)S(1)}, u32[]{:S(2)}, u32[]{:S(2)}) %collective-permute-start) | collective-permute-done | bytes 196640 | tf_op jit(solution)/shard_map/ppermute | solution.py:26
  10.3 0.7 copy-done.6
  11.0 5.5 %before_exchange.3 = (bf16[16,272,128]{2,1,0:T(8,128)(2,1)}, f32[128,2048]{1,0:T(8,128)}, f32[128,2048]{1,0:T(8,128)}) custom-call(bf16[128,4096]{1,0:T(8,128)(2,1)} %q_ref.5, bf16[128,4096]{1,0:T(8,128)(2,1)} %k_end.3, bf16[128,4096]{1,0:T(8,128)(2,1)} %v_end.3, bf16[128,4096]{1,0:T(8,128)(2,1)} %og_ref.7, bf16[24,4096]{1,0:T(8,128)(2,1)} %copy-done.6, ...), custom_call_target="tpu_custom_call" | custom-call | flops 13107200 | bytes 5242880 | tf_op jit(solution)/shard_map/before_exchange/pallas_call | solution.py:145
  16.5 5.3 %all-to-all-start.1 = ((bf16[16,272,128]{2,1,0:T(8,128)(2,1)}), bf16[16,272,128]{2,1,0:T(8,128)(2,1)S(1)}, u32[]{:S(2)}, u32[]{:S(2)}) async-start(bf16[16,272,128]{2,1,0:T(8,128)(2,1)} %get-tuple-element.23), calls=%async_computation.1 | async-start | bytes 2228224 | tf_op jit(solution)/shard_map/all_to_all | solution.py:445
  21.8 5.5 %before_exchange.2 = (bf16[16,272,128]{2,1,0:T(8,128)(2,1)}, f32[128,2048]{1,0:T(8,128)}, f32[128,2048]{1,0:T(8,128)}) custom-call(bf16[128,4096]{1,0:T(8,128)(2,1)} %q_ref.5, bf16[128,4096]{1,0:T(8,128)(2,1)} %k_end.3, bf16[128,4096]{1,0:T(8,128)(2,1)} %v_end.3, bf16[128,4096]{1,0:T(8,128)(2,1)} %og_ref.7, bf16[24,4096]{1,0:T(8,128)(2,1)} %copy-done.6, ...), custom_call_target="tpu_custom_call" | custom-call | flops 13107200 | bytes 5242880 | tf_op jit(solution)/shard_map/before_exchange/pallas_call | solution.py:145
  27.3 21.1 %all-to-all-done.1.in_ref = bf16[16,272,128]{2,1,0:T(8,128)(2,1)S(1)} async-done(((bf16[16,272,128]{2,1,0:T(8,128)(2,1)}), bf16[16,272,128]{2,1,0:T(8,128)(2,1)S(1)}, u32[]{:S(2)}, u32[]{:S(2)}) %all-to-all-start.1) | async-done | bytes 1114144 | tf_op jit(solution)/shard_map/all_to_all | solution.py:445
  48.4 4.6 %all-to-all-start = ((bf16[16,272,128]{2,1,0:T(8,128)(2,1)}), bf16[16,272,128]{2,1,0:T(8,128)(2,1)S(1)}, u32[]{:S(2)}, u32[]{:S(2)}) async-start(bf16[16,272,128]{2,1,0:T(8,128)(2,1)} %get-tuple-element.21), calls=%async_computation | async-start | bytes 2228224 | tf_op jit(solution)/shard_map/all_to_all | solution.py:445
  53.0 13.8 %long_products.2 = bf16[16,288,128]{2,1,0:T(8,128)(2,1)} custom-call(bf16[16,272,128]{2,1,0:T(8,128)(2,1)} %copy-done.3), custom_call_target="tpu_custom_call" | custom-call | flops 3221225472 | bytes 2359296 | tf_op jit(solution)/shard_map/long_products/pallas_call | solution.py:277
  66.8 12.7 %all-to-all-done.in_ref = bf16[16,272,128]{2,1,0:T(8,128)(2,1)S(1)} async-done(((bf16[16,272,128]{2,1,0:T(8,128)(2,1)}), bf16[16,272,128]{2,1,0:T(8,128)(2,1)S(1)}, u32[]{:S(2)}, u32[]{:S(2)}) %all-to-all-start) | async-done | bytes 1114144 | tf_op jit(solution)/shard_map/all_to_all | solution.py:445
  79.6 1.0 copy-done.2
  80.6 4.6 %all-to-all-start.2 = ((bf16[16,288,128]{2,1,0:T(8,128)(2,1)}), bf16[16,288,128]{2,1,0:T(8,128)(2,1)S(1)}, u32[]{:S(2)}, u32[]{:S(2)}) async-start(bf16[16,288,128]{2,1,0:T(8,128)(2,1)} %long_products.2), calls=%async_computation.2 | async-start | bytes 2359296 | tf_op jit(solution)/shard_map/all_to_all | solution.py:451
  85.2 2.1 collective-permute-start.1
  87.3 3.3 %collective-permute-start.2 = (bf16[128,4096]{1,0:T(8,128)(2,1)}, bf16[128,4096]{1,0:T(8,128)(2,1)}, u32[]{:S(2)}, u32[]{:S(2)}) collective-permute-start(bf16[128,4096]{1,0:T(8,128)(2,1)} %v_ref.4), channel_id=1, source_target_pairs={{0,2},{2,4},{4,6},{6,8},{8,10},{10,12},{12,14},{14,16},{16,18},{18... | collective-permute-start | bytes 3145736 | tf_op jit(solution)/shard_map/ppermute | solution.py:26
  90.7 33.9 %collective-permute-done.1.kp_ref = bf16[128,4096]{1,0:T(8,128)(2,1)S(1)} collective-permute-done((bf16[128,4096]{1,0:T(8,128)(2,1)S(1)}, bf16[128,4096]{1,0:T(8,128)(2,1)S(1)}, u32[]{:S(2)}, u32[]{:S(2)}) %collective-permute-start.1) | collective-permute-done | bytes 1048608 | tf_op jit(solution)/shard_map/ppermute | solution.py:26
  124.5 11.3 %collective-permute-done.2.vp_ref = bf16[128,4096]{1,0:T(8,128)(2,1)} collective-permute-done((bf16[128,4096]{1,0:T(8,128)(2,1)}, bf16[128,4096]{1,0:T(8,128)(2,1)}, u32[]{:S(2)}, u32[]{:S(2)}) %collective-permute-start.2) | collective-permute-done | bytes 1048608 | tf_op jit(solution)/shard_map/ppermute | solution.py:26
  135.9 14.1 %attend.1 = bf16[128,4096]{1,0:T(8,128)(2,1)} custom-call(s32[1]{0:T(128)} %bitcast.place_ref, bf16[128,4096]{1,0:T(8,128)(2,1)} %q_ref.4, bf16[128,4096]{1,0:T(8,128)(2,1)} %k_ref.4, bf16[128,4096]{1,0:T(8,128)(2,1)} %v_ref.4, bf16[128,4096]{1,0:T(8,128)(2,1)} %copy-done.5, bf16[128,4096]{1,0:T(8,128)(2,1)} %collective-permute-done.2.vp_ref), custom_call_target="tpu_custom_call" | custom-call | flops 536870912 | bytes 6291456 | tf_op jit(solution)/shard_map/attend/pallas_call | solution.py:66
  149.9 13.8 %long_products.3 = bf16[16,288,128]{2,1,0:T(8,128)(2,1)} custom-call(bf16[16,272,128]{2,1,0:T(8,128)(2,1)} %copy-done.2), custom_call_target="tpu_custom_call" | custom-call | flops 3221225472 | bytes 2359296 | tf_op jit(solution)/shard_map/long_products/pallas_call | solution.py:277
  163.8 0.0 all-to-all-done.2.in_ref
  163.8 4.4 %all-to-all-start.3 = ((bf16[16,288,128]{2,1,0:T(8,128)(2,1)}), bf16[16,288,128]{2,1,0:T(8,128)(2,1)S(1)}, u32[]{:S(2)}, u32[]{:S(2)}) async-start(bf16[16,288,128]{2,1,0:T(8,128)(2,1)} %long_products.3), calls=%async_computation.3 | async-start | bytes 2359296 | tf_op jit(solution)/shard_map/all_to_all | solution.py:451
  168.2 3.1 %collective-permute-start.3 = (bf16[24,4096]{1,0:T(8,128)(2,1)S(1)}, bf16[24,4096]{1,0:T(8,128)(2,1)S(1)}, u32[]{:S(2)}, u32[]{:S(2)}) collective-permute-start(bf16[24,4096]{1,0:T(8,128)(2,1)S(1)} %pad_maximum_fusion.1), channel_id=1, source_target_pairs={{2,0},{4,2},{6,4},{8,6},{10,8},{12,10},{14,12},{16,14},{18,16},{20... | collective-permute-start | bytes 589832 | tf_op jit(solution)/shard_map/ppermute | solution.py:26
  171.3 0.6 convert_reduce_fusion
  171.9 24.2 %all-to-all-done.3.in_ref = bf16[16,288,128]{2,1,0:T(8,128)(2,1)S(1)} async-done(((bf16[16,288,128]{2,1,0:T(8,128)(2,1)}), bf16[16,288,128]{2,1,0:T(8,128)(2,1)S(1)}, u32[]{:S(2)}, u32[]{:S(2)}) %all-to-all-start.3) | async-done | bytes 1179680 | tf_op jit(solution)/shard_map/all_to_all | solution.py:451
  196.1 0.7 convert_reduce_fusion.1
  198.1 2.9 %collective-permute-start.4 = (f32[1,1]{1,0:T(1,128)}, f32[1,1]{1,0:T(1,128)}, u32[]{:S(2)}, u32[]{:S(2)}) collective-permute-start(f32[1,1]{1,0:T(1,128)} %bitcast.1), channel_id=1, source_target_pairs={{0,1},{1,0},{2,3},{3,2},{4,5},{5,4},{6,7},{7,6},{8,9},{9,8},{10,11... | collective-permute-start | bytes 20 | tf_op jit(solution)/shard_map/ppermute | solution.py:457
  201.0 0.7 copy-done.7
  201.6 5.9 %after_exchange.2 = (bf16[128,4096]{1,0:T(8,128)(2,1)}, bf16[128,4096]{1,0:T(8,128)(2,1)}, bf16[128,4096]{1,0:T(8,128)(2,1)}, f32[128,128]{1,0:T(8,128)}) custom-call(bf16[16,288,128]{2,1,0:T(8,128)(2,1)} %copy-done.1, bf16[128,4096]{1,0:T(8,128)(2,1)} %og_ref.7, f32[128,2048]{1,0:T(8,128)} %get-tuple-element.27.sk_ref, ...), custom_call_target="tpu_custom_call" | custom-call | flops 15728640 | bytes 5767168 | tf_op jit(solution)/shard_map/after_exchange/pallas_call | solution.py:385
  207.5 0.0 copy-start.8
  207.5 5.9 %after_exchange.3 = (bf16[128,4096]{1,0:T(8,128)(2,1)}, bf16[128,4096]{1,0:T(8,128)(2,1)}, bf16[128,4096]{1,0:T(8,128)(2,1)}, f32[128,128]{1,0:T(8,128)}) custom-call(bf16[16,288,128]{2,1,0:T(8,128)(2,1)} %copy-done, bf16[128,4096]{1,0:T(8,128)(2,1)} %og_ref.7, ...), custom_call_target="tpu_custom_call", output_to_operand_aliasing={{0}: (8, {}), {1}: (9, {}), {2}: (10, {})} | custom-call | flops 15728640 | bytes 5767168 | tf_op jit(solution)/shard_map/after_exchange/pallas_call | solution.py:385
  214.1 1.5 maximum_multiply_fusion
  (20 shorter events, 0.1 us)
Async XLA Ops:
  2.5 7.9 %collective-permute-start = (bf16[24,4096]{1,0:T(8,128)(2,1)S(1)}, bf16[24,4096]{1,0:T(8,128)(2,1)S(1)}, u32[]{:S(2)}, u32[]{:S(2)}) collective-permute-start(bf16[24,4096]{1,0:T(8,128)(2,1)S(1)} %pad_maximum_fusion), channel_id=1, source_target_pairs={{0,2},{2,4},{4,6},{6,8},{8,10},{10,12},{12,14},{14,16},{16,18},{18... | collective-permute-start | bytes 589832 | tf_op jit(solution)/shard_map/ppermute | solution.py:26
  10.3 0.7 copy-start.6
  16.5 31.9 %all-to-all-start.1 = ((bf16[16,272,128]{2,1,0:T(8,128)(2,1)}), bf16[16,272,128]{2,1,0:T(8,128)(2,1)S(1)}, u32[]{:S(2)}, u32[]{:S(2)}) async-start(bf16[16,272,128]{2,1,0:T(8,128)(2,1)} %get-tuple-element.23), calls=%async_computation.1 | async-start | bytes 2228224 | tf_op jit(solution)/shard_map/all_to_all | solution.py:445
  48.4 4.6 %copy-start.3 = (bf16[16,272,128]{2,1,0:T(8,128)(2,1)}, bf16[16,272,128]{2,1,0:T(8,128)(2,1)S(1)}, u32[]{:S(2)}) copy-start(bf16[16,272,128]{2,1,0:T(8,128)(2,1)S(1)} %all-to-all-done.1.in_ref) | copy-start | bytes 3342340
  48.4 31.2 %all-to-all-start = ((bf16[16,272,128]{2,1,0:T(8,128)(2,1)}), bf16[16,272,128]{2,1,0:T(8,128)(2,1)S(1)}, u32[]{:S(2)}, u32[]{:S(2)}) async-start(bf16[16,272,128]{2,1,0:T(8,128)(2,1)} %get-tuple-element.21), calls=%async_computation | async-start | bytes 2228224 | tf_op jit(solution)/shard_map/all_to_all | solution.py:445
  66.8 18.4 %copy-start.4 = (bf16[128,4096]{1,0:T(8,128)(2,1)S(1)}, bf16[128,4096]{1,0:T(8,128)(2,1)}, u32[]{:S(2)}) copy-start(bf16[128,4096]{1,0:T(8,128)(2,1)} %k_ref.4) | copy-start | bytes 3145732
  79.6 1.0 copy-start.2
  80.6 83.2 %all-to-all-start.2 = ((bf16[16,288,128]{2,1,0:T(8,128)(2,1)}), bf16[16,288,128]{2,1,0:T(8,128)(2,1)S(1)}, u32[]{:S(2)}, u32[]{:S(2)}) async-start(bf16[16,288,128]{2,1,0:T(8,128)(2,1)} %long_products.2), calls=%async_computation.2 | async-start | bytes 2359296 | tf_op jit(solution)/shard_map/all_to_all | solution.py:451
  85.2 39.3 %collective-permute-start.1 = (bf16[128,4096]{1,0:T(8,128)(2,1)S(1)}, bf16[128,4096]{1,0:T(8,128)(2,1)S(1)}, u32[]{:S(2)}, u32[]{:S(2)}) collective-permute-start(bf16[128,4096]{1,0:T(8,128)(2,1)S(1)} %copy-done.4), channel_id=1, source_target_pairs={{0,2},{2,4},{4,6},{6,8},{8,10},{10,12},{12,14},{14,16},{16,18},{18... | collective-permute-start | bytes 3145736 | tf_op jit(solution)/shard_map/ppermute | solution.py:26
  87.3 48.6 %collective-permute-start.2 = (bf16[128,4096]{1,0:T(8,128)(2,1)}, bf16[128,4096]{1,0:T(8,128)(2,1)}, u32[]{:S(2)}, u32[]{:S(2)}) collective-permute-start(bf16[128,4096]{1,0:T(8,128)(2,1)} %v_ref.4), channel_id=1, source_target_pairs={{0,2},{2,4},{4,6},{6,8},{8,10},{10,12},{12,14},{14,16},{16,18},{18... | collective-permute-start | bytes 3145736 | tf_op jit(solution)/shard_map/ppermute | solution.py:26
  124.5 11.3 %copy-start.5 = (bf16[128,4096]{1,0:T(8,128)(2,1)}, bf16[128,4096]{1,0:T(8,128)(2,1)S(1)}, u32[]{:S(2)}) copy-start(bf16[128,4096]{1,0:T(8,128)(2,1)S(1)} %collective-permute-done.1.kp_ref) | copy-start | bytes 3145732
  163.8 4.4 %slice-start = ((bf16[128,4096]{1,0:T(8,128)(2,1)}), bf16[8,4096]{1,0:T(8,128)(2,1)S(1)}, s32[]{:S(2)}) async-start(bf16[128,4096]{1,0:T(8,128)(2,1)} %og_ref.7), calls=%async_computation.4 | async-start | bytes 131072 | tf_op jit(solution)/shard_map/slice | solution.py:434
  163.8 7.5 %copy-start = (bf16[16,288,128]{2,1,0:T(8,128)(2,1)}, bf16[16,288,128]{2,1,0:T(8,128)(2,1)S(1)}, u32[]{:S(2)}) copy-start(bf16[16,288,128]{2,1,0:T(8,128)(2,1)S(1)} %all-to-all-done.2.in_ref) | copy-start | bytes 3538948
  163.8 32.3 %all-to-all-start.3 = ((bf16[16,288,128]{2,1,0:T(8,128)(2,1)}), bf16[16,288,128]{2,1,0:T(8,128)(2,1)S(1)}, u32[]{:S(2)}, u32[]{:S(2)}) async-start(bf16[16,288,128]{2,1,0:T(8,128)(2,1)} %long_products.3), calls=%async_computation.3 | async-start | bytes 2359296 | tf_op jit(solution)/shard_map/all_to_all | solution.py:451
  168.2 32.8 %collective-permute-start.3 = (bf16[24,4096]{1,0:T(8,128)(2,1)S(1)}, bf16[24,4096]{1,0:T(8,128)(2,1)S(1)}, u32[]{:S(2)}, u32[]{:S(2)}) collective-permute-start(bf16[24,4096]{1,0:T(8,128)(2,1)S(1)} %pad_maximum_fusion.1), channel_id=1, source_target_pairs={{2,0},{4,2},{6,4},{8,6},{10,8},{12,10},{14,12},{16,14},{18,16},{20... | collective-permute-start | bytes 589832 | tf_op jit(solution)/shard_map/ppermute | solution.py:26
  196.1 4.9 %copy-start.1 = (bf16[16,288,128]{2,1,0:T(8,128)(2,1)}, bf16[16,288,128]{2,1,0:T(8,128)(2,1)S(1)}, u32[]{:S(2)}) copy-start(bf16[16,288,128]{2,1,0:T(8,128)(2,1)S(1)} %all-to-all-done.3.in_ref) | copy-start | bytes 3538948
  198.1 15.3 %collective-permute-start.4 = (f32[1,1]{1,0:T(1,128)}, f32[1,1]{1,0:T(1,128)}, u32[]{:S(2)}, u32[]{:S(2)}) collective-permute-start(f32[1,1]{1,0:T(1,128)} %bitcast.1), channel_id=1, source_target_pairs={{0,1},{1,0},{2,3},{3,2},{4,5},{5,4},{6,7},{7,6},{8,9},{9,8},{10,11... | collective-permute-start | bytes 20 | tf_op jit(solution)/shard_map/ppermute | solution.py:457
  201.0 0.7 copy-start.7
  207.5 6.6 %copy-start.8 = (f32[128,128]{1,0:T(8,128)S(1)}, f32[128,128]{1,0:T(8,128)}, u32[]{:S(2)}) copy-start(f32[128,128]{1,0:T(8,128)} %get-tuple-element.35) | copy-start | bytes 196612

commit v3 on v2

--- a/solution.py
+++ b/solution.py
@@ -441,6 +441,8 @@
         send, short_k, short_v = before_exchange(
             hyena_query, hyena_key, hyena_value, output_grad, tail, short_filter, long_filter, n, chunk, chunks
         )
+        if chunk + 1 < chunks:
+            send, tail = lax.optimization_barrier((send, tail))
         shorts.append((short_k, short_v))
         received.append(lax.all_to_all(send, "ctx", split_axis=0, concat_axis=0, tiled=True))
     attention = attend(query_heads, key_heads, value_heads, key_prev, value_prev, position)
@@ -448,6 +450,8 @@
     returned = []
     for chunk in range(chunks):
         results = long_products(received[chunk], cpd, gpd)
+        if chunk + 1 < chunks:
+            results, received[chunk + 1] = lax.optimization_barrier((results, received[chunk + 1]))
         returned.append(lax.all_to_all(results, "ctx", split_axis=0, concat_axis=0, tiled=True))
     norm_at = returned[0].shape[1] - 2 * EDGE * max(1, cpd // LANES) + EDGE - 2
     own_squares = sum(jnp.sum(r[:, norm_at : norm_at + 2, 0].astype(F32)) for r in returned).reshape(1, 1)

time: 217 us -> 217 us (level)
    all_to_all x2, waiting for transfers between devices: 24.2 us -> 38.3 us  [on_device(): lax.all_to_all(results, 'ctx', split_axis=0, concat_axis=0, tiled=True)]
    all_to_all x2, waiting for transfers between devices: 33.8 us -> 21.1 us  [on_device(): lax.all_to_all(send, 'ctx', split_axis=0, concat_axis=0, tiled=True)]
where the time goes in v3:
time: 217 us; the launch traced here: 216 us
  waiting for transfers between devices  109 us (50%)
  Pallas kernels  64.4 us (30%)
  starting transfers between devices  32.1 us (15%)
  local copies, waits for them, and re-layouts  4.86 us (2%)
  other arithmetic  2.88 us (1%)
  between operations  2.74 us (1%)
    ppermute x4, waiting for transfers between devices, shifted(): return lax.ppermute(block, axis, route)  49.8 us
    all_to_all x2, waiting for transfers between devices, on_device(): lax.all_to_all(results, 'ctx', split_axis=0, concat_axis=0, tiled=True)  38.3 us
    pallas_call x2, Pallas kernels, long_products(): pl.pallas_call(functools.partial(long_kernel, cpd, gpd), in_specs=[pl.Blo...  27.7 us
    all_to_all x2, waiting for transfers between devices, on_device(): lax.all_to_all(send, 'ctx', split_axis=0, concat_axis=0, tiled=True)  21.1 us
    pallas_call x1, Pallas kernels, attend(): pl.pallas_call(attend_kernel, grid=(channels // tile,), in_specs=[pl.Bloc...  14.1 us
    pallas_call x2, Pallas kernels, after_exchange(): pl.pallas_call(functools.partial(after_kernel, cpd, gpd), grid=(channels...  11.7 us
    pallas_call x2, Pallas kernels, before_exchange(): pl.pallas_call(functools.partial(before_kernel, cpd, gpd), grid=(channels...  11 us
    ppermute x4, starting transfers between devices, shifted(): return lax.ppermute(block, axis, route)  10.4 us
  transfers between devices with their start and end apart: 9, of which 6 were waited for; matrix products, arithmetic and copies ran while one was open for 1% of the time, Pallas kernels for 27%

profile of v3, /device:TPU:16, one launch (start us, length us, event | category | flops | bytes accessed | tf_op | source)
XLA Modules:
  0.0 216.2 jit_solution(12676174251048995840)
XLA Ops:
  0.6 0.8 slice.24
  1.5 1.6 fusion
  3.1 1.9 collective-permute-start
  5.0 6.0 %collective-permute-done.tail_ref = bf16[24,4096]{1,0:T(8,128)(2,1)S(1)} collective-permute-done((bf16[24,4096]{1,0:T(8,128)(2,1)S(1)}, bf16[24,4096]{1,0:T(8,128)(2,1)S(1)}, u32[]{:S(2)}, u32[]{:S(2)}) %collective-permute-start) | collective-permute-done | bytes 196640 | tf_op jit(solution)/shard_map/ppermute | solution.py:26
  11.0 0.7 copy-done.5
  11.7 5.5 %before_exchange.2 = (bf16[16,272,128]{2,1,0:T(8,128)(2,1)}, f32[128,2048]{1,0:T(8,128)}, f32[128,2048]{1,0:T(8,128)}) custom-call(bf16[128,4096]{1,0:T(8,128)(2,1)} %q_ref.5, bf16[128,4096]{1,0:T(8,128)(2,1)} %k_end.3, bf16[128,4096]{1,0:T(8,128)(2,1)} %v_end.3, bf16[128,4096]{1,0:T(8,128)(2,1)} %og_ref.7, bf16[24,4096]{1,0:T(8,128)(2,1)} %copy-done.5, ...), custom_call_target="tpu_custom_call" | custom-call | flops 13107200 | bytes 5242880 | tf_op jit(solution)/shard_map/before_exchange/pallas_call | solution.py:145
  17.2 5.3 %all-to-all-start = ((bf16[16,272,128]{2,1,0:T(8,128)(2,1)}), bf16[16,272,128]{2,1,0:T(8,128)(2,1)S(1)}, u32[]{:S(2)}, u32[]{:S(2)}) async-start(bf16[16,272,128]{2,1,0:T(8,128)(2,1)} %get-tuple-element.26), calls=%async_computation | async-start | bytes 2228224 | tf_op jit(solution)/shard_map/all_to_all | solution.py:447
  22.5 5.5 %before_exchange.3 = (bf16[16,272,128]{2,1,0:T(8,128)(2,1)}, f32[128,2048]{1,0:T(8,128)}, f32[128,2048]{1,0:T(8,128)}) custom-call(bf16[128,4096]{1,0:T(8,128)(2,1)} %q_ref.5, bf16[128,4096]{1,0:T(8,128)(2,1)} %k_end.3, bf16[128,4096]{1,0:T(8,128)(2,1)} %v_end.3, bf16[128,4096]{1,0:T(8,128)(2,1)} %og_ref.7, bf16[24,4096]{1,0:T(8,128)(2,1)} %copy-done.5, ...), custom_call_target="tpu_custom_call" | custom-call | flops 13107200 | bytes 5242880 | tf_op jit(solution)/shard_map/before_exchange/pallas_call | solution.py:145
  27.9 0.0 copy-start.4
  28.0 21.1 %all-to-all-done.in_ref = bf16[16,272,128]{2,1,0:T(8,128)(2,1)S(1)} async-done(((bf16[16,272,128]{2,1,0:T(8,128)(2,1)}), bf16[16,272,128]{2,1,0:T(8,128)(2,1)S(1)}, u32[]{:S(2)}, u32[]{:S(2)}) %all-to-all-start) | async-done | bytes 1114144 | tf_op jit(solution)/shard_map/all_to_all | solution.py:447
  49.0 4.6 %all-to-all-start.1 = ((bf16[16,272,128]{2,1,0:T(8,128)(2,1)}), bf16[16,272,128]{2,1,0:T(8,128)(2,1)S(1)}, u32[]{:S(2)}, u32[]{:S(2)}) async-start(bf16[16,272,128]{2,1,0:T(8,128)(2,1)} %get-tuple-element.30), calls=%async_computation.1 | async-start | bytes 2228224 | tf_op jit(solution)/shard_map/all_to_all | solution.py:447
  53.7 2.1 collective-permute-start.1
  55.7 3.3 %collective-permute-start.2 = (bf16[128,4096]{1,0:T(8,128)(2,1)}, bf16[128,4096]{1,0:T(8,128)(2,1)}, u32[]{:S(2)}, u32[]{:S(2)}) collective-permute-start(bf16[128,4096]{1,0:T(8,128)(2,1)} %v_ref.4), channel_id=1, source_target_pairs={{0,2},{2,4},{4,6},{6,8},{8,10},{10,12},{12,14},{14,16},{16,18},{18... | collective-permute-start | bytes 3145736 | tf_op jit(solution)/shard_map/ppermute | solution.py:26
  59.1 32.6 %collective-permute-done.1.kp_ref = bf16[128,4096]{1,0:T(8,128)(2,1)} collective-permute-done((bf16[128,4096]{1,0:T(8,128)(2,1)S(1)}, bf16[128,4096]{1,0:T(8,128)(2,1)}, u32[]{:S(2)}, u32[]{:S(2)}) %collective-permute-start.1) | collective-permute-done | bytes 1048608 | tf_op jit(solution)/shard_map/ppermute | solution.py:26
  91.7 11.2 %collective-permute-done.2.vp_ref = bf16[128,4096]{1,0:T(8,128)(2,1)} collective-permute-done((bf16[128,4096]{1,0:T(8,128)(2,1)}, bf16[128,4096]{1,0:T(8,128)(2,1)}, u32[]{:S(2)}, u32[]{:S(2)}) %collective-permute-start.2) | collective-permute-done | bytes 1048608 | tf_op jit(solution)/shard_map/ppermute | solution.py:26
  102.9 14.1 %attend.1 = bf16[128,4096]{1,0:T(8,128)(2,1)} custom-call(s32[1]{0:T(128)} %bitcast.place_ref, bf16[128,4096]{1,0:T(8,128)(2,1)} %q_ref.4, bf16[128,4096]{1,0:T(8,128)(2,1)} %k_ref.4, bf16[128,4096]{1,0:T(8,128)(2,1)} %v_ref.4, bf16[128,4096]{1,0:T(8,128)(2,1)} %collective-permute-done.1.kp_ref, bf16[128,4096]{1,0:T(8,128)(2,1)} %collective-permute-done.2.vp_ref), custom_call_target="tpu_custom_call" | custom-call | flops 536870912 | bytes 6291456 | tf_op jit(solution)/shard_map/attend/pallas_call | solution.py:66
  117.0 13.8 %long_products.2 = bf16[16,288,128]{2,1,0:T(8,128)(2,1)} custom-call(bf16[16,272,128]{2,1,0:T(8,128)(2,1)} %copy-done.2), custom_call_target="tpu_custom_call" | custom-call | flops 3221225472 | bytes 2359296 | tf_op jit(solution)/shard_map/long_products/pallas_call | solution.py:277
  130.8 1.0 copy-done.3
  131.9 4.2 %all-to-all-start.3 = ((bf16[16,288,128]{2,1,0:T(8,128)(2,1)}), bf16[16,288,128]{2,1,0:T(8,128)(2,1)S(1)}, u32[]{:S(2)}, u32[]{:S(2)}) async-start(bf16[16,288,128]{2,1,0:T(8,128)(2,1)} %long_products.2), calls=%async_computation.3 | async-start | bytes 2359296 | tf_op jit(solution)/shard_map/all_to_all | solution.py:455
  136.1 13.8 %long_products.3 = bf16[16,288,128]{2,1,0:T(8,128)(2,1)} custom-call(bf16[16,272,128]{2,1,0:T(8,128)(2,1)} %copy-done.3), custom_call_target="tpu_custom_call" | custom-call | flops 3221225472 | bytes 2359296 | tf_op jit(solution)/shard_map/long_products/pallas_call | solution.py:277
  149.9 14.1 %all-to-all-done.3.in_ref = bf16[16,288,128]{2,1,0:T(8,128)(2,1)S(1)} async-done(((bf16[16,288,128]{2,1,0:T(8,128)(2,1)}), bf16[16,288,128]{2,1,0:T(8,128)(2,1)S(1)}, u32[]{:S(2)}, u32[]{:S(2)}) %all-to-all-start.3) | async-done | bytes 1179680 | tf_op jit(solution)/shard_map/all_to_all | solution.py:455
  164.1 4.6 %all-to-all-start.2 = ((bf16[16,288,128]{2,1,0:T(8,128)(2,1)}), bf16[16,288,128]{2,1,0:T(8,128)(2,1)S(1)}, u32[]{:S(2)}, u32[]{:S(2)}) async-start(bf16[16,288,128]{2,1,0:T(8,128)(2,1)} %long_products.3), calls=%async_computation.2 | async-start | bytes 2359296 | tf_op jit(solution)/shard_map/all_to_all | solution.py:455
  168.7 3.1 %collective-permute-start.3 = (bf16[24,4096]{1,0:T(8,128)(2,1)S(1)}, bf16[24,4096]{1,0:T(8,128)(2,1)S(1)}, u32[]{:S(2)}, u32[]{:S(2)}) collective-permute-start(bf16[24,4096]{1,0:T(8,128)(2,1)S(1)} %pad_maximum_fusion.1), channel_id=1, source_target_pairs={{2,0},{4,2},{6,4},{8,6},{10,8},{12,10},{14,12},{16,14},{18,16},{20... | collective-permute-start | bytes 589832 | tf_op jit(solution)/shard_map/ppermute | solution.py:26
  171.9 0.6 convert_reduce_fusion.1
  172.5 24.2 %all-to-all-done.2.in_ref = bf16[16,288,128]{2,1,0:T(8,128)(2,1)S(1)} async-done(((bf16[16,288,128]{2,1,0:T(8,128)(2,1)}), bf16[16,288,128]{2,1,0:T(8,128)(2,1)S(1)}, u32[]{:S(2)}, u32[]{:S(2)}) %all-to-all-start.2) | async-done | bytes 1179680 | tf_op jit(solution)/shard_map/all_to_all | solution.py:455
  196.7 0.7 convert_reduce_fusion
  198.7 2.9 %collective-permute-start.4 = (f32[1,1]{1,0:T(1,128)}, f32[1,1]{1,0:T(1,128)}, u32[]{:S(2)}, u32[]{:S(2)}) collective-permute-start(f32[1,1]{1,0:T(1,128)} %bitcast.1), channel_id=1, source_target_pairs={{0,1},{1,0},{2,3},{3,2},{4,5},{5,4},{6,7},{7,6},{8,9},{9,8},{10,11... | collective-permute-start | bytes 20 | tf_op jit(solution)/shard_map/ppermute | solution.py:461
  201.6 0.7 copy-done.6
  202.2 5.9 %after_exchange.2 = (bf16[128,4096]{1,0:T(8,128)(2,1)}, bf16[128,4096]{1,0:T(8,128)(2,1)}, bf16[128,4096]{1,0:T(8,128)(2,1)}, f32[128,128]{1,0:T(8,128)}) custom-call(bf16[16,288,128]{2,1,0:T(8,128)(2,1)} %copy-done.1, bf16[128,4096]{1,0:T(8,128)(2,1)} %og_ref.7, f32[128,2048]{1,0:T(8,128)} %get-tuple-element.35.sk_ref, ...), custom_call_target="tpu_custom_call" | custom-call | flops 15728640 | bytes 5767168 | tf_op jit(solution)/shard_map/after_exchange/pallas_call | solution.py:385
  208.1 0.0 copy-start.9
  208.1 5.9 %after_exchange.3 = (bf16[128,4096]{1,0:T(8,128)(2,1)}, bf16[128,4096]{1,0:T(8,128)(2,1)}, bf16[128,4096]{1,0:T(8,128)(2,1)}, f32[128,128]{1,0:T(8,128)}) custom-call(bf16[16,288,128]{2,1,0:T(8,128)(2,1)} %copy-done, bf16[128,4096]{1,0:T(8,128)(2,1)} %og_ref.7, ...), custom_call_target="tpu_custom_call", output_to_operand_aliasing={{0}: (8, {}), {1}: (9, {}), {2}: (10, {})} | custom-call | flops 15728640 | bytes 5767168 | tf_op jit(solution)/shard_map/after_exchange/pallas_call | solution.py:385
  214.7 1.5 maximum_multiply_fusion
  (22 shorter events, 0.1 us)
Async XLA Ops:
  3.1 7.9 %collective-permute-start = (bf16[24,4096]{1,0:T(8,128)(2,1)S(1)}, bf16[24,4096]{1,0:T(8,128)(2,1)S(1)}, u32[]{:S(2)}, u32[]{:S(2)}) collective-permute-start(bf16[24,4096]{1,0:T(8,128)(2,1)S(1)} %pad_maximum_fusion), channel_id=1, source_target_pairs={{0,2},{2,4},{4,6},{6,8},{8,10},{10,12},{12,14},{14,16},{16,18},{18... | collective-permute-start | bytes 589832 | tf_op jit(solution)/shard_map/ppermute | solution.py:26
  11.0 0.7 copy-start.5
  17.2 31.9 %all-to-all-start = ((bf16[16,272,128]{2,1,0:T(8,128)(2,1)}), bf16[16,272,128]{2,1,0:T(8,128)(2,1)S(1)}, u32[]{:S(2)}, u32[]{:S(2)}) async-start(bf16[16,272,128]{2,1,0:T(8,128)(2,1)} %get-tuple-element.26), calls=%async_computation | async-start | bytes 2228224 | tf_op jit(solution)/shard_map/all_to_all | solution.py:447
  27.9 25.7 %copy-start.4 = (bf16[128,4096]{1,0:T(8,128)(2,1)S(1)}, bf16[128,4096]{1,0:T(8,128)(2,1)}, u32[]{:S(2)}) copy-start(bf16[128,4096]{1,0:T(8,128)(2,1)} %k_ref.4) | copy-start | bytes 3145732
  49.0 67.9 %copy-start.2 = (bf16[16,272,128]{2,1,0:T(8,128)(2,1)}, bf16[16,272,128]{2,1,0:T(8,128)(2,1)S(1)}, u32[]{:S(2)}) copy-start(bf16[16,272,128]{2,1,0:T(8,128)(2,1)S(1)} %all-to-all-done.in_ref) | copy-start | bytes 3342340
  49.0 81.8 %all-to-all-start.1 = ((bf16[16,272,128]{2,1,0:T(8,128)(2,1)}), bf16[16,272,128]{2,1,0:T(8,128)(2,1)S(1)}, u32[]{:S(2)}, u32[]{:S(2)}) async-start(bf16[16,272,128]{2,1,0:T(8,128)(2,1)} %get-tuple-element.30), calls=%async_computation.1 | async-start | bytes 2228224 | tf_op jit(solution)/shard_map/all_to_all | solution.py:447
  53.7 38.0 %collective-permute-start.1 = (bf16[128,4096]{1,0:T(8,128)(2,1)S(1)}, bf16[128,4096]{1,0:T(8,128)(2,1)}, u32[]{:S(2)}, u32[]{:S(2)}) collective-permute-start(bf16[128,4096]{1,0:T(8,128)(2,1)S(1)} %copy-done.4), channel_id=1, source_target_pairs={{0,2},{2,4},{4,6},{6,8},{8,10},{10,12},{12,14},{14,16},{16,18},{18... | collective-permute-start | bytes 3145736 | tf_op jit(solution)/shard_map/ppermute | solution.py:26
  55.7 47.2 %collective-permute-start.2 = (bf16[128,4096]{1,0:T(8,128)(2,1)}, bf16[128,4096]{1,0:T(8,128)(2,1)}, u32[]{:S(2)}, u32[]{:S(2)}) collective-permute-start(bf16[128,4096]{1,0:T(8,128)(2,1)} %v_ref.4), channel_id=1, source_target_pairs={{0,2},{2,4},{4,6},{6,8},{8,10},{10,12},{12,14},{14,16},{16,18},{18... | collective-permute-start | bytes 3145736 | tf_op jit(solution)/shard_map/ppermute | solution.py:26
  130.8 1.0 copy-start.3
  131.9 32.2 %all-to-all-start.3 = ((bf16[16,288,128]{2,1,0:T(8,128)(2,1)}), bf16[16,288,128]{2,1,0:T(8,128)(2,1)S(1)}, u32[]{:S(2)}, u32[]{:S(2)}) async-start(bf16[16,288,128]{2,1,0:T(8,128)(2,1)} %long_products.2), calls=%async_computation.3 | async-start | bytes 2359296 | tf_op jit(solution)/shard_map/all_to_all | solution.py:455
  149.9 18.8 %slice-start = ((bf16[128,4096]{1,0:T(8,128)(2,1)}), bf16[8,4096]{1,0:T(8,128)(2,1)S(1)}, s32[]{:S(2)}) async-start(bf16[128,4096]{1,0:T(8,128)(2,1)} %og_ref.7), calls=%async_computation.4 | async-start | bytes 131072 | tf_op jit(solution)/shard_map/slice | solution.py:434
  149.9 18.8 %copy-start.7 = (bf16[8,4096]{1,0:T(8,128)(2,1)S(1)}, bf16[8,4096]{1,0:T(8,128)(2,1)}, u32[]{:S(2)}) copy-start(bf16[8,4096]{1,0:T(8,128)(2,1)} %get-tuple-element.45) | copy-start | bytes 196612
  149.9 18.8 %copy-start.8 = (bf16[8,4096]{1,0:T(8,128)(2,1)S(1)}, bf16[8,4096]{1,0:T(8,128)(2,1)}, u32[]{:S(2)}) copy-start(bf16[8,4096]{1,0:T(8,128)(2,1)} %get-tuple-element.50) | copy-start | bytes 196612
  164.1 7.8 %copy-start.1 = (bf16[16,288,128]{2,1,0:T(8,128)(2,1)}, bf16[16,288,128]{2,1,0:T(8,128)(2,1)S(1)}, u32[]{:S(2)}) copy-start(bf16[16,288,128]{2,1,0:T(8,128)(2,1)S(1)} %all-to-all-done.3.in_ref) | copy-start | bytes 3538948
  164.1 32.6 %all-to-all-start.2 = ((bf16[16,288,128]{2,1,0:T(8,128)(2,1)}), bf16[16,288,128]{2,1,0:T(8,128)(2,1)S(1)}, u32[]{:S(2)}, u32[]{:S(2)}) async-start(bf16[16,288,128]{2,1,0:T(8,128)(2,1)} %long_products.3), calls=%async_computation.2 | async-start | bytes 2359296 | tf_op jit(solution)/shard_map/all_to_all | solution.py:455
  168.7 32.8 %collective-permute-start.3 = (bf16[24,4096]{1,0:T(8,128)(2,1)S(1)}, bf16[24,4096]{1,0:T(8,128)(2,1)S(1)}, u32[]{:S(2)}, u32[]{:S(2)}) collective-permute-start(bf16[24,4096]{1,0:T(8,128)(2,1)S(1)} %pad_maximum_fusion.1), channel_id=1, source_target_pairs={{2,0},{4,2},{6,4},{8,6},{10,8},{12,10},{14,12},{16,14},{18,16},{20... | collective-permute-start | bytes 589832 | tf_op jit(solution)/shard_map/ppermute | solution.py:26
  196.7 11.4 %copy-start = (bf16[16,288,128]{2,1,0:T(8,128)(2,1)}, bf16[16,288,128]{2,1,0:T(8,128)(2,1)S(1)}, u32[]{:S(2)}) copy-start(bf16[16,288,128]{2,1,0:T(8,128)(2,1)S(1)} %all-to-all-done.2.in_ref) | copy-start | bytes 3538948
  198.7 15.3 %collective-permute-start.4 = (f32[1,1]{1,0:T(1,128)}, f32[1,1]{1,0:T(1,128)}, u32[]{:S(2)}, u32[]{:S(2)}) collective-permute-start(f32[1,1]{1,0:T(1,128)} %bitcast.1), channel_id=1, source_target_pairs={{0,1},{1,0},{2,3},{3,2},{4,5},{5,4},{6,7},{7,6},{8,9},{9,8},{10,11... | collective-permute-start | bytes 20 | tf_op jit(solution)/shard_map/ppermute | solution.py:461
  201.6 0.7 copy-start.6
  208.1 6.6 %copy-start.9 = (f32[128,128]{1,0:T(8,128)S(1)}, f32[128,128]{1,0:T(8,128)}, u32[]{:S(2)}) copy-start(f32[128,128]{1,0:T(8,128)} %get-tuple-element.43) | copy-start | bytes 196612

commit v4 on v2

--- a/solution.py
+++ b/solution.py
@@ -129,31 +129,33 @@
         send_ref[dest, 2 * cpd :, :] = long_rows[pl.ds(first, filter_rows), :].astype(BF16)
 
 
-def before_exchange(query, key, value, out_grad, tail, taps, long_filter, n, chunk, chunks):
-    rows = query.shape[0]
-    channels = query.shape[1] // chunks
-    groups = long_filter.shape[1] // chunks
-    cpd, gpd = channels // n, groups // n
-    tile = min(channels, max(512, cpd))
+def before_exchange(query, key, value, out_grad, tail, taps, long_filter, n, chunks):
+    rows, channels = query.shape
+    groups = long_filter.shape[1]
+    cpd, gpd = channels // (n * chunks), groups // (n * chunks)
+    tile = min(channels // chunks, max(512, cpd))
     per_tile = tile // cpd
     filter_rows = round_up(gpd, 16)
     send_rows = 2 * cpd + filter_rows
-    first = chunk * channels // tile
-    block = pl.BlockSpec((rows, tile), lambda i: (0, first + i))
-    own = pl.BlockSpec((rows, tile), lambda i: (0, i))
+    steps = n // per_tile
+    block = pl.BlockSpec((rows, tile), lambda i: (0, i))
     ext = pltpu.VMEM((tile // LANES, rows + EDGE, LANES), F32)
     return pl.pallas_call(
         functools.partial(before_kernel, cpd, gpd),
         grid=(channels // tile,),
         in_specs=[block] * 4
         + [
-            pl.BlockSpec((3 * EDGE, tile), lambda i: (0, first + i)),
-            pl.BlockSpec((3, taps.shape[1], tile), lambda i: (0, 0, first + i)),
-            pl.BlockSpec((rows, groups), lambda i: (0, chunk)),
+            pl.BlockSpec((3 * EDGE, tile), lambda i: (0, i)),
+            pl.BlockSpec((3, taps.shape[1], tile), lambda i: (0, 0, i)),
+            pl.BlockSpec((rows, groups), lambda i: (0, 0)),
         ],
-        out_specs=[pl.BlockSpec((per_tile, send_rows, rows), lambda i: (i, 0, 0)), own, own],
+        out_specs=[
+            pl.BlockSpec((per_tile, send_rows, rows), lambda i: (i % steps, i // steps, 0)),
+            block,
+            block,
+        ],
         out_shape=[
-            jax.ShapeDtypeStruct((n, send_rows, rows), BF16),
+            jax.ShapeDtypeStruct((n, chunks * send_rows, rows), BF16),
             jax.ShapeDtypeStruct((rows, channels), F32),
             jax.ShapeDtypeStruct((rows, channels), F32),
         ],
@@ -269,15 +271,17 @@
             out_ref[a, at : at + 2 * EDGE, :] = tile.astype(BF16)
 
 
-def long_products(received, cpd, gpd):
+def long_products(received, cpd, gpd, chunk, chunks):
     n, send_rows, rows = received.shape
+    send_rows = send_rows // chunks
     filter_rows = send_rows - 2 * cpd
     out_rows = send_rows + 2 * EDGE * max(1, cpd // LANES)
     span = n * rows
     return pl.pallas_call(
         functools.partial(long_kernel, cpd, gpd),
-        in_specs=[pl.BlockSpec(memory_space=pltpu.VMEM)],
-        out_specs=pl.BlockSpec(memory_space=pltpu.VMEM),
+        grid=(1,),
+        in_specs=[pl.BlockSpec((n, send_rows, rows), lambda i: (0, chunk, 0))],
+        out_specs=pl.BlockSpec((n, out_rows, rows), lambda i: (0, 0, 0)),
         out_shape=jax.ShapeDtypeStruct((n, out_rows, rows), BF16),
         scratch_shapes=[
             pltpu.VMEM((filter_rows, span), F32),
@@ -378,7 +382,6 @@
     per_tile = tile // cpd
     first = chunk * channels // tile
     block = pl.BlockSpec((rows, tile), lambda i: (0, first + i))
-    own = pl.BlockSpec((rows, tile), lambda i: (0, i))
     end = pl.BlockSpec((16, tile), lambda i: (rows // 16 - 1, first + i))
     ext = pltpu.VMEM((tile // LANES, rows + EDGE, LANES), F32)
     grad = jax.ShapeDtypeStruct(out_grad.shape, BF16)
@@ -388,8 +391,8 @@
         in_specs=[
             pl.BlockSpec((per_tile, in_rows, rows), lambda i: (i, 0, 0)),
             block,
-            own,
-            own,
+            block,
+            block,
             end,
             end,
             pl.BlockSpec((3 * EDGE, tile), lambda i: (0, first + i)),
@@ -435,20 +438,19 @@
     )
     chunks = 2 if gpd % 4 == 0 else 1
     cpd, gpd = cpd // chunks, gpd // chunks
-    received = []
-    shorts = []
-    for chunk in range(chunks):
-        send, short_k, short_v = before_exchange(
-            hyena_query, hyena_key, hyena_value, output_grad, tail, short_filter, long_filter, n, chunk, chunks
-        )
-        shorts.append((short_k, short_v))
-        received.append(lax.all_to_all(send, "ctx", split_axis=0, concat_axis=0, tiled=True))
-    attention = attend(query_heads, key_heads, value_heads, key_prev, value_prev, position)
-    received[0], attention = lax.optimization_barrier((received[0], attention))
+    send, short_k, short_v = before_exchange(
+        hyena_query, hyena_key, hyena_value, output_grad, tail, short_filter, long_filter, n, chunks
+    )
+    received = lax.all_to_all(send, "ctx", split_axis=0, concat_axis=0, tiled=True)
     returned = []
     for chunk in range(chunks):
-        results = long_products(received[chunk], cpd, gpd)
+        results = long_products(received, cpd, gpd, chunk, chunks)
+        if chunk == 0:
+            results, received, key_prev, value_prev = lax.optimization_barrier(
+                (results, received, key_prev, value_prev)
+            )
         returned.append(lax.all_to_all(results, "ctx", split_axis=0, concat_axis=0, tiled=True))
+    attention = attend(query_heads, key_heads, value_heads, key_prev, value_prev, position)
     norm_at = returned[0].shape[1] - 2 * EDGE * max(1, cpd // LANES) + EDGE - 2
     own_squares = sum(jnp.sum(r[:, norm_at : norm_at + 2, 0].astype(F32)) for r in returned).reshape(1, 1)
     squares = own_squares
@@ -459,7 +461,7 @@
     raws = []
     for chunk in range(chunks):
         *grads, raw = after_exchange(
-            returned[chunk], output_grad, *shorts[chunk], hyena_key, hyena_value, following, short_filter,
+            returned[chunk], output_grad, short_k, short_v, hyena_key, hyena_value, following, short_filter,
             groups, chunk, chunks, grads,
         )
         raws.append(raw)

time: 217 us -> 185 us (0.85)
  waiting for transfers between devices: 109 us -> 82.6 us
  starting transfers between devices: 32.2 us -> 27.6 us
    ppermute x4, waiting for transfers between devices: 51.2 us -> 12.9 us  [shifted(): return lax.ppermute(block, axis, route)]
    all_to_all x2 -> x1, waiting for transfers between devices: 33.8 us -> 45.6 us  [on_device(): lax.all_to_all(send, 'ctx', split_axis=0, concat_axis=0, tiled=True)]
    all_to_all x2 -> x1, starting transfers between devices: 9.94 us -> 5.43 us  [on_device(): lax.all_to_all(send, 'ctx', split_axis=0, concat_axis=0, tiled=True)]
    pallas_call x2 -> x1, Pallas kernels: 10.9 us -> 9.89 us  [before_exchange(): pl.pallas_call(functools.partial(before_kernel, cpd, gpd), grid=(channels...]
  transfers between devices with their start and end apart: 9 -> 8, of which waited for: 6 -> 5; matrix products, arithmetic and copies ran while one was open for 1% -> 1% of each run, Pallas kernels for 27% -> 29%
where the time goes in v4:
time: 185 us; the launch traced here: 184 us
  waiting for transfers between devices  82.6 us (45%)
  Pallas kernels  63.4 us (34%)
  starting transfers between devices  27.6 us (15%)
  local copies, waits for them, and re-layouts  5.16 us (3%)
  other arithmetic  2.87 us (2%)
  between operations  2.7 us (1%)
    all_to_all x1, waiting for transfers between devices, on_device(): lax.all_to_all(send, 'ctx', split_axis=0, concat_axis=0, tiled=True)  45.6 us
    pallas_call x2, Pallas kernels, long_products(): pl.pallas_call(functools.partial(long_kernel, cpd, gpd), grid=(1,), in_sp...  27.7 us
    all_to_all x2, waiting for transfers between devices, on_device(): lax.all_to_all(results, 'ctx', split_axis=0, concat_axis=0, tiled=True)  24.2 us
    pallas_call x1, Pallas kernels, attend(): pl.pallas_call(attend_kernel, grid=(channels // tile,), in_specs=[pl.Bloc...  14.1 us
    ppermute x4, waiting for transfers between devices, shifted(): return lax.ppermute(block, axis, route)  12.9 us
    pallas_call x2, Pallas kernels, after_exchange(): pl.pallas_call(functools.partial(after_kernel, cpd, gpd), grid=(channels...  11.7 us
    ppermute x4, starting transfers between devices, shifted(): return lax.ppermute(block, axis, route)  10.4 us
    pallas_call x1, Pallas kernels, before_exchange(): pl.pallas_call(functools.partial(before_kernel, cpd, gpd), grid=(channels...  9.89 us
  transfers between devices with their start and end apart: 8, of which 5 were waited for; matrix products, arithmetic and copies ran while one was open for 1% of the time, Pallas kernels for 29%

profile of v4, /device:TPU:16, one launch (start us, length us, event | category | flops | bytes accessed | tf_op | source)
XLA Modules:
  0.0 184.3 jit_solution(7237160459398994946)
XLA Ops:
  0.6 0.8 slice.24
  1.5 1.6 fusion
  3.1 1.9 %collective-permute-start = (bf16[24,4096]{1,0:T(8,128)(2,1)S(1)}, bf16[24,4096]{1,0:T(8,128)(2,1)S(1)}, u32[]{:S(2)}, u32[]{:S(2)}) collective-permute-start(bf16[24,4096]{1,0:T(8,128)(2,1)S(1)} %pad_maximum_fusion), channel_id=1, source_target_pairs={{0,2},{2,4},{4,6},{6,8},{8,10},{10,12},{12,14},{14,16},{16,18},{18... | collective-permute-start | bytes 589832 | tf_op jit(solution)/shard_map/ppermute | solution.py:26
  5.0 6.0 %collective-permute-done.tail_ref = bf16[24,4096]{1,0:T(8,128)(2,1)S(1)} collective-permute-done((bf16[24,4096]{1,0:T(8,128)(2,1)S(1)}, bf16[24,4096]{1,0:T(8,128)(2,1)S(1)}, u32[]{:S(2)}, u32[]{:S(2)}) %collective-permute-start) | collective-permute-done | bytes 196640 | tf_op jit(solution)/shard_map/ppermute | solution.py:26
  11.0 0.7 copy-done.6
  11.6 9.9 %before_exchange.1 = (bf16[16,544,128]{2,1,0:T(8,128)(2,1)}, f32[128,4096]{1,0:T(8,128)}, f32[128,4096]{1,0:T(8,128)}) custom-call(bf16[128,4096]{1,0:T(8,128)(2,1)} %q_ref.2, bf16[128,4096]{1,0:T(8,128)(2,1)} %k_end.3, bf16[128,4096]{1,0:T(8,128)(2,1)} %v_end.3, bf16[128,4096]{1,0:T(8,128)(2,1)} %og_ref.5, bf16[24,4096]{1,0:T(8,128)(2,1)} %copy-done.6, ...), custom_call_target="tpu_custom_call" | custom-call | flops 26214400 | bytes 10485760 | tf_op jit(solution)/shard_map/before_exchange/pallas_call | solution.py:143
  21.5 5.4 %all-to-all-start = ((bf16[16,544,128]{2,1,0:T(8,128)(2,1)}), bf16[16,544,128]{2,1,0:T(8,128)(2,1)S(1)}, u32[]{:S(2)}, u32[]{:S(2)}) async-start(bf16[16,544,128]{2,1,0:T(8,128)(2,1)} %get-tuple-element.20), calls=%async_computation | async-start | bytes 4456448 | tf_op jit(solution)/shard_map/all_to_all | solution.py:444
  27.0 0.0 copy-done.3
  27.0 2.1 %collective-permute-start.1 = (bf16[128,4096]{1,0:T(8,128)(2,1)S(1)}, bf16[128,4096]{1,0:T(8,128)(2,1)}, u32[]{:S(2)}, u32[]{:S(2)}) collective-permute-start(bf16[128,4096]{1,0:T(8,128)(2,1)S(1)} %copy-done.3), channel_id=1, source_target_pairs={{0,2},{2,4},{4,6},{6,8},{8,10},{10,12},{12,14},{14,16},{16,18},{18... | collective-permute-start | bytes 3145736 | tf_op jit(solution)/shard_map/ppermute | solution.py:26
  29.0 3.3 %collective-permute-start.2 = (bf16[128,4096]{1,0:T(8,128)(2,1)}, bf16[128,4096]{1,0:T(8,128)(2,1)}, u32[]{:S(2)}, u32[]{:S(2)}) collective-permute-start(bf16[128,4096]{1,0:T(8,128)(2,1)} %v_ref.3), channel_id=1, source_target_pairs={{0,2},{2,4},{4,6},{6,8},{8,10},{10,12},{12,14},{14,16},{16,18},{18... | collective-permute-start | bytes 3145736 | tf_op jit(solution)/shard_map/ppermute | solution.py:26
  32.4 45.6 %all-to-all-done.in_ref = bf16[16,544,128]{2,1,0:T(8,128)(2,1)S(1)} async-done(((bf16[16,544,128]{2,1,0:T(8,128)(2,1)}), bf16[16,544,128]{2,1,0:T(8,128)(2,1)S(1)}, u32[]{:S(2)}, u32[]{:S(2)}) %all-to-all-start) | async-done | bytes 2228256 | tf_op jit(solution)/shard_map/all_to_all | solution.py:444
  77.9 1.4 copy-done.2
  79.3 13.8 %long_products.2 = bf16[16,288,128]{2,1,0:T(8,128)(2,1)} custom-call(bf16[16,544,128]{2,1,0:T(8,128)(2,1)} %copy-done.2), custom_call_target="tpu_custom_call" | custom-call | flops 3221225472 | bytes 2359296 | tf_op jit(solution)/shard_map/long_products/pallas_call | solution.py:280
  93.1 0.0 collective-permute-done.1.kp_ref
  93.1 6.9 %collective-permute-done.2.vp_ref = bf16[128,4096]{1,0:T(8,128)(2,1)} collective-permute-done((bf16[128,4096]{1,0:T(8,128)(2,1)}, bf16[128,4096]{1,0:T(8,128)(2,1)}, u32[]{:S(2)}, u32[]{:S(2)}) %collective-permute-start.2) | collective-permute-done | bytes 1048608 | tf_op jit(solution)/shard_map/ppermute | solution.py:26
  100.0 4.2 %all-to-all-start.2 = ((bf16[16,288,128]{2,1,0:T(8,128)(2,1)}), bf16[16,288,128]{2,1,0:T(8,128)(2,1)S(1)}, u32[]{:S(2)}, u32[]{:S(2)}) async-start(bf16[16,288,128]{2,1,0:T(8,128)(2,1)} %long_products.2), calls=%async_computation.2 | async-start | bytes 2359296 | tf_op jit(solution)/shard_map/all_to_all | solution.py:452
  104.3 13.9 %long_products.3 = bf16[16,288,128]{2,1,0:T(8,128)(2,1)} custom-call(bf16[16,544,128]{2,1,0:T(8,128)(2,1)} %copy-done.2), custom_call_target="tpu_custom_call" | custom-call | flops 3221225472 | bytes 2359296 | tf_op jit(solution)/shard_map/long_products/pallas_call | solution.py:280
  118.2 14.1 %all-to-all-done.2.in_ref = bf16[16,288,128]{2,1,0:T(8,128)(2,1)S(1)} async-done(((bf16[16,288,128]{2,1,0:T(8,128)(2,1)}), bf16[16,288,128]{2,1,0:T(8,128)(2,1)S(1)}, u32[]{:S(2)}, u32[]{:S(2)}) %all-to-all-start.2) | async-done | bytes 1179680 | tf_op jit(solution)/shard_map/all_to_all | solution.py:452
  132.2 4.6 %all-to-all-start.1 = ((bf16[16,288,128]{2,1,0:T(8,128)(2,1)}), bf16[16,288,128]{2,1,0:T(8,128)(2,1)S(1)}, u32[]{:S(2)}, u32[]{:S(2)}) async-start(bf16[16,288,128]{2,1,0:T(8,128)(2,1)} %long_products.3), calls=%async_computation.1 | async-start | bytes 2359296 | tf_op jit(solution)/shard_map/all_to_all | solution.py:452
  136.9 3.1 %collective-permute-start.3 = (bf16[24,4096]{1,0:T(8,128)(2,1)S(1)}, bf16[24,4096]{1,0:T(8,128)(2,1)S(1)}, u32[]{:S(2)}, u32[]{:S(2)}) collective-permute-start(bf16[24,4096]{1,0:T(8,128)(2,1)S(1)} %pad_maximum_fusion.1), channel_id=1, source_target_pairs={{2,0},{4,2},{6,4},{8,6},{10,8},{12,10},{14,12},{16,14},{18,16},{20... | collective-permute-start | bytes 589832 | tf_op jit(solution)/shard_map/ppermute | solution.py:26
  140.1 14.1 %attend.1 = bf16[128,4096]{1,0:T(8,128)(2,1)} custom-call(s32[1]{0:T(128)} %bitcast.place_ref, bf16[128,4096]{1,0:T(8,128)(2,1)} %q_ref.3, bf16[128,4096]{1,0:T(8,128)(2,1)} %k_ref.3, bf16[128,4096]{1,0:T(8,128)(2,1)} %v_ref.3, bf16[128,4096]{1,0:T(8,128)(2,1)} %collective-permute-done.1.kp_ref, bf16[128,4096]{1,0:T(8,128)(2,1)} %collective-permute-done.2.vp_ref), custom_call_target="tpu_custom_call" | custom-call | flops 536870912 | bytes 6291456 | tf_op jit(solution)/shard_map/attend/pallas_call | solution.py:66
  154.1 0.6 convert_reduce_fusion.1
  154.8 10.1 %all-to-all-done.1.in_ref = bf16[16,288,128]{2,1,0:T(8,128)(2,1)S(1)} async-done(((bf16[16,288,128]{2,1,0:T(8,128)(2,1)}), bf16[16,288,128]{2,1,0:T(8,128)(2,1)S(1)}, u32[]{:S(2)}, u32[]{:S(2)}) %all-to-all-start.1) | async-done | bytes 1179680 | tf_op jit(solution)/shard_map/all_to_all | solution.py:452
  164.9 0.7 convert_reduce_fusion
  166.9 2.9 %collective-permute-start.4 = (f32[1,1]{1,0:T(1,128)}, f32[1,1]{1,0:T(1,128)}, u32[]{:S(2)}, u32[]{:S(2)}) collective-permute-start(f32[1,1]{1,0:T(1,128)} %bitcast.1), channel_id=1, source_target_pairs={{0,1},{1,0},{2,3},{3,2},{4,5},{5,4},{6,7},{7,6},{8,9},{9,8},{10,11... | collective-permute-start | bytes 20 | tf_op jit(solution)/shard_map/ppermute | solution.py:459
  169.7 0.0 collective-permute-done.3.next_ref
  169.7 0.7 copy-done.4
  170.4 5.9 %after_exchange.2 = (bf16[128,4096]{1,0:T(8,128)(2,1)}, bf16[128,4096]{1,0:T(8,128)(2,1)}, bf16[128,4096]{1,0:T(8,128)(2,1)}, f32[128,128]{1,0:T(8,128)}) custom-call(bf16[16,288,128]{2,1,0:T(8,128)(2,1)} %copy-done, bf16[128,4096]{1,0:T(8,128)(2,1)} %og_ref.5, f32[128,4096]{1,0:T(8,128)} %get-tuple-element.24.sk_ref, f32[128,4096]{1,0:T(8,128)} %get-tuple-element.25.sv_ref, ...), custom_call_target="tpu_custom_call" | custom-call | flops 15728640 | bytes 5767168 | tf_op jit(solution)/shard_map/after_exchange/pallas_call | solution.py:388
  176.3 0.0 copy-done.1
  176.3 0.0 copy-start.7
  176.3 5.9 %after_exchange.3 = (bf16[128,4096]{1,0:T(8,128)(2,1)}, bf16[128,4096]{1,0:T(8,128)(2,1)}, bf16[128,4096]{1,0:T(8,128)(2,1)}, f32[128,128]{1,0:T(8,128)}) custom-call(bf16[16,288,128]{2,1,0:T(8,128)(2,1)} %copy-done.1, bf16[128,4096]{1,0:T(8,128)(2,1)} %og_ref.5, ...), custom_call_target="tpu_custom_call", output_to_operand_aliasing={{0}: (8, {}), {1}: (9, {}), {2}: (10, {})} | custom-call | flops 15728640 | bytes 5767168 | tf_op jit(solution)/shard_map/after_exchange/pallas_call | solution.py:388
  182.8 1.5 maximum_multiply_fusion
  (15 shorter events, 0.1 us)
Async XLA Ops:
  3.1 7.9 %collective-permute-start = (bf16[24,4096]{1,0:T(8,128)(2,1)S(1)}, bf16[24,4096]{1,0:T(8,128)(2,1)S(1)}, u32[]{:S(2)}, u32[]{:S(2)}) collective-permute-start(bf16[24,4096]{1,0:T(8,128)(2,1)S(1)} %pad_maximum_fusion), channel_id=1, source_target_pairs={{0,2},{2,4},{4,6},{6,8},{8,10},{10,12},{12,14},{14,16},{16,18},{18... | collective-permute-start | bytes 589832 | tf_op jit(solution)/shard_map/ppermute | solution.py:26
  11.0 0.7 copy-start.6
  21.5 5.4 %copy-start.3 = (bf16[128,4096]{1,0:T(8,128)(2,1)S(1)}, bf16[128,4096]{1,0:T(8,128)(2,1)}, u32[]{:S(2)}) copy-start(bf16[128,4096]{1,0:T(8,128)(2,1)} %k_ref.3) | copy-start | bytes 3145732
  21.5 56.4 %all-to-all-start = ((bf16[16,544,128]{2,1,0:T(8,128)(2,1)}), bf16[16,544,128]{2,1,0:T(8,128)(2,1)S(1)}, u32[]{:S(2)}, u32[]{:S(2)}) async-start(bf16[16,544,128]{2,1,0:T(8,128)(2,1)} %get-tuple-element.20), calls=%async_computation | async-start | bytes 4456448 | tf_op jit(solution)/shard_map/all_to_all | solution.py:444
  27.0 66.1 %collective-permute-start.1 = (bf16[128,4096]{1,0:T(8,128)(2,1)S(1)}, bf16[128,4096]{1,0:T(8,128)(2,1)}, u32[]{:S(2)}, u32[]{:S(2)}) collective-permute-start(bf16[128,4096]{1,0:T(8,128)(2,1)S(1)} %copy-done.3), channel_id=1, source_target_pairs={{0,2},{2,4},{4,6},{6,8},{8,10},{10,12},{12,14},{14,16},{16,18},{18... | collective-permute-start | bytes 3145736 | tf_op jit(solution)/shard_map/ppermute | solution.py:26
  29.0 71.0 %collective-permute-start.2 = (bf16[128,4096]{1,0:T(8,128)(2,1)}, bf16[128,4096]{1,0:T(8,128)(2,1)}, u32[]{:S(2)}, u32[]{:S(2)}) collective-permute-start(bf16[128,4096]{1,0:T(8,128)(2,1)} %v_ref.3), channel_id=1, source_target_pairs={{0,2},{2,4},{4,6},{6,8},{8,10},{10,12},{12,14},{14,16},{16,18},{18... | collective-permute-start | bytes 3145736 | tf_op jit(solution)/shard_map/ppermute | solution.py:26
  77.9 1.4 copy-start.2
  100.0 32.2 %all-to-all-start.2 = ((bf16[16,288,128]{2,1,0:T(8,128)(2,1)}), bf16[16,288,128]{2,1,0:T(8,128)(2,1)S(1)}, u32[]{:S(2)}, u32[]{:S(2)}) async-start(bf16[16,288,128]{2,1,0:T(8,128)(2,1)} %long_products.2), calls=%async_computation.2 | async-start | bytes 2359296 | tf_op jit(solution)/shard_map/all_to_all | solution.py:452
  118.2 18.7 %slice-start = ((bf16[128,4096]{1,0:T(8,128)(2,1)}), bf16[8,4096]{1,0:T(8,128)(2,1)S(1)}, s32[]{:S(2)}) async-start(bf16[128,4096]{1,0:T(8,128)(2,1)} %og_ref.5), calls=%async_computation.3 | async-start | bytes 131072 | tf_op jit(solution)/shard_map/slice | solution.py:437
  118.2 18.7 %copy-start.5 = (bf16[8,4096]{1,0:T(8,128)(2,1)S(1)}, bf16[8,4096]{1,0:T(8,128)(2,1)}, u32[]{:S(2)}) copy-start(bf16[8,4096]{1,0:T(8,128)(2,1)} %get-tuple-element.40) | copy-start | bytes 196612
  132.2 21.9 %copy-start = (bf16[16,288,128]{2,1,0:T(8,128)(2,1)}, bf16[16,288,128]{2,1,0:T(8,128)(2,1)S(1)}, u32[]{:S(2)}) copy-start(bf16[16,288,128]{2,1,0:T(8,128)(2,1)S(1)} %all-to-all-done.2.in_ref) | copy-start | bytes 3538948
  132.2 32.6 %all-to-all-start.1 = ((bf16[16,288,128]{2,1,0:T(8,128)(2,1)}), bf16[16,288,128]{2,1,0:T(8,128)(2,1)S(1)}, u32[]{:S(2)}, u32[]{:S(2)}) async-start(bf16[16,288,128]{2,1,0:T(8,128)(2,1)} %long_products.3), calls=%async_computation.1 | async-start | bytes 2359296 | tf_op jit(solution)/shard_map/all_to_all | solution.py:452
  136.9 32.8 %collective-permute-start.3 = (bf16[24,4096]{1,0:T(8,128)(2,1)S(1)}, bf16[24,4096]{1,0:T(8,128)(2,1)S(1)}, u32[]{:S(2)}, u32[]{:S(2)}) collective-permute-start(bf16[24,4096]{1,0:T(8,128)(2,1)S(1)} %pad_maximum_fusion.1), channel_id=1, source_target_pairs={{2,0},{4,2},{6,4},{8,6},{10,8},{12,10},{14,12},{16,14},{18,16},{20... | collective-permute-start | bytes 589832 | tf_op jit(solution)/shard_map/ppermute | solution.py:26
  164.9 11.4 %copy-start.1 = (bf16[16,288,128]{2,1,0:T(8,128)(2,1)}, bf16[16,288,128]{2,1,0:T(8,128)(2,1)S(1)}, u32[]{:S(2)}) copy-start(bf16[16,288,128]{2,1,0:T(8,128)(2,1)S(1)} %all-to-all-done.1.in_ref) | copy-start | bytes 3538948
  166.9 15.3 %collective-permute-start.4 = (f32[1,1]{1,0:T(1,128)}, f32[1,1]{1,0:T(1,128)}, u32[]{:S(2)}, u32[]{:S(2)}) collective-permute-start(f32[1,1]{1,0:T(1,128)} %bitcast.1), channel_id=1, source_target_pairs={{0,1},{1,0},{2,3},{3,2},{4,5},{5,4},{6,7},{7,6},{8,9},{9,8},{10,11... | collective-permute-start | bytes 20 | tf_op jit(solution)/shard_map/ppermute | solution.py:459
  169.7 0.7 copy-start.4
  176.3 6.5 %copy-start.7 = (f32[128,128]{1,0:T(8,128)S(1)}, f32[128,128]{1,0:T(8,128)}, u32[]{:S(2)}) copy-start(f32[128,128]{1,0:T(8,128)} %get-tuple-element.33) | copy-start | bytes 196612

commit v5 on v4

--- a/solution.py
+++ b/solution.py
@@ -28,6 +28,12 @@
 
 def round_up(value, step):
     return -(-value // step) * step
+
+
+def reversal(size):
+    row = lax.broadcasted_iota(jnp.int32, (size, size), 0)
+    col = lax.broadcasted_iota(jnp.int32, (size, size), 1)
+    return jnp.where(row + col == size - 1, 1.0, 0.0).astype(BF16)
 
 
 def attend_kernel(place_ref, q_ref, k_ref, v_ref, kp_ref, vp_ref, out_ref):
@@ -102,6 +108,7 @@
         long_rows[...] = jnp.zeros_like(long_rows)
         long_rows[0:groups, :] = long_ref[...].T
 
+    turn = reversal(rows)
     for j in range(q_ref.shape[1] // LANES):
         at = slice(j * LANES, (j + 1) * LANES)
         tail = tail_ref[:, at].astype(F32)
@@ -116,6 +123,7 @@
         sv_ref[:, at] = short_v
         mixed = (short_k * short_v).T.astype(BF16)
         delta = (og_ref[:, at].astype(F32) * short_q).T.astype(BF16)
+        delta = jnp.dot(delta, turn, preferred_element_type=F32).astype(BF16)
         width = min(cpd, LANES)
         for piece in range(LANES // width):
             channel = j * LANES + piece * width
@@ -173,68 +181,64 @@
     gw = cpd // gpd
     span = n * rows
     filter_rows = send_rows - 2 * cpd
+    taps[:, 0:rows] = jnp.zeros((filter_rows, rows), F32)
     for a in range(n):
-        taps[:, a * rows : (a + 1) * rows] = in_ref[a, 2 * cpd :, :].astype(F32)
+        taps[:, (a + 1) * rows : (a + 2) * rows] = in_ref[a, 2 * cpd :, :].astype(F32)
+    for slot in range(2):
+        wide[slot, :, 0:rows] = jnp.zeros((rows, rows), BF16)
+        gram[slot, :, span:] = jnp.zeros((rows, rows), F32)
     if gpd < filter_rows:
         raw[...] = jnp.zeros_like(raw)
-    row8 = lax.broadcasted_iota(jnp.int32, (8, span), 0)
-    row_tile = lax.broadcasted_iota(jnp.int32, (8, rows), 0)
-    lane_tile = lax.broadcasted_iota(jnp.int32, (8, rows), 1)
-    no_rows = jnp.zeros((gw, rows), BF16)
-
-    def keep_upper(block, first):
-        head = jnp.where(lane_tile >= row_tile + first, block[:, :rows], 0.0)
-        return jnp.concatenate([head, block[:, rows:]], 1)
+    turn = reversal(rows)
 
     def one_group(g, slot):
-        base = jnp.broadcast_to(taps[pl.ds(g, 1), :], (8, span))
-        for bit in (1, 2, 4):
-            base = jnp.where((row8 & bit) != 0, pltpu.roll(base, bit, 1), base)
-        for m in range(0, rows // 8, 2):
-            low = base if m == 0 else pltpu.roll(base, 8 * m, 1)
-            high = pltpu.roll(base, 8 * m + 8, 1)
-            pair = jnp.concatenate([keep_upper(low, 8 * m), keep_upper(high, 8 * m + 8)], 0)
-            wide[slot, 8 * m : 8 * m + 16, :] = pair.astype(BF16)
+        line = jnp.broadcast_to(taps[pl.ds(g, 1), :], (16, span + rows))
+        base = pltpu.roll(line, 0, 1, stride=1, stride_axis=0).astype(BF16)
+        for m in range(rows // 16):
+            moved = base if m == 0 else pltpu.roll(base, 16 * m, 1)
+            wide[slot, 16 * m : 16 * m + 16, rows:] = moved[:, rows:]
         first = pl.multiple_of(g * gw, gw)
-        x = in_ref[:, pl.ds(first, gw), :].reshape(n * gw, rows)
+        x = in_ref[:, pl.ds(first, gw), :]
         second = pl.multiple_of(cpd + g * gw, gw)
-        d = in_ref[:, pl.ds(second, gw), :].reshape(n * gw, rows)
-        x_turned = x.astype(F32).T.astype(BF16)
-        conv = None
-        back = None
+        d = in_ref[:, pl.ds(second, gw), :]
+        both = [jnp.concatenate([x[a], d[n - 1 - a]], 0) for a in range(n)]
+        lhs = jnp.concatenate(
+            [jnp.concatenate([both[a], both[a + 1]], 1) for a in range(0, n, 2)], 0
+        )
+        total = None
+        for k in range(n // 2):
+            skip = 2 * gw * k
+            low = 2 * rows * k
+            tile = jnp.concatenate(
+                [wide[slot, :, low + rows : low + 3 * rows], wide[slot, :, low : low + 2 * rows]], 0
+            )
+            part = jnp.dot(lhs[: n * gw - skip], tile, preferred_element_type=F32)
+            total = part if k == 0 else jnp.concatenate([total[:skip], total[skip:] + part], 0)
+        for a in range(n):
+            at = slice(a % 2 * rows, (a % 2 + 1) * rows)
+            top = a // 2 * 2 * gw
+            out_ref[a, pl.ds(first, gw), :] = total[top : top + gw, at].astype(BF16)
+            out_ref[n - 1 - a, pl.ds(second, gw), :] = total[top + gw : top + 2 * gw, at].astype(BF16)
+        x_turned = x.reshape(n * gw, rows).astype(F32).T.astype(BF16)
+        d = d.reshape(n * gw, rows)
+        no_rows = jnp.zeros((n * gw, rows), BF16)
+
+        def offset(k):
+            held = (k + 1) * gw
+            if held == n * gw:
+                return d
+            return jnp.concatenate([d[n * gw - held :], no_rows[held:]], 0)
+
         for k in range(0, n, 2):
-            count = (n - k) * gw
-            at = slice(k * rows, (k + 2) * rows)
-            ahead = jnp.concatenate([no_rows, x[: count - gw]], 0)
-            stacked = jnp.concatenate(
-                [
-                    wide[slot, :, k * rows : (k + 1) * rows],
-                    wide[slot, :, (k + 1) * rows : (k + 2) * rows],
-                ],
-                0,
+            pairs = jnp.concatenate([offset(k), offset(k + 1)], 1)
+            gram[slot, :, k * rows : (k + 2) * rows] = jnp.dot(
+                x_turned, pairs, preferred_element_type=F32
             )
-            part = jnp.dot(
-                jnp.concatenate([x[:count], ahead], 1), stacked, preferred_element_type=F32
-            )
-            conv = part if k == 0 else jnp.concatenate([conv[: k * gw], conv[k * gw :] + part], 0)
-            later = jnp.concatenate([d[(k + 1) * gw :], no_rows], 0)
-            pairs = jnp.concatenate([d[k * gw :], later], 1)
-            part = lax.dot_general(
-                pairs, wide[slot, :, at], (((1,), (1,)), ((), ())), preferred_element_type=F32
-            )
-            back = part if k == 0 else jnp.concatenate([back[:count] + part, back[count:]], 0)
-            if k > 0:
-                pairs = jnp.concatenate([pairs, jnp.zeros((k * gw, 2 * rows), BF16)], 0)
-            gram[slot, :, at] = jnp.dot(x_turned, pairs, preferred_element_type=F32)
-        out_ref[:, pl.ds(first, gw), :] = conv.astype(BF16).reshape(n, gw, rows)
-        out_ref[:, pl.ds(second, gw), :] = back.astype(BF16).reshape(n, gw, rows)
-        total = keep_upper(gram[slot, 0:8, :], 0)
+        sums = gram[slot, 0:8, :]
         for m in range(1, rows // 8):
-            block = keep_upper(gram[slot, 8 * m : 8 * m + 8, :], 8 * m)
-            total = total + pltpu.roll(block, span - 8 * m, 1)
-        for bit in (1, 2, 4):
-            total = jnp.where((row8 & bit) != 0, pltpu.roll(total, span - bit, 1), total)
-        line = jnp.sum(total, axis=0, keepdims=True)
+            sums = sums + pltpu.roll(gram[slot, 8 * m : 8 * m + 8, :], 8 * m, 1)
+        sums = pltpu.roll(sums, 0, 1, stride=1, stride_axis=0)
+        line = jnp.sum(sums, axis=0, keepdims=True)[:, :span]
         raw[pl.ds(g, 1), :] = line
         return line * line
 
@@ -247,11 +251,14 @@
     upper = total.astype(BF16).astype(F32)
     lower = total - upper
     for a in range(n):
-        out_ref[a, 2 * cpd : 2 * cpd + filter_rows, :] = raw[:, a * rows : (a + 1) * rows].astype(BF16)
+        tile = raw[:, (n - 1 - a) * rows : (n - a) * rows].astype(BF16)
+        out_ref[a, 2 * cpd : 2 * cpd + filter_rows, :] = jnp.dot(
+            tile, turn, preferred_element_type=F32
+        ).astype(BF16)
     halo_at = 2 * cpd + filter_rows
     row = lax.broadcasted_iota(jnp.int32, (2 * EDGE, 2 * rows), 0)
     lane = lax.broadcasted_iota(jnp.int32, (2 * EDGE, 2 * rows), 1)
-    wanted = jnp.where(row < EDGE, row, rows - EDGE + row)
+    wanted = jnp.where(row < EDGE, row, 2 * rows - 1 + EDGE - row)
     pick = jnp.where(lane == wanted, 1.0, 0.0).astype(BF16)
     row_out = lax.broadcasted_iota(jnp.int32, (2 * EDGE, rows), 0)
     for a in range(n):
@@ -284,9 +291,9 @@
         out_specs=pl.BlockSpec((n, out_rows, rows), lambda i: (0, 0, 0)),
         out_shape=jax.ShapeDtypeStruct((n, out_rows, rows), BF16),
         scratch_shapes=[
-            pltpu.VMEM((filter_rows, span), F32),
-            pltpu.VMEM((2, rows, span), BF16),
-            pltpu.VMEM((2, rows, span), F32),
+            pltpu.VMEM((filter_rows, span + rows), F32),
+            pltpu.VMEM((2, rows, span + rows), BF16),
+            pltpu.VMEM((2, rows, span + rows), F32),
             pltpu.VMEM((filter_rows, span), F32),
         ],
         compiler_params=params(),
@@ -326,6 +333,7 @@
     halo_rows = 2 * EDGE * max(1, cpd // LANES)
     halo_at = in_rows - halo_rows
     end_rows = k_end.shape[0]
+    turn = reversal(rows)
     for j in range(og_ref.shape[1] // LANES):
         at = slice(j * LANES, (j + 1) * LANES)
         if cpd >= LANES:
@@ -342,7 +350,7 @@
                 [in_ref[d, halo_at:, :].astype(F32)[:, :cpd] for d in dests], 1
             )
         conv = conv.astype(F32).T
-        back = back.astype(F32).T
+        back = jnp.dot(back, turn, preferred_element_type=F32).T
         following = next_ref[:, at].astype(F32)
         taps_k = taps_ref[1, :, at]
         taps_v = taps_ref[2, :, at]
@@ -433,14 +441,13 @@
     )
     key_prev = shifted(key_heads, "ctx", 1)
     value_prev = shifted(value_heads, "ctx", 1)
-    following = shifted(
-        jnp.concatenate([a[:EDGE] for a in (output_grad, hyena_key, hyena_value)], 0), "ctx", -1
-    )
     chunks = 2 if gpd % 4 == 0 else 1
     cpd, gpd = cpd // chunks, gpd // chunks
     send, short_k, short_v = before_exchange(
         hyena_query, hyena_key, hyena_value, output_grad, tail, short_filter, long_filter, n, chunks
     )
+    send, *sources = lax.optimization_barrier((send, output_grad, hyena_key, hyena_value))
+    following = shifted(jnp.concatenate([a[:EDGE] for a in sources], 0), "ctx", -1)
     received = lax.all_to_all(send, "ctx", split_axis=0, concat_axis=0, tiled=True)
     returned = []
     for chunk in range(chunks):
@@ -451,15 +458,20 @@
             )
         returned.append(lax.all_to_all(results, "ctx", split_axis=0, concat_axis=0, tiled=True))
     attention = attend(query_heads, key_heads, value_heads, key_prev, value_prev, position)
-    norm_at = returned[0].shape[1] - 2 * EDGE * max(1, cpd // LANES) + EDGE - 2
-    own_squares = sum(jnp.sum(r[:, norm_at : norm_at + 2, 0].astype(F32)) for r in returned).reshape(1, 1)
-    squares = own_squares
-    for distance in range(1, tp):
-        route = [(i, (i + distance) % tp) for i in range(tp)]
-        squares = squares + lax.ppermute(own_squares, "tp", route)
     grads = ()
     raws = []
+    norm_at = returned[0].shape[1] - 2 * EDGE * max(1, cpd // LANES) + EDGE - 2
+    own_squares = jnp.zeros((1, 1), F32)
+    squares = own_squares
     for chunk in range(chunks):
+        if chunk > 0:
+            returned[chunk], *grads = lax.optimization_barrier((returned[chunk], *grads))
+        own_squares = own_squares + jnp.sum(returned[chunk][:, norm_at : norm_at + 2, 0].astype(F32))
+        if chunk + 1 == chunks:
+            squares = own_squares
+            for distance in range(1, tp):
+                route = [(i, (i + distance) % tp) for i in range(tp)]
+                squares = squares + lax.ppermute(own_squares, "tp", route)
         *grads, raw = after_exchange(
             returned[chunk], output_grad, short_k, short_v, hyena_key, hyena_value, following, short_filter,
             groups, chunk, chunks, grads,

time: 185 us -> 188 us (1.016)
  waiting for transfers between devices: 82.6 us -> 91.4 us
  Pallas kernels: 63.4 us -> 54.8 us
    ppermute x4, waiting for transfers between devices: 12.9 us -> 27.8 us  [shifted(): return lax.ppermute(block, axis, route)]
    pallas_call x2, Pallas kernels: 27.7 us -> 19.8 us  [long_products(): pl.pallas_call(functools.partial(long_kernel, cpd, gpd), grid=(1,), in_sp...]
    all_to_all x2, waiting for transfers between devices: 24.2 us -> 18 us  [on_device(): lax.all_to_all(results, 'ctx', split_axis=0, concat_axis=0, tiled=True)]
  transfers between devices with their start and end apart: 8 -> 8, of which waited for: 5 -> 5; matrix products, arithmetic and copies ran while one was open for 1% -> 0% of each run, Pallas kernels for 29% -> 24%
where the time goes in v5:
time: 188 us; the launch traced here: 186 us
  waiting for transfers between devices  91.4 us (49%)
  Pallas kernels  54.8 us (29%)
  starting transfers between devices  27.6 us (15%)
  local copies, waits for them, and re-layouts  6.3 us (3%)
  other arithmetic  2.98 us (2%)
  between operations  2.57 us (1%)
    all_to_all x1, waiting for transfers between devices, on_device(): lax.all_to_all(send, 'ctx', split_axis=0, concat_axis=0, tiled=True)  45.6 us
    ppermute x4, waiting for transfers between devices, shifted(): return lax.ppermute(block, axis, route)  27.8 us
    pallas_call x2, Pallas kernels, long_products(): pl.pallas_call(functools.partial(long_kernel, cpd, gpd), grid=(1,), in_sp...  19.8 us
    all_to_all x2, waiting for transfers between devices, on_device(): lax.all_to_all(results, 'ctx', split_axis=0, concat_axis=0, tiled=True)  18 us
    pallas_call x1, Pallas kernels, attend(): pl.pallas_call(attend_kernel, grid=(channels // tile,), in_specs=[pl.Bloc...  14.1 us
    pallas_call x2, Pallas kernels, after_exchange(): pl.pallas_call(functools.partial(after_kernel, cpd, gpd), grid=(channels...  11.3 us
    ppermute x4, starting transfers between devices, shifted(): return lax.ppermute(block, axis, route)  10.4 us
    pallas_call x1, Pallas kernels, before_exchange(): pl.pallas_call(functools.partial(before_kernel, cpd, gpd), grid=(channels...  9.69 us
  transfers between devices with their start and end apart: 8, of which 5 were waited for; matrix products, arithmetic and copies ran while one was open for 0% of the time, Pallas kernels for 24%

profile of v5, /device:TPU:16, one launch (start us, length us, event | category | flops | bytes accessed | tf_op | source)
XLA Modules:
  0.0 185.7 jit_solution(10259469140374127793)
XLA Ops:
  0.6 0.8 slice.24
  1.5 0.8 slice.25
  2.3 0.8 slice.26
  3.2 1.9 %collective-permute-start = (bf16[24,4096]{1,0:T(8,128)(2,1)S(1)}, bf16[24,4096]{1,0:T(8,128)(2,1)S(1)}, u32[]{:S(2)}, u32[]{:S(2)}) collective-permute-start(bf16[24,4096]{1,0:T(8,128)(2,1)S(1)} %pad_maximum_fusion), channel_id=1, source_target_pairs={{0,2},{2,4},{4,6},{6,8},{8,10},{10,12},{12,14},{14,16},{16,18},{18... | collective-permute-start | bytes 589832 | tf_op jit(solution)/shard_map/ppermute | solution.py:26
  5.1 6.0 %collective-permute-done.tail_ref = bf16[24,4096]{1,0:T(8,128)(2,1)S(1)} collective-permute-done((bf16[24,4096]{1,0:T(8,128)(2,1)S(1)}, bf16[24,4096]{1,0:T(8,128)(2,1)S(1)}, u32[]{:S(2)}, u32[]{:S(2)}) %collective-permute-start) | collective-permute-done | bytes 196640 | tf_op jit(solution)/shard_map/ppermute | solution.py:26
  11.1 0.7 copy-done.5
  11.7 9.7 %before_exchange.1 = (bf16[16,544,128]{2,1,0:T(8,128)(2,1)}, f32[128,4096]{1,0:T(8,128)}, f32[128,4096]{1,0:T(8,128)}) custom-call(bf16[128,4096]{1,0:T(8,128)(2,1)} %q_ref.2, bf16[128,4096]{1,0:T(8,128)(2,1)} %k_end.3, bf16[128,4096]{1,0:T(8,128)(2,1)} %v_end.3, bf16[128,4096]{1,0:T(8,128)(2,1)} %og_ref.5, bf16[24,4096]{1,0:T(8,128)(2,1)} %copy-done.5, ...), custom_call_target="tpu_custom_call" | custom-call | flops 26214400 | bytes 10485760 | tf_op jit(solution)/shard_map/before_exchange/pallas_call | solution.py:151
  21.4 5.4 %all-to-all-start = ((bf16[16,544,128]{2,1,0:T(8,128)(2,1)}), bf16[16,544,128]{2,1,0:T(8,128)(2,1)S(1)}, u32[]{:S(2)}, u32[]{:S(2)}) async-start(bf16[16,544,128]{2,1,0:T(8,128)(2,1)} %get-tuple-element.29), calls=%async_computation | async-start | bytes 4456448 | tf_op jit(solution)/shard_map/all_to_all | solution.py:451
  26.9 0.0 copy-done.3
  26.9 2.1 %collective-permute-start.1 = (bf16[128,4096]{1,0:T(8,128)(2,1)S(1)}, bf16[128,4096]{1,0:T(8,128)(2,1)}, u32[]{:S(2)}, u32[]{:S(2)}) collective-permute-start(bf16[128,4096]{1,0:T(8,128)(2,1)S(1)} %copy-done.3), channel_id=1, source_target_pairs={{0,2},{2,4},{4,6},{6,8},{8,10},{10,12},{12,14},{14,16},{16,18},{18... | collective-permute-start | bytes 3145736 | tf_op jit(solution)/shard_map/ppermute | solution.py:26
  28.9 3.3 %collective-permute-start.2 = (bf16[128,4096]{1,0:T(8,128)(2,1)}, bf16[128,4096]{1,0:T(8,128)(2,1)}, u32[]{:S(2)}, u32[]{:S(2)}) collective-permute-start(bf16[128,4096]{1,0:T(8,128)(2,1)} %v_ref.3), channel_id=1, source_target_pairs={{0,2},{2,4},{4,6},{6,8},{8,10},{10,12},{12,14},{14,16},{16,18},{18... | collective-permute-start | bytes 3145736 | tf_op jit(solution)/shard_map/ppermute | solution.py:26
  32.3 45.6 %all-to-all-done.in_ref = bf16[16,544,128]{2,1,0:T(8,128)(2,1)S(1)} async-done(((bf16[16,544,128]{2,1,0:T(8,128)(2,1)}), bf16[16,544,128]{2,1,0:T(8,128)(2,1)S(1)}, u32[]{:S(2)}, u32[]{:S(2)}) %all-to-all-start) | async-done | bytes 2228256 | tf_op jit(solution)/shard_map/all_to_all | solution.py:451
  77.9 1.4 copy-done.2
  79.2 9.8 %long_products.2 = bf16[16,288,128]{2,1,0:T(8,128)(2,1)} custom-call(bf16[16,544,128]{2,1,0:T(8,128)(2,1)} %copy-done.2), custom_call_target="tpu_custom_call" | custom-call | flops 3221225472 | bytes 2359296 | tf_op jit(solution)/shard_map/long_products/pallas_call | solution.py:287
  89.1 0.0 collective-permute-done.1.kp_ref
  89.1 10.9 %collective-permute-done.2.vp_ref = bf16[128,4096]{1,0:T(8,128)(2,1)} collective-permute-done((bf16[128,4096]{1,0:T(8,128)(2,1)}, bf16[128,4096]{1,0:T(8,128)(2,1)}, u32[]{:S(2)}, u32[]{:S(2)}) %collective-permute-start.2) | collective-permute-done | bytes 1048608 | tf_op jit(solution)/shard_map/ppermute | solution.py:26
  100.0 4.2 %all-to-all-start.2 = ((bf16[16,288,128]{2,1,0:T(8,128)(2,1)}), bf16[16,288,128]{2,1,0:T(8,128)(2,1)S(1)}, u32[]{:S(2)}, u32[]{:S(2)}) async-start(bf16[16,288,128]{2,1,0:T(8,128)(2,1)} %long_products.2), calls=%async_computation.2 | async-start | bytes 2359296 | tf_op jit(solution)/shard_map/all_to_all | solution.py:459
  104.2 9.9 %long_products.3 = bf16[16,288,128]{2,1,0:T(8,128)(2,1)} custom-call(bf16[16,544,128]{2,1,0:T(8,128)(2,1)} %copy-done.2), custom_call_target="tpu_custom_call" | custom-call | flops 3221225472 | bytes 2359296 | tf_op jit(solution)/shard_map/long_products/pallas_call | solution.py:287
  114.1 18.0 %all-to-all-done.2.in_ref = bf16[16,288,128]{2,1,0:T(8,128)(2,1)S(1)} async-done(((bf16[16,288,128]{2,1,0:T(8,128)(2,1)}), bf16[16,288,128]{2,1,0:T(8,128)(2,1)S(1)}, u32[]{:S(2)}, u32[]{:S(2)}) %all-to-all-start.2) | async-done | bytes 1179680 | tf_op jit(solution)/shard_map/all_to_all | solution.py:459
  132.2 1.0 copy-done.1
  133.2 4.6 %all-to-all-start.1 = ((bf16[16,288,128]{2,1,0:T(8,128)(2,1)}), bf16[16,288,128]{2,1,0:T(8,128)(2,1)S(1)}, u32[]{:S(2)}, u32[]{:S(2)}) async-start(bf16[16,288,128]{2,1,0:T(8,128)(2,1)} %long_products.3), calls=%async_computation.1 | async-start | bytes 2359296 | tf_op jit(solution)/shard_map/all_to_all | solution.py:459
  137.8 3.1 %collective-permute-start.3 = (bf16[24,4096]{1,0:T(8,128)(2,1)S(1)}, bf16[24,4096]{1,0:T(8,128)(2,1)S(1)}, u32[]{:S(2)}, u32[]{:S(2)}) collective-permute-start(bf16[24,4096]{1,0:T(8,128)(2,1)S(1)} %pad_maximum_fusion.1), channel_id=1, source_target_pairs={{2,0},{4,2},{6,4},{8,6},{10,8},{12,10},{14,12},{16,14},{18,16},{20... | collective-permute-start | bytes 589832 | tf_op jit(solution)/shard_map/ppermute | solution.py:26
  141.0 14.1 %attend.1 = bf16[128,4096]{1,0:T(8,128)(2,1)} custom-call(s32[1]{0:T(128)} %bitcast.place_ref, bf16[128,4096]{1,0:T(8,128)(2,1)} %q_ref.3, bf16[128,4096]{1,0:T(8,128)(2,1)} %k_ref.3, bf16[128,4096]{1,0:T(8,128)(2,1)} %v_ref.3, bf16[128,4096]{1,0:T(8,128)(2,1)} %collective-permute-done.1.kp_ref, bf16[128,4096]{1,0:T(8,128)(2,1)} %collective-permute-done.2.vp_ref), custom_call_target="tpu_custom_call" | custom-call | flops 536870912 | bytes 6291456 | tf_op jit(solution)/shard_map/attend/pallas_call | solution.py:72
  155.1 11.0 %collective-permute-done.3.next_ref = bf16[24,4096]{1,0:T(8,128)(2,1)S(1)} collective-permute-done((bf16[24,4096]{1,0:T(8,128)(2,1)S(1)}, bf16[24,4096]{1,0:T(8,128)(2,1)S(1)}, u32[]{:S(2)}, u32[]{:S(2)}) %collective-permute-start.3) | collective-permute-done | bytes 196640 | tf_op jit(solution)/shard_map/ppermute | solution.py:26
  166.0 0.7 copy-done.4
  166.7 5.6 %after_exchange.2 = (bf16[128,4096]{1,0:T(8,128)(2,1)}, bf16[128,4096]{1,0:T(8,128)(2,1)}, bf16[128,4096]{1,0:T(8,128)(2,1)}, f32[128,128]{1,0:T(8,128)}) custom-call(bf16[16,288,128]{2,1,0:T(8,128)(2,1)} %copy-done.1, bf16[128,4096]{1,0:T(8,128)(2,1)} %og_ref.5, f32[128,4096]{1,0:T(8,128)} %get-tuple-element.34.sk_ref, ...), custom_call_target="tpu_custom_call" | custom-call | flops 15728640 | bytes 5767168 | tf_op jit(solution)/shard_map/after_exchange/pallas_call | solution.py:396
  172.3 0.0 all-to-all-done.1.in_ref
  172.4 1.4 convert_reduce_fusion
  175.0 0.0 copy-start.6
  175.0 2.9 %collective-permute-start.4 = (f32[1,1]{1,0:T(1,128)}, f32[1,1]{1,0:T(1,128)}, u32[]{:S(2)}, u32[]{:S(2)}) collective-permute-start(f32[1,1]{1,0:T(1,128)} %bitcast.1), channel_id=1, source_target_pairs={{0,1},{1,0},{2,3},{3,2},{4,5},{5,4},{6,7},{7,6},{8,9},{9,8},{10,11... | collective-permute-start | bytes 20 | tf_op jit(solution)/shard_map/ppermute | solution.py:474
  177.9 5.6 %after_exchange.3 = (bf16[128,4096]{1,0:T(8,128)(2,1)}, bf16[128,4096]{1,0:T(8,128)(2,1)}, bf16[128,4096]{1,0:T(8,128)(2,1)}, f32[128,128]{1,0:T(8,128)}) custom-call(bf16[16,288,128]{2,1,0:T(8,128)(2,1)} %copy-done, bf16[128,4096]{1,0:T(8,128)(2,1)} %og_ref.5, ...), custom_call_target="tpu_custom_call", output_to_operand_aliasing={{0}: (8, {}), {1}: (9, {}), {2}: (10, {})} | custom-call | flops 15728640 | bytes 5767168 | tf_op jit(solution)/shard_map/after_exchange/pallas_call | solution.py:396
  184.2 1.5 maximum_multiply_fusion
  (17 shorter events, 0.1 us)
Async XLA Ops:
  3.2 7.9 %collective-permute-start = (bf16[24,4096]{1,0:T(8,128)(2,1)S(1)}, bf16[24,4096]{1,0:T(8,128)(2,1)S(1)}, u32[]{:S(2)}, u32[]{:S(2)}) collective-permute-start(bf16[24,4096]{1,0:T(8,128)(2,1)S(1)} %pad_maximum_fusion), channel_id=1, source_target_pairs={{0,2},{2,4},{4,6},{6,8},{8,10},{10,12},{12,14},{14,16},{16,18},{18... | collective-permute-start | bytes 589832 | tf_op jit(solution)/shard_map/ppermute | solution.py:26
  11.1 0.7 copy-start.5
  21.4 5.4 %copy-start.3 = (bf16[128,4096]{1,0:T(8,128)(2,1)S(1)}, bf16[128,4096]{1,0:T(8,128)(2,1)}, u32[]{:S(2)}) copy-start(bf16[128,4096]{1,0:T(8,128)(2,1)} %k_ref.3) | copy-start | bytes 3145732
  21.4 56.4 %all-to-all-start = ((bf16[16,544,128]{2,1,0:T(8,128)(2,1)}), bf16[16,544,128]{2,1,0:T(8,128)(2,1)S(1)}, u32[]{:S(2)}, u32[]{:S(2)}) async-start(bf16[16,544,128]{2,1,0:T(8,128)(2,1)} %get-tuple-element.29), calls=%async_computation | async-start | bytes 4456448 | tf_op jit(solution)/shard_map/all_to_all | solution.py:451
  26.9 62.2 %collective-permute-start.1 = (bf16[128,4096]{1,0:T(8,128)(2,1)S(1)}, bf16[128,4096]{1,0:T(8,128)(2,1)}, u32[]{:S(2)}, u32[]{:S(2)}) collective-permute-start(bf16[128,4096]{1,0:T(8,128)(2,1)S(1)} %copy-done.3), channel_id=1, source_target_pairs={{0,2},{2,4},{4,6},{6,8},{8,10},{10,12},{12,14},{14,16},{16,18},{18... | collective-permute-start | bytes 3145736 | tf_op jit(solution)/shard_map/ppermute | solution.py:26
  28.9 71.0 %collective-permute-start.2 = (bf16[128,4096]{1,0:T(8,128)(2,1)}, bf16[128,4096]{1,0:T(8,128)(2,1)}, u32[]{:S(2)}, u32[]{:S(2)}) collective-permute-start(bf16[128,4096]{1,0:T(8,128)(2,1)} %v_ref.3), channel_id=1, source_target_pairs={{0,2},{2,4},{4,6},{6,8},{8,10},{10,12},{12,14},{14,16},{16,18},{18... | collective-permute-start | bytes 3145736 | tf_op jit(solution)/shard_map/ppermute | solution.py:26
  77.8 1.4 copy-start.2
  100.0 32.2 %all-to-all-start.2 = ((bf16[16,288,128]{2,1,0:T(8,128)(2,1)}), bf16[16,288,128]{2,1,0:T(8,128)(2,1)S(1)}, u32[]{:S(2)}, u32[]{:S(2)}) async-start(bf16[16,288,128]{2,1,0:T(8,128)(2,1)} %long_products.2), calls=%async_computation.2 | async-start | bytes 2359296 | tf_op jit(solution)/shard_map/all_to_all | solution.py:459
  114.1 23.7 %slice-start = ((bf16[128,4096]{1,0:T(8,128)(2,1)}), bf16[8,4096]{1,0:T(8,128)(2,1)S(1)}, s32[]{:S(2)}) async-start(bf16[128,4096]{1,0:T(8,128)(2,1)} %k_end.3), calls=%async_computation.3 | async-start | bytes 131072 | tf_op jit(solution)/shard_map/slice | solution.py:450
  114.1 23.7 %slice-start.1 = ((bf16[128,4096]{1,0:T(8,128)(2,1)}), bf16[8,4096]{1,0:T(8,128)(2,1)S(1)}, s32[]{:S(2)}) async-start(bf16[128,4096]{1,0:T(8,128)(2,1)} %v_end.3), calls=%async_computation.4 | async-start | bytes 131072 | tf_op jit(solution)/shard_map/slice | solution.py:450
  114.1 23.7 %slice-start.2 = ((bf16[128,4096]{1,0:T(8,128)(2,1)}), bf16[8,4096]{1,0:T(8,128)(2,1)S(1)}, s32[]{:S(2)}) async-start(bf16[128,4096]{1,0:T(8,128)(2,1)} %og_ref.5), calls=%async_computation.5 | async-start | bytes 131072 | tf_op jit(solution)/shard_map/slice | solution.py:450
  132.2 1.0 copy-start.1
  133.2 39.2 %all-to-all-start.1 = ((bf16[16,288,128]{2,1,0:T(8,128)(2,1)}), bf16[16,288,128]{2,1,0:T(8,128)(2,1)S(1)}, u32[]{:S(2)}, u32[]{:S(2)}) async-start(bf16[16,288,128]{2,1,0:T(8,128)(2,1)} %long_products.3), calls=%async_computation.1 | async-start | bytes 2359296 | tf_op jit(solution)/shard_map/all_to_all | solution.py:459
  137.8 28.2 %collective-permute-start.3 = (bf16[24,4096]{1,0:T(8,128)(2,1)S(1)}, bf16[24,4096]{1,0:T(8,128)(2,1)S(1)}, u32[]{:S(2)}, u32[]{:S(2)}) collective-permute-start(bf16[24,4096]{1,0:T(8,128)(2,1)S(1)} %pad_maximum_fusion.1), channel_id=1, source_target_pairs={{2,0},{4,2},{6,4},{8,6},{10,8},{12,10},{14,12},{16,14},{18,16},{20... | collective-permute-start | bytes 589832 | tf_op jit(solution)/shard_map/ppermute | solution.py:26
  166.0 0.7 copy-start.4
  172.4 5.5 %copy-start = (bf16[16,288,128]{2,1,0:T(8,128)(2,1)}, bf16[16,288,128]{2,1,0:T(8,128)(2,1)S(1)}, u32[]{:S(2)}) copy-start(bf16[16,288,128]{2,1,0:T(8,128)(2,1)S(1)} %all-to-all-done.1.in_ref) | copy-start | bytes 3538948
  175.0 9.1 %copy-start.6 = (f32[128,128]{1,0:T(8,128)S(1)}, f32[128,128]{1,0:T(8,128)}, u32[]{:S(2)}) copy-start(f32[128,128]{1,0:T(8,128)} %get-tuple-element.49) | copy-start | bytes 196612
  175.0 8.5 %collective-permute-start.4 = (f32[1,1]{1,0:T(1,128)}, f32[1,1]{1,0:T(1,128)}, u32[]{:S(2)}, u32[]{:S(2)}) collective-permute-start(f32[1,1]{1,0:T(1,128)} %bitcast.1), channel_id=1, source_target_pairs={{0,1},{1,0},{2,3},{3,2},{4,5},{5,4},{6,7},{7,6},{8,9},{9,8},{10,11... | collective-permute-start | bytes 20 | tf_op jit(solution)/shard_map/ppermute | solution.py:474

commit v6 on v5

--- a/solution.py
+++ b/solution.py
@@ -14,16 +14,26 @@
 F32 = jnp.float32
 BF16 = jnp.bfloat16
 VMEM_BYTES = 60 * 1024 * 1024
-
-
-def params():
-    return pltpu.CompilerParams(vmem_limit_bytes=VMEM_BYTES)
+LONG_VMEM = 20 * 1024 * 1024
+
+
+def params(size=VMEM_BYTES):
+    return pltpu.CompilerParams(vmem_limit_bytes=size)
 
 
 def shifted(block, axis, distance):
     devices = range(lax.axis_size(axis))
     route = [(i - distance, i) for i in devices if i - distance in devices]
     return lax.ppermute(block, axis, route)
+
+
+def total_over(value, axis):
+    size = lax.axis_size(axis)
+    distance = 1
+    while distance < size:
+        value = value + lax.ppermute(value, axis, [(i, i ^ distance) for i in range(size)])
+        distance *= 2
+    return value
 
 
 def round_up(value, step):
@@ -83,6 +93,27 @@
         ),
         name="attend",
     )(position.astype(jnp.int32).reshape(1), query, key, value, key_prev, value_prev)
+
+
+def edge_kernel(first, *refs):
+    *sources, out_ref = refs
+    parts = [r[...].astype(F32) for r in sources]
+    parts = [p[:EDGE] if first else p[p.shape[0] - EDGE :] for p in parts]
+    out_ref[...] = jnp.concatenate(parts, 0).astype(BF16)
+
+
+def edge_rows(arrays, first):
+    rows, channels = arrays[0].shape
+    block = pl.BlockSpec((16, channels), lambda i: (0 if first else rows // 16 - 1, 0))
+    return pl.pallas_call(
+        functools.partial(edge_kernel, first),
+        grid=(1,),
+        in_specs=[block] * len(arrays),
+        out_specs=pl.BlockSpec((len(arrays) * EDGE, channels), lambda i: (0, 0)),
+        out_shape=jax.ShapeDtypeStruct((len(arrays) * EDGE, channels), BF16),
+        compiler_params=params(),
+        name="edge_rows",
+    )(*arrays)
 
 
 def taps_causal(ext_ref, before, signal, filter_taps):
@@ -176,7 +207,8 @@
     )(query, key, value, out_grad, tail, taps, long_filter)
 
 
-def long_kernel(cpd, gpd, in_ref, out_ref, taps, wide, gram, raw):
+def conv_kernel(cpd, gpd, in_ref, *refs):
+    *raw_ref, out_ref, taps, wide = refs
     n, send_rows, rows = in_ref.shape
     gw = cpd // gpd
     span = n * rows
@@ -186,10 +218,6 @@
         taps[:, (a + 1) * rows : (a + 2) * rows] = in_ref[a, 2 * cpd :, :].astype(F32)
     for slot in range(2):
         wide[slot, :, 0:rows] = jnp.zeros((rows, rows), BF16)
-        gram[slot, :, span:] = jnp.zeros((rows, rows), F32)
-    if gpd < filter_rows:
-        raw[...] = jnp.zeros_like(raw)
-    turn = reversal(rows)
 
     def one_group(g, slot):
         line = jnp.broadcast_to(taps[pl.ds(g, 1), :], (16, span + rows))
@@ -219,48 +247,18 @@
             top = a // 2 * 2 * gw
             out_ref[a, pl.ds(first, gw), :] = total[top : top + gw, at].astype(BF16)
             out_ref[n - 1 - a, pl.ds(second, gw), :] = total[top + gw : top + 2 * gw, at].astype(BF16)
-        x_turned = x.reshape(n * gw, rows).astype(F32).T.astype(BF16)
-        d = d.reshape(n * gw, rows)
-        no_rows = jnp.zeros((n * gw, rows), BF16)
-
-        def offset(k):
-            held = (k + 1) * gw
-            if held == n * gw:
-                return d
-            return jnp.concatenate([d[n * gw - held :], no_rows[held:]], 0)
-
-        for k in range(0, n, 2):
-            pairs = jnp.concatenate([offset(k), offset(k + 1)], 1)
-            gram[slot, :, k * rows : (k + 2) * rows] = jnp.dot(
-                x_turned, pairs, preferred_element_type=F32
-            )
-        sums = gram[slot, 0:8, :]
-        for m in range(1, rows // 8):
-            sums = sums + pltpu.roll(gram[slot, 8 * m : 8 * m + 8, :], 8 * m, 1)
-        sums = pltpu.roll(sums, 0, 1, stride=1, stride_axis=0)
-        line = jnp.sum(sums, axis=0, keepdims=True)[:, :span]
-        raw[pl.ds(g, 1), :] = line
-        return line * line
-
-    def body(i, squares):
-        squares = squares + one_group(2 * i, 0)
-        return squares + one_group(2 * i + 1, 1)
-
-    squares = lax.fori_loop(0, gpd // 2, body, jnp.zeros((1, span), F32))
-    total = jnp.sum(squares, axis=1, keepdims=True)
-    upper = total.astype(BF16).astype(F32)
-    lower = total - upper
-    for a in range(n):
-        tile = raw[:, (n - 1 - a) * rows : (n - a) * rows].astype(BF16)
-        out_ref[a, 2 * cpd : 2 * cpd + filter_rows, :] = jnp.dot(
-            tile, turn, preferred_element_type=F32
-        ).astype(BF16)
-    halo_at = 2 * cpd + filter_rows
+
+    def body(i, carry):
+        one_group(2 * i, 0)
+        one_group(2 * i + 1, 1)
+        return carry
+
+    lax.fori_loop(0, gpd // 2, body, 0)
+    halo_at = 2 * cpd
     row = lax.broadcasted_iota(jnp.int32, (2 * EDGE, 2 * rows), 0)
     lane = lax.broadcasted_iota(jnp.int32, (2 * EDGE, 2 * rows), 1)
     wanted = jnp.where(row < EDGE, row, 2 * rows - 1 + EDGE - row)
     pick = jnp.where(lane == wanted, 1.0, 0.0).astype(BF16)
-    row_out = lax.broadcasted_iota(jnp.int32, (2 * EDGE, rows), 0)
     for a in range(n):
         if a + 1 < n:
             results = jnp.concatenate([out_ref[a + 1, 0:cpd, :], out_ref[a + 1, cpd : 2 * cpd, :]], 1)
@@ -272,35 +270,112 @@
         else:
             halo = jnp.zeros((2 * EDGE, max(cpd, LANES)), F32)
         for j in range(halo.shape[1] // LANES):
-            tile = halo[:, j * LANES : (j + 1) * LANES]
-            tile = jnp.where(row_out == EDGE - 2, upper, jnp.where(row_out == EDGE - 1, lower, tile))
             at = halo_at + 2 * EDGE * j
-            out_ref[a, at : at + 2 * EDGE, :] = tile.astype(BF16)
-
-
-def long_products(received, cpd, gpd, chunk, chunks):
+            out_ref[a, at : at + 2 * EDGE, :] = halo[:, j * LANES : (j + 1) * LANES].astype(BF16)
+    for ref in raw_ref:
+        out_ref[:, out_ref.shape[1] - ref.shape[1] :, :] = ref[...]
+
+
+def long_convs(received, raw, cpd, gpd, chunk, chunks):
     n, send_rows, rows = received.shape
     send_rows = send_rows // chunks
     filter_rows = send_rows - 2 * cpd
-    out_rows = send_rows + 2 * EDGE * max(1, cpd // LANES)
+    out_rows = 2 * cpd + 2 * EDGE * max(1, cpd // LANES) + sum(r.shape[1] for r in raw)
     span = n * rows
     return pl.pallas_call(
-        functools.partial(long_kernel, cpd, gpd),
+        functools.partial(conv_kernel, cpd, gpd),
         grid=(1,),
-        in_specs=[pl.BlockSpec((n, send_rows, rows), lambda i: (0, chunk, 0))],
+        in_specs=[pl.BlockSpec((n, send_rows, rows), lambda i: (0, chunk, 0))]
+        + [pl.BlockSpec(r.shape, lambda i: (0, 0, 0)) for r in raw],
         out_specs=pl.BlockSpec((n, out_rows, rows), lambda i: (0, 0, 0)),
         out_shape=jax.ShapeDtypeStruct((n, out_rows, rows), BF16),
         scratch_shapes=[
             pltpu.VMEM((filter_rows, span + rows), F32),
             pltpu.VMEM((2, rows, span + rows), BF16),
+        ],
+        compiler_params=params(LONG_VMEM),
+        cost_estimate=pl.CostEstimate(
+            flops=4 * cpd * span * span, bytes_accessed=4 * n * out_rows * rows, transcendentals=0
+        ),
+        name="long_convs",
+    )(received, *raw)
+
+
+def gram_kernel(cpd, gpd, chunks, in_ref, out_ref, squares_ref, gram, raw):
+    n, send_rows, rows = in_ref.shape
+    send_rows = send_rows // chunks
+    gw = cpd // gpd
+    span = n * rows
+    for slot in range(2):
+        gram[slot, :, span:] = jnp.zeros((rows, rows), F32)
+    if gpd * chunks < raw.shape[0]:
+        raw[...] = jnp.zeros_like(raw)
+    no_rows = jnp.zeros((n * gw, rows), BF16)
+
+    def one_group(base, line_at, g, slot):
+        first = pl.multiple_of(base + g * gw, gw)
+        second = pl.multiple_of(base + cpd + g * gw, gw)
+        x = in_ref[:, pl.ds(first, gw), :].reshape(n * gw, rows)
+        d = in_ref[:, pl.ds(second, gw), :].reshape(n * gw, rows)
+        x_turned = x.astype(F32).T.astype(BF16)
+
+        def offset(k):
+            held = (k + 1) * gw
+            if held == n * gw:
+                return d
+            return jnp.concatenate([d[n * gw - held :], no_rows[held:]], 0)
+
+        for k in range(0, n, 2):
+            pairs = jnp.concatenate([offset(k), offset(k + 1)], 1)
+            gram[slot, :, k * rows : (k + 2) * rows] = jnp.dot(
+                x_turned, pairs, preferred_element_type=F32
+            )
+        sums = gram[slot, 0:8, :]
+        for m in range(1, rows // 8):
+            sums = sums + pltpu.roll(gram[slot, 8 * m : 8 * m + 8, :], 8 * m, 1)
+        sums = pltpu.roll(sums, 0, 1, stride=1, stride_axis=0)
+        line = jnp.sum(sums, axis=0, keepdims=True)[:, :span]
+        raw[pl.ds(line_at + g, 1), :] = line
+        return line * line
+
+    squares = jnp.zeros((1, span), F32)
+    for chunk in range(chunks):
+
+        def body(i, total, chunk=chunk):
+            total = total + one_group(chunk * send_rows, chunk * gpd, 2 * i, 0)
+            return total + one_group(chunk * send_rows, chunk * gpd, 2 * i + 1, 1)
+
+        squares = lax.fori_loop(0, gpd // 2, body, squares)
+    squares_ref[...] = jnp.sum(squares, axis=1, keepdims=True)
+    turn = reversal(rows)
+    for a in range(n):
+        tile = raw[:, (n - 1 - a) * rows : (n - a) * rows].astype(BF16)
+        out_ref[a] = jnp.dot(tile, turn, preferred_element_type=F32).astype(BF16)
+
+
+def filter_products(received, cpd, gpd, chunks):
+    n, _, rows = received.shape
+    span = n * rows
+    raw_rows = round_up(gpd * chunks, 16)
+    return pl.pallas_call(
+        functools.partial(gram_kernel, cpd, gpd, chunks),
+        in_specs=[pl.BlockSpec(memory_space=pltpu.VMEM)],
+        out_specs=[pl.BlockSpec(memory_space=pltpu.VMEM)] * 2,
+        out_shape=[
+            jax.ShapeDtypeStruct((n, raw_rows, rows), BF16),
+            jax.ShapeDtypeStruct((1, 1), F32),
+        ],
+        scratch_shapes=[
             pltpu.VMEM((2, rows, span + rows), F32),
-            pltpu.VMEM((filter_rows, span), F32),
+            pltpu.VMEM((raw_rows, span), F32),
         ],
-        compiler_params=params(),
+        compiler_params=params(LONG_VMEM),
         cost_estimate=pl.CostEstimate(
-            flops=6 * cpd * span * span, bytes_accessed=4 * n * out_rows * rows, transcendentals=0
+            flops=2 * cpd * chunks * span * span,
+            bytes_accessed=2 * received.size,
+            transcendentals=0,
         ),
-        name="long_products",
+        name="filter_products",
     )(received)
 
 
@@ -323,15 +398,16 @@
 
 
 def after_kernel(
-    cpd, gpd, in_ref, og_ref, sk_ref, sv_ref, k_end, v_end, next_ref, taps_ref,
-    *refs,
+    cpd, gpd, chunks, last, in_ref, og_ref, sk_ref, sv_ref, k_end, v_end, next_ref, taps_ref, *refs
 ):
-    dq_ref, dk_ref, dv_ref, raw_ref, raw_rows, ext_q, ext_k, ext_v = refs[-8:]
+    *refs, ext_q, ext_k, ext_v = refs
+    if last:
+        *refs, raw_ref, raw_rows = refs
+    dq_ref, dk_ref, dv_ref = refs[-3:]
     step = pl.program_id(0)
     per_tile, in_rows, rows = in_ref.shape
-    groups = raw_ref.shape[1]
     halo_rows = 2 * EDGE * max(1, cpd // LANES)
-    halo_at = in_rows - halo_rows
+    halo_at = 2 * cpd
     end_rows = k_end.shape[0]
     turn = reversal(rows)
     for j in range(og_ref.shape[1] // LANES):
@@ -347,7 +423,7 @@
             conv = jnp.concatenate([in_ref[d, 0:cpd, :] for d in dests], 0)
             back = jnp.concatenate([in_ref[d, cpd : 2 * cpd, :] for d in dests], 0)
             halo = jnp.concatenate(
-                [in_ref[d, halo_at:, :].astype(F32)[:, :cpd] for d in dests], 1
+                [in_ref[d, halo_at : halo_at + halo_rows, :].astype(F32)[:, :cpd] for d in dests], 1
             )
         conv = conv.astype(F32).T
         back = jnp.dot(back, turn, preferred_element_type=F32).T
@@ -370,22 +446,28 @@
         dv_ref[:, at] = taps_anti(
             ext_v.at[j], back * sk_ref[:, at], halo[EDGE:] * next_k, taps_v
         ).astype(BF16)
+    if not last:
+        return
+    scale = refs[0][0, 0]
+    half = raw_rows.shape[0] // chunks
     for dest in range(per_tile):
-        lines = in_ref[dest, 2 * cpd : halo_at, :].astype(F32)
-        raw_rows[pl.ds((step * per_tile + dest) * gpd, gpd), :] = lines[:gpd]
+        lines = in_ref[dest, halo_at + halo_rows :, :].astype(F32)
+        for chunk in range(chunks):
+            at = chunk * half + (step * per_tile + dest) * gpd
+            raw_rows[pl.ds(at, gpd), :] = lines[chunk * gpd : (chunk + 1) * gpd]
 
     @pl.when(step == pl.num_programs(0) - 1)
     def _():
-        raw_ref[...] = raw_rows[...].T
+        raw_ref[...] = raw_rows[...].T * scale
 
 
 def after_exchange(
-    returned, out_grad, short_k, short_v, key, value, following, taps, groups, chunk, chunks, grads
+    returned, out_grad, short_k, short_v, key, value, following, taps, groups, chunk, chunks, grads, scale
 ):
     n, in_rows, rows = returned.shape
     channels = out_grad.shape[1] // chunks
-    groups = groups // chunks
-    cpd, gpd = channels // n, groups // n
+    cpd, gpd = channels // n, groups // (n * chunks)
+    last = chunk + 1 == chunks
     tile = min(channels, max(512, cpd))
     per_tile = tile // cpd
     first = chunk * channels // tile
@@ -394,7 +476,7 @@
     ext = pltpu.VMEM((tile // LANES, rows + EDGE, LANES), F32)
     grad = jax.ShapeDtypeStruct(out_grad.shape, BF16)
     return pl.pallas_call(
-        functools.partial(after_kernel, cpd, gpd),
+        functools.partial(after_kernel, cpd, gpd, chunks, last),
         grid=(channels // tile,),
         in_specs=[
             pl.BlockSpec((per_tile, in_rows, rows), lambda i: (i, 0, 0)),
@@ -406,17 +488,18 @@
             pl.BlockSpec((3 * EDGE, tile), lambda i: (0, first + i)),
             pl.BlockSpec((3, taps.shape[1], tile), lambda i: (0, 0, first + i)),
         ]
+        + [pl.BlockSpec(memory_space=pltpu.SMEM)] * len(scale)
         + [pl.BlockSpec(memory_space=pl.ANY)] * len(grads),
-        input_output_aliases={8 + i: i for i in range(len(grads))},
-        out_specs=[block, block, block, pl.BlockSpec((rows, groups), lambda i: (0, 0))],
-        out_shape=[grad, grad, grad, jax.ShapeDtypeStruct((rows, groups), F32)],
-        scratch_shapes=[pltpu.VMEM((groups, rows), F32), ext, ext, ext],
+        input_output_aliases={8 + len(scale) + i: i for i in range(len(grads))},
+        out_specs=[block] * 3 + [pl.BlockSpec((rows, groups), lambda i: (0, 0))] * len(scale),
+        out_shape=[grad] * 3 + [jax.ShapeDtypeStruct((rows, groups), F32)] * len(scale),
+        scratch_shapes=[pltpu.VMEM((groups, rows), F32)] * len(scale) + [ext, ext, ext],
         compiler_params=params(),
         cost_estimate=pl.CostEstimate(
             flops=60 * rows * channels, bytes_accessed=22 * rows * channels, transcendentals=0
         ),
         name="after_exchange",
-    )(returned, out_grad, short_k, short_v, key, value, following, taps, *grads)
+    )(returned, out_grad, short_k, short_v, key, value, following, taps, *scale, *grads)
 
 
 def on_device(
@@ -436,9 +519,7 @@
     tp = lax.axis_size("tp")
     cpd, gpd = channels // n, groups // n
     position = lax.axis_index("ctx")
-    tail = shifted(
-        jnp.concatenate([a[rows - EDGE :] for a in (hyena_query, hyena_key, hyena_value)], 0), "ctx", 1
-    )
+    tail = shifted(edge_rows((hyena_query, hyena_key, hyena_value), False), "ctx", 1)
     key_prev = shifted(key_heads, "ctx", 1)
     value_prev = shifted(value_heads, "ctx", 1)
     chunks = 2 if gpd % 4 == 0 else 1
@@ -446,41 +527,37 @@
     send, short_k, short_v = before_exchange(
         hyena_query, hyena_key, hyena_value, output_grad, tail, short_filter, long_filter, n, chunks
     )
-    send, *sources = lax.optimization_barrier((send, output_grad, hyena_key, hyena_value))
-    following = shifted(jnp.concatenate([a[:EDGE] for a in sources], 0), "ctx", -1)
+    send, key_prev, *sources = lax.optimization_barrier(
+        (send, key_prev, output_grad, hyena_key, hyena_value)
+    )
     received = lax.all_to_all(send, "ctx", split_axis=0, concat_axis=0, tiled=True)
+    following = shifted(edge_rows(sources, True), "ctx", -1)
     returned = []
     for chunk in range(chunks):
-        results = long_products(received, cpd, gpd, chunk, chunks)
+        raw = ()
+        if chunk + 1 == chunks:
+            *raw, squares = filter_products(received, cpd, gpd, chunks)
+            squares = total_over(squares, "tp")
+            squares = total_over(squares, "ctx")
+        results = long_convs(received, raw, cpd, gpd, chunk, chunks)
         if chunk == 0:
-            results, received, key_prev, value_prev = lax.optimization_barrier(
-                (results, received, key_prev, value_prev)
+            results, received, value_prev, following = lax.optimization_barrier(
+                (results, received, value_prev, following)
             )
         returned.append(lax.all_to_all(results, "ctx", split_axis=0, concat_axis=0, tiled=True))
     attention = attend(query_heads, key_heads, value_heads, key_prev, value_prev, position)
+    bound = math.sqrt(rows * n * groups * tp)
+    factor = jnp.minimum(1.0, bound / jnp.sqrt(squares))
     grads = ()
-    raws = []
-    norm_at = returned[0].shape[1] - 2 * EDGE * max(1, cpd // LANES) + EDGE - 2
-    own_squares = jnp.zeros((1, 1), F32)
-    squares = own_squares
     for chunk in range(chunks):
         if chunk > 0:
             returned[chunk], *grads = lax.optimization_barrier((returned[chunk], *grads))
-        own_squares = own_squares + jnp.sum(returned[chunk][:, norm_at : norm_at + 2, 0].astype(F32))
-        if chunk + 1 == chunks:
-            squares = own_squares
-            for distance in range(1, tp):
-                route = [(i, (i + distance) % tp) for i in range(tp)]
-                squares = squares + lax.ppermute(own_squares, "tp", route)
-        *grads, raw = after_exchange(
+        scale = (factor,) if chunk + 1 == chunks else ()
+        grads = after_exchange(
             returned[chunk], output_grad, short_k, short_v, hyena_key, hyena_value, following, short_filter,
-            groups, chunk, chunks, grads,
-        )
-        raws.append(raw)
-    bound = math.sqrt(rows * n * groups * tp)
-    factor = jnp.minimum(1.0, bound / jnp.sqrt(squares))
-    raw_grad = raws[0] if chunks == 1 else jnp.concatenate(raws, 1)
-    return (attention, *grads, raw_grad * factor)
+            groups, chunk, chunks, grads, scale,
+        )
+    return (attention, *grads)
 
 
 def solution(mesh):

time: 188 us -> 180 us (0.957)
  waiting for transfers between devices: 91.4 us -> 76.5 us
  starting transfers between devices: 27.6 us -> 35.7 us
  Pallas kernels: 54.8 us -> 58.8 us
  local copies, waits for them, and re-layouts: 6.3 us -> 2.69 us
  other arithmetic: 2.98 us -> 0 us
    ppermute x4, waiting for transfers between devices: 27.8 us -> 17.9 us  [shifted(): return lax.ppermute(block, axis, route)]
    all_to_all x2, waiting for transfers between devices: 18 us -> 11.2 us  [on_device(): lax.all_to_all(results, 'ctx', split_axis=0, concat_axis=0, tiled=True)]
    ppermute x1 -> x5, starting transfers between devices: 2.85 us -> 9.56 us  [total_over(): lax.ppermute(value, axis, [(i, i ^ distance) for i in range(size)])]
    ppermute x1 -> x5, waiting for transfers between devices: 0.01 us -> 4.66 us  [total_over(): lax.ppermute(value, axis, [(i, i ^ distance) for i in range(size)])]
    pallas_call x4 -> x7, Pallas kernels: 31.1 us -> 35.1 us  [the longest x2 11.1 us: after_exchange(): pl.pallas_call(functools.partial(after_kernel, cpd, gpd, chunks, last), g...]
    all_to_all x1, waiting for transfers between devices: 45.6 us -> 42.8 us  [on_device(): lax.all_to_all(send, 'ctx', split_axis=0, concat_axis=0, tiled=True)]
    slice x9 -> x0, local copies, waits for them, and re-layouts: 2.55 us -> none  [the longest x3 2.53 us: on_device(): a[rows - EDGE:]]
  transfers between devices with their start and end apart: 8 -> 12, of which waited for: 5 -> 8; matrix products, arithmetic and copies ran while one was open for 0% -> 0% of each run, Pallas kernels for 24% -> 30%
where the time goes in v6:
time: 180 us; the launch traced here: 178 us
  waiting for transfers between devices  76.5 us (42%)
  Pallas kernels  58.8 us (33%)
  starting transfers between devices  35.7 us (20%)
  between operations  4.42 us (2%)
  local copies, waits for them, and re-layouts  2.69 us (1%)
    all_to_all x1, waiting for transfers between devices, on_device(): lax.all_to_all(send, 'ctx', split_axis=0, concat_axis=0, tiled=True)  42.8 us
    ppermute x4, waiting for transfers between devices, shifted(): return lax.ppermute(block, axis, route)  17.9 us
    pallas_call x1, Pallas kernels, attend(): pl.pallas_call(attend_kernel, grid=(channels // tile,), in_specs=[pl.Bloc...  14.1 us
    ppermute x4, starting transfers between devices, shifted(): return lax.ppermute(block, axis, route)  11.9 us
    all_to_all x2, waiting for transfers between devices, on_device(): lax.all_to_all(results, 'ctx', split_axis=0, concat_axis=0, tiled=True)  11.2 us
    pallas_call x2, Pallas kernels, after_exchange(): pl.pallas_call(functools.partial(after_kernel, cpd, gpd, chunks, last), g...  11.1 us
    pallas_call x2, Pallas kernels, long_convs(): pl.pallas_call(functools.partial(conv_kernel, cpd, gpd), grid=(1,), in_sp...  10.3 us
    pallas_call x1, Pallas kernels, filter_products(): pl.pallas_call(functools.partial(gram_kernel, cpd, gpd, chunks), in_specs...  10.2 us
  transfers between devices with their start and end apart: 12, of which 8 were waited for; matrix products, arithmetic and copies ran while one was open for 0% of the time, Pallas kernels for 30%

profile of v6, /device:TPU:16, one launch (start us, length us, event | category | flops | bytes accessed | tf_op | source)
XLA Modules:
  0.0 178.2 jit_solution(426103352806472904)
XLA Ops:
  0.6 1.9 %collective-permute-start.1 = (bf16[128,4096]{1,0:T(8,128)(2,1)}, bf16[128,4096]{1,0:T(8,128)(2,1)S(1)}, u32[]{:S(2)}, u32[]{:S(2)}) collective-permute-start(bf16[128,4096]{1,0:T(8,128)(2,1)} %k_ref.3), channel_id=1, source_target_pairs={{0,2},{2,4},{4,6},{6,8},{8,10},{10,12},{12,14},{14,16},{16,18},{18... | collective-permute-start | bytes 3145736 | tf_op jit(solution)/shard_map/ppermute | solution.py:27
  2.6 1.7 edge_rows.2
  4.3 3.5 %collective-permute-start = (bf16[24,4096]{1,0:T(8,128)(2,1)}, bf16[24,4096]{1,0:T(8,128)(2,1)S(1)}, u32[]{:S(2)}, u32[]{:S(2)}) collective-permute-start(bf16[24,4096]{1,0:T(8,128)(2,1)} %edge_rows.2), channel_id=1, source_target_pairs={{0,2},{2,4},{4,6},{6,8},{8,10},{10,12},{12,14},{14,16},{16,18},{18... | collective-permute-start | bytes 589832 | tf_op jit(solution)/shard_map/ppermute | solution.py:27
  7.8 12.2 %collective-permute-done.tail_ref = bf16[24,4096]{1,0:T(8,128)(2,1)S(1)} collective-permute-done((bf16[24,4096]{1,0:T(8,128)(2,1)}, bf16[24,4096]{1,0:T(8,128)(2,1)S(1)}, u32[]{:S(2)}, u32[]{:S(2)}) %collective-permute-start) | collective-permute-done | bytes 196640 | tf_op jit(solution)/shard_map/ppermute | solution.py:27
  20.0 0.7 copy-done.5
  20.6 9.7 %before_exchange.1 = (bf16[16,544,128]{2,1,0:T(8,128)(2,1)}, f32[128,4096]{1,0:T(8,128)}, f32[128,4096]{1,0:T(8,128)}) custom-call(bf16[128,4096]{1,0:T(8,128)(2,1)} %q_ref.2, bf16[128,4096]{1,0:T(8,128)(2,1)} %k_end.3, bf16[128,4096]{1,0:T(8,128)(2,1)} %v_end.3, bf16[128,4096]{1,0:T(8,128)(2,1)} %og_ref.5, bf16[24,4096]{1,0:T(8,128)(2,1)} %copy-done.5, ...), custom_call_target="tpu_custom_call" | custom-call | flops 26214400 | bytes 10485760 | tf_op jit(solution)/shard_map/before_exchange/pallas_call | solution.py:182
  30.4 1.0 copy-done.3
  31.3 5.4 %all-to-all-start = ((bf16[16,544,128]{2,1,0:T(8,128)(2,1)}), bf16[16,544,128]{2,1,0:T(8,128)(2,1)S(1)}, u32[]{:S(2)}, u32[]{:S(2)}) async-start(bf16[16,544,128]{2,1,0:T(8,128)(2,1)} %get-tuple-element.32), calls=%async_computation | async-start | bytes 4456448 | tf_op jit(solution)/shard_map/all_to_all | solution.py:533
  36.7 2.1 %collective-permute-start.2 = (bf16[128,4096]{1,0:T(8,128)(2,1)S(1)}, bf16[128,4096]{1,0:T(8,128)(2,1)}, u32[]{:S(2)}, u32[]{:S(2)}) collective-permute-start(bf16[128,4096]{1,0:T(8,128)(2,1)S(1)} %copy-done.2), channel_id=1, source_target_pairs={{0,2},{2,4},{4,6},{6,8},{8,10},{10,12},{12,14},{14,16},{16,18},{18... | collective-permute-start | bytes 3145736 | tf_op jit(solution)/shard_map/ppermute | solution.py:27
  38.8 1.7 edge_rows.3
  40.5 4.4 %collective-permute-start.3 = (bf16[24,4096]{1,0:T(8,128)(2,1)}, bf16[24,4096]{1,0:T(8,128)(2,1)S(1)}, u32[]{:S(2)}, u32[]{:S(2)}) collective-permute-start(bf16[24,4096]{1,0:T(8,128)(2,1)} %edge_rows.3), channel_id=1, source_target_pairs={{2,0},{4,2},{6,4},{8,6},{10,8},{12,10},{14,12},{16,14},{18,16},{20... | collective-permute-start | bytes 589832 | tf_op jit(solution)/shard_map/ppermute | solution.py:27
  44.9 42.8 %all-to-all-done.in_ref = bf16[16,544,128]{2,1,0:T(8,128)(2,1)S(1)} async-done(((bf16[16,544,128]{2,1,0:T(8,128)(2,1)}), bf16[16,544,128]{2,1,0:T(8,128)(2,1)S(1)}, u32[]{:S(2)}, u32[]{:S(2)}) %all-to-all-start) | async-done | bytes 2228256 | tf_op jit(solution)/shard_map/all_to_all | solution.py:533
  87.7 5.1 %long_convs.2 = bf16[16,272,128]{2,1,0:T(8,128)(2,1)} custom-call(bf16[16,544,128]{2,1,0:T(8,128)(2,1)S(1)} %all-to-all-done.in_ref), custom_call_target="tpu_custom_call" | custom-call | flops 2147483648 | bytes 2228224 | tf_op jit(solution)/shard_map/long_convs/pallas_call | solution.py:285
  92.8 5.7 %collective-permute-done.2.vp_ref = bf16[128,4096]{1,0:T(8,128)(2,1)} collective-permute-done((bf16[128,4096]{1,0:T(8,128)(2,1)S(1)}, bf16[128,4096]{1,0:T(8,128)(2,1)}, u32[]{:S(2)}, u32[]{:S(2)}) %collective-permute-start.2) | collective-permute-done | bytes 1048608 | tf_op jit(solution)/shard_map/ppermute | solution.py:27
  98.6 4.2 %all-to-all-start.2 = ((bf16[16,272,128]{2,1,0:T(8,128)(2,1)}), bf16[16,272,128]{2,1,0:T(8,128)(2,1)S(1)}, u32[]{:S(2)}, u32[]{:S(2)}) async-start(bf16[16,272,128]{2,1,0:T(8,128)(2,1)} %long_convs.2), calls=%async_computation.2 | async-start | bytes 2228224 | tf_op jit(solution)/shard_map/all_to_all | solution.py:547
  102.8 10.2 %filter_products.1 = (bf16[16,16,128]{2,1,0:T(8,128)(2,1)S(1)}, f32[1,1]{1,0:T(1,128)}) custom-call(bf16[16,544,128]{2,1,0:T(8,128)(2,1)S(1)} %all-to-all-done.in_ref), custom_call_target="tpu_custom_call" | custom-call | flops 2147483648 | bytes 2228224 | tf_op jit(solution)/shard_map/filter_products/pallas_call | solution.py:360
  113.0 5.2 %long_convs.3 = bf16[16,288,128]{2,1,0:T(8,128)(2,1)} custom-call(bf16[16,544,128]{2,1,0:T(8,128)(2,1)S(1)} %all-to-all-done.in_ref, bf16[16,16,128]{2,1,0:T(8,128)(2,1)S(1)} %get-tuple-element.38.refs_0_), custom_call_target="tpu_custom_call" | custom-call | flops 2147483648 | bytes 2359296 | tf_op jit(solution)/shard_map/long_convs/pallas_call | solution.py:285
  118.2 11.2 %all-to-all-done.2.in_ref = bf16[16,272,128]{2,1,0:T(8,128)(2,1)S(1)} async-done(((bf16[16,272,128]{2,1,0:T(8,128)(2,1)}), bf16[16,272,128]{2,1,0:T(8,128)(2,1)S(1)}, u32[]{:S(2)}, u32[]{:S(2)}) %all-to-all-start.2) | async-done | bytes 1114144 | tf_op jit(solution)/shard_map/all_to_all | solution.py:547
  129.4 4.6 %all-to-all-start.1 = ((bf16[16,288,128]{2,1,0:T(8,128)(2,1)}), bf16[16,288,128]{2,1,0:T(8,128)(2,1)S(1)}, u32[]{:S(2)}, u32[]{:S(2)}) async-start(bf16[16,288,128]{2,1,0:T(8,128)(2,1)} %long_convs.3), calls=%async_computation.1 | async-start | bytes 2359296 | tf_op jit(solution)/shard_map/all_to_all | solution.py:547
  134.0 1.5 collective-permute-start.4
  135.5 14.1 %attend.1 = bf16[128,4096]{1,0:T(8,128)(2,1)} custom-call(s32[1]{0:T(128)} %bitcast.place_ref, bf16[128,4096]{1,0:T(8,128)(2,1)} %q_ref.3, bf16[128,4096]{1,0:T(8,128)(2,1)} %k_ref.3, bf16[128,4096]{1,0:T(8,128)(2,1)} %v_ref.3, bf16[128,4096]{1,0:T(8,128)(2,1)} %copy-done.3, bf16[128,4096]{1,0:T(8,128)(2,1)} %collective-permute-done.2.vp_ref), custom_call_target="tpu_custom_call" | custom-call | flops 536870912 | bytes 6291456 | tf_op jit(solution)/shard_map/attend/pallas_call | solution.py:82
  150.8 0.9 collective-permute-start.5
  151.7 0.3 collective-permute-done.5
  152.6 2.8 %collective-permute-start.6 = (f32[1,1]{1,0:T(1,128)}, f32[1,1]{1,0:T(1,128)}, u32[]{:S(2)}, u32[]{:S(2)}) collective-permute-start(f32[1,1]{1,0:T(1,128)} %add.16), channel_id=1, source_target_pairs={{0,4},{2,6},{4,0},{6,2},{8,12},{10,14},{12,8},{14,10},{16,20},{18,... | collective-permute-start | bytes 20 | tf_op jit(solution)/shard_map/ppermute | solution.py:34
  155.4 0.7 collective-permute-done.6
  156.7 2.8 %collective-permute-start.7 = (f32[1,1]{1,0:T(1,128)}, f32[1,1]{1,0:T(1,128)}, u32[]{:S(2)}, u32[]{:S(2)}) collective-permute-start(f32[1,1]{1,0:T(1,128)} %add.17), channel_id=1, source_target_pairs={{0,8},{2,10},{4,12},{6,14},{8,0},{10,2},{12,4},{14,6},{16,24},{18,... | collective-permute-start | bytes 20 | tf_op jit(solution)/shard_map/ppermute | solution.py:34
  159.6 0.7 collective-permute-done.7
  160.9 1.5 collective-permute-start.8
  162.4 2.9 %collective-permute-done.8 = f32[1,1]{1,0:T(1,128)} collective-permute-done((f32[1,1]{1,0:T(1,128)}, f32[1,1]{1,0:T(1,128)}, u32[]{:S(2)}, u32[]{:S(2)}) %collective-permute-start.8) | collective-permute-done | bytes 36 | tf_op jit(solution)/shard_map/ppermute | solution.py:34
  166.0 5.4 %after_exchange.2 = (bf16[128,4096]{1,0:T(8,128)(2,1)}, bf16[128,4096]{1,0:T(8,128)(2,1)}, bf16[128,4096]{1,0:T(8,128)(2,1)}) custom-call(bf16[16,272,128]{2,1,0:T(8,128)(2,1)} %copy-done.1, bf16[128,4096]{1,0:T(8,128)(2,1)} %og_ref.5, f32[128,4096]{1,0:T(8,128)} %get-tuple-element.40.sk_ref, f32[128,4096]{1,0:T(8,128)} %get-tuple-element.41.sv_ref, ...), custom_call_target="tpu_custom_call" | custom-call | flops 15728640 | bytes 5767168 | tf_op jit(solution)/shard_map/after_exchange/pallas_call | solution.py:478
  171.5 1.0 copy-done
  172.5 5.7 %after_exchange.3 = (bf16[128,4096]{1,0:T(8,128)(2,1)}, bf16[128,4096]{1,0:T(8,128)(2,1)}, bf16[128,4096]{1,0:T(8,128)(2,1)}, f32[128,256]{1,0:T(8,128)}) custom-call(bf16[16,288,128]{2,1,0:T(8,128)(2,1)} %copy-done, bf16[128,4096]{1,0:T(8,128)(2,1)} %og_ref.5, ...), custom_call_target="tpu_custom_call", output_to_operand_aliasing={{0}: (9, {}), {1}: (10, {}), {2}: (11, {})} | custom-call | flops 15728640 | bytes 5767168 | tf_op jit(solution)/shard_map/after_exchange/pallas_call | solution.py:478
  (13 shorter events, 0.0 us)
Async XLA Ops:
  0.6 29.7 %collective-permute-start.1 = (bf16[128,4096]{1,0:T(8,128)(2,1)}, bf16[128,4096]{1,0:T(8,128)(2,1)S(1)}, u32[]{:S(2)}, u32[]{:S(2)}) collective-permute-start(bf16[128,4096]{1,0:T(8,128)(2,1)} %k_ref.3), channel_id=1, source_target_pairs={{0,2},{2,4},{4,6},{6,8},{8,10},{10,12},{12,14},{14,16},{16,18},{18... | collective-permute-start | bytes 3145736 | tf_op jit(solution)/shard_map/ppermute | solution.py:27
  4.3 15.7 %collective-permute-start = (bf16[24,4096]{1,0:T(8,128)(2,1)}, bf16[24,4096]{1,0:T(8,128)(2,1)S(1)}, u32[]{:S(2)}, u32[]{:S(2)}) collective-permute-start(bf16[24,4096]{1,0:T(8,128)(2,1)} %edge_rows.2), channel_id=1, source_target_pairs={{0,2},{2,4},{4,6},{6,8},{8,10},{10,12},{12,14},{14,16},{16,18},{18... | collective-permute-start | bytes 589832 | tf_op jit(solution)/shard_map/ppermute | solution.py:27
  20.0 0.7 copy-start.5
  30.3 1.0 copy-start.3
  31.3 5.4 %copy-start.2 = (bf16[128,4096]{1,0:T(8,128)(2,1)S(1)}, bf16[128,4096]{1,0:T(8,128)(2,1)}, u32[]{:S(2)}) copy-start(bf16[128,4096]{1,0:T(8,128)(2,1)} %v_ref.3) | copy-start | bytes 3145732
  31.3 56.4 %all-to-all-start = ((bf16[16,544,128]{2,1,0:T(8,128)(2,1)}), bf16[16,544,128]{2,1,0:T(8,128)(2,1)S(1)}, u32[]{:S(2)}, u32[]{:S(2)}) async-start(bf16[16,544,128]{2,1,0:T(8,128)(2,1)} %get-tuple-element.32), calls=%async_computation | async-start | bytes 4456448 | tf_op jit(solution)/shard_map/all_to_all | solution.py:533
  36.7 61.8 %collective-permute-start.2 = (bf16[128,4096]{1,0:T(8,128)(2,1)S(1)}, bf16[128,4096]{1,0:T(8,128)(2,1)}, u32[]{:S(2)}, u32[]{:S(2)}) collective-permute-start(bf16[128,4096]{1,0:T(8,128)(2,1)S(1)} %copy-done.2), channel_id=1, source_target_pairs={{0,2},{2,4},{4,6},{6,8},{8,10},{10,12},{12,14},{14,16},{16,18},{18... | collective-permute-start | bytes 3145736 | tf_op jit(solution)/shard_map/ppermute | solution.py:27
  40.5 58.0 %collective-permute-start.3 = (bf16[24,4096]{1,0:T(8,128)(2,1)}, bf16[24,4096]{1,0:T(8,128)(2,1)S(1)}, u32[]{:S(2)}, u32[]{:S(2)}) collective-permute-start(bf16[24,4096]{1,0:T(8,128)(2,1)} %edge_rows.3), channel_id=1, source_target_pairs={{2,0},{4,2},{6,4},{8,6},{10,8},{12,10},{14,12},{16,14},{18,16},{20... | collective-permute-start | bytes 589832 | tf_op jit(solution)/shard_map/ppermute | solution.py:27
  98.6 14.4 %copy-start.4 = (bf16[24,4096]{1,0:T(8,128)(2,1)}, bf16[24,4096]{1,0:T(8,128)(2,1)S(1)}, u32[]{:S(2)}) copy-start(bf16[24,4096]{1,0:T(8,128)(2,1)S(1)} %collective-permute-done.3.next_ref) | copy-start | bytes 589828
  98.6 30.8 %all-to-all-start.2 = ((bf16[16,272,128]{2,1,0:T(8,128)(2,1)}), bf16[16,272,128]{2,1,0:T(8,128)(2,1)S(1)}, u32[]{:S(2)}, u32[]{:S(2)}) async-start(bf16[16,272,128]{2,1,0:T(8,128)(2,1)} %long_convs.2), calls=%async_computation.2 | async-start | bytes 2228224 | tf_op jit(solution)/shard_map/all_to_all | solution.py:547
  129.4 20.2 %copy-start.1 = (bf16[16,272,128]{2,1,0:T(8,128)(2,1)}, bf16[16,272,128]{2,1,0:T(8,128)(2,1)S(1)}, u32[]{:S(2)}) copy-start(bf16[16,272,128]{2,1,0:T(8,128)(2,1)S(1)} %all-to-all-done.2.in_ref) | copy-start | bytes 3342340
  129.4 42.1 %all-to-all-start.1 = ((bf16[16,288,128]{2,1,0:T(8,128)(2,1)}), bf16[16,288,128]{2,1,0:T(8,128)(2,1)S(1)}, u32[]{:S(2)}, u32[]{:S(2)}) async-start(bf16[16,288,128]{2,1,0:T(8,128)(2,1)} %long_convs.3), calls=%async_computation.1 | async-start | bytes 2359296 | tf_op jit(solution)/shard_map/all_to_all | solution.py:547
  134.0 15.6 %collective-permute-start.4 = (f32[1,1]{1,0:T(1,128)}, f32[1,1]{1,0:T(1,128)}, u32[]{:S(2)}, u32[]{:S(2)}) collective-permute-start(f32[1,1]{1,0:T(1,128)} %get-tuple-element.47), channel_id=1, source_target_pairs={{0,1},{1,0},{2,3},{3,2},{4,5},{5,4},{6,7},{7,6},{8,9},{9,8},{10,11... | collective-permute-start | bytes 20 | tf_op jit(solution)/shard_map/ppermute | solution.py:34
  150.8 1.2 collective-permute-start.5
  152.6 3.6 %collective-permute-start.6 = (f32[1,1]{1,0:T(1,128)}, f32[1,1]{1,0:T(1,128)}, u32[]{:S(2)}, u32[]{:S(2)}) collective-permute-start(f32[1,1]{1,0:T(1,128)} %add.16), channel_id=1, source_target_pairs={{0,4},{2,6},{4,0},{6,2},{8,12},{10,14},{12,8},{14,10},{16,20},{18,... | collective-permute-start | bytes 20 | tf_op jit(solution)/shard_map/ppermute | solution.py:34
  156.7 3.6 %collective-permute-start.7 = (f32[1,1]{1,0:T(1,128)}, f32[1,1]{1,0:T(1,128)}, u32[]{:S(2)}, u32[]{:S(2)}) collective-permute-start(f32[1,1]{1,0:T(1,128)} %add.17), channel_id=1, source_target_pairs={{0,8},{2,10},{4,12},{6,14},{8,0},{10,2},{12,4},{14,6},{16,24},{18,... | collective-permute-start | bytes 20 | tf_op jit(solution)/shard_map/ppermute | solution.py:34
  160.9 4.5 %collective-permute-start.8 = (f32[1,1]{1,0:T(1,128)}, f32[1,1]{1,0:T(1,128)}, u32[]{:S(2)}, u32[]{:S(2)}) collective-permute-start(f32[1,1]{1,0:T(1,128)} %add.18), channel_id=1, source_target_pairs={{0,16},{2,18},{4,20},{6,22},{8,24},{10,26},{12,28},{14,30},{16,0},... | collective-permute-start | bytes 20 | tf_op jit(solution)/shard_map/ppermute | solution.py:34
  171.5 1.0 copy-start

commit v7 on v6

--- a/solution.py
+++ b/solution.py
@@ -46,53 +46,106 @@
     return jnp.where(row + col == size - 1, 1.0, 0.0).astype(BF16)
 
 
-def attend_kernel(place_ref, q_ref, k_ref, v_ref, kp_ref, vp_ref, out_ref):
+SCALE = 1.0 / math.sqrt(HEAD_DIM)
+NT = (((1,), (1,)), ((), ()))
+
+
+def attend_next_kernel(q_ref, k_ref, v_ref, out_ref, log_ref):
     rows = q_ref.shape[0]
+    heads = q_ref.shape[1] // HEAD_DIM
+    step = pl.program_id(0)
+    lane = lax.broadcasted_iota(jnp.int32, (rows, log_ref.shape[1]), 1)
+
+    @pl.when(step == 0)
+    def _():
+        log_ref[...] = jnp.zeros_like(log_ref)
+
+    logs = log_ref[...]
+    for head in range(heads):
+        at = slice(head * HEAD_DIM, (head + 1) * HEAD_DIM)
+        score = lax.dot_general(q_ref[:, at], k_ref[:, at], NT, preferred_element_type=F32) * SCALE
+        largest = jnp.max(score, axis=1, keepdims=True)
+        raised = jnp.exp(score - largest)
+        total = jnp.sum(raised, axis=1, keepdims=True)
+        weight = (raised * (1.0 / total)).astype(BF16)
+        mixed = jnp.dot(weight, v_ref[:, at], preferred_element_type=F32)
+        out_ref[:, at] = mixed.astype(BF16)
+        logs = jnp.where(lane == step * heads + head, largest + jnp.log(total), logs)
+    log_ref[...] = logs
+
+
+def attend_own_kernel(place_ref, q_ref, k_ref, v_ref, prev_ref, log_ref, out_ref):
+    rows = q_ref.shape[0]
+    heads = q_ref.shape[1] // HEAD_DIM
+    step = pl.program_id(0)
     row = lax.broadcasted_iota(jnp.int32, (rows, rows), 0)
     col = lax.broadcasted_iota(jnp.int32, (rows, rows), 1)
     own_ok = col <= row
-    prev_ok = jnp.broadcast_to(place_ref[0], (rows, rows)) > 0
-    contract = (((1,), (1,)), ((), ()))
-    for head in range(q_ref.shape[1] // HEAD_DIM):
+    lane = lax.broadcasted_iota(jnp.int32, (rows, log_ref.shape[1]), 1)
+    has_prev = jnp.broadcast_to(place_ref[0], (rows, 1)) > 0
+    for head in range(heads):
         at = slice(head * HEAD_DIM, (head + 1) * HEAD_DIM)
-        scale = 1.0 / math.sqrt(HEAD_DIM)
-        query = q_ref[:, at]
-        own = lax.dot_general(query, k_ref[:, at], contract, preferred_element_type=F32) * scale
-        prev = lax.dot_general(query, kp_ref[:, at], contract, preferred_element_type=F32) * scale
+        log = jnp.sum(
+            jnp.where(lane == step * heads + head, log_ref[...], 0.0), axis=1, keepdims=True
+        )
+        log = jnp.where(has_prev, log, -jnp.inf)
+        own = lax.dot_general(q_ref[:, at], k_ref[:, at], NT, preferred_element_type=F32) * SCALE
         own = jnp.where(own_ok, own, -jnp.inf)
-        prev = jnp.where(prev_ok, prev, -jnp.inf)
-        largest = jnp.max(jnp.maximum(own, prev), axis=1, keepdims=True)
+        largest = jnp.maximum(jnp.max(own, axis=1, keepdims=True), log)
         own = jnp.exp(own - largest)
-        prev = jnp.exp(prev - largest)
-        total = jnp.sum(own + prev, axis=1, keepdims=True)
-        inverse = 1.0 / total
-        own = (own * inverse).astype(BF16)
-        prev = (prev * inverse).astype(BF16)
-        mixed = jnp.dot(own, v_ref[:, at], preferred_element_type=F32) + jnp.dot(
-            prev, vp_ref[:, at], preferred_element_type=F32
-        )
+        prev = jnp.exp(log - largest)
+        inverse = 1.0 / (jnp.sum(own, axis=1, keepdims=True) + prev)
+        weight = (own * inverse).astype(BF16)
+        mixed = jnp.dot(weight, v_ref[:, at], preferred_element_type=F32)
+        mixed = mixed + (prev * inverse) * prev_ref[:, at].astype(F32)
         out_ref[:, at] = mixed.astype(BF16)
 
 
-def attend(query, key, value, key_prev, value_prev, position):
+def attend_cost(rows, channels):
+    heads = channels // HEAD_DIM
+    return pl.CostEstimate(
+        flops=4 * heads * rows * rows * HEAD_DIM,
+        bytes_accessed=10 * rows * channels,
+        transcendentals=heads * rows * rows,
+    )
+
+
+def attend_next(query, key, value):
     rows, channels = query.shape
     tile = min(512, channels)
     block = pl.BlockSpec((rows, tile), lambda i: (0, i))
-    heads = channels // HEAD_DIM
+    lanes = round_up(channels // HEAD_DIM, LANES)
     return pl.pallas_call(
-        attend_kernel,
+        attend_next_kernel,
         grid=(channels // tile,),
-        in_specs=[pl.BlockSpec(memory_space=pltpu.SMEM)] + [block] * 5,
+        in_specs=[block] * 3,
+        out_specs=[block, pl.BlockSpec((rows, lanes), lambda i: (0, 0))],
+        out_shape=[
+            jax.ShapeDtypeStruct((rows, channels), BF16),
+            jax.ShapeDtypeStruct((rows, lanes), F32),
+        ],
+        compiler_params=params(),
+        cost_estimate=attend_cost(rows, channels),
+        name="attend_next",
+    )(query, key, value)
+
+
+def attend_own(query, key, value, prev, log, position):
+    rows, channels = query.shape
+    tile = min(512, channels)
+    block = pl.BlockSpec((rows, tile), lambda i: (0, i))
+    return pl.pallas_call(
+        attend_own_kernel,
+        grid=(channels // tile,),
+        in_specs=[pl.BlockSpec(memory_space=pltpu.SMEM)]
+        + [block] * 4
+        + [pl.BlockSpec(log.shape, lambda i: (0, 0))],
         out_specs=block,
         out_shape=jax.ShapeDtypeStruct((rows, channels), BF16),
         compiler_params=params(),
-        cost_estimate=pl.CostEstimate(
-            flops=8 * heads * rows * rows * HEAD_DIM,
-            bytes_accessed=12 * rows * channels,
-            transcendentals=2 * heads * rows * rows,
-        ),
-        name="attend",
-    )(position.astype(jnp.int32).reshape(1), query, key, value, key_prev, value_prev)
+        cost_estimate=attend_cost(rows, channels),
+        name="attend_own",
+    )(position.astype(jnp.int32).reshape(1), query, key, value, prev, log)
 
 
 def edge_kernel(first, *refs):
@@ -127,7 +180,7 @@
 
 
 def before_kernel(
-    cpd, gpd, q_ref, k_ref, v_ref, og_ref, tail_ref, taps_ref, long_ref, send_ref, sk_ref, sv_ref,
+    cpd, gpd, q_ref, k_ref, v_ref, og_ref, tail_ref, taps_ref, long_ref, send_ref,
     long_rows, ext_q, ext_k, ext_v,
 ):
     step = pl.program_id(0)
@@ -150,8 +203,6 @@
         short_v = taps_causal(
             ext_v.at[j], tail[2 * EDGE : 3 * EDGE], v_ref[:, at].astype(F32), taps_ref[2, :, at]
         )
-        sk_ref[:, at] = short_k
-        sv_ref[:, at] = short_v
         mixed = (short_k * short_v).T.astype(BF16)
         delta = (og_ref[:, at].astype(F32) * short_q).T.astype(BF16)
         delta = jnp.dot(delta, turn, preferred_element_type=F32).astype(BF16)
@@ -188,20 +239,12 @@
             pl.BlockSpec((3, taps.shape[1], tile), lambda i: (0, 0, i)),
             pl.BlockSpec((rows, groups), lambda i: (0, 0)),
         ],
-        out_specs=[
-            pl.BlockSpec((per_tile, send_rows, rows), lambda i: (i % steps, i // steps, 0)),
-            block,
-            block,
-        ],
-        out_shape=[
-            jax.ShapeDtypeStruct((n, chunks * send_rows, rows), BF16),
-            jax.ShapeDtypeStruct((rows, channels), F32),
-            jax.ShapeDtypeStruct((rows, channels), F32),
-        ],
+        out_specs=pl.BlockSpec((per_tile, send_rows, rows), lambda i: (i % steps, i // steps, 0)),
+        out_shape=jax.ShapeDtypeStruct((n, chunks * send_rows, rows), BF16),
         scratch_shapes=[pltpu.VMEM((round_up(groups, 8) + filter_rows, rows), F32), ext, ext, ext],
         compiler_params=params(),
         cost_estimate=pl.CostEstimate(
-            flops=50 * rows * channels, bytes_accessed=20 * rows * channels, transcendentals=0
+            flops=50 * rows * channels, bytes_accessed=12 * rows * channels, transcendentals=0
         ),
         name="before_exchange",
     )(query, key, value, out_grad, tail, taps, long_filter)
@@ -398,9 +441,9 @@
 
 
 def after_kernel(
-    cpd, gpd, chunks, last, in_ref, og_ref, sk_ref, sv_ref, k_end, v_end, next_ref, taps_ref, *refs
+    cpd, gpd, chunks, last, in_ref, og_ref, k_ref, v_ref, tail_ref, next_ref, taps_ref, *refs
 ):
-    *refs, ext_q, ext_k, ext_v = refs
+    *refs, ext_q, ext_k, ext_v, ext_in_k, ext_in_v = refs
     if last:
         *refs, raw_ref, raw_rows = refs
     dq_ref, dk_ref, dv_ref = refs[-3:]
@@ -408,7 +451,6 @@
     per_tile, in_rows, rows = in_ref.shape
     halo_rows = 2 * EDGE * max(1, cpd // LANES)
     halo_at = 2 * cpd
-    end_rows = k_end.shape[0]
     turn = reversal(rows)
     for j in range(og_ref.shape[1] // LANES):
         at = slice(j * LANES, (j + 1) * LANES)
@@ -430,21 +472,22 @@
         following = next_ref[:, at].astype(F32)
         taps_k = taps_ref[1, :, at]
         taps_v = taps_ref[2, :, at]
-        next_k = short_edge(
-            k_end[:, at].astype(F32)[end_rows - EDGE :], following[EDGE : 2 * EDGE], taps_k
-        )
-        next_v = short_edge(
-            v_end[:, at].astype(F32)[end_rows - EDGE :], following[2 * EDGE : 3 * EDGE], taps_v
-        )
+        tail = tail_ref[:, at].astype(F32)
+        key = k_ref[:, at].astype(F32)
+        value = v_ref[:, at].astype(F32)
+        short_k = taps_causal(ext_in_k.at[j], tail[EDGE : 2 * EDGE], key, taps_k)
+        short_v = taps_causal(ext_in_v.at[j], tail[2 * EDGE : 3 * EDGE], value, taps_v)
+        next_k = short_edge(key[rows - EDGE :], following[EDGE : 2 * EDGE], taps_k)
+        next_v = short_edge(value[rows - EDGE :], following[2 * EDGE : 3 * EDGE], taps_v)
         grad_q = og_ref[:, at].astype(F32) * conv
         dq_ref[:, at] = taps_anti(
             ext_q.at[j], grad_q, following[0:EDGE] * halo[0:EDGE], taps_ref[0, :, at]
         ).astype(BF16)
         dk_ref[:, at] = taps_anti(
-            ext_k.at[j], back * sv_ref[:, at], halo[EDGE:] * next_v, taps_k
+            ext_k.at[j], back * short_v, halo[EDGE:] * next_v, taps_k
         ).astype(BF16)
         dv_ref[:, at] = taps_anti(
-            ext_v.at[j], back * sk_ref[:, at], halo[EDGE:] * next_k, taps_v
+            ext_v.at[j], back * short_k, halo[EDGE:] * next_k, taps_v
         ).astype(BF16)
     if not last:
         return
@@ -462,7 +505,7 @@
 
 
 def after_exchange(
-    returned, out_grad, short_k, short_v, key, value, following, taps, groups, chunk, chunks, grads, scale
+    returned, out_grad, key, value, tail, following, taps, groups, chunk, chunks, grads, scale
 ):
     n, in_rows, rows = returned.shape
     channels = out_grad.shape[1] // chunks
@@ -472,7 +515,6 @@
     per_tile = tile // cpd
     first = chunk * channels // tile
     block = pl.BlockSpec((rows, tile), lambda i: (0, first + i))
-    end = pl.BlockSpec((16, tile), lambda i: (rows // 16 - 1, first + i))
     ext = pltpu.VMEM((tile // LANES, rows + EDGE, LANES), F32)
     grad = jax.ShapeDtypeStruct(out_grad.shape, BF16)
     return pl.pallas_call(
@@ -483,23 +525,22 @@
             block,
             block,
             block,
-            end,
-            end,
+            pl.BlockSpec((3 * EDGE, tile), lambda i: (0, first + i)),
             pl.BlockSpec((3 * EDGE, tile), lambda i: (0, first + i)),
             pl.BlockSpec((3, taps.shape[1], tile), lambda i: (0, 0, first + i)),
         ]
         + [pl.BlockSpec(memory_space=pltpu.SMEM)] * len(scale)
         + [pl.BlockSpec(memory_space=pl.ANY)] * len(grads),
-        input_output_aliases={8 + len(scale) + i: i for i in range(len(grads))},
+        input_output_aliases={7 + len(scale) + i: i for i in range(len(grads))},
         out_specs=[block] * 3 + [pl.BlockSpec((rows, groups), lambda i: (0, 0))] * len(scale),
         out_shape=[grad] * 3 + [jax.ShapeDtypeStruct((rows, groups), F32)] * len(scale),
-        scratch_shapes=[pltpu.VMEM((groups, rows), F32)] * len(scale) + [ext, ext, ext],
+        scratch_shapes=[pltpu.VMEM((groups, rows), F32)] * len(scale) + [ext] * 5,
         compiler_params=params(),
         cost_estimate=pl.CostEstimate(
-            flops=60 * rows * channels, bytes_accessed=22 * rows * channels, transcendentals=0
+            flops=90 * rows * channels, bytes_accessed=18 * rows * channels, transcendentals=0
         ),
         name="after_exchange",
-    )(returned, out_grad, short_k, short_v, key, value, following, taps, *scale, *grads)
+    )(returned, out_grad, key, value, tail, following, taps, *scale, *grads)
 
 
 def on_device(
@@ -520,19 +561,22 @@
     cpd, gpd = channels // n, groups // n
     position = lax.axis_index("ctx")
     tail = shifted(edge_rows((hyena_query, hyena_key, hyena_value), False), "ctx", 1)
-    key_prev = shifted(key_heads, "ctx", 1)
-    value_prev = shifted(value_heads, "ctx", 1)
+    query_next = shifted(query_heads, "ctx", -1)
     chunks = 2 if gpd % 4 == 0 else 1
     cpd, gpd = cpd // chunks, gpd // chunks
-    send, short_k, short_v = before_exchange(
+    send = before_exchange(
         hyena_query, hyena_key, hyena_value, output_grad, tail, short_filter, long_filter, n, chunks
     )
-    send, key_prev, *sources = lax.optimization_barrier(
-        (send, key_prev, output_grad, hyena_key, hyena_value)
+    send, query_next, *sources = lax.optimization_barrier(
+        (send, query_next, output_grad, hyena_key, hyena_value)
     )
     received = lax.all_to_all(send, "ctx", split_axis=0, concat_axis=0, tiled=True)
     following = shifted(edge_rows(sources, True), "ctx", -1)
+    part, log = attend_next(query_next, key_heads, value_heads)
+    part = shifted(part, "ctx", 1)
+    log = shifted(log, "ctx", 1)
     returned = []
+    attention = ()
     for chunk in range(chunks):
         raw = ()
         if chunk + 1 == chunks:
@@ -541,11 +585,13 @@
             squares = total_over(squares, "ctx")
         results = long_convs(received, raw, cpd, gpd, chunk, chunks)
         if chunk == 0:
-            results, received, value_prev, following = lax.optimization_barrier(
-                (results, received, value_prev, following)
+            results, received, part, log, following = lax.optimization_barrier(
+                (results, received, part, log, following)
             )
+            attention = attend_own(query_heads, key_heads, value_heads, part, log, position)
+        if chunk > 0:
+            results, attention = lax.optimization_barrier((results, attention))
         returned.append(lax.all_to_all(results, "ctx", split_axis=0, concat_axis=0, tiled=True))
-    attention = attend(query_heads, key_heads, value_heads, key_prev, value_prev, position)
     bound = math.sqrt(rows * n * groups * tp)
     factor = jnp.minimum(1.0, bound / jnp.sqrt(squares))
     grads = ()
@@ -554,8 +600,8 @@
             returned[chunk], *grads = lax.optimization_barrier((returned[chunk], *grads))
         scale = (factor,) if chunk + 1 == chunks else ()
         grads = after_exchange(
-            returned[chunk], output_grad, short_k, short_v, hyena_key, hyena_value, following, short_filter,
-            groups, chunk, chunks, grads, scale,
+            returned[chunk], output_grad, hyena_key, hyena_value, tail, following, short_filter, groups,
+            chunk, chunks, grads, scale,
         )
     return (attention, *grads)
 

time: 180 us -> 185 us (1.028)
  the two profiles are of different devices: /device:TPU:16 before, /device:TPU:0 now
where the time goes in v7:
time: 185 us; the launch traced here: 184 us
  starting transfers between devices  74.9 us (40%)
  Pallas kernels  72.1 us (39%)
  waiting for transfers between devices  27.5 us (15%)
  between operations  4.93 us (3%)
  local copies, waits for them, and re-layouts  4.72 us (3%)
    all_to_all x2, starting transfers between devices, on_device(): lax.all_to_all(results, 'ctx', split_axis=0, concat_axis=0, tiled=True)  24.1 us
    all_to_all x1, waiting for transfers between devices, on_device(): lax.all_to_all(send, 'ctx', split_axis=0, concat_axis=0, tiled=True)  20.8 us
    ppermute x5, starting transfers between devices, total_over(): lax.ppermute(value, axis, [(i, i ^ distance) for i in range(size)])  20.4 us
    all_to_all x1, starting transfers between devices, on_device(): lax.all_to_all(send, 'ctx', split_axis=0, concat_axis=0, tiled=True)  18.4 us
    pallas_call x1, Pallas kernels, attend_own(): pl.pallas_call(attend_own_kernel, grid=(channels // tile,), in_specs=[pl....  13.3 us
    pallas_call x1, Pallas kernels, attend_next(): pl.pallas_call(attend_next_kernel, grid=(channels // tile,), in_specs=[bl...  13.1 us
    pallas_call x2, Pallas kernels, after_exchange(): pl.pallas_call(functools.partial(after_kernel, cpd, gpd, chunks, last), g...  12.9 us
    ppermute x5, starting transfers between devices, shifted(): return lax.ppermute(block, axis, route)  12.1 us
  transfers between devices with their start and end apart: 13, of which 6 were waited for; matrix products, arithmetic and copies ran while one was open for 0% of the time, Pallas kernels for 36%

profile of v7, /device:TPU:0, one launch (start us, length us, event | category | flops | bytes accessed | tf_op | source)
XLA Modules:
  0.0 184.2 jit_solution(15453624535009365132)
XLA Ops:
  0.6 1.3 collective-permute-start.1
  1.9 1.7 edge_rows.2
  3.7 3.0 %collective-permute-start = (bf16[24,4096]{1,0:T(8,128)(2,1)}, bf16[24,4096]{1,0:T(8,128)(2,1)S(1)}, u32[]{:S(2)}, u32[]{:S(2)}) collective-permute-start(bf16[24,4096]{1,0:T(8,128)(2,1)} %edge_rows.2), channel_id=1, source_target_pairs={{0,2},{2,4},{4,6},{6,8},{8,10},{10,12},{12,14},{14,16},{16,18},{18... | collective-permute-start | bytes 589832 | tf_op jit(solution)/shard_map/ppermute | solution.py:27
  6.7 1.3 collective-permute-done.tail_ref
  7.9 0.7 copy-done.2
  8.6 8.8 %before_exchange.1 = bf16[16,544,128]{2,1,0:T(8,128)(2,1)} custom-call(bf16[128,4096]{1,0:T(8,128)(2,1)} %q_ref.2, bf16[128,4096]{1,0:T(8,128)(2,1)} %k_ref.9, bf16[128,4096]{1,0:T(8,128)(2,1)} %v_ref.9, bf16[128,4096]{1,0:T(8,128)(2,1)} %og_ref.5, bf16[24,4096]{1,0:T(8,128)(2,1)} %copy-done.2, f32[3,7,4096]{2,1,0:T(8,128)} %taps_ref.5, f32[128,256]{1,0:T(8,128)} %long_ref.1), custom_call_target="tpu_custom_call" | custom-call | flops 26214400 | bytes 6291456 | tf_op jit(solution)/shard_map/before_exchange/pallas_call | solution.py:233
  17.4 1.0 copy-done.3
  18.4 18.4 %all-to-all-start = ((bf16[16,544,128]{2,1,0:T(8,128)(2,1)}), bf16[16,544,128]{2,1,0:T(8,128)(2,1)S(1)}, u32[]{:S(2)}, u32[]{:S(2)}) async-start(bf16[16,544,128]{2,1,0:T(8,128)(2,1)} %before_exchange.1), calls=%async_computation | async-start | bytes 4456448 | tf_op jit(solution)/shard_map/all_to_all | solution.py:573
  36.8 13.1 %attend_next.1 = (bf16[128,4096]{1,0:T(8,128)(2,1)}, f32[128,128]{1,0:T(8,128)}) custom-call(bf16[128,4096]{1,0:T(8,128)(2,1)} %copy-done.3, bf16[128,4096]{1,0:T(8,128)(2,1)} %k_ref.7, bf16[128,4096]{1,0:T(8,128)(2,1)} %v_ref.7), custom_call_target="tpu_custom_call" | custom-call | flops 268435456 | bytes 5242880 | tf_op jit(solution)/shard_map/attend_next/pallas_call | solution.py:118
  50.0 2.4 %collective-permute-start.2 = (bf16[128,4096]{1,0:T(8,128)(2,1)}, bf16[128,4096]{1,0:T(8,128)(2,1)S(1)}, u32[]{:S(2)}, u32[]{:S(2)}) collective-permute-start(bf16[128,4096]{1,0:T(8,128)(2,1)} %get-tuple-element.34), channel_id=1, source_target_pairs={{0,2},{2,4},{4,6},{6,8},{8,10},{10,12},{12,14},{14,16},{16,18},{18... | collective-permute-start | bytes 3145736 | tf_op jit(solution)/shard_map/ppermute | solution.py:27
  52.3 1.7 edge_rows.3
  54.1 1.3 collective-permute-start.4
  55.3 4.1 %collective-permute-start.3 = (f32[128,128]{1,0:T(8,128)}, f32[128,128]{1,0:T(8,128)S(1)}, u32[]{:S(2)}, u32[]{:S(2)}) collective-permute-start(f32[128,128]{1,0:T(8,128)} %get-tuple-element.35), channel_id=1, source_target_pairs={{0,2},{2,4},{4,6},{6,8},{8,10},{10,12},{12,14},{14,16},{16,18},{18... | collective-permute-start | bytes 196616 | tf_op jit(solution)/shard_map/ppermute | solution.py:27
  59.5 20.8 %all-to-all-done.in_ref = bf16[16,544,128]{2,1,0:T(8,128)(2,1)S(1)} async-done(((bf16[16,544,128]{2,1,0:T(8,128)(2,1)}), bf16[16,544,128]{2,1,0:T(8,128)(2,1)S(1)}, u32[]{:S(2)}, u32[]{:S(2)}) %all-to-all-start) | async-done | bytes 2228256 | tf_op jit(solution)/shard_map/all_to_all | solution.py:573
  80.2 5.1 %long_convs.2 = bf16[16,272,128]{2,1,0:T(8,128)(2,1)} custom-call(bf16[16,544,128]{2,1,0:T(8,128)(2,1)S(1)} %all-to-all-done.in_ref), custom_call_target="tpu_custom_call" | custom-call | flops 2147483648 | bytes 2228224 | tf_op jit(solution)/shard_map/long_convs/pallas_call | solution.py:328
  85.4 0.6 copy-done.6
  86.4 18.1 %all-to-all-start.2 = ((bf16[16,272,128]{2,1,0:T(8,128)(2,1)}), bf16[16,272,128]{2,1,0:T(8,128)(2,1)S(1)}, u32[]{:S(2)}, u32[]{:S(2)}) async-start(bf16[16,272,128]{2,1,0:T(8,128)(2,1)} %long_convs.2), calls=%async_computation.2 | async-start | bytes 2228224 | tf_op jit(solution)/shard_map/all_to_all | solution.py:594
  104.5 13.3 %attend_own.1 = bf16[128,4096]{1,0:T(8,128)(2,1)} custom-call(s32[1]{0:T(128)} %bitcast.place_ref, bf16[128,4096]{1,0:T(8,128)(2,1)} %q_ref.3, bf16[128,4096]{1,0:T(8,128)(2,1)} %k_ref.7, bf16[128,4096]{1,0:T(8,128)(2,1)} %v_ref.7, bf16[128,4096]{1,0:T(8,128)(2,1)} %copy-done.4, f32[128,128]{1,0:T(8,128)} %copy-done.6), custom_call_target="tpu_custom_call" | custom-call | flops 268435456 | bytes 5242880 | tf_op jit(solution)/shard_map/attend_own/pallas_call | solution.py:137
  117.9 10.2 %filter_products.1 = (bf16[16,16,128]{2,1,0:T(8,128)(2,1)S(1)}, f32[1,1]{1,0:T(1,128)}) custom-call(bf16[16,544,128]{2,1,0:T(8,128)(2,1)S(1)} %all-to-all-done.in_ref), custom_call_target="tpu_custom_call" | custom-call | flops 2147483648 | bytes 2228224 | tf_op jit(solution)/shard_map/filter_products/pallas_call | solution.py:403
  128.1 5.2 %long_convs.3 = bf16[16,288,128]{2,1,0:T(8,128)(2,1)} custom-call(bf16[16,544,128]{2,1,0:T(8,128)(2,1)S(1)} %all-to-all-done.in_ref, bf16[16,16,128]{2,1,0:T(8,128)(2,1)S(1)} %get-tuple-element.40.refs_0_), custom_call_target="tpu_custom_call" | custom-call | flops 2147483648 | bytes 2359296 | tf_op jit(solution)/shard_map/long_convs/pallas_call | solution.py:328
  133.2 1.0 copy-done.1
  134.2 6.0 %all-to-all-start.1 = ((bf16[16,288,128]{2,1,0:T(8,128)(2,1)}), bf16[16,288,128]{2,1,0:T(8,128)(2,1)S(1)}, u32[]{:S(2)}, u32[]{:S(2)}) async-start(bf16[16,288,128]{2,1,0:T(8,128)(2,1)} %long_convs.3), calls=%async_computation.1 | async-start | bytes 2359296 | tf_op jit(solution)/shard_map/all_to_all | solution.py:594
  140.2 1.6 collective-permute-start.5
  141.8 2.1 %collective-permute-done.5 = f32[1,1]{1,0:T(1,128)} collective-permute-done((f32[1,1]{1,0:T(1,128)}, f32[1,1]{1,0:T(1,128)}, u32[]{:S(2)}, u32[]{:S(2)}) %collective-permute-start.5) | collective-permute-done | bytes 36 | tf_op jit(solution)/shard_map/ppermute | solution.py:34
  145.2 0.9 collective-permute-start.6
  147.1 3.2 %collective-permute-start.7 = (f32[1,1]{1,0:T(1,128)}, f32[1,1]{1,0:T(1,128)}, u32[]{:S(2)}, u32[]{:S(2)}) collective-permute-start(f32[1,1]{1,0:T(1,128)} %add.16), channel_id=1, source_target_pairs={{0,4},{2,6},{4,0},{6,2},{8,12},{10,14},{12,8},{14,10},{16,20},{18,... | collective-permute-start | bytes 20 | tf_op jit(solution)/shard_map/ppermute | solution.py:34
  151.4 9.1 %collective-permute-start.8 = (f32[1,1]{1,0:T(1,128)}, f32[1,1]{1,0:T(1,128)}, u32[]{:S(2)}, u32[]{:S(2)}) collective-permute-start(f32[1,1]{1,0:T(1,128)} %add.17), channel_id=1, source_target_pairs={{0,8},{2,10},{4,12},{6,14},{8,0},{10,2},{12,4},{14,6},{16,24},{18,... | collective-permute-start | bytes 20 | tf_op jit(solution)/shard_map/ppermute | solution.py:34
  161.2 5.6 %collective-permute-start.9 = (f32[1,1]{1,0:T(1,128)}, f32[1,1]{1,0:T(1,128)}, u32[]{:S(2)}, u32[]{:S(2)}) collective-permute-start(f32[1,1]{1,0:T(1,128)} %add.18), channel_id=1, source_target_pairs={{0,16},{2,18},{4,20},{6,22},{8,24},{10,26},{12,28},{14,30},{16,0},... | collective-permute-start | bytes 20 | tf_op jit(solution)/shard_map/ppermute | solution.py:34
  166.8 2.8 %collective-permute-done.9 = f32[1,1]{1,0:T(1,128)} collective-permute-done((f32[1,1]{1,0:T(1,128)}, f32[1,1]{1,0:T(1,128)}, u32[]{:S(2)}, u32[]{:S(2)}) %collective-permute-start.9) | collective-permute-done | bytes 36 | tf_op jit(solution)/shard_map/ppermute | solution.py:34
  170.3 6.3 %after_exchange.2 = (bf16[128,4096]{1,0:T(8,128)(2,1)}, bf16[128,4096]{1,0:T(8,128)(2,1)}, bf16[128,4096]{1,0:T(8,128)(2,1)}) custom-call(bf16[16,272,128]{2,1,0:T(8,128)(2,1)} %copy-done.1, bf16[128,4096]{1,0:T(8,128)(2,1)} %og_ref.5, bf16[128,4096]{1,0:T(8,128)(2,1)} %k_ref.9, bf16[128,4096]{1,0:T(8,128)(2,1)} %v_ref.9, bf16[24,4096]{1,0:T(8,128)(2,1)} %copy-done.2, ...), custom_call_target="tpu_custom_call" | custom-call | flops 23592960 | bytes 4718592 | tf_op jit(solution)/shard_map/after_exchange/pallas_call | solution.py:520
  176.6 1.0 copy-done
  177.7 6.6 %after_exchange.3 = (bf16[128,4096]{1,0:T(8,128)(2,1)}, bf16[128,4096]{1,0:T(8,128)(2,1)}, bf16[128,4096]{1,0:T(8,128)(2,1)}, f32[128,256]{1,0:T(8,128)}) custom-call(bf16[16,288,128]{2,1,0:T(8,128)(2,1)} %copy-done, bf16[128,4096]{1,0:T(8,128)(2,1)} %og_ref.5, bf16[128,4096]{1,0:T(8,128)(2,1)} %k_ref.9, ...), custom_call_target="tpu_custom_call", output_to_operand_aliasing={{0}: (8, {}), {1}: (9, {}), {2}: (10, {})} | custom-call | flops 23592960 | bytes 4718592 | tf_op jit(solution)/shard_map/after_exchange/pallas_call | solution.py:520
  (18 shorter events, 1.1 us)
Async XLA Ops:
  0.6 16.8 %collective-permute-start.1 = (bf16[128,4096]{1,0:T(8,128)(2,1)}, bf16[128,4096]{1,0:T(8,128)(2,1)S(1)}, u32[]{:S(2)}, u32[]{:S(2)}) collective-permute-start(bf16[128,4096]{1,0:T(8,128)(2,1)} %q_ref.3), channel_id=1, source_target_pairs={{2,0},{4,2},{6,4},{8,6},{10,8},{12,10},{14,12},{16,14},{18,16},{20... | collective-permute-start | bytes 3145736 | tf_op jit(solution)/shard_map/ppermute | solution.py:27
  3.7 4.3 %collective-permute-start = (bf16[24,4096]{1,0:T(8,128)(2,1)}, bf16[24,4096]{1,0:T(8,128)(2,1)S(1)}, u32[]{:S(2)}, u32[]{:S(2)}) collective-permute-start(bf16[24,4096]{1,0:T(8,128)(2,1)} %edge_rows.2), channel_id=1, source_target_pairs={{0,2},{2,4},{4,6},{6,8},{8,10},{10,12},{12,14},{14,16},{16,18},{18... | collective-permute-start | bytes 589832 | tf_op jit(solution)/shard_map/ppermute | solution.py:27
  7.9 0.7 copy-start.2
  17.4 1.0 copy-start.3
  18.4 61.8 %all-to-all-start = ((bf16[16,544,128]{2,1,0:T(8,128)(2,1)}), bf16[16,544,128]{2,1,0:T(8,128)(2,1)S(1)}, u32[]{:S(2)}, u32[]{:S(2)}) async-start(bf16[16,544,128]{2,1,0:T(8,128)(2,1)} %before_exchange.1), calls=%async_computation | async-start | bytes 4456448 | tf_op jit(solution)/shard_map/all_to_all | solution.py:573
  50.0 35.4 %collective-permute-start.2 = (bf16[128,4096]{1,0:T(8,128)(2,1)}, bf16[128,4096]{1,0:T(8,128)(2,1)S(1)}, u32[]{:S(2)}, u32[]{:S(2)}) collective-permute-start(bf16[128,4096]{1,0:T(8,128)(2,1)} %get-tuple-element.34), channel_id=1, source_target_pairs={{0,2},{2,4},{4,6},{6,8},{8,10},{10,12},{12,14},{14,16},{16,18},{18... | collective-permute-start | bytes 3145736 | tf_op jit(solution)/shard_map/ppermute | solution.py:27
  54.1 31.3 %collective-permute-start.4 = (bf16[24,4096]{1,0:T(8,128)(2,1)}, bf16[24,4096]{1,0:T(8,128)(2,1)S(1)}, u32[]{:S(2)}, u32[]{:S(2)}) collective-permute-start(bf16[24,4096]{1,0:T(8,128)(2,1)} %edge_rows.3), channel_id=1, source_target_pairs={{2,0},{4,2},{6,4},{8,6},{10,8},{12,10},{14,12},{16,14},{18,16},{20... | collective-permute-start | bytes 589832 | tf_op jit(solution)/shard_map/ppermute | solution.py:27
  55.3 30.0 %collective-permute-start.3 = (f32[128,128]{1,0:T(8,128)}, f32[128,128]{1,0:T(8,128)S(1)}, u32[]{:S(2)}, u32[]{:S(2)}) collective-permute-start(f32[128,128]{1,0:T(8,128)} %get-tuple-element.35), channel_id=1, source_target_pairs={{0,2},{2,4},{4,6},{6,8},{8,10},{10,12},{12,14},{14,16},{16,18},{18... | collective-permute-start | bytes 196616 | tf_op jit(solution)/shard_map/ppermute | solution.py:27
  85.3 0.6 copy-start.6
  85.4 32.5 %copy-start.5 = (bf16[24,4096]{1,0:T(8,128)(2,1)}, bf16[24,4096]{1,0:T(8,128)(2,1)S(1)}, u32[]{:S(2)}) copy-start(bf16[24,4096]{1,0:T(8,128)(2,1)S(1)} %collective-permute-done.4.next_ref) | copy-start | bytes 589828
  85.4 1.0 copy-start.4
  86.4 46.8 %all-to-all-start.2 = ((bf16[16,272,128]{2,1,0:T(8,128)(2,1)}), bf16[16,272,128]{2,1,0:T(8,128)(2,1)S(1)}, u32[]{:S(2)}, u32[]{:S(2)}) async-start(bf16[16,272,128]{2,1,0:T(8,128)(2,1)} %long_convs.2), calls=%async_computation.2 | async-start | bytes 2228224 | tf_op jit(solution)/shard_map/all_to_all | solution.py:594
  133.2 1.0 copy-start.1
  134.2 42.4 %all-to-all-start.1 = ((bf16[16,288,128]{2,1,0:T(8,128)(2,1)}), bf16[16,288,128]{2,1,0:T(8,128)(2,1)S(1)}, u32[]{:S(2)}, u32[]{:S(2)}) async-start(bf16[16,288,128]{2,1,0:T(8,128)(2,1)} %long_convs.3), calls=%async_computation.1 | async-start | bytes 2359296 | tf_op jit(solution)/shard_map/all_to_all | solution.py:594
  140.2 3.7 %collective-permute-start.5 = (f32[1,1]{1,0:T(1,128)}, f32[1,1]{1,0:T(1,128)}, u32[]{:S(2)}, u32[]{:S(2)}) collective-permute-start(f32[1,1]{1,0:T(1,128)} %get-tuple-element.51), channel_id=1, source_target_pairs={{0,1},{1,0},{2,3},{3,2},{4,5},{5,4},{6,7},{7,6},{8,9},{9,8},{10,11... | collective-permute-start | bytes 20 | tf_op jit(solution)/shard_map/ppermute | solution.py:34
  145.2 1.2 collective-permute-start.6
  147.1 3.6 %collective-permute-start.7 = (f32[1,1]{1,0:T(1,128)}, f32[1,1]{1,0:T(1,128)}, u32[]{:S(2)}, u32[]{:S(2)}) collective-permute-start(f32[1,1]{1,0:T(1,128)} %add.16), channel_id=1, source_target_pairs={{0,4},{2,6},{4,0},{6,2},{8,12},{10,14},{12,8},{14,10},{16,20},{18,... | collective-permute-start | bytes 20 | tf_op jit(solution)/shard_map/ppermute | solution.py:34
  151.4 9.1 %collective-permute-start.8 = (f32[1,1]{1,0:T(1,128)}, f32[1,1]{1,0:T(1,128)}, u32[]{:S(2)}, u32[]{:S(2)}) collective-permute-start(f32[1,1]{1,0:T(1,128)} %add.17), channel_id=1, source_target_pairs={{0,8},{2,10},{4,12},{6,14},{8,0},{10,2},{12,4},{14,6},{16,24},{18,... | collective-permute-start | bytes 20 | tf_op jit(solution)/shard_map/ppermute | solution.py:34
  161.2 8.4 %collective-permute-start.9 = (f32[1,1]{1,0:T(1,128)}, f32[1,1]{1,0:T(1,128)}, u32[]{:S(2)}, u32[]{:S(2)}) collective-permute-start(f32[1,1]{1,0:T(1,128)} %add.18), channel_id=1, source_target_pairs={{0,16},{2,18},{4,20},{6,22},{8,24},{10,26},{12,28},{14,30},{16,0},... | collective-permute-start | bytes 20 | tf_op jit(solution)/shard_map/ppermute | solution.py:34
  176.6 1.1 copy-start

commit v8 on v7

--- a/solution.py
+++ b/solution.py
@@ -60,17 +60,23 @@
     def _():
         log_ref[...] = jnp.zeros_like(log_ref)
 
+    places = [slice(head * HEAD_DIM, (head + 1) * HEAD_DIM) for head in range(heads)]
+    scores = [
+        lax.dot_general(q_ref[:, at], k_ref[:, at], NT, preferred_element_type=F32) * SCALE
+        for at in places
+    ]
+    largest = [jnp.max(score, axis=1, keepdims=True) for score in scores]
+    raised = [jnp.exp(score - top) for score, top in zip(scores, largest)]
+    totals = [jnp.sum(r, axis=1, keepdims=True) for r in raised]
+    weights = [(r * (1.0 / total)).astype(BF16) for r, total in zip(raised, totals)]
+    mixed = [
+        jnp.dot(weight, v_ref[:, at], preferred_element_type=F32) for weight, at in zip(weights, places)
+    ]
     logs = log_ref[...]
-    for head in range(heads):
-        at = slice(head * HEAD_DIM, (head + 1) * HEAD_DIM)
-        score = lax.dot_general(q_ref[:, at], k_ref[:, at], NT, preferred_element_type=F32) * SCALE
-        largest = jnp.max(score, axis=1, keepdims=True)
-        raised = jnp.exp(score - largest)
-        total = jnp.sum(raised, axis=1, keepdims=True)
-        weight = (raised * (1.0 / total)).astype(BF16)
-        mixed = jnp.dot(weight, v_ref[:, at], preferred_element_type=F32)
-        out_ref[:, at] = mixed.astype(BF16)
-        logs = jnp.where(lane == step * heads + head, largest + jnp.log(total), logs)
+    for head, at in enumerate(places):
+        out_ref[:, at] = mixed[head].astype(BF16)
+        log = largest[head] + jnp.log(totals[head])
+        logs = jnp.where(lane == step * heads + head, log, logs)
     log_ref[...] = logs
 
 
@@ -83,22 +89,32 @@
     own_ok = col <= row
     lane = lax.broadcasted_iota(jnp.int32, (rows, log_ref.shape[1]), 1)
     has_prev = jnp.broadcast_to(place_ref[0], (rows, 1)) > 0
-    for head in range(heads):
-        at = slice(head * HEAD_DIM, (head + 1) * HEAD_DIM)
-        log = jnp.sum(
-            jnp.where(lane == step * heads + head, log_ref[...], 0.0), axis=1, keepdims=True
-        )
-        log = jnp.where(has_prev, log, -jnp.inf)
-        own = lax.dot_general(q_ref[:, at], k_ref[:, at], NT, preferred_element_type=F32) * SCALE
-        own = jnp.where(own_ok, own, -jnp.inf)
-        largest = jnp.maximum(jnp.max(own, axis=1, keepdims=True), log)
-        own = jnp.exp(own - largest)
-        prev = jnp.exp(log - largest)
-        inverse = 1.0 / (jnp.sum(own, axis=1, keepdims=True) + prev)
-        weight = (own * inverse).astype(BF16)
-        mixed = jnp.dot(weight, v_ref[:, at], preferred_element_type=F32)
-        mixed = mixed + (prev * inverse) * prev_ref[:, at].astype(F32)
-        out_ref[:, at] = mixed.astype(BF16)
+    places = [slice(head * HEAD_DIM, (head + 1) * HEAD_DIM) for head in range(heads)]
+    scores = [
+        lax.dot_general(q_ref[:, at], k_ref[:, at], NT, preferred_element_type=F32) * SCALE
+        for at in places
+    ]
+    scores = [jnp.where(own_ok, score, -jnp.inf) for score in scores]
+    logs = [
+        jnp.sum(jnp.where(lane == step * heads + head, log_ref[...], 0.0), axis=1, keepdims=True)
+        for head in range(heads)
+    ]
+    logs = [jnp.where(has_prev, log, -jnp.inf) for log in logs]
+    largest = [
+        jnp.maximum(jnp.max(score, axis=1, keepdims=True), log) for score, log in zip(scores, logs)
+    ]
+    raised = [jnp.exp(score - top) for score, top in zip(scores, largest)]
+    prevs = [jnp.exp(log - top) for log, top in zip(logs, largest)]
+    inverses = [
+        1.0 / (jnp.sum(r, axis=1, keepdims=True) + prev) for r, prev in zip(raised, prevs)
+    ]
+    weights = [(r * inverse).astype(BF16) for r, inverse in zip(raised, inverses)]
+    mixed = [
+        jnp.dot(weight, v_ref[:, at], preferred_element_type=F32) for weight, at in zip(weights, places)
+    ]
+    for head, at in enumerate(places):
+        total = mixed[head] + (prevs[head] * inverses[head]) * prev_ref[:, at].astype(F32)
+        out_ref[:, at] = total.astype(BF16)
 
 
 def attend_cost(rows, channels):
@@ -252,6 +268,11 @@
 
 def conv_kernel(cpd, gpd, in_ref, *refs):
     *raw_ref, out_ref, taps, wide = refs
+    upper = lower = 0.0
+    if raw_ref:
+        *raw_ref, squares_ref = raw_ref
+        upper = squares_ref[...].astype(BF16).astype(F32)
+        lower = squares_ref[...] - upper
     n, send_rows, rows = in_ref.shape
     gw = cpd // gpd
     span = n * rows
@@ -262,38 +283,50 @@
     for slot in range(2):
         wide[slot, :, 0:rows] = jnp.zeros((rows, rows), BF16)
 
-    def one_group(g, slot):
-        line = jnp.broadcast_to(taps[pl.ds(g, 1), :], (16, span + rows))
-        base = pltpu.roll(line, 0, 1, stride=1, stride_axis=0).astype(BF16)
+    def body(i, carry):
+        slots = range(2)
+        firsts = [pl.multiple_of((2 * i + slot) * gw, gw) for slot in slots]
+        seconds = [pl.multiple_of(cpd + (2 * i + slot) * gw, gw) for slot in slots]
+        bases = []
+        for slot in slots:
+            line = jnp.broadcast_to(taps[pl.ds(2 * i + slot, 1), :], (16, span + rows))
+            bases.append(pltpu.roll(line, 0, 1, stride=1, stride_axis=0).astype(BF16))
         for m in range(rows // 16):
-            moved = base if m == 0 else pltpu.roll(base, 16 * m, 1)
-            wide[slot, 16 * m : 16 * m + 16, rows:] = moved[:, rows:]
-        first = pl.multiple_of(g * gw, gw)
-        x = in_ref[:, pl.ds(first, gw), :]
-        second = pl.multiple_of(cpd + g * gw, gw)
-        d = in_ref[:, pl.ds(second, gw), :]
-        both = [jnp.concatenate([x[a], d[n - 1 - a]], 0) for a in range(n)]
-        lhs = jnp.concatenate(
-            [jnp.concatenate([both[a], both[a + 1]], 1) for a in range(0, n, 2)], 0
-        )
-        total = None
+            for slot in slots:
+                moved = bases[slot] if m == 0 else pltpu.roll(bases[slot], 16 * m, 1)
+                wide[slot, 16 * m : 16 * m + 16, rows:] = moved[:, rows:]
+        stacks = []
+        for slot in slots:
+            x = in_ref[:, pl.ds(firsts[slot], gw), :]
+            d = in_ref[:, pl.ds(seconds[slot], gw), :]
+            both = [jnp.concatenate([x[a], d[n - 1 - a]], 0) for a in range(n)]
+            stacks.append(
+                jnp.concatenate(
+                    [jnp.concatenate([both[a], both[a + 1]], 1) for a in range(0, n, 2)], 0
+                )
+            )
+        totals = [None, None]
         for k in range(n // 2):
             skip = 2 * gw * k
             low = 2 * rows * k
-            tile = jnp.concatenate(
-                [wide[slot, :, low + rows : low + 3 * rows], wide[slot, :, low : low + 2 * rows]], 0
-            )
-            part = jnp.dot(lhs[: n * gw - skip], tile, preferred_element_type=F32)
-            total = part if k == 0 else jnp.concatenate([total[:skip], total[skip:] + part], 0)
-        for a in range(n):
-            at = slice(a % 2 * rows, (a % 2 + 1) * rows)
-            top = a // 2 * 2 * gw
-            out_ref[a, pl.ds(first, gw), :] = total[top : top + gw, at].astype(BF16)
-            out_ref[n - 1 - a, pl.ds(second, gw), :] = total[top + gw : top + 2 * gw, at].astype(BF16)
-
-    def body(i, carry):
-        one_group(2 * i, 0)
-        one_group(2 * i + 1, 1)
+            for slot in slots:
+                tile = jnp.concatenate(
+                    [wide[slot, :, low + rows : low + 3 * rows], wide[slot, :, low : low + 2 * rows]], 0
+                )
+                part = jnp.dot(stacks[slot][: n * gw - skip], tile, preferred_element_type=F32)
+                total = totals[slot]
+                totals[slot] = (
+                    part if k == 0 else jnp.concatenate([total[:skip], total[skip:] + part], 0)
+                )
+        for slot in slots:
+            total = totals[slot]
+            for a in range(n):
+                at = slice(a % 2 * rows, (a % 2 + 1) * rows)
+                top = a // 2 * 2 * gw
+                out_ref[a, pl.ds(firsts[slot], gw), :] = total[top : top + gw, at].astype(BF16)
+                out_ref[n - 1 - a, pl.ds(seconds[slot], gw), :] = total[
+                    top + gw : top + 2 * gw, at
+                ].astype(BF16)
         return carry
 
     lax.fori_loop(0, gpd // 2, body, 0)
@@ -302,6 +335,7 @@
     lane = lax.broadcasted_iota(jnp.int32, (2 * EDGE, 2 * rows), 1)
     wanted = jnp.where(row < EDGE, row, 2 * rows - 1 + EDGE - row)
     pick = jnp.where(lane == wanted, 1.0, 0.0).astype(BF16)
+    row_out = lax.broadcasted_iota(jnp.int32, (2 * EDGE, rows), 0)
     for a in range(n):
         if a + 1 < n:
             results = jnp.concatenate([out_ref[a + 1, 0:cpd, :], out_ref[a + 1, cpd : 2 * cpd, :]], 1)
@@ -314,7 +348,9 @@
             halo = jnp.zeros((2 * EDGE, max(cpd, LANES)), F32)
         for j in range(halo.shape[1] // LANES):
             at = halo_at + 2 * EDGE * j
-            out_ref[a, at : at + 2 * EDGE, :] = halo[:, j * LANES : (j + 1) * LANES].astype(BF16)
+            tile = halo[:, j * LANES : (j + 1) * LANES]
+            tile = jnp.where(row_out == EDGE - 2, upper, jnp.where(row_out == EDGE - 1, lower, tile))
+            out_ref[a, at : at + 2 * EDGE, :] = tile.astype(BF16)
     for ref in raw_ref:
         out_ref[:, out_ref.shape[1] - ref.shape[1] :, :] = ref[...]
 
@@ -323,13 +359,13 @@
     n, send_rows, rows = received.shape
     send_rows = send_rows // chunks
     filter_rows = send_rows - 2 * cpd
-    out_rows = 2 * cpd + 2 * EDGE * max(1, cpd // LANES) + sum(r.shape[1] for r in raw)
+    out_rows = 2 * cpd + 2 * EDGE * max(1, cpd // LANES) + sum(r.shape[1] for r in raw[:1])
     span = n * rows
     return pl.pallas_call(
         functools.partial(conv_kernel, cpd, gpd),
         grid=(1,),
         in_specs=[pl.BlockSpec((n, send_rows, rows), lambda i: (0, chunk, 0))]
-        + [pl.BlockSpec(r.shape, lambda i: (0, 0, 0)) for r in raw],
+        + [pl.BlockSpec(r.shape, lambda i, r=r: (0,) * r.ndim) for r in raw],
         out_specs=pl.BlockSpec((n, out_rows, rows), lambda i: (0, 0, 0)),
         out_shape=jax.ShapeDtypeStruct((n, out_rows, rows), BF16),
         scratch_shapes=[
@@ -355,38 +391,43 @@
         raw[...] = jnp.zeros_like(raw)
     no_rows = jnp.zeros((n * gw, rows), BF16)
 
-    def one_group(base, line_at, g, slot):
-        first = pl.multiple_of(base + g * gw, gw)
-        second = pl.multiple_of(base + cpd + g * gw, gw)
-        x = in_ref[:, pl.ds(first, gw), :].reshape(n * gw, rows)
-        d = in_ref[:, pl.ds(second, gw), :].reshape(n * gw, rows)
-        x_turned = x.astype(F32).T.astype(BF16)
-
-        def offset(k):
-            held = (k + 1) * gw
-            if held == n * gw:
-                return d
-            return jnp.concatenate([d[n * gw - held :], no_rows[held:]], 0)
-
-        for k in range(0, n, 2):
-            pairs = jnp.concatenate([offset(k), offset(k + 1)], 1)
-            gram[slot, :, k * rows : (k + 2) * rows] = jnp.dot(
-                x_turned, pairs, preferred_element_type=F32
-            )
-        sums = gram[slot, 0:8, :]
-        for m in range(1, rows // 8):
-            sums = sums + pltpu.roll(gram[slot, 8 * m : 8 * m + 8, :], 8 * m, 1)
-        sums = pltpu.roll(sums, 0, 1, stride=1, stride_axis=0)
-        line = jnp.sum(sums, axis=0, keepdims=True)[:, :span]
-        raw[pl.ds(line_at + g, 1), :] = line
-        return line * line
+    def offset(d, k):
+        held = (k + 1) * gw
+        if held == n * gw:
+            return d
+        return jnp.concatenate([d[n * gw - held :], no_rows[held:]], 0)
 
     squares = jnp.zeros((1, span), F32)
     for chunk in range(chunks):
-
-        def body(i, total, chunk=chunk):
-            total = total + one_group(chunk * send_rows, chunk * gpd, 2 * i, 0)
-            return total + one_group(chunk * send_rows, chunk * gpd, 2 * i + 1, 1)
+        base = chunk * send_rows
+
+        def body(i, squares, chunk=chunk, base=base):
+            slots = range(2)
+            turned, shifting = [], []
+            for slot in slots:
+                first = pl.multiple_of(base + (2 * i + slot) * gw, gw)
+                second = pl.multiple_of(base + cpd + (2 * i + slot) * gw, gw)
+                x = in_ref[:, pl.ds(first, gw), :].reshape(n * gw, rows)
+                shifting.append(in_ref[:, pl.ds(second, gw), :].reshape(n * gw, rows))
+                turned.append(x.astype(F32).T.astype(BF16))
+            for k in range(0, n, 2):
+                for slot in slots:
+                    d = shifting[slot]
+                    pairs = jnp.concatenate([offset(d, k), offset(d, k + 1)], 1)
+                    gram[slot, :, k * rows : (k + 2) * rows] = jnp.dot(
+                        turned[slot], pairs, preferred_element_type=F32
+                    )
+            sums = [gram[slot, 0:8, :] for slot in slots]
+            for m in range(1, rows // 8):
+                for slot in slots:
+                    block = gram[slot, 8 * m : 8 * m + 8, :]
+                    sums[slot] = sums[slot] + pltpu.roll(block, 8 * m, 1)
+            sums = [pltpu.roll(total, 0, 1, stride=1, stride_axis=0) for total in sums]
+            for slot in slots:
+                line = jnp.sum(sums[slot], axis=0, keepdims=True)[:, :span]
+                raw[pl.ds(chunk * gpd + 2 * i + slot, 1), :] = line
+                squares = squares + line * line
+            return squares
 
         squares = lax.fori_loop(0, gpd // 2, body, squares)
     squares_ref[...] = jnp.sum(squares, axis=1, keepdims=True)
@@ -441,11 +482,11 @@
 
 
 def after_kernel(
-    cpd, gpd, chunks, last, in_ref, og_ref, k_ref, v_ref, tail_ref, next_ref, taps_ref, *refs
+    cpd, gpd, chunks, last, bound, in_ref, og_ref, k_ref, v_ref, tail_ref, next_ref, taps_ref, *refs
 ):
     *refs, ext_q, ext_k, ext_v, ext_in_k, ext_in_v = refs
     if last:
-        *refs, raw_ref, raw_rows = refs
+        *refs, raw_ref, raw_rows, total_ref = refs
     dq_ref, dk_ref, dv_ref = refs[-3:]
     step = pl.program_id(0)
     per_tile, in_rows, rows = in_ref.shape
@@ -491,7 +532,16 @@
         ).astype(BF16)
     if not last:
         return
-    scale = refs[0][0, 0]
+    squares = jnp.zeros((1, LANES), F32)
+    for dest in range(per_tile):
+        parts = in_ref[dest, halo_at : halo_at + 2 * EDGE, :].astype(F32)
+        squares = squares + parts[EDGE - 2 : EDGE - 1] + parts[EDGE - 1 : EDGE]
+
+    @pl.when(step == 0)
+    def _():
+        total_ref[...] = jnp.zeros_like(total_ref)
+
+    total_ref[...] = total_ref[...] + squares
     half = raw_rows.shape[0] // chunks
     for dest in range(per_tile):
         lines = in_ref[dest, halo_at + halo_rows :, :].astype(F32)
@@ -501,11 +551,12 @@
 
     @pl.when(step == pl.num_programs(0) - 1)
     def _():
-        raw_ref[...] = raw_rows[...].T * scale
+        factor = jnp.minimum(1.0, bound / jnp.sqrt(total_ref[...]))[:, 0:1]
+        raw_ref[...] = raw_rows[...].T * factor
 
 
 def after_exchange(
-    returned, out_grad, key, value, tail, following, taps, groups, chunk, chunks, grads, scale
+    returned, out_grad, key, value, tail, following, taps, groups, chunk, chunks, grads, bound
 ):
     n, in_rows, rows = returned.shape
     channels = out_grad.shape[1] // chunks
@@ -518,7 +569,7 @@
     ext = pltpu.VMEM((tile // LANES, rows + EDGE, LANES), F32)
     grad = jax.ShapeDtypeStruct(out_grad.shape, BF16)
     return pl.pallas_call(
-        functools.partial(after_kernel, cpd, gpd, chunks, last),
+        functools.partial(after_kernel, cpd, gpd, chunks, last, bound),
         grid=(channels // tile,),
         in_specs=[
             pl.BlockSpec((per_tile, in_rows, rows), lambda i: (i, 0, 0)),
@@ -529,18 +580,18 @@
             pl.BlockSpec((3 * EDGE, tile), lambda i: (0, first + i)),
             pl.BlockSpec((3, taps.shape[1], tile), lambda i: (0, 0, first + i)),
         ]
-        + [pl.BlockSpec(memory_space=pltpu.SMEM)] * len(scale)
         + [pl.BlockSpec(memory_space=pl.ANY)] * len(grads),
-        input_output_aliases={7 + len(scale) + i: i for i in range(len(grads))},
-        out_specs=[block] * 3 + [pl.BlockSpec((rows, groups), lambda i: (0, 0))] * len(scale),
-        out_shape=[grad] * 3 + [jax.ShapeDtypeStruct((rows, groups), F32)] * len(scale),
-        scratch_shapes=[pltpu.VMEM((groups, rows), F32)] * len(scale) + [ext] * 5,
+        input_output_aliases={7 + i: i for i in range(len(grads))},
+        out_specs=[block] * 3 + [pl.BlockSpec((rows, groups), lambda i: (0, 0))] * last,
+        out_shape=[grad] * 3 + [jax.ShapeDtypeStruct((rows, groups), F32)] * last,
+        scratch_shapes=[pltpu.VMEM((groups, rows), F32), pltpu.VMEM((1, LANES), F32)] * last
+        + [ext] * 5,
         compiler_params=params(),
         cost_estimate=pl.CostEstimate(
             flops=90 * rows * channels, bytes_accessed=18 * rows * channels, transcendentals=0
         ),
         name="after_exchange",
-    )(returned, out_grad, key, value, tail, following, taps, *scale, *grads)
+    )(returned, out_grad, key, value, tail, following, taps, *grads)
 
 
 def on_device(
@@ -561,7 +612,8 @@
     cpd, gpd = channels // n, groups // n
     position = lax.axis_index("ctx")
     tail = shifted(edge_rows((hyena_query, hyena_key, hyena_value), False), "ctx", 1)
-    query_next = shifted(query_heads, "ctx", -1)
+    queries, tail = lax.optimization_barrier((query_heads, tail))
+    query_next = shifted(queries, "ctx", -1)
     chunks = 2 if gpd % 4 == 0 else 1
     cpd, gpd = cpd // chunks, gpd // chunks
     send = before_exchange(
@@ -576,32 +628,28 @@
     part = shifted(part, "ctx", 1)
     log = shifted(log, "ctx", 1)
     returned = []
-    attention = ()
     for chunk in range(chunks):
         raw = ()
         if chunk + 1 == chunks:
-            *raw, squares = filter_products(received, cpd, gpd, chunks)
-            squares = total_over(squares, "tp")
-            squares = total_over(squares, "ctx")
+            raw, squares = filter_products(received, cpd, gpd, chunks)
+            raw = (raw, total_over(squares, "tp"))
         results = long_convs(received, raw, cpd, gpd, chunk, chunks)
         if chunk == 0:
             results, received, part, log, following = lax.optimization_barrier(
                 (results, received, part, log, following)
             )
-            attention = attend_own(query_heads, key_heads, value_heads, part, log, position)
-        if chunk > 0:
-            results, attention = lax.optimization_barrier((results, attention))
         returned.append(lax.all_to_all(results, "ctx", split_axis=0, concat_axis=0, tiled=True))
+    attention = attend_own(query_heads, key_heads, value_heads, part, log, position)
     bound = math.sqrt(rows * n * groups * tp)
-    factor = jnp.minimum(1.0, bound / jnp.sqrt(squares))
     grads = ()
     for chunk in range(chunks):
         if chunk > 0:
-            returned[chunk], *grads = lax.optimization_barrier((returned[chunk], *grads))
-        scale = (factor,) if chunk + 1 == chunks else ()
+            returned[chunk], attention, *grads = lax.optimization_barrier(
+                (returned[chunk], attention, *grads)
+            )
         grads = after_exchange(
             returned[chunk], output_grad, hyena_key, hyena_value, tail, following, short_filter, groups,
-            chunk, chunks, grads, scale,
+            chunk, chunks, grads, bound,
         )
     return (attention, *grads)
 

time: 185 us -> 169 us (0.914)
  the two profiles are of different devices: /device:TPU:0 before, /device:TPU:16 now
where the time goes in v8:
time: 169 us; the launch traced here: 168 us
  waiting for transfers between devices  73.3 us (43%)
  Pallas kernels  59.4 us (35%)
  starting transfers between devices  29.1 us (17%)
  local copies, waits for them, and re-layouts  4 us (2%)
  between operations  1.99 us (1%)
    all_to_all x1, waiting for transfers between devices, on_device(): lax.all_to_all(send, 'ctx', split_axis=0, concat_axis=0, tiled=True)  33.2 us
    all_to_all x2, waiting for transfers between devices, on_device(): lax.all_to_all(results, 'ctx', split_axis=0, concat_axis=0, tiled=True)  22.1 us
    ppermute x5, waiting for transfers between devices, shifted(): return lax.ppermute(block, axis, route)  16 us
    pallas_call x2, Pallas kernels, after_exchange(): pl.pallas_call(functools.partial(after_kernel, cpd, gpd, chunks, last, bo...  13 us
    ppermute x5, starting transfers between devices, shifted(): return lax.ppermute(block, axis, route)  12.2 us
    pallas_call x2, Pallas kernels, long_convs(): pl.pallas_call(functools.partial(conv_kernel, cpd, gpd), grid=(1,), in_sp...  10.3 us
    all_to_all x2, starting transfers between devices, on_device(): lax.all_to_all(results, 'ctx', split_axis=0, concat_axis=0, tiled=True)  8.85 us
    pallas_call x1, Pallas kernels, before_exchange(): pl.pallas_call(functools.partial(before_kernel, cpd, gpd), grid=(channels...  8.84 us
  transfers between devices with their start and end apart: 9, of which 7 were waited for; matrix products, arithmetic and copies ran while one was open for 0% of the time, Pallas kernels for 30%

profile of v8, /device:TPU:16, one launch (start us, length us, event | category | flops | bytes accessed | tf_op | source)
XLA Modules:
  0.0 167.8 jit_solution(1540389782651547557)
XLA Ops:
  0.6 0.0 copy-start.4
  0.6 1.8 %edge_rows.2 = bf16[24,4096]{1,0:T(8,128)(2,1)} custom-call(bf16[128,4096]{1,0:T(8,128)(2,1)} %q_ref.2, bf16[128,4096]{1,0:T(8,128)(2,1)} %k_ref.9, bf16[128,4096]{1,0:T(8,128)(2,1)} %v_ref.9), custom_call_target="tpu_custom_call" | custom-call | tf_op jit(solution)/shard_map/edge_rows/pallas_call | solution.py:177
  2.5 1.9 %collective-permute-start = (bf16[24,4096]{1,0:T(8,128)(2,1)}, bf16[24,4096]{1,0:T(8,128)(2,1)S(1)}, u32[]{:S(2)}, u32[]{:S(2)}) collective-permute-start(bf16[24,4096]{1,0:T(8,128)(2,1)} %edge_rows.2), channel_id=1, source_target_pairs={{0,2},{2,4},{4,6},{6,8},{8,10},{10,12},{12,14},{14,16},{16,18},{18... | collective-permute-start | bytes 589832 | tf_op jit(solution)/shard_map/ppermute | solution.py:27
  4.4 6.2 %collective-permute-done.tail_ref = bf16[24,4096]{1,0:T(8,128)(2,1)S(1)} collective-permute-done((bf16[24,4096]{1,0:T(8,128)(2,1)}, bf16[24,4096]{1,0:T(8,128)(2,1)S(1)}, u32[]{:S(2)}, u32[]{:S(2)}) %collective-permute-start) | collective-permute-done | bytes 196640 | tf_op jit(solution)/shard_map/ppermute | solution.py:27
  10.5 1.9 %collective-permute-start.1 = (bf16[128,4096]{1,0:T(8,128)(2,1)S(1)}, bf16[128,4096]{1,0:T(8,128)(2,1)S(1)}, u32[]{:S(2)}, u32[]{:S(2)}) collective-permute-start(bf16[128,4096]{1,0:T(8,128)(2,1)S(1)} %copy-done.4), channel_id=1, source_target_pairs={{2,0},{4,2},{6,4},{8,6},{10,8},{12,10},{14,12},{16,14},{18,16},{20... | collective-permute-start | bytes 3145736 | tf_op jit(solution)/shard_map/ppermute | solution.py:27
  12.5 8.8 %before_exchange.1 = bf16[16,544,128]{2,1,0:T(8,128)(2,1)} custom-call(bf16[128,4096]{1,0:T(8,128)(2,1)} %q_ref.2, bf16[128,4096]{1,0:T(8,128)(2,1)} %k_ref.9, bf16[128,4096]{1,0:T(8,128)(2,1)} %v_ref.9, bf16[128,4096]{1,0:T(8,128)(2,1)} %og_ref.5, bf16[24,4096]{1,0:T(8,128)(2,1)} %copy-done.2, f32[3,7,4096]{2,1,0:T(8,128)} %taps_ref.5, f32[128,256]{1,0:T(8,128)} %long_ref.1), custom_call_target="tpu_custom_call" | custom-call | flops 26214400 | bytes 6291456 | tf_op jit(solution)/shard_map/before_exchange/pallas_call | solution.py:249
  21.3 3.4 %collective-permute-done.1.q_ref = bf16[128,4096]{1,0:T(8,128)(2,1)S(1)} collective-permute-done((bf16[128,4096]{1,0:T(8,128)(2,1)S(1)}, bf16[128,4096]{1,0:T(8,128)(2,1)S(1)}, u32[]{:S(2)}, u32[]{:S(2)}) %collective-permute-start.1) | collective-permute-done | bytes 1048608 | tf_op jit(solution)/shard_map/ppermute | solution.py:27
  24.8 1.0 copy-done.3
  25.7 6.6 %all-to-all-start = ((bf16[16,544,128]{2,1,0:T(8,128)(2,1)}), bf16[16,544,128]{2,1,0:T(8,128)(2,1)S(1)}, u32[]{:S(2)}, u32[]{:S(2)}) async-start(bf16[16,544,128]{2,1,0:T(8,128)(2,1)} %before_exchange.1), calls=%async_computation | async-start | bytes 4456448 | tf_op jit(solution)/shard_map/all_to_all | solution.py:625
  32.3 7.7 %attend_next.1 = (bf16[128,4096]{1,0:T(8,128)(2,1)}, f32[128,128]{1,0:T(8,128)}) custom-call(bf16[128,4096]{1,0:T(8,128)(2,1)} %copy-done.3, bf16[128,4096]{1,0:T(8,128)(2,1)} %k_ref.7, bf16[128,4096]{1,0:T(8,128)(2,1)} %v_ref.7), custom_call_target="tpu_custom_call" | custom-call | flops 268435456 | bytes 5242880 | tf_op jit(solution)/shard_map/attend_next/pallas_call | solution.py:134
  40.0 2.0 %collective-permute-start.2 = (bf16[128,4096]{1,0:T(8,128)(2,1)}, bf16[128,4096]{1,0:T(8,128)(2,1)S(1)}, u32[]{:S(2)}, u32[]{:S(2)}) collective-permute-start(bf16[128,4096]{1,0:T(8,128)(2,1)} %get-tuple-element.37), channel_id=1, source_target_pairs={{0,2},{2,4},{4,6},{6,8},{8,10},{10,12},{12,14},{14,16},{16,18},{18... | collective-permute-start | bytes 3145736 | tf_op jit(solution)/shard_map/ppermute | solution.py:27
  42.1 1.7 %edge_rows.3 = bf16[24,4096]{1,0:T(8,128)(2,1)} custom-call(bf16[128,4096]{1,0:T(8,128)(2,1)} %og_ref.5, bf16[128,4096]{1,0:T(8,128)(2,1)} %k_ref.9, bf16[128,4096]{1,0:T(8,128)(2,1)} %v_ref.9), custom_call_target="tpu_custom_call" | custom-call | tf_op jit(solution)/shard_map/edge_rows/pallas_call | solution.py:177
  43.8 4.4 %collective-permute-start.4 = (bf16[24,4096]{1,0:T(8,128)(2,1)}, bf16[24,4096]{1,0:T(8,128)(2,1)S(1)}, u32[]{:S(2)}, u32[]{:S(2)}) collective-permute-start(bf16[24,4096]{1,0:T(8,128)(2,1)} %edge_rows.3), channel_id=1, source_target_pairs={{2,0},{4,2},{6,4},{8,6},{10,8},{12,10},{14,12},{16,14},{18,16},{20... | collective-permute-start | bytes 589832 | tf_op jit(solution)/shard_map/ppermute | solution.py:27
  48.2 1.9 %collective-permute-start.3 = (f32[128,128]{1,0:T(8,128)}, f32[128,128]{1,0:T(8,128)S(1)}, u32[]{:S(2)}, u32[]{:S(2)}) collective-permute-start(f32[128,128]{1,0:T(8,128)} %get-tuple-element.38), channel_id=1, source_target_pairs={{0,2},{2,4},{4,6},{6,8},{8,10},{10,12},{12,14},{14,16},{16,18},{18... | collective-permute-start | bytes 196616 | tf_op jit(solution)/shard_map/ppermute | solution.py:27
  50.1 33.2 %all-to-all-done.in_ref = bf16[16,544,128]{2,1,0:T(8,128)(2,1)S(1)} async-done(((bf16[16,544,128]{2,1,0:T(8,128)(2,1)}), bf16[16,544,128]{2,1,0:T(8,128)(2,1)S(1)}, u32[]{:S(2)}, u32[]{:S(2)}) %all-to-all-start) | async-done | bytes 2228256 | tf_op jit(solution)/shard_map/all_to_all | solution.py:625
  83.3 5.1 %long_convs.2 = bf16[16,272,128]{2,1,0:T(8,128)(2,1)} custom-call(bf16[16,544,128]{2,1,0:T(8,128)(2,1)S(1)} %all-to-all-done.in_ref), custom_call_target="tpu_custom_call" | custom-call | flops 2147483648 | bytes 2228224 | tf_op jit(solution)/shard_map/long_convs/pallas_call | solution.py:364
  88.4 6.4 %collective-permute-done.3.log_ref = f32[128,128]{1,0:T(8,128)S(1)} collective-permute-done((f32[128,128]{1,0:T(8,128)}, f32[128,128]{1,0:T(8,128)S(1)}, u32[]{:S(2)}, u32[]{:S(2)}) %collective-permute-start.3) | collective-permute-done | bytes 65568 | tf_op jit(solution)/shard_map/ppermute | solution.py:27
  94.8 0.9 copy-done.7
  95.7 0.1 copy-done.5
  95.8 4.2 %all-to-all-start.2 = ((bf16[16,272,128]{2,1,0:T(8,128)(2,1)}), bf16[16,272,128]{2,1,0:T(8,128)(2,1)S(1)}, u32[]{:S(2)}, u32[]{:S(2)}) async-start(bf16[16,272,128]{2,1,0:T(8,128)(2,1)} %long_convs.2), calls=%async_computation.2 | async-start | bytes 2228224 | tf_op jit(solution)/shard_map/all_to_all | solution.py:641
  100.0 8.1 %filter_products.1 = (bf16[16,16,128]{2,1,0:T(8,128)(2,1)S(1)}, f32[1,1]{1,0:T(1,128)}) custom-call(bf16[16,544,128]{2,1,0:T(8,128)(2,1)S(1)} %all-to-all-done.in_ref), custom_call_target="tpu_custom_call" | custom-call | flops 2147483648 | bytes 2228224 | tf_op jit(solution)/shard_map/filter_products/pallas_call | solution.py:444
  108.1 1.5 collective-permute-start.5
  109.6 2.1 %collective-permute-done.5 = f32[1,1]{1,0:T(1,128)} collective-permute-done((f32[1,1]{1,0:T(1,128)}, f32[1,1]{1,0:T(1,128)}, u32[]{:S(2)}, u32[]{:S(2)}) %collective-permute-start.5) | collective-permute-done | bytes 36 | tf_op jit(solution)/shard_map/ppermute | solution.py:34
  113.0 5.2 %long_convs.3 = bf16[16,288,128]{2,1,0:T(8,128)(2,1)} custom-call(bf16[16,544,128]{2,1,0:T(8,128)(2,1)S(1)} %all-to-all-done.in_ref, bf16[16,16,128]{2,1,0:T(8,128)(2,1)S(1)} %get-tuple-element.43.refs_0_, f32[1,1]{1,0:T(1,128)S(6)} %add.3.refs_1_), custom_call_target="tpu_custom_call" | custom-call | flops 2147483648 | bytes 2359296 | tf_op jit(solution)/shard_map/long_convs/pallas_call | solution.py:364
  118.2 8.3 %all-to-all-done.2.in_ref = bf16[16,272,128]{2,1,0:T(8,128)(2,1)S(1)} async-done(((bf16[16,272,128]{2,1,0:T(8,128)(2,1)}), bf16[16,272,128]{2,1,0:T(8,128)(2,1)S(1)}, u32[]{:S(2)}, u32[]{:S(2)}) %all-to-all-start.2) | async-done | bytes 1114144 | tf_op jit(solution)/shard_map/all_to_all | solution.py:641
  126.6 1.0 copy-done.1
  127.5 4.6 %all-to-all-start.1 = ((bf16[16,288,128]{2,1,0:T(8,128)(2,1)}), bf16[16,288,128]{2,1,0:T(8,128)(2,1)S(1)}, u32[]{:S(2)}, u32[]{:S(2)}) async-start(bf16[16,288,128]{2,1,0:T(8,128)(2,1)} %long_convs.3), calls=%async_computation.1 | async-start | bytes 2359296 | tf_op jit(solution)/shard_map/all_to_all | solution.py:641
  132.2 8.0 %attend_own.1 = bf16[128,4096]{1,0:T(8,128)(2,1)} custom-call(s32[1]{0:T(128)} %bitcast.place_ref, bf16[128,4096]{1,0:T(8,128)(2,1)} %q_ref.3, bf16[128,4096]{1,0:T(8,128)(2,1)} %k_ref.7, bf16[128,4096]{1,0:T(8,128)(2,1)} %v_ref.7, bf16[128,4096]{1,0:T(8,128)(2,1)} %copy-done.5, f32[128,128]{1,0:T(8,128)} %copy-done.7), custom_call_target="tpu_custom_call" | custom-call | flops 268435456 | bytes 5242880 | tf_op jit(solution)/shard_map/attend_own/pallas_call | solution.py:153
  140.2 6.3 %after_exchange.2 = (bf16[128,4096]{1,0:T(8,128)(2,1)}, bf16[128,4096]{1,0:T(8,128)(2,1)}, bf16[128,4096]{1,0:T(8,128)(2,1)}) custom-call(bf16[16,272,128]{2,1,0:T(8,128)(2,1)} %copy-done.1, bf16[128,4096]{1,0:T(8,128)(2,1)} %og_ref.5, bf16[128,4096]{1,0:T(8,128)(2,1)} %k_ref.9, bf16[128,4096]{1,0:T(8,128)(2,1)} %v_ref.9, bf16[24,4096]{1,0:T(8,128)(2,1)} %copy-done.2, ...), custom_call_target="tpu_custom_call" | custom-call | flops 23592960 | bytes 4718592 | tf_op jit(solution)/shard_map/after_exchange/pallas_call | solution.py:571
  146.5 13.7 %all-to-all-done.1.in_ref = bf16[16,288,128]{2,1,0:T(8,128)(2,1)S(1)} async-done(((bf16[16,288,128]{2,1,0:T(8,128)(2,1)}), bf16[16,288,128]{2,1,0:T(8,128)(2,1)S(1)}, u32[]{:S(2)}, u32[]{:S(2)}) %all-to-all-start.1) | async-done | bytes 1179680 | tf_op jit(solution)/shard_map/all_to_all | solution.py:641
  160.2 1.0 copy-done
  161.2 6.6 %after_exchange.3 = (bf16[128,4096]{1,0:T(8,128)(2,1)}, bf16[128,4096]{1,0:T(8,128)(2,1)}, bf16[128,4096]{1,0:T(8,128)(2,1)}, f32[128,256]{1,0:T(8,128)}) custom-call(bf16[16,288,128]{2,1,0:T(8,128)(2,1)} %copy-done, bf16[128,4096]{1,0:T(8,128)(2,1)} %og_ref.5, bf16[128,4096]{1,0:T(8,128)(2,1)} %k_ref.9, ...), custom_call_target="tpu_custom_call", output_to_operand_aliasing={{0}: (7, {}), {1}: (8, {}), {2}: (9, {})} | custom-call | flops 23592960 | bytes 4718592 | tf_op jit(solution)/shard_map/after_exchange/pallas_call | solution.py:571
  (12 shorter events, 0.0 us)
Async XLA Ops:
  0.6 9.9 %copy-start.4 = (bf16[128,4096]{1,0:T(8,128)(2,1)S(1)}, bf16[128,4096]{1,0:T(8,128)(2,1)}, u32[]{:S(2)}) copy-start(bf16[128,4096]{1,0:T(8,128)(2,1)} %q_ref.3) | copy-start | bytes 3145732
  2.5 8.1 %collective-permute-start = (bf16[24,4096]{1,0:T(8,128)(2,1)}, bf16[24,4096]{1,0:T(8,128)(2,1)S(1)}, u32[]{:S(2)}, u32[]{:S(2)}) collective-permute-start(bf16[24,4096]{1,0:T(8,128)(2,1)} %edge_rows.2), channel_id=1, source_target_pairs={{0,2},{2,4},{4,6},{6,8},{8,10},{10,12},{12,14},{14,16},{16,18},{18... | collective-permute-start | bytes 589832 | tf_op jit(solution)/shard_map/ppermute | solution.py:27
  10.5 1.9 %copy-start.2 = (bf16[24,4096]{1,0:T(8,128)(2,1)}, bf16[24,4096]{1,0:T(8,128)(2,1)S(1)}, u32[]{:S(2)}) copy-start(bf16[24,4096]{1,0:T(8,128)(2,1)S(1)} %collective-permute-done.tail_ref) | copy-start | bytes 589828
  10.5 14.2 %collective-permute-start.1 = (bf16[128,4096]{1,0:T(8,128)(2,1)S(1)}, bf16[128,4096]{1,0:T(8,128)(2,1)S(1)}, u32[]{:S(2)}, u32[]{:S(2)}) collective-permute-start(bf16[128,4096]{1,0:T(8,128)(2,1)S(1)} %copy-done.4), channel_id=1, source_target_pairs={{2,0},{4,2},{6,4},{8,6},{10,8},{12,10},{14,12},{16,14},{18,16},{20... | collective-permute-start | bytes 3145736 | tf_op jit(solution)/shard_map/ppermute | solution.py:27
  24.8 1.0 copy-start.3
  25.7 57.5 %all-to-all-start = ((bf16[16,544,128]{2,1,0:T(8,128)(2,1)}), bf16[16,544,128]{2,1,0:T(8,128)(2,1)S(1)}, u32[]{:S(2)}, u32[]{:S(2)}) async-start(bf16[16,544,128]{2,1,0:T(8,128)(2,1)} %before_exchange.1), calls=%async_computation | async-start | bytes 4456448 | tf_op jit(solution)/shard_map/all_to_all | solution.py:625
  40.0 54.7 %collective-permute-start.2 = (bf16[128,4096]{1,0:T(8,128)(2,1)}, bf16[128,4096]{1,0:T(8,128)(2,1)S(1)}, u32[]{:S(2)}, u32[]{:S(2)}) collective-permute-start(bf16[128,4096]{1,0:T(8,128)(2,1)} %get-tuple-element.37), channel_id=1, source_target_pairs={{0,2},{2,4},{4,6},{6,8},{8,10},{10,12},{12,14},{14,16},{16,18},{18... | collective-permute-start | bytes 3145736 | tf_op jit(solution)/shard_map/ppermute | solution.py:27
  43.8 51.0 %collective-permute-start.4 = (bf16[24,4096]{1,0:T(8,128)(2,1)}, bf16[24,4096]{1,0:T(8,128)(2,1)S(1)}, u32[]{:S(2)}, u32[]{:S(2)}) collective-permute-start(bf16[24,4096]{1,0:T(8,128)(2,1)} %edge_rows.3), channel_id=1, source_target_pairs={{2,0},{4,2},{6,4},{8,6},{10,8},{12,10},{14,12},{16,14},{18,16},{20... | collective-permute-start | bytes 589832 | tf_op jit(solution)/shard_map/ppermute | solution.py:27
  48.2 46.6 %collective-permute-start.3 = (f32[128,128]{1,0:T(8,128)}, f32[128,128]{1,0:T(8,128)S(1)}, u32[]{:S(2)}, u32[]{:S(2)}) collective-permute-start(f32[128,128]{1,0:T(8,128)} %get-tuple-element.38), channel_id=1, source_target_pairs={{0,2},{2,4},{4,6},{6,8},{8,10},{10,12},{12,14},{14,16},{16,18},{18... | collective-permute-start | bytes 196616 | tf_op jit(solution)/shard_map/ppermute | solution.py:27
  94.7 1.0 copy-start.7
  94.7 13.4 %copy-start.6 = (bf16[24,4096]{1,0:T(8,128)(2,1)}, bf16[24,4096]{1,0:T(8,128)(2,1)S(1)}, u32[]{:S(2)}) copy-start(bf16[24,4096]{1,0:T(8,128)(2,1)S(1)} %collective-permute-done.4.next_ref) | copy-start | bytes 589828
  94.8 1.0 copy-start.5
  95.8 30.8 %all-to-all-start.2 = ((bf16[16,272,128]{2,1,0:T(8,128)(2,1)}), bf16[16,272,128]{2,1,0:T(8,128)(2,1)S(1)}, u32[]{:S(2)}, u32[]{:S(2)}) async-start(bf16[16,272,128]{2,1,0:T(8,128)(2,1)} %long_convs.2), calls=%async_computation.2 | async-start | bytes 2228224 | tf_op jit(solution)/shard_map/all_to_all | solution.py:641
  108.1 3.6 %collective-permute-start.5 = (f32[1,1]{1,0:T(1,128)}, f32[1,1]{1,0:T(1,128)}, u32[]{:S(2)}, u32[]{:S(2)}) collective-permute-start(f32[1,1]{1,0:T(1,128)} %get-tuple-element.44), channel_id=1, source_target_pairs={{0,1},{1,0},{2,3},{3,2},{4,5},{5,4},{6,7},{7,6},{8,9},{9,8},{10,11... | collective-permute-start | bytes 20 | tf_op jit(solution)/shard_map/ppermute | solution.py:34
  126.6 1.0 copy-start.1
  127.5 32.6 %all-to-all-start.1 = ((bf16[16,288,128]{2,1,0:T(8,128)(2,1)}), bf16[16,288,128]{2,1,0:T(8,128)(2,1)S(1)}, u32[]{:S(2)}, u32[]{:S(2)}) async-start(bf16[16,288,128]{2,1,0:T(8,128)(2,1)} %long_convs.3), calls=%async_computation.1 | async-start | bytes 2359296 | tf_op jit(solution)/shard_map/all_to_all | solution.py:641
  160.2 1.0 copy-start

commit v9 on v8

--- a/solution.py
+++ b/solution.py
@@ -50,118 +50,57 @@
 NT = (((1,), (1,)), ((), ()))
 
 
-def attend_next_kernel(q_ref, k_ref, v_ref, out_ref, log_ref):
+def attend_kernel(place_ref, q_ref, k_ref, v_ref, kp_ref, vp_ref, out_ref):
     rows = q_ref.shape[0]
     heads = q_ref.shape[1] // HEAD_DIM
-    step = pl.program_id(0)
-    lane = lax.broadcasted_iota(jnp.int32, (rows, log_ref.shape[1]), 1)
-
-    @pl.when(step == 0)
-    def _():
-        log_ref[...] = jnp.zeros_like(log_ref)
-
-    places = [slice(head * HEAD_DIM, (head + 1) * HEAD_DIM) for head in range(heads)]
-    scores = [
-        lax.dot_general(q_ref[:, at], k_ref[:, at], NT, preferred_element_type=F32) * SCALE
-        for at in places
-    ]
-    largest = [jnp.max(score, axis=1, keepdims=True) for score in scores]
-    raised = [jnp.exp(score - top) for score, top in zip(scores, largest)]
-    totals = [jnp.sum(r, axis=1, keepdims=True) for r in raised]
-    weights = [(r * (1.0 / total)).astype(BF16) for r, total in zip(raised, totals)]
-    mixed = [
-        jnp.dot(weight, v_ref[:, at], preferred_element_type=F32) for weight, at in zip(weights, places)
-    ]
-    logs = log_ref[...]
-    for head, at in enumerate(places):
-        out_ref[:, at] = mixed[head].astype(BF16)
-        log = largest[head] + jnp.log(totals[head])
-        logs = jnp.where(lane == step * heads + head, log, logs)
-    log_ref[...] = logs
-
-
-def attend_own_kernel(place_ref, q_ref, k_ref, v_ref, prev_ref, log_ref, out_ref):
-    rows = q_ref.shape[0]
-    heads = q_ref.shape[1] // HEAD_DIM
-    step = pl.program_id(0)
     row = lax.broadcasted_iota(jnp.int32, (rows, rows), 0)
     col = lax.broadcasted_iota(jnp.int32, (rows, rows), 1)
     own_ok = col <= row
-    lane = lax.broadcasted_iota(jnp.int32, (rows, log_ref.shape[1]), 1)
-    has_prev = jnp.broadcast_to(place_ref[0], (rows, 1)) > 0
+    prev_ok = jnp.broadcast_to(place_ref[0], (rows, rows)) > 0
     places = [slice(head * HEAD_DIM, (head + 1) * HEAD_DIM) for head in range(heads)]
-    scores = [
-        lax.dot_general(q_ref[:, at], k_ref[:, at], NT, preferred_element_type=F32) * SCALE
-        for at in places
-    ]
-    scores = [jnp.where(own_ok, score, -jnp.inf) for score in scores]
-    logs = [
-        jnp.sum(jnp.where(lane == step * heads + head, log_ref[...], 0.0), axis=1, keepdims=True)
-        for head in range(heads)
-    ]
-    logs = [jnp.where(has_prev, log, -jnp.inf) for log in logs]
-    largest = [
-        jnp.maximum(jnp.max(score, axis=1, keepdims=True), log) for score, log in zip(scores, logs)
-    ]
-    raised = [jnp.exp(score - top) for score, top in zip(scores, largest)]
-    prevs = [jnp.exp(log - top) for log, top in zip(logs, largest)]
-    inverses = [
-        1.0 / (jnp.sum(r, axis=1, keepdims=True) + prev) for r, prev in zip(raised, prevs)
-    ]
-    weights = [(r * inverse).astype(BF16) for r, inverse in zip(raised, inverses)]
+
+    def scores(ref, allowed):
+        products = [
+            lax.dot_general(q_ref[:, at], ref[:, at], NT, preferred_element_type=F32) for at in places
+        ]
+        return [jnp.where(allowed, product * SCALE, -jnp.inf) for product in products]
+
+    own, prev = scores(k_ref, own_ok), scores(kp_ref, prev_ok)
+    largest = [jnp.max(jnp.maximum(o, p), axis=1, keepdims=True) for o, p in zip(own, prev)]
+    own = [jnp.exp(o - top) for o, top in zip(own, largest)]
+    prev = [jnp.exp(p - top) for p, top in zip(prev, largest)]
+    totals = [jnp.sum(o + p, axis=1, keepdims=True) for o, p in zip(own, prev)]
+    inverses = [1.0 / total for total in totals]
+    own = [(o * inverse).astype(BF16) for o, inverse in zip(own, inverses)]
+    prev = [(p * inverse).astype(BF16) for p, inverse in zip(prev, inverses)]
     mixed = [
-        jnp.dot(weight, v_ref[:, at], preferred_element_type=F32) for weight, at in zip(weights, places)
+        jnp.dot(o, v_ref[:, at], preferred_element_type=F32)
+        + jnp.dot(p, vp_ref[:, at], preferred_element_type=F32)
+        for o, p, at in zip(own, prev, places)
     ]
     for head, at in enumerate(places):
-        total = mixed[head] + (prevs[head] * inverses[head]) * prev_ref[:, at].astype(F32)
-        out_ref[:, at] = total.astype(BF16)
-
-
-def attend_cost(rows, channels):
-    heads = channels // HEAD_DIM
-    return pl.CostEstimate(
-        flops=4 * heads * rows * rows * HEAD_DIM,
-        bytes_accessed=10 * rows * channels,
-        transcendentals=heads * rows * rows,
-    )
-
-
-def attend_next(query, key, value):
+        out_ref[:, at] = mixed[head].astype(BF16)
+
+
+def attend(query, key, value, key_prev, value_prev, position):
     rows, channels = query.shape
     tile = min(512, channels)
-    block = pl.BlockSpec((rows, tile), lambda i: (0, i))
-    lanes = round_up(channels // HEAD_DIM, LANES)
-    return pl.pallas_call(
-        attend_next_kernel,
-        grid=(channels // tile,),
-        in_specs=[block] * 3,
-        out_specs=[block, pl.BlockSpec((rows, lanes), lambda i: (0, 0))],
-        out_shape=[
-            jax.ShapeDtypeStruct((rows, channels), BF16),
-            jax.ShapeDtypeStruct((rows, lanes), F32),
-        ],
-        compiler_params=params(),
-        cost_estimate=attend_cost(rows, channels),
-        name="attend_next",
-    )(query, key, value)
-
-
-def attend_own(query, key, value, prev, log, position):
-    rows, channels = query.shape
-    tile = min(512, channels)
+    heads = channels // HEAD_DIM
     block = pl.BlockSpec((rows, tile), lambda i: (0, i))
     return pl.pallas_call(
-        attend_own_kernel,
+        attend_kernel,
         grid=(channels // tile,),
-        in_specs=[pl.BlockSpec(memory_space=pltpu.SMEM)]
-        + [block] * 4
-        + [pl.BlockSpec(log.shape, lambda i: (0, 0))],
+        in_specs=[pl.BlockSpec(memory_space=pltpu.SMEM)] + [block] * 5,
         out_specs=block,
         out_shape=jax.ShapeDtypeStruct((rows, channels), BF16),
-        compiler_params=params(),
-        cost_estimate=attend_cost(rows, channels),
-        name="attend_own",
-    )(position.astype(jnp.int32).reshape(1), query, key, value, prev, log)
+        compiler_params=params(LONG_VMEM),
+        cost_estimate=pl.CostEstimate(
+            flops=8 * heads * rows * rows * HEAD_DIM,
+            bytes_accessed=12 * rows * channels,
+            transcendentals=2 * heads * rows * rows,
+        ),
+        name="attend",
+    )(position.astype(jnp.int32).reshape(1), query, key, value, key_prev, value_prev)
 
 
 def edge_kernel(first, *refs):
@@ -185,14 +124,20 @@
     )(*arrays)
 
 
-def taps_causal(ext_ref, before, signal, filter_taps):
-    rows = signal.shape[0]
-    ext_ref[0:EDGE, :] = before
-    ext_ref[EDGE : EDGE + rows, :] = signal
-    total = filter_taps[0:1] * signal
-    for s in range(1, filter_taps.shape[0]):
-        total = total + filter_taps[s : s + 1] * ext_ref[EDGE - s : EDGE - s + rows, :]
-    return total
+def taps_causal(ext_ref, befores, signals, filters):
+    rows = signals[0].shape[0]
+    for j, signal in enumerate(signals):
+        ext_ref[j, 0:EDGE, :] = befores[j]
+        ext_ref[j, EDGE : EDGE + rows, :] = signal
+    totals = [taps[0:1] * signal for signal, taps in zip(signals, filters)]
+    for s in range(1, filters[0].shape[0]):
+        for j, taps in enumerate(filters):
+            totals[j] = totals[j] + taps[s : s + 1] * ext_ref[j, EDGE - s : EDGE - s + rows, :]
+    return totals
+
+
+def columns_of(width):
+    return [slice(j * LANES, (j + 1) * LANES) for j in range(width // LANES)]
 
 
 def before_kernel(
@@ -209,26 +154,30 @@
         long_rows[0:groups, :] = long_ref[...].T
 
     turn = reversal(rows)
-    for j in range(q_ref.shape[1] // LANES):
-        at = slice(j * LANES, (j + 1) * LANES)
-        tail = tail_ref[:, at].astype(F32)
-        short_q = taps_causal(ext_q.at[j], tail[0:EDGE], q_ref[:, at].astype(F32), taps_ref[0, :, at])
-        short_k = taps_causal(
-            ext_k.at[j], tail[EDGE : 2 * EDGE], k_ref[:, at].astype(F32), taps_ref[1, :, at]
+    places = columns_of(q_ref.shape[1])
+    tails = [tail_ref[:, at].astype(F32) for at in places]
+
+    def short(which, ref, ext):
+        return taps_causal(
+            ext,
+            [tail[which * EDGE : (which + 1) * EDGE] for tail in tails],
+            [ref[:, at].astype(F32) for at in places],
+            [taps_ref[which, :, at] for at in places],
         )
-        short_v = taps_causal(
-            ext_v.at[j], tail[2 * EDGE : 3 * EDGE], v_ref[:, at].astype(F32), taps_ref[2, :, at]
-        )
-        mixed = (short_k * short_v).T.astype(BF16)
-        delta = (og_ref[:, at].astype(F32) * short_q).T.astype(BF16)
-        delta = jnp.dot(delta, turn, preferred_element_type=F32).astype(BF16)
-        width = min(cpd, LANES)
+
+    short_k, short_v = short(1, k_ref, ext_k), short(2, v_ref, ext_v)
+    mixed = [(k * v).T.astype(BF16) for k, v in zip(short_k, short_v)]
+    short_q = short(0, q_ref, ext_q)
+    delta = [(og_ref[:, at].astype(F32) * q).T.astype(BF16) for q, at in zip(short_q, places)]
+    delta = [jnp.dot(d, turn, preferred_element_type=F32).astype(BF16) for d in delta]
+    width = min(cpd, LANES)
+    for j in range(len(places)):
         for piece in range(LANES // width):
             channel = j * LANES + piece * width
             dest, low = channel // cpd, channel % cpd
             rows_at = slice(piece * width, (piece + 1) * width)
-            send_ref[dest, low : low + width, :] = mixed[rows_at]
-            send_ref[dest, cpd + low : cpd + low + width, :] = delta[rows_at]
+            send_ref[dest, low : low + width, :] = mixed[j][rows_at]
+            send_ref[dest, cpd + low : cpd + low + width, :] = delta[j][rows_at]
     filter_rows = send_ref.shape[1] - 2 * cpd
     for dest in range(per_tile):
         first = (step * per_tile + dest) * gpd
@@ -463,14 +412,16 @@
     )(received)
 
 
-def taps_anti(ext_ref, signal, after, filter_taps):
-    rows = signal.shape[0]
-    ext_ref[0:rows, :] = signal
-    ext_ref[rows : rows + EDGE, :] = after
-    total = filter_taps[0:1] * signal
-    for s in range(1, filter_taps.shape[0]):
-        total = total + filter_taps[s : s + 1] * ext_ref[s : s + rows, :]
-    return total
+def taps_anti(ext_ref, signals, afters, filters):
+    rows = signals[0].shape[0]
+    for j, signal in enumerate(signals):
+        ext_ref[j, 0:rows, :] = signal
+        ext_ref[j, rows : rows + EDGE, :] = afters[j]
+    totals = [taps[0:1] * signal for signal, taps in zip(signals, filters)]
+    for s in range(1, filters[0].shape[0]):
+        for j, taps in enumerate(filters):
+            totals[j] = totals[j] + taps[s : s + 1] * ext_ref[j, s : s + rows, :]
+    return totals
 
 
 def short_edge(before, signal, filter_taps):
@@ -493,8 +444,11 @@
     halo_rows = 2 * EDGE * max(1, cpd // LANES)
     halo_at = 2 * cpd
     turn = reversal(rows)
-    for j in range(og_ref.shape[1] // LANES):
-        at = slice(j * LANES, (j + 1) * LANES)
+    places = columns_of(og_ref.shape[1])
+    tails = [tail_ref[:, at].astype(F32) for at in places]
+    nexts = [next_ref[:, at].astype(F32) for at in places]
+    convs, backs, halos = [], [], []
+    for j in range(len(places)):
         if cpd >= LANES:
             dest, low = j * LANES // cpd, j * LANES % cpd
             conv = in_ref[dest, low : low + LANES, :]
@@ -508,28 +462,50 @@
             halo = jnp.concatenate(
                 [in_ref[d, halo_at : halo_at + halo_rows, :].astype(F32)[:, :cpd] for d in dests], 1
             )
-        conv = conv.astype(F32).T
-        back = jnp.dot(back, turn, preferred_element_type=F32).T
-        following = next_ref[:, at].astype(F32)
-        taps_k = taps_ref[1, :, at]
-        taps_v = taps_ref[2, :, at]
-        tail = tail_ref[:, at].astype(F32)
-        key = k_ref[:, at].astype(F32)
-        value = v_ref[:, at].astype(F32)
-        short_k = taps_causal(ext_in_k.at[j], tail[EDGE : 2 * EDGE], key, taps_k)
-        short_v = taps_causal(ext_in_v.at[j], tail[2 * EDGE : 3 * EDGE], value, taps_v)
-        next_k = short_edge(key[rows - EDGE :], following[EDGE : 2 * EDGE], taps_k)
-        next_v = short_edge(value[rows - EDGE :], following[2 * EDGE : 3 * EDGE], taps_v)
-        grad_q = og_ref[:, at].astype(F32) * conv
-        dq_ref[:, at] = taps_anti(
-            ext_q.at[j], grad_q, following[0:EDGE] * halo[0:EDGE], taps_ref[0, :, at]
-        ).astype(BF16)
-        dk_ref[:, at] = taps_anti(
-            ext_k.at[j], back * short_v, halo[EDGE:] * next_v, taps_k
-        ).astype(BF16)
-        dv_ref[:, at] = taps_anti(
-            ext_v.at[j], back * short_k, halo[EDGE:] * next_k, taps_v
-        ).astype(BF16)
+        convs.append(conv)
+        backs.append(back)
+        halos.append(halo)
+    convs = [conv.astype(F32).T for conv in convs]
+    backs = [jnp.dot(back, turn, preferred_element_type=F32) for back in backs]
+    backs = [back.T for back in backs]
+    taps = [[taps_ref[which, :, at] for at in places] for which in range(3)]
+    keys = [k_ref[:, at].astype(F32) for at in places]
+    values = [v_ref[:, at].astype(F32) for at in places]
+    short_k = taps_causal(ext_in_k, [tail[EDGE : 2 * EDGE] for tail in tails], keys, taps[1])
+    short_v = taps_causal(ext_in_v, [tail[2 * EDGE : 3 * EDGE] for tail in tails], values, taps[2])
+    next_k = [
+        short_edge(k[rows - EDGE :], f[EDGE : 2 * EDGE], t) for k, f, t in zip(keys, nexts, taps[1])
+    ]
+    next_v = [
+        short_edge(v[rows - EDGE :], f[2 * EDGE : 3 * EDGE], t)
+        for v, f, t in zip(values, nexts, taps[2])
+    ]
+
+    def store(ref, ext, signals, afters, filters):
+        for at, total in zip(places, taps_anti(ext, signals, afters, filters)):
+            ref[:, at] = total.astype(BF16)
+
+    store(
+        dq_ref,
+        ext_q,
+        [og_ref[:, at].astype(F32) * conv for at, conv in zip(places, convs)],
+        [f[0:EDGE] * halo[0:EDGE] for f, halo in zip(nexts, halos)],
+        taps[0],
+    )
+    store(
+        dk_ref,
+        ext_k,
+        [back * v for back, v in zip(backs, short_v)],
+        [halo[EDGE:] * v for halo, v in zip(halos, next_v)],
+        taps[1],
+    )
+    store(
+        dv_ref,
+        ext_v,
+        [back * k for back, k in zip(backs, short_k)],
+        [halo[EDGE:] * k for halo, k in zip(halos, next_k)],
+        taps[2],
+    )
     if not last:
         return
     squares = jnp.zeros((1, LANES), F32)
@@ -586,7 +562,7 @@
         out_shape=[grad] * 3 + [jax.ShapeDtypeStruct((rows, groups), F32)] * last,
         scratch_shapes=[pltpu.VMEM((groups, rows), F32), pltpu.VMEM((1, LANES), F32)] * last
         + [ext] * 5,
-        compiler_params=params(),
+        compiler_params=params(LONG_VMEM),
         cost_estimate=pl.CostEstimate(
             flops=90 * rows * channels, bytes_accessed=18 * rows * channels, transcendentals=0
         ),
@@ -612,34 +588,28 @@
     cpd, gpd = channels // n, groups // n
     position = lax.axis_index("ctx")
     tail = shifted(edge_rows((hyena_query, hyena_key, hyena_value), False), "ctx", 1)
-    queries, tail = lax.optimization_barrier((query_heads, tail))
-    query_next = shifted(queries, "ctx", -1)
+    key_prev = shifted(key_heads, "ctx", 1)
+    value_prev = shifted(value_heads, "ctx", 1)
     chunks = 2 if gpd % 4 == 0 else 1
     cpd, gpd = cpd // chunks, gpd // chunks
     send = before_exchange(
         hyena_query, hyena_key, hyena_value, output_grad, tail, short_filter, long_filter, n, chunks
     )
-    send, query_next, *sources = lax.optimization_barrier(
-        (send, query_next, output_grad, hyena_key, hyena_value)
-    )
+    send, *sources = lax.optimization_barrier((send, output_grad, hyena_key, hyena_value))
     received = lax.all_to_all(send, "ctx", split_axis=0, concat_axis=0, tiled=True)
     following = shifted(edge_rows(sources, True), "ctx", -1)
-    part, log = attend_next(query_next, key_heads, value_heads)
-    part = shifted(part, "ctx", 1)
-    log = shifted(log, "ctx", 1)
     returned = []
     for chunk in range(chunks):
         raw = ()
         if chunk + 1 == chunks:
             raw, squares = filter_products(received, cpd, gpd, chunks)
+            raw, key_prev, value_prev = lax.optimization_barrier((raw, key_prev, value_prev))
             raw = (raw, total_over(squares, "tp"))
         results = long_convs(received, raw, cpd, gpd, chunk, chunks)
         if chunk == 0:
-            results, received, part, log, following = lax.optimization_barrier(
-                (results, received, part, log, following)
-            )
+            results, received, following = lax.optimization_barrier((results, received, following))
         returned.append(lax.all_to_all(results, "ctx", split_axis=0, concat_axis=0, tiled=True))
-    attention = attend_own(query_heads, key_heads, value_heads, part, log, position)
+    attention = attend(query_heads, key_heads, value_heads, key_prev, value_prev, position)
     bound = math.sqrt(rows * n * groups * tp)
     grads = ()
     for chunk in range(chunks):

time: 169 us -> 189 us (1.12)
  waiting for transfers between devices: 73.3 us -> 99.1 us
  Pallas kernels: 59.4 us -> 46.2 us
  local copies, waits for them, and re-layouts: 4 us -> 14.3 us
  starting transfers between devices: 29.1 us -> 26.2 us
    ppermute x5 -> x4, waiting for transfers between devices: 16 us -> 40.8 us  [shifted(): return lax.ppermute(block, axis, route)]
    all_to_all x1, waiting for transfers between devices: 33.2 us -> 45.6 us  [on_device(): lax.all_to_all(send, 'ctx', split_axis=0, concat_axis=0, tiled=True)]
    all_to_all x2, waiting for transfers between devices: 22.1 us -> 10.5 us  [on_device(): lax.all_to_all(results, 'ctx', split_axis=0, concat_axis=0, tiled=True)]
    unnamed x16 -> x42, local copies, waits for them, and re-layouts: 4 us -> 14.3 us
    pallas_call x2 -> x1, Pallas kernels: 15.7 us -> 6.22 us  [attend(): pl.pallas_call(attend_kernel, grid=(channels // tile,), in_specs=[pl.Bloc...]
    pallas_call x2, Pallas kernels: 10.3 us -> 8.23 us  [long_convs(): pl.pallas_call(functools.partial(conv_kernel, cpd, gpd), grid=(1,), in_sp...]
    ppermute x5 -> x4, starting transfers between devices: 12.2 us -> 10.4 us  [shifted(): return lax.ppermute(block, axis, route)]
  transfers between devices with their start and end apart: 9 -> 8, of which waited for: 7 -> 6; matrix products, arithmetic and copies ran while one was open for 0% -> 0% of each run, Pallas kernels for 30% -> 16%
where the time goes in v9:
time: 189 us; the launch traced here: 188 us
  waiting for transfers between devices  99.1 us (52%)
  Pallas kernels  46.2 us (24%)
  starting transfers between devices  26.2 us (14%)
  local copies, waits for them, and re-layouts  14.3 us (8%)
  between operations  2.05 us (1%)
    all_to_all x1, waiting for transfers between devices, on_device(): lax.all_to_all(send, 'ctx', split_axis=0, concat_axis=0, tiled=True)  45.6 us
    ppermute x4, waiting for transfers between devices, shifted(): return lax.ppermute(block, axis, route)  40.8 us
    unnamed x42, local copies, waits for them, and re-layouts  14.3 us
    pallas_call x2, Pallas kernels, after_exchange(): pl.pallas_call(functools.partial(after_kernel, cpd, gpd, chunks, last, bo...  11.3 us
    all_to_all x2, waiting for transfers between devices, on_device(): lax.all_to_all(results, 'ctx', split_axis=0, concat_axis=0, tiled=True)  10.5 us
    ppermute x4, starting transfers between devices, shifted(): return lax.ppermute(block, axis, route)  10.4 us
    all_to_all x2, starting transfers between devices, on_device(): lax.all_to_all(results, 'ctx', split_axis=0, concat_axis=0, tiled=True)  8.98 us
    pallas_call x1, Pallas kernels, before_exchange(): pl.pallas_call(functools.partial(before_kernel, cpd, gpd), grid=(channels...  8.86 us
  transfers between devices with their start and end apart: 8, of which 6 were waited for; matrix products, arithmetic and copies ran while one was open for 0% of the time, Pallas kernels for 16%

profile of v9, /device:TPU:16, one launch (start us, length us, event | category | flops | bytes accessed | tf_op | source)
XLA Modules:
  0.0 187.8 jit_solution(4901981223447813374)
XLA Ops:
  0.6 1.7 edge_rows.2
  2.4 1.9 %collective-permute-start = (bf16[24,4096]{1,0:T(8,128)(2,1)}, bf16[24,4096]{1,0:T(8,128)(2,1)S(1)}, u32[]{:S(2)}, u32[]{:S(2)}) collective-permute-start(bf16[24,4096]{1,0:T(8,128)(2,1)} %edge_rows.2), channel_id=1, source_target_pairs={{0,2},{2,4},{4,6},{6,8},{8,10},{10,12},{12,14},{14,16},{16,18},{18... | collective-permute-start | bytes 589832 | tf_op jit(solution)/shard_map/ppermute | solution.py:27
  4.3 6.2 %collective-permute-done.tail_ref = bf16[24,4096]{1,0:T(8,128)(2,1)S(1)} collective-permute-done((bf16[24,4096]{1,0:T(8,128)(2,1)}, bf16[24,4096]{1,0:T(8,128)(2,1)S(1)}, u32[]{:S(2)}, u32[]{:S(2)}) %collective-permute-start) | collective-permute-done | bytes 196640 | tf_op jit(solution)/shard_map/ppermute | solution.py:27
  11.1 8.9 %before_exchange.1 = bf16[16,544,128]{2,1,0:T(8,128)(2,1)} custom-call(bf16[128,4096]{1,0:T(8,128)(2,1)} %q_ref.2, bf16[128,4096]{1,0:T(8,128)(2,1)} %k_ref.7, bf16[128,4096]{1,0:T(8,128)(2,1)} %v_ref.7, bf16[128,4096]{1,0:T(8,128)(2,1)} %og_ref.5, bf16[24,4096]{1,0:T(8,128)(2,1)} %copy-done.6, f32[3,7,4096]{2,1,0:T(8,128)} %taps_ref.5, f32[128,256]{1,0:T(8,128)} %long_ref.1), custom_call_target="tpu_custom_call" | custom-call | flops 26214400 | bytes 6291456 | tf_op jit(solution)/shard_map/before_exchange/pallas_call | solution.py:198
  20.0 5.3 %all-to-all-start = ((bf16[16,544,128]{2,1,0:T(8,128)(2,1)}), bf16[16,544,128]{2,1,0:T(8,128)(2,1)S(1)}, u32[]{:S(2)}, u32[]{:S(2)}) async-start(bf16[16,544,128]{2,1,0:T(8,128)(2,1)} %before_exchange.1), calls=%async_computation | async-start | bytes 4456448 | tf_op jit(solution)/shard_map/all_to_all | solution.py:599
  25.3 1.7 edge_rows.3
  27.0 3.1 %collective-permute-start.1 = (bf16[24,4096]{1,0:T(8,128)(2,1)}, bf16[24,4096]{1,0:T(8,128)(2,1)S(1)}, u32[]{:S(2)}, u32[]{:S(2)}) collective-permute-start(bf16[24,4096]{1,0:T(8,128)(2,1)} %edge_rows.3), channel_id=1, source_target_pairs={{2,0},{4,2},{6,4},{8,6},{10,8},{12,10},{14,12},{16,14},{18,16},{20... | collective-permute-start | bytes 589832 | tf_op jit(solution)/shard_map/ppermute | solution.py:27
  30.1 45.6 %all-to-all-done.in_ref = bf16[16,544,128]{2,1,0:T(8,128)(2,1)S(1)} async-done(((bf16[16,544,128]{2,1,0:T(8,128)(2,1)}), bf16[16,544,128]{2,1,0:T(8,128)(2,1)S(1)}, u32[]{:S(2)}, u32[]{:S(2)}) %all-to-all-start) | async-done | bytes 2228256 | tf_op jit(solution)/shard_map/all_to_all | solution.py:599
  75.7 4.1 %long_convs.2 = bf16[16,272,128]{2,1,0:T(8,128)(2,1)S(1)} custom-call(bf16[16,544,128]{2,1,0:T(8,128)(2,1)S(1)} %all-to-all-done.in_ref), custom_call_target="tpu_custom_call" | custom-call | flops 2147483648 | bytes 2228224 | tf_op jit(solution)/shard_map/long_convs/pallas_call | solution.py:313
  79.8 1.0 copy-done.10
  81.5 4.7 %all-to-all-start.2 = ((bf16[16,272,128]{2,1,0:T(8,128)(2,1)}), bf16[16,272,128]{2,1,0:T(8,128)(2,1)S(1)}, u32[]{:S(2)}, u32[]{:S(2)}) async-start(bf16[16,272,128]{2,1,0:T(8,128)(2,1)} %copy-done.10), calls=%async_computation.2 | async-start | bytes 2228224 | tf_op jit(solution)/shard_map/all_to_all | solution.py:611
  86.2 2.0 %collective-permute-start.2 = (bf16[128,4096]{1,0:T(8,128)(2,1)}, bf16[128,4096]{1,0:T(8,128)(2,1)S(1)}, u32[]{:S(2)}, u32[]{:S(2)}) collective-permute-start(bf16[128,4096]{1,0:T(8,128)(2,1)} %k_ref.5), channel_id=1, source_target_pairs={{0,2},{2,4},{4,6},{6,8},{8,10},{10,12},{12,14},{14,16},{16,18},{18... | collective-permute-start | bytes 3145736 | tf_op jit(solution)/shard_map/ppermute | solution.py:27
  88.3 3.3 %collective-permute-start.3 = (bf16[128,4096]{1,0:T(8,128)(2,1)}, bf16[128,4096]{1,0:T(8,128)(2,1)S(1)}, u32[]{:S(2)}, u32[]{:S(2)}) collective-permute-start(bf16[128,4096]{1,0:T(8,128)(2,1)} %v_ref.5), channel_id=1, source_target_pairs={{0,2},{2,4},{4,6},{6,8},{8,10},{10,12},{12,14},{14,16},{16,18},{18... | collective-permute-start | bytes 3145736 | tf_op jit(solution)/shard_map/ppermute | solution.py:27
  91.6 8.2 %filter_products.1 = (bf16[16,16,128]{2,1,0:T(8,128)(2,1)S(1)}, f32[1,1]{1,0:T(1,128)}) custom-call(bf16[16,544,128]{2,1,0:T(8,128)(2,1)S(1)} %all-to-all-done.in_ref), custom_call_target="tpu_custom_call" | custom-call | flops 2147483648 | bytes 2228224 | tf_op jit(solution)/shard_map/filter_products/pallas_call | solution.py:393
  99.8 24.3 %collective-permute-done.2.kp_ref = bf16[128,4096]{1,0:T(8,128)(2,1)S(1)} collective-permute-done((bf16[128,4096]{1,0:T(8,128)(2,1)}, bf16[128,4096]{1,0:T(8,128)(2,1)S(1)}, u32[]{:S(2)}, u32[]{:S(2)}) %collective-permute-start.2) | collective-permute-done | bytes 1048608 | tf_op jit(solution)/shard_map/ppermute | solution.py:27
  124.1 1.0 copy-done.14
  125.1 10.3 %collective-permute-done.3.vp_ref = bf16[128,4096]{1,0:T(8,128)(2,1)S(1)} collective-permute-done((bf16[128,4096]{1,0:T(8,128)(2,1)}, bf16[128,4096]{1,0:T(8,128)(2,1)S(1)}, u32[]{:S(2)}, u32[]{:S(2)}) %collective-permute-start.3) | collective-permute-done | bytes 1048608 | tf_op jit(solution)/shard_map/ppermute | solution.py:27
  136.3 1.5 collective-permute-start.4
  137.8 2.1 %collective-permute-done.4 = f32[1,1]{1,0:T(1,128)} collective-permute-done((f32[1,1]{1,0:T(1,128)}, f32[1,1]{1,0:T(1,128)}, u32[]{:S(2)}, u32[]{:S(2)}) %collective-permute-start.4) | collective-permute-done | bytes 36 | tf_op jit(solution)/shard_map/ppermute | solution.py:34
  141.2 4.1 %long_convs.3 = bf16[16,288,128]{2,1,0:T(8,128)(2,1)S(1)} custom-call(bf16[16,544,128]{2,1,0:T(8,128)(2,1)S(1)} %all-to-all-done.in_ref, bf16[16,16,128]{2,1,0:T(8,128)(2,1)S(1)} %get-tuple-element.35.refs_0_, f32[1,1]{1,0:T(1,128)S(6)} %add.3.refs_1_), custom_call_target="tpu_custom_call" | custom-call | flops 2147483648 | bytes 2359296 | tf_op jit(solution)/shard_map/long_convs/pallas_call | solution.py:313
  145.4 1.1 copy-done.9
  146.4 1.0 copy-done.3
  147.4 4.3 %all-to-all-start.1 = ((bf16[16,288,128]{2,1,0:T(8,128)(2,1)}), bf16[16,288,128]{2,1,0:T(8,128)(2,1)}, u32[]{:S(2)}, u32[]{:S(2)}) async-start(bf16[16,288,128]{2,1,0:T(8,128)(2,1)} %copy-done.9), calls=%async_computation.1 | async-start | bytes 2359296 | tf_op jit(solution)/shard_map/all_to_all | solution.py:611
  151.7 1.2 copy-done.11
  152.9 1.2 copy-done.12
  154.1 1.2 copy-done.13
  155.4 1.2 copy-done.15
  156.6 1.2 copy-done.17
  157.9 6.2 %attend.1 = bf16[128,4096]{1,0:T(8,128)(2,1)} custom-call(s32[1]{0:T(128)} %bitcast.place_ref, bf16[128,4096]{1,0:T(8,128)(2,1)S(1)} %copy-done.11, bf16[128,4096]{1,0:T(8,128)(2,1)S(1)} %copy-done.12, bf16[128,4096]{1,0:T(8,128)(2,1)S(1)} %copy-done.13, bf16[128,4096]{1,0:T(8,128)(2,1)S(1)} %copy-done.15, bf16[128,4096]{1,0:T(8,128)(2,1)S(1)} %copy-done.17), custom_call_target="tpu_custom_call" | custom-call | flops 536870912 | bytes 6291456 | tf_op jit(solution)/shard_map/attend/pallas_call | solution.py:90
  164.1 5.0 %after_exchange.2 = (bf16[128,4096]{1,0:T(8,128)(2,1)}, bf16[128,4096]{1,0:T(8,128)(2,1)}, bf16[128,4096]{1,0:T(8,128)(2,1)}) custom-call(bf16[16,272,128]{2,1,0:T(8,128)(2,1)S(1)} %copy-done.4, bf16[128,4096]{1,0:T(8,128)(2,1)S(1)} %copy-done.2, bf16[128,4096]{1,0:T(8,128)(2,1)S(1)} %copy-done, bf16[128,4096]{1,0:T(8,128)(2,1)S(1)} %copy-done.1, ...), custom_call_target="tpu_custom_call" | custom-call | flops 23592960 | bytes 4718592 | tf_op jit(solution)/shard_map/after_exchange/pallas_call | solution.py:547
  169.2 10.5 %all-to-all-done.1.in_ref = bf16[16,288,128]{2,1,0:T(8,128)(2,1)} async-done(((bf16[16,288,128]{2,1,0:T(8,128)(2,1)}), bf16[16,288,128]{2,1,0:T(8,128)(2,1)}, u32[]{:S(2)}, u32[]{:S(2)}) %all-to-all-start.1) | async-done | bytes 1179680 | tf_op jit(solution)/shard_map/all_to_all | solution.py:611
  181.6 6.3 %after_exchange.3 = (bf16[128,4096]{1,0:T(8,128)(2,1)}, bf16[128,4096]{1,0:T(8,128)(2,1)}, bf16[128,4096]{1,0:T(8,128)(2,1)}, f32[128,256]{1,0:T(8,128)}) custom-call(bf16[16,288,128]{2,1,0:T(8,128)(2,1)} %all-to-all-done.1.in_ref, bf16[128,4096]{1,0:T(8,128)(2,1)S(1)} %copy-done.2, ...), custom_call_target="tpu_custom_call", output_to_operand_aliasing={{0}: (7, {}), {1}: (8, {}), {2}: (9, {})} | custom-call | flops 23592960 | bytes 4718592 | tf_op jit(solution)/shard_map/after_exchange/pallas_call | solution.py:547
  (35 shorter events, 4.2 us)
Async XLA Ops:
  2.4 8.1 %collective-permute-start = (bf16[24,4096]{1,0:T(8,128)(2,1)}, bf16[24,4096]{1,0:T(8,128)(2,1)S(1)}, u32[]{:S(2)}, u32[]{:S(2)}) collective-permute-start(bf16[24,4096]{1,0:T(8,128)(2,1)} %edge_rows.2), channel_id=1, source_target_pairs={{0,2},{2,4},{4,6},{6,8},{8,10},{10,12},{12,14},{14,16},{16,18},{18... | collective-permute-start | bytes 589832 | tf_op jit(solution)/shard_map/ppermute | solution.py:27
  10.4 0.7 copy-start.6
  20.0 55.7 %all-to-all-start = ((bf16[16,544,128]{2,1,0:T(8,128)(2,1)}), bf16[16,544,128]{2,1,0:T(8,128)(2,1)S(1)}, u32[]{:S(2)}, u32[]{:S(2)}) async-start(bf16[16,544,128]{2,1,0:T(8,128)(2,1)} %before_exchange.1), calls=%async_computation | async-start | bytes 4456448 | tf_op jit(solution)/shard_map/all_to_all | solution.py:599
  27.0 53.9 %collective-permute-start.1 = (bf16[24,4096]{1,0:T(8,128)(2,1)}, bf16[24,4096]{1,0:T(8,128)(2,1)S(1)}, u32[]{:S(2)}, u32[]{:S(2)}) collective-permute-start(bf16[24,4096]{1,0:T(8,128)(2,1)} %edge_rows.3), channel_id=1, source_target_pairs={{2,0},{4,2},{6,4},{8,6},{10,8},{12,10},{14,12},{16,14},{18,16},{20... | collective-permute-start | bytes 589832 | tf_op jit(solution)/shard_map/ppermute | solution.py:27
  79.8 1.0 copy-start.10
  80.8 0.7 copy-start.18
  81.5 64.9 %all-to-all-start.2 = ((bf16[16,272,128]{2,1,0:T(8,128)(2,1)}), bf16[16,272,128]{2,1,0:T(8,128)(2,1)S(1)}, u32[]{:S(2)}, u32[]{:S(2)}) async-start(bf16[16,272,128]{2,1,0:T(8,128)(2,1)} %copy-done.10), calls=%async_computation.2 | async-start | bytes 2228224 | tf_op jit(solution)/shard_map/all_to_all | solution.py:611
  86.2 37.9 %collective-permute-start.2 = (bf16[128,4096]{1,0:T(8,128)(2,1)}, bf16[128,4096]{1,0:T(8,128)(2,1)S(1)}, u32[]{:S(2)}, u32[]{:S(2)}) collective-permute-start(bf16[128,4096]{1,0:T(8,128)(2,1)} %k_ref.5), channel_id=1, source_target_pairs={{0,2},{2,4},{4,6},{6,8},{8,10},{10,12},{12,14},{14,16},{16,18},{18... | collective-permute-start | bytes 3145736 | tf_op jit(solution)/shard_map/ppermute | solution.py:27
  88.3 47.1 %collective-permute-start.3 = (bf16[128,4096]{1,0:T(8,128)(2,1)}, bf16[128,4096]{1,0:T(8,128)(2,1)S(1)}, u32[]{:S(2)}, u32[]{:S(2)}) collective-permute-start(bf16[128,4096]{1,0:T(8,128)(2,1)} %v_ref.5), channel_id=1, source_target_pairs={{0,2},{2,4},{4,6},{6,8},{8,10},{10,12},{12,14},{14,16},{16,18},{18... | collective-permute-start | bytes 3145736 | tf_op jit(solution)/shard_map/ppermute | solution.py:27
  124.1 1.0 copy-start.14
  135.3 1.0 copy-start.16
  136.3 3.6 %collective-permute-start.4 = (f32[1,1]{1,0:T(1,128)}, f32[1,1]{1,0:T(1,128)}, u32[]{:S(2)}, u32[]{:S(2)}) collective-permute-start(f32[1,1]{1,0:T(1,128)} %get-tuple-element.36), channel_id=1, source_target_pairs={{0,1},{1,0},{2,3},{3,2},{4,5},{5,4},{6,7},{7,6},{8,9},{9,8},{10,11... | collective-permute-start | bytes 20 | tf_op jit(solution)/shard_map/ppermute | solution.py:34
  145.4 1.1 copy-start.9
  146.4 1.0 copy-start.3
  147.4 32.3 %all-to-all-start.1 = ((bf16[16,288,128]{2,1,0:T(8,128)(2,1)}), bf16[16,288,128]{2,1,0:T(8,128)(2,1)}, u32[]{:S(2)}, u32[]{:S(2)}) async-start(bf16[16,288,128]{2,1,0:T(8,128)(2,1)} %copy-done.9), calls=%async_computation.1 | async-start | bytes 2359296 | tf_op jit(solution)/shard_map/all_to_all | solution.py:611
  151.7 1.2 copy-start.11
  152.9 1.2 copy-start.12
  154.1 1.2 copy-start.13
  155.4 1.2 copy-start.15
  156.6 1.2 copy-start.17
  157.8 6.3 %copy-start = (bf16[128,4096]{1,0:T(8,128)(2,1)S(1)}, bf16[128,4096]{1,0:T(8,128)(2,1)}, u32[]{:S(2)}) copy-start(bf16[128,4096]{1,0:T(8,128)(2,1)} %k_ref.7) | copy-start | bytes 3145732
  157.8 6.3 %copy-start.1 = (bf16[128,4096]{1,0:T(8,128)(2,1)S(1)}, bf16[128,4096]{1,0:T(8,128)(2,1)}, u32[]{:S(2)}) copy-start(bf16[128,4096]{1,0:T(8,128)(2,1)} %v_ref.7) | copy-start | bytes 3145732
  157.8 6.3 %copy-start.2 = (bf16[128,4096]{1,0:T(8,128)(2,1)S(1)}, bf16[128,4096]{1,0:T(8,128)(2,1)}, u32[]{:S(2)}) copy-start(bf16[128,4096]{1,0:T(8,128)(2,1)} %og_ref.5) | copy-start | bytes 3145732
  157.8 6.3 %copy-start.4 = (bf16[16,272,128]{2,1,0:T(8,128)(2,1)S(1)}, bf16[16,272,128]{2,1,0:T(8,128)(2,1)}, u32[]{:S(2)}) copy-start(bf16[16,272,128]{2,1,0:T(8,128)(2,1)} %copy-done.3) | copy-start | bytes 3342340
  157.8 6.3 %copy-start.5 = (f32[3,7,4096]{2,1,0:T(8,128)S(1)}, f32[3,7,4096]{2,1,0:T(8,128)}, u32[]{:S(2)}) copy-start(f32[3,7,4096]{2,1,0:T(8,128)} %taps_ref.5) | copy-start | bytes 1032196
  157.8 6.3 %copy-start.7 = (bf16[24,4096]{1,0:T(8,128)(2,1)S(1)}, bf16[24,4096]{1,0:T(8,128)(2,1)}, u32[]{:S(2)}) copy-start(bf16[24,4096]{1,0:T(8,128)(2,1)} %copy-done.6) | copy-start | bytes 589828
  157.8 6.3 %copy-start.19 = (bf16[24,4096]{1,0:T(8,128)(2,1)S(1)}, bf16[24,4096]{1,0:T(8,128)(2,1)}, u32[]{:S(2)}) copy-start(bf16[24,4096]{1,0:T(8,128)(2,1)} %copy-done.18) | copy-start | bytes 589828
  179.7 0.9 copy-start.8
  180.6 0.9 copy-start.20

commit v10 on v9

--- a/solution.py
+++ b/solution.py
@@ -50,57 +50,150 @@
 NT = (((1,), (1,)), ((), ()))
 
 
-def attend_kernel(place_ref, q_ref, k_ref, v_ref, kp_ref, vp_ref, out_ref):
-    rows = q_ref.shape[0]
-    heads = q_ref.shape[1] // HEAD_DIM
+LOG_LANES = 32
+
+
+def places_of(width):
+    return [slice(head * HEAD_DIM, (head + 1) * HEAD_DIM) for head in range(width // HEAD_DIM)]
+
+
+def attend_next_kernel(q_ref, k_ref, v_ref, out_ref, logs_ref):
+    rows, width = q_ref.shape
+    heads = width // HEAD_DIM
+    step = pl.program_id(0)
+    lane = lax.broadcasted_iota(jnp.int32, (rows, LANES), 1)
+
+    @pl.when(step == 0)
+    def _():
+        logs_ref[...] = jnp.zeros_like(logs_ref)
+
+    places = places_of(width)
+    scores = [
+        lax.dot_general(q_ref[:, at], k_ref[:, at], NT, preferred_element_type=F32) * SCALE
+        for at in places
+    ]
+    largest = [jnp.max(score, axis=1, keepdims=True) for score in scores]
+    raised = [jnp.exp(score - top) for score, top in zip(scores, largest)]
+    totals = [jnp.sum(r, axis=1, keepdims=True) for r in raised]
+    weights = [(r * (1.0 / total)).astype(BF16) for r, total in zip(raised, totals)]
+    mixed = [
+        jnp.dot(weight, v_ref[:, at], preferred_element_type=F32) for weight, at in zip(weights, places)
+    ]
+    logs = logs_ref[...]
+    for head in range(heads):
+        log = largest[head] + jnp.log(totals[head])
+        logs = jnp.where(lane == step * heads + head, log, logs)
+    logs_ref[...] = logs
+    first = pl.multiple_of(step * width, LANES)
+    out_ref[:, pl.ds(first, width)] = jnp.concatenate([m.astype(BF16) for m in mixed], 1)
+
+    @pl.when(step == pl.num_programs(0) - 1)
+    def _():
+        upper = logs.astype(BF16).astype(F32)
+        middle = (logs - upper).astype(BF16).astype(F32)
+        lower = logs - upper - middle
+        terms = upper + pltpu.roll(middle, LOG_LANES, 1) + pltpu.roll(lower, 2 * LOG_LANES, 1)
+        out_ref[:, out_ref.shape[1] - LANES :] = terms.astype(BF16)
+
+
+def attend_own_kernel(
+    steps, place_ref, q_ref, k_ref, v_ref, part0_ref, part1_ref, log0_ref, log1_ref, out_ref
+):
+    rows, width = q_ref.shape
+    heads = width // HEAD_DIM
+    step = pl.program_id(0)
     row = lax.broadcasted_iota(jnp.int32, (rows, rows), 0)
     col = lax.broadcasted_iota(jnp.int32, (rows, rows), 1)
     own_ok = col <= row
-    prev_ok = jnp.broadcast_to(place_ref[0], (rows, rows)) > 0
-    places = [slice(head * HEAD_DIM, (head + 1) * HEAD_DIM) for head in range(heads)]
-
-    def scores(ref, allowed):
-        products = [
-            lax.dot_general(q_ref[:, at], ref[:, at], NT, preferred_element_type=F32) for at in places
-        ]
-        return [jnp.where(allowed, product * SCALE, -jnp.inf) for product in products]
-
-    own, prev = scores(k_ref, own_ok), scores(kp_ref, prev_ok)
-    largest = [jnp.max(jnp.maximum(o, p), axis=1, keepdims=True) for o, p in zip(own, prev)]
-    own = [jnp.exp(o - top) for o, top in zip(own, largest)]
-    prev = [jnp.exp(p - top) for p, top in zip(prev, largest)]
-    totals = [jnp.sum(o + p, axis=1, keepdims=True) for o, p in zip(own, prev)]
-    inverses = [1.0 / total for total in totals]
-    own = [(o * inverse).astype(BF16) for o, inverse in zip(own, inverses)]
-    prev = [(p * inverse).astype(BF16) for p, inverse in zip(prev, inverses)]
+    lane = lax.broadcasted_iota(jnp.int32, (rows, LANES), 1)
+    has_prev = jnp.broadcast_to(place_ref[0], (rows, 1)) > 0
+    late = step >= steps
+    places = places_of(width)
+    terms = jnp.where(late, log1_ref[...].astype(F32), log0_ref[...].astype(F32))
+    first = jnp.where(late, step - steps, step) * heads
+    scores = [
+        lax.dot_general(q_ref[:, at], k_ref[:, at], NT, preferred_element_type=F32) * SCALE
+        for at in places
+    ]
+    scores = [jnp.where(own_ok, score, -jnp.inf) for score in scores]
+    logs = [
+        jnp.sum(
+            jnp.where((lane & (LOG_LANES - 1)) == first + head, terms, 0.0), axis=1, keepdims=True
+        )
+        for head in range(heads)
+    ]
+    logs = [jnp.where(has_prev, log, -jnp.inf) for log in logs]
+    largest = [
+        jnp.maximum(jnp.max(score, axis=1, keepdims=True), log) for score, log in zip(scores, logs)
+    ]
+    raised = [jnp.exp(score - top) for score, top in zip(scores, largest)]
+    prevs = [jnp.exp(log - top) for log, top in zip(logs, largest)]
+    inverses = [
+        1.0 / (jnp.sum(r, axis=1, keepdims=True) + prev) for r, prev in zip(raised, prevs)
+    ]
+    weights = [(r * inverse).astype(BF16) for r, inverse in zip(raised, inverses)]
     mixed = [
-        jnp.dot(o, v_ref[:, at], preferred_element_type=F32)
-        + jnp.dot(p, vp_ref[:, at], preferred_element_type=F32)
-        for o, p, at in zip(own, prev, places)
+        jnp.dot(weight, v_ref[:, at], preferred_element_type=F32) for weight, at in zip(weights, places)
     ]
     for head, at in enumerate(places):
-        out_ref[:, at] = mixed[head].astype(BF16)
-
-
-def attend(query, key, value, key_prev, value_prev, position):
+        part = jnp.where(late, part1_ref[:, at].astype(F32), part0_ref[:, at].astype(F32))
+        total = mixed[head] + (prevs[head] * inverses[head]) * part
+        out_ref[:, at] = total.astype(BF16)
+
+
+def attend_cost(rows, channels):
+    heads = channels // HEAD_DIM
+    return pl.CostEstimate(
+        flops=4 * heads * rows * rows * HEAD_DIM,
+        bytes_accessed=10 * rows * channels,
+        transcendentals=heads * rows * rows,
+    )
+
+
+def attend_next(query, key, value, part):
     rows, channels = query.shape
     tile = min(512, channels)
-    heads = channels // HEAD_DIM
+    steps = channels // tile
+    there = pl.BlockSpec((rows, tile), lambda i: (0, part * steps + i))
+    return pl.pallas_call(
+        attend_next_kernel,
+        grid=(steps,),
+        in_specs=[pl.BlockSpec((rows, tile), lambda i: (0, i)), there, there],
+        out_specs=pl.BlockSpec((rows, channels + LANES), lambda i: (0, 0)),
+        out_shape=jax.ShapeDtypeStruct((rows, channels + LANES), BF16),
+        scratch_shapes=[pltpu.VMEM((rows, LANES), F32)],
+        compiler_params=params(),
+        cost_estimate=attend_cost(rows, channels),
+        name="attend_next",
+    )(query, key, value)
+
+
+def attend_own(query, key, value, parts, position):
+    rows, channels = query.shape
+    tile = min(512, channels // 2)
+    steps = channels // 2 // tile
     block = pl.BlockSpec((rows, tile), lambda i: (0, i))
+    log_at = channels // 2 // LANES
+    log = pl.BlockSpec((rows, LANES), lambda i: (0, log_at))
     return pl.pallas_call(
-        attend_kernel,
-        grid=(channels // tile,),
-        in_specs=[pl.BlockSpec(memory_space=pltpu.SMEM)] + [block] * 5,
+        functools.partial(attend_own_kernel, steps),
+        grid=(2 * steps,),
+        in_specs=[
+            pl.BlockSpec(memory_space=pltpu.SMEM),
+            block,
+            block,
+            block,
+            pl.BlockSpec((rows, tile), lambda i: (0, jnp.minimum(i, steps - 1))),
+            pl.BlockSpec((rows, tile), lambda i: (0, jnp.maximum(i - steps, 0))),
+            log,
+            log,
+        ],
         out_specs=block,
         out_shape=jax.ShapeDtypeStruct((rows, channels), BF16),
-        compiler_params=params(LONG_VMEM),
-        cost_estimate=pl.CostEstimate(
-            flops=8 * heads * rows * rows * HEAD_DIM,
-            bytes_accessed=12 * rows * channels,
-            transcendentals=2 * heads * rows * rows,
-        ),
-        name="attend",
-    )(position.astype(jnp.int32).reshape(1), query, key, value, key_prev, value_prev)
+        compiler_params=params(),
+        cost_estimate=attend_cost(rows, channels),
+        name="attend_own",
+    )(position.astype(jnp.int32).reshape(1), query, key, value, *parts, *parts)
 
 
 def edge_kernel(first, *refs):
@@ -562,7 +655,7 @@
         out_shape=[grad] * 3 + [jax.ShapeDtypeStruct((rows, groups), F32)] * last,
         scratch_shapes=[pltpu.VMEM((groups, rows), F32), pltpu.VMEM((1, LANES), F32)] * last
         + [ext] * 5,
-        compiler_params=params(LONG_VMEM),
+        compiler_params=params(),
         cost_estimate=pl.CostEstimate(
             flops=90 * rows * channels, bytes_accessed=18 * rows * channels, transcendentals=0
         ),
@@ -588,28 +681,37 @@
     cpd, gpd = channels // n, groups // n
     position = lax.axis_index("ctx")
     tail = shifted(edge_rows((hyena_query, hyena_key, hyena_value), False), "ctx", 1)
-    key_prev = shifted(key_heads, "ctx", 1)
-    value_prev = shifted(value_heads, "ctx", 1)
+    half = channels // 2
+    early, tail = lax.optimization_barrier((query_heads[:, :half], tail))
+    early = shifted(early, "ctx", -1)
     chunks = 2 if gpd % 4 == 0 else 1
     cpd, gpd = cpd // chunks, gpd // chunks
     send = before_exchange(
         hyena_query, hyena_key, hyena_value, output_grad, tail, short_filter, long_filter, n, chunks
     )
-    send, *sources = lax.optimization_barrier((send, output_grad, hyena_key, hyena_value))
+    send, early, late, *sources = lax.optimization_barrier(
+        (send, early, query_heads[:, half:], output_grad, hyena_key, hyena_value)
+    )
     received = lax.all_to_all(send, "ctx", split_axis=0, concat_axis=0, tiled=True)
     following = shifted(edge_rows(sources, True), "ctx", -1)
+    late = shifted(late, "ctx", -1)
+    parts = [shifted(attend_next(early, key_heads, value_heads, 0), "ctx", 1)]
     returned = []
     for chunk in range(chunks):
         raw = ()
         if chunk + 1 == chunks:
             raw, squares = filter_products(received, cpd, gpd, chunks)
-            raw, key_prev, value_prev = lax.optimization_barrier((raw, key_prev, value_prev))
             raw = (raw, total_over(squares, "tp"))
         results = long_convs(received, raw, cpd, gpd, chunk, chunks)
         if chunk == 0:
-            results, received, following = lax.optimization_barrier((results, received, following))
+            results, received, following, late, parts[0] = lax.optimization_barrier(
+                (results, received, following, late, parts[0])
+            )
+            parts.append(shifted(attend_next(late, key_heads, value_heads, 1), "ctx", 1))
+        else:
+            results, parts[1] = lax.optimization_barrier((results, parts[1]))
         returned.append(lax.all_to_all(results, "ctx", split_axis=0, concat_axis=0, tiled=True))
-    attention = attend(query_heads, key_heads, value_heads, key_prev, value_prev, position)
+    attention = attend_own(query_heads, key_heads, value_heads, parts, position)
     bound = math.sqrt(rows * n * groups * tp)
     grads = ()
     for chunk in range(chunks):

time: 189 us -> 165 us (0.87)
  waiting for transfers between devices: 99.1 us -> 65.7 us
  Pallas kernels: 46.2 us -> 60.9 us
  local copies, waits for them, and re-layouts: 14.3 us -> 4.7 us
  starting transfers between devices: 26.2 us -> 30.8 us
    ppermute x4 -> x6, waiting for transfers between devices: 40.8 us -> 13.5 us  [shifted(): return lax.ppermute(block, axis, route)]
    pallas_call x1 -> x3, Pallas kernels: 6.22 us -> 17.2 us  [the longest x2 9.16 us: attend_next(): pl.pallas_call(attend_next_kernel, grid=(steps,), in_specs=[pl.BlockSpec(...]
    unnamed x42 -> x16, local copies, waits for them, and re-layouts: 14.3 us -> 3.79 us
    all_to_all x1, waiting for transfers between devices: 45.6 us -> 36.3 us  [on_device(): lax.all_to_all(send, 'ctx', split_axis=0, concat_axis=0, tiled=True)]
    ppermute x4 -> x6, starting transfers between devices: 10.4 us -> 14.2 us  [shifted(): return lax.ppermute(block, axis, route)]
    all_to_all x2, waiting for transfers between devices: 10.5 us -> 13.7 us  [on_device(): lax.all_to_all(results, 'ctx', split_axis=0, concat_axis=0, tiled=True)]
    pallas_call x2, Pallas kernels: 8.23 us -> 10.3 us  [long_convs(): pl.pallas_call(functools.partial(conv_kernel, cpd, gpd), grid=(1,), in_sp...]
  transfers between devices with their start and end apart: 8 -> 10, of which waited for: 6 -> 6; matrix products, arithmetic and copies ran while one was open for 0% -> 1% of each run, Pallas kernels for 16% -> 32%
where the time goes in v10:
time: 165 us; the launch traced here: 164 us
  waiting for transfers between devices  65.7 us (40%)
  Pallas kernels  60.9 us (37%)
  starting transfers between devices  30.8 us (19%)
  local copies, waits for them, and re-layouts  4.7 us (3%)
  between operations  2.02 us (1%)
    all_to_all x1, waiting for transfers between devices, on_device(): lax.all_to_all(send, 'ctx', split_axis=0, concat_axis=0, tiled=True)  36.3 us
    ppermute x6, starting transfers between devices, shifted(): return lax.ppermute(block, axis, route)  14.2 us
    all_to_all x2, waiting for transfers between devices, on_device(): lax.all_to_all(results, 'ctx', split_axis=0, concat_axis=0, tiled=True)  13.7 us
    ppermute x6, waiting for transfers between devices, shifted(): return lax.ppermute(block, axis, route)  13.5 us
    pallas_call x2, Pallas kernels, after_exchange(): pl.pallas_call(functools.partial(after_kernel, cpd, gpd, chunks, last, bo...  12.8 us
    pallas_call x2, Pallas kernels, long_convs(): pl.pallas_call(functools.partial(conv_kernel, cpd, gpd), grid=(1,), in_sp...  10.3 us
    all_to_all x2, starting transfers between devices, on_device(): lax.all_to_all(results, 'ctx', split_axis=0, concat_axis=0, tiled=True)  9.67 us
    pallas_call x2, Pallas kernels, attend_next(): pl.pallas_call(attend_next_kernel, grid=(steps,), in_specs=[pl.BlockSpec(...  9.16 us
  transfers between devices with their start and end apart: 10, of which 6 were waited for; matrix products, arithmetic and copies ran while one was open for 1% of the time, Pallas kernels for 32%

profile of v10, /device:TPU:16, one launch (start us, length us, event | category | flops | bytes accessed | tf_op | source)
XLA Modules:
  0.0 164.1 jit_solution(14200658420270973120)
XLA Ops:
  0.6 1.8 %edge_rows.2 = bf16[24,4096]{1,0:T(8,128)(2,1)} custom-call(bf16[128,4096]{1,0:T(8,128)(2,1)} %q_ref.2, bf16[128,4096]{1,0:T(8,128)(2,1)} %k_ref.11, bf16[128,4096]{1,0:T(8,128)(2,1)} %v_ref.11), custom_call_target="tpu_custom_call" | custom-call | tf_op jit(solution)/shard_map/edge_rows/pallas_call | solution.py:209
  2.5 1.9 %collective-permute-start = (bf16[24,4096]{1,0:T(8,128)(2,1)}, bf16[24,4096]{1,0:T(8,128)(2,1)S(1)}, u32[]{:S(2)}, u32[]{:S(2)}) collective-permute-start(bf16[24,4096]{1,0:T(8,128)(2,1)} %edge_rows.2), channel_id=1, source_target_pairs={{0,2},{2,4},{4,6},{6,8},{8,10},{10,12},{12,14},{14,16},{16,18},{18... | collective-permute-start | bytes 589832 | tf_op jit(solution)/shard_map/ppermute | solution.py:27
  4.4 0.9 fusion
  5.3 5.3 %collective-permute-done.tail_ref = bf16[24,4096]{1,0:T(8,128)(2,1)S(1)} collective-permute-done((bf16[24,4096]{1,0:T(8,128)(2,1)}, bf16[24,4096]{1,0:T(8,128)(2,1)S(1)}, u32[]{:S(2)}, u32[]{:S(2)}) %collective-permute-start) | collective-permute-done | bytes 196640 | tf_op jit(solution)/shard_map/ppermute | solution.py:27
  10.5 1.9 %collective-permute-start.1 = (bf16[128,2048]{1,0:T(8,128)(2,1)S(1)}, bf16[128,2048]{1,0:T(8,128)(2,1)S(1)}, u32[]{:S(2)}, u32[]{:S(2)}) collective-permute-start(bf16[128,2048]{1,0:T(8,128)(2,1)S(1)} %get-tuple-element.35), channel_id=1, source_target_pairs={{2,0},{4,2},{6,4},{8,6},{10,8},{12,10},{14,12},{16,14},{18,16},{20... | collective-permute-start | bytes 1572872 | tf_op jit(solution)/shard_map/ppermute | solution.py:27
  12.5 8.9 %before_exchange.1 = bf16[16,544,128]{2,1,0:T(8,128)(2,1)} custom-call(bf16[128,4096]{1,0:T(8,128)(2,1)} %q_ref.2, bf16[128,4096]{1,0:T(8,128)(2,1)} %k_ref.11, bf16[128,4096]{1,0:T(8,128)(2,1)} %v_ref.11, bf16[128,4096]{1,0:T(8,128)(2,1)} %og_ref.5, bf16[24,4096]{1,0:T(8,128)(2,1)} %copy-done.4, f32[3,7,4096]{2,1,0:T(8,128)} %taps_ref.5, f32[128,256]{1,0:T(8,128)} %long_ref.1), custom_call_target="tpu_custom_call" | custom-call | flops 26214400 | bytes 6291456 | tf_op jit(solution)/shard_map/before_exchange/pallas_call | solution.py:291
  21.4 0.8 copy-done.7
  22.2 5.4 %all-to-all-start = ((bf16[16,544,128]{2,1,0:T(8,128)(2,1)}), bf16[16,544,128]{2,1,0:T(8,128)(2,1)S(1)}, u32[]{:S(2)}, u32[]{:S(2)}) async-start(bf16[16,544,128]{2,1,0:T(8,128)(2,1)} %before_exchange.1), calls=%async_computation | async-start | bytes 4456448 | tf_op jit(solution)/shard_map/all_to_all | solution.py:695
  27.6 4.6 %attend_next.2 = bf16[128,2176]{1,0:T(8,128)(2,1)} custom-call(bf16[128,2048]{1,0:T(8,128)(2,1)} %copy-done.7, bf16[128,4096]{1,0:T(8,128)(2,1)} %k_ref.9, bf16[128,4096]{1,0:T(8,128)(2,1)} %v_ref.9), custom_call_target="tpu_custom_call" | custom-call | flops 134217728 | bytes 2621440 | tf_op jit(solution)/shard_map/attend_next/pallas_call | solution.py:158
  32.1 2.0 %collective-permute-start.4 = (bf16[128,2176]{1,0:T(8,128)(2,1)}, bf16[128,2176]{1,0:T(8,128)(2,1)S(1)}, u32[]{:S(2)}, u32[]{:S(2)}) collective-permute-start(bf16[128,2176]{1,0:T(8,128)(2,1)} %attend_next.2), channel_id=1, source_target_pairs={{0,2},{2,4},{4,6},{6,8},{8,10},{10,12},{12,14},{14,16},{16,18},{18... | collective-permute-start | bytes 1671176 | tf_op jit(solution)/shard_map/ppermute | solution.py:27
  34.2 4.4 %collective-permute-start.3 = (bf16[128,2048]{1,0:T(8,128)(2,1)}, bf16[128,2048]{1,0:T(8,128)(2,1)S(1)}, u32[]{:S(2)}, u32[]{:S(2)}) collective-permute-start(bf16[128,2048]{1,0:T(8,128)(2,1)} %get-tuple-element.40), channel_id=1, source_target_pairs={{2,0},{4,2},{6,4},{8,6},{10,8},{12,10},{14,12},{16,14},{18,16},{20... | collective-permute-start | bytes 1572872 | tf_op jit(solution)/shard_map/ppermute | solution.py:27
  38.6 1.7 %edge_rows.3 = bf16[24,4096]{1,0:T(8,128)(2,1)} custom-call(bf16[128,4096]{1,0:T(8,128)(2,1)} %og_ref.5, bf16[128,4096]{1,0:T(8,128)(2,1)} %k_ref.11, bf16[128,4096]{1,0:T(8,128)(2,1)} %v_ref.11), custom_call_target="tpu_custom_call" | custom-call | tf_op jit(solution)/shard_map/edge_rows/pallas_call | solution.py:209
  40.3 1.9 %collective-permute-start.2 = (bf16[24,4096]{1,0:T(8,128)(2,1)}, bf16[24,4096]{1,0:T(8,128)(2,1)S(1)}, u32[]{:S(2)}, u32[]{:S(2)}) collective-permute-start(bf16[24,4096]{1,0:T(8,128)(2,1)} %edge_rows.3), channel_id=1, source_target_pairs={{2,0},{4,2},{6,4},{8,6},{10,8},{12,10},{14,12},{16,14},{18,16},{20... | collective-permute-start | bytes 589832 | tf_op jit(solution)/shard_map/ppermute | solution.py:27
  42.2 36.3 %all-to-all-done.in_ref = bf16[16,544,128]{2,1,0:T(8,128)(2,1)S(1)} async-done(((bf16[16,544,128]{2,1,0:T(8,128)(2,1)}), bf16[16,544,128]{2,1,0:T(8,128)(2,1)S(1)}, u32[]{:S(2)}, u32[]{:S(2)}) %all-to-all-start) | async-done | bytes 2228256 | tf_op jit(solution)/shard_map/all_to_all | solution.py:695
  78.5 5.1 %long_convs.2 = bf16[16,272,128]{2,1,0:T(8,128)(2,1)} custom-call(bf16[16,544,128]{2,1,0:T(8,128)(2,1)S(1)} %all-to-all-done.in_ref), custom_call_target="tpu_custom_call" | custom-call | flops 2147483648 | bytes 2228224 | tf_op jit(solution)/shard_map/long_convs/pallas_call | solution.py:406
  83.6 0.5 collective-permute-done.2.next_ref
  84.1 0.8 copy-done.6
  85.1 5.5 %all-to-all-start.2 = ((bf16[16,272,128]{2,1,0:T(8,128)(2,1)}), bf16[16,272,128]{2,1,0:T(8,128)(2,1)S(1)}, u32[]{:S(2)}, u32[]{:S(2)}) async-start(bf16[16,272,128]{2,1,0:T(8,128)(2,1)} %long_convs.2), calls=%async_computation.2 | async-start | bytes 2228224 | tf_op jit(solution)/shard_map/all_to_all | solution.py:713
  90.5 4.6 %attend_next.3 = bf16[128,2176]{1,0:T(8,128)(2,1)} custom-call(bf16[128,2048]{1,0:T(8,128)(2,1)} %copy-done.6, bf16[128,4096]{1,0:T(8,128)(2,1)} %k_ref.9, bf16[128,4096]{1,0:T(8,128)(2,1)} %v_ref.9), custom_call_target="tpu_custom_call" | custom-call | flops 134217728 | bytes 2621440 | tf_op jit(solution)/shard_map/attend_next/pallas_call | solution.py:158
  95.1 2.0 %collective-permute-start.6 = (bf16[128,2176]{1,0:T(8,128)(2,1)}, bf16[128,2176]{1,0:T(8,128)(2,1)}, u32[]{:S(2)}, u32[]{:S(2)}) collective-permute-start(bf16[128,2176]{1,0:T(8,128)(2,1)} %attend_next.3), channel_id=1, source_target_pairs={{0,2},{2,4},{4,6},{6,8},{8,10},{10,12},{12,14},{14,16},{16,18},{18... | collective-permute-start | bytes 1671176 | tf_op jit(solution)/shard_map/ppermute | solution.py:27
  97.2 8.2 %filter_products.1 = (bf16[16,16,128]{2,1,0:T(8,128)(2,1)S(1)}, f32[1,1]{1,0:T(1,128)}) custom-call(bf16[16,544,128]{2,1,0:T(8,128)(2,1)S(1)} %all-to-all-done.in_ref), custom_call_target="tpu_custom_call" | custom-call | flops 2147483648 | bytes 2228224 | tf_op jit(solution)/shard_map/filter_products/pallas_call | solution.py:486
  105.3 1.5 collective-permute-start.5
  106.8 2.3 %collective-permute-done.5 = f32[1,1]{1,0:T(1,128)} collective-permute-done((f32[1,1]{1,0:T(1,128)}, f32[1,1]{1,0:T(1,128)}, u32[]{:S(2)}, u32[]{:S(2)}) %collective-permute-start.5) | collective-permute-done | bytes 36 | tf_op jit(solution)/shard_map/ppermute | solution.py:34
  110.4 5.2 %long_convs.3 = bf16[16,288,128]{2,1,0:T(8,128)(2,1)} custom-call(bf16[16,544,128]{2,1,0:T(8,128)(2,1)S(1)} %all-to-all-done.in_ref, bf16[16,16,128]{2,1,0:T(8,128)(2,1)S(1)} %get-tuple-element.43.refs_0_, f32[1,1]{1,0:T(1,128)S(6)} %add.3.refs_1_), custom_call_target="tpu_custom_call" | custom-call | flops 2147483648 | bytes 2359296 | tf_op jit(solution)/shard_map/long_convs/pallas_call | solution.py:406
  115.6 7.7 %collective-permute-done.6.part1_ref.log1_ref = bf16[128,2176]{1,0:T(8,128)(2,1)} collective-permute-done((bf16[128,2176]{1,0:T(8,128)(2,1)}, bf16[128,2176]{1,0:T(8,128)(2,1)}, u32[]{:S(2)}, u32[]{:S(2)}) %collective-permute-start.6) | collective-permute-done | bytes 557088 | tf_op jit(solution)/shard_map/ppermute | solution.py:27
  123.3 1.0 copy-done.1
  124.3 4.2 %all-to-all-start.1 = ((bf16[16,288,128]{2,1,0:T(8,128)(2,1)}), bf16[16,288,128]{2,1,0:T(8,128)(2,1)S(1)}, u32[]{:S(2)}, u32[]{:S(2)}) async-start(bf16[16,288,128]{2,1,0:T(8,128)(2,1)} %long_convs.3), calls=%async_computation.1 | async-start | bytes 2359296 | tf_op jit(solution)/shard_map/all_to_all | solution.py:713
  128.5 8.0 %attend_own.1 = bf16[128,4096]{1,0:T(8,128)(2,1)} custom-call(s32[1]{0:T(128)} %bitcast.place_ref, bf16[128,4096]{1,0:T(8,128)(2,1)} %q_ref.3, bf16[128,4096]{1,0:T(8,128)(2,1)} %k_ref.9, bf16[128,4096]{1,0:T(8,128)(2,1)} %v_ref.9, bf16[128,2176]{1,0:T(8,128)(2,1)} %copy-done.3, bf16[128,2176]{1,0:T(8,128)(2,1)} %collective-permute-done.6.part1_ref.log1_ref, ...), custom_call_target="tpu_custom_call" | custom-call | flops 268435456 | bytes 5242880 | tf_op jit(solution)/shard_map/attend_own/pallas_call | solution.py:178
  136.5 6.3 %after_exchange.2 = (bf16[128,4096]{1,0:T(8,128)(2,1)}, bf16[128,4096]{1,0:T(8,128)(2,1)}, bf16[128,4096]{1,0:T(8,128)(2,1)}) custom-call(bf16[16,272,128]{2,1,0:T(8,128)(2,1)} %copy-done.1, bf16[128,4096]{1,0:T(8,128)(2,1)} %og_ref.5, bf16[128,4096]{1,0:T(8,128)(2,1)} %k_ref.11, bf16[128,4096]{1,0:T(8,128)(2,1)} %v_ref.11, bf16[24,4096]{1,0:T(8,128)(2,1)} %copy-done.4, ...), custom_call_target="tpu_custom_call" | custom-call | flops 23592960 | bytes 4718592 | tf_op jit(solution)/shard_map/after_exchange/pallas_call | solution.py:640
  142.8 13.7 %all-to-all-done.1.in_ref = bf16[16,288,128]{2,1,0:T(8,128)(2,1)S(1)} async-done(((bf16[16,288,128]{2,1,0:T(8,128)(2,1)}), bf16[16,288,128]{2,1,0:T(8,128)(2,1)S(1)}, u32[]{:S(2)}, u32[]{:S(2)}) %all-to-all-start.1) | async-done | bytes 1179680 | tf_op jit(solution)/shard_map/all_to_all | solution.py:713
  156.5 1.0 copy-done
  157.5 6.6 %after_exchange.3 = (bf16[128,4096]{1,0:T(8,128)(2,1)}, bf16[128,4096]{1,0:T(8,128)(2,1)}, bf16[128,4096]{1,0:T(8,128)(2,1)}, f32[128,256]{1,0:T(8,128)}) custom-call(bf16[16,288,128]{2,1,0:T(8,128)(2,1)} %copy-done, bf16[128,4096]{1,0:T(8,128)(2,1)} %og_ref.5, bf16[128,4096]{1,0:T(8,128)(2,1)} %k_ref.11, ...), custom_call_target="tpu_custom_call", output_to_operand_aliasing={{0}: (7, {}), {1}: (8, {}), {2}: (9, {})} | custom-call | flops 23592960 | bytes 4718592 | tf_op jit(solution)/shard_map/after_exchange/pallas_call | solution.py:640
  (16 shorter events, 0.2 us)
Async XLA Ops:
  0.6 3.7 %copy-start.2 = (bf16[128,4096]{1,0:T(8,128)(2,1)S(1)}, bf16[128,4096]{1,0:T(8,128)(2,1)}, u32[]{:S(2)}) copy-start(bf16[128,4096]{1,0:T(8,128)(2,1)} %q_ref.3) | copy-start | bytes 3145732
  2.5 8.1 %collective-permute-start = (bf16[24,4096]{1,0:T(8,128)(2,1)}, bf16[24,4096]{1,0:T(8,128)(2,1)S(1)}, u32[]{:S(2)}, u32[]{:S(2)}) collective-permute-start(bf16[24,4096]{1,0:T(8,128)(2,1)} %edge_rows.2), channel_id=1, source_target_pairs={{0,2},{2,4},{4,6},{6,8},{8,10},{10,12},{12,14},{14,16},{16,18},{18... | collective-permute-start | bytes 589832 | tf_op jit(solution)/shard_map/ppermute | solution.py:27
  10.5 1.9 %copy-start.4 = (bf16[24,4096]{1,0:T(8,128)(2,1)}, bf16[24,4096]{1,0:T(8,128)(2,1)S(1)}, u32[]{:S(2)}) copy-start(bf16[24,4096]{1,0:T(8,128)(2,1)S(1)} %collective-permute-done.tail_ref) | copy-start | bytes 589828
  10.5 10.8 %collective-permute-start.1 = (bf16[128,2048]{1,0:T(8,128)(2,1)S(1)}, bf16[128,2048]{1,0:T(8,128)(2,1)S(1)}, u32[]{:S(2)}, u32[]{:S(2)}) collective-permute-start(bf16[128,2048]{1,0:T(8,128)(2,1)S(1)} %get-tuple-element.35), channel_id=1, source_target_pairs={{2,0},{4,2},{6,4},{8,6},{10,8},{12,10},{14,12},{16,14},{18,16},{20... | collective-permute-start | bytes 1572872 | tf_op jit(solution)/shard_map/ppermute | solution.py:27
  21.4 0.8 copy-start.7
  22.2 56.3 %all-to-all-start = ((bf16[16,544,128]{2,1,0:T(8,128)(2,1)}), bf16[16,544,128]{2,1,0:T(8,128)(2,1)S(1)}, u32[]{:S(2)}, u32[]{:S(2)}) async-start(bf16[16,544,128]{2,1,0:T(8,128)(2,1)} %before_exchange.1), calls=%async_computation | async-start | bytes 4456448 | tf_op jit(solution)/shard_map/all_to_all | solution.py:695
  32.1 51.9 %collective-permute-start.4 = (bf16[128,2176]{1,0:T(8,128)(2,1)}, bf16[128,2176]{1,0:T(8,128)(2,1)S(1)}, u32[]{:S(2)}, u32[]{:S(2)}) collective-permute-start(bf16[128,2176]{1,0:T(8,128)(2,1)} %attend_next.2), channel_id=1, source_target_pairs={{0,2},{2,4},{4,6},{6,8},{8,10},{10,12},{12,14},{14,16},{16,18},{18... | collective-permute-start | bytes 1671176 | tf_op jit(solution)/shard_map/ppermute | solution.py:27
  34.2 49.9 %collective-permute-start.3 = (bf16[128,2048]{1,0:T(8,128)(2,1)}, bf16[128,2048]{1,0:T(8,128)(2,1)S(1)}, u32[]{:S(2)}, u32[]{:S(2)}) collective-permute-start(bf16[128,2048]{1,0:T(8,128)(2,1)} %get-tuple-element.40), channel_id=1, source_target_pairs={{2,0},{4,2},{6,4},{8,6},{10,8},{12,10},{14,12},{16,14},{18,16},{20... | collective-permute-start | bytes 1572872 | tf_op jit(solution)/shard_map/ppermute | solution.py:27
  40.3 43.7 %collective-permute-start.2 = (bf16[24,4096]{1,0:T(8,128)(2,1)}, bf16[24,4096]{1,0:T(8,128)(2,1)S(1)}, u32[]{:S(2)}, u32[]{:S(2)}) collective-permute-start(bf16[24,4096]{1,0:T(8,128)(2,1)} %edge_rows.3), channel_id=1, source_target_pairs={{2,0},{4,2},{6,4},{8,6},{10,8},{12,10},{14,12},{16,14},{18,16},{20... | collective-permute-start | bytes 589832 | tf_op jit(solution)/shard_map/ppermute | solution.py:27
  84.1 21.2 %copy-start.5 = (bf16[24,4096]{1,0:T(8,128)(2,1)}, bf16[24,4096]{1,0:T(8,128)(2,1)S(1)}, u32[]{:S(2)}) copy-start(bf16[24,4096]{1,0:T(8,128)(2,1)S(1)} %collective-permute-done.2.next_ref) | copy-start | bytes 589828
  84.1 0.8 copy-start.6
  84.1 1.0 copy-start.3
  85.1 38.2 %all-to-all-start.2 = ((bf16[16,272,128]{2,1,0:T(8,128)(2,1)}), bf16[16,272,128]{2,1,0:T(8,128)(2,1)S(1)}, u32[]{:S(2)}, u32[]{:S(2)}) async-start(bf16[16,272,128]{2,1,0:T(8,128)(2,1)} %long_convs.2), calls=%async_computation.2 | async-start | bytes 2228224 | tf_op jit(solution)/shard_map/all_to_all | solution.py:713
  95.1 28.1 %collective-permute-start.6 = (bf16[128,2176]{1,0:T(8,128)(2,1)}, bf16[128,2176]{1,0:T(8,128)(2,1)}, u32[]{:S(2)}, u32[]{:S(2)}) collective-permute-start(bf16[128,2176]{1,0:T(8,128)(2,1)} %attend_next.3), channel_id=1, source_target_pairs={{0,2},{2,4},{4,6},{6,8},{8,10},{10,12},{12,14},{14,16},{16,18},{18... | collective-permute-start | bytes 1671176 | tf_op jit(solution)/shard_map/ppermute | solution.py:27
  105.3 3.8 %collective-permute-start.5 = (f32[1,1]{1,0:T(1,128)}, f32[1,1]{1,0:T(1,128)}, u32[]{:S(2)}, u32[]{:S(2)}) collective-permute-start(f32[1,1]{1,0:T(1,128)} %get-tuple-element.44), channel_id=1, source_target_pairs={{0,1},{1,0},{2,3},{3,2},{4,5},{5,4},{6,7},{7,6},{8,9},{9,8},{10,11... | collective-permute-start | bytes 20 | tf_op jit(solution)/shard_map/ppermute | solution.py:34
  123.3 1.0 copy-start.1
  124.3 32.2 %all-to-all-start.1 = ((bf16[16,288,128]{2,1,0:T(8,128)(2,1)}), bf16[16,288,128]{2,1,0:T(8,128)(2,1)S(1)}, u32[]{:S(2)}, u32[]{:S(2)}) async-start(bf16[16,288,128]{2,1,0:T(8,128)(2,1)} %long_convs.3), calls=%async_computation.1 | async-start | bytes 2359296 | tf_op jit(solution)/shard_map/all_to_all | solution.py:713
  156.5 1.0 copy-start

commit v11 on v10

--- a/solution.py
+++ b/solution.py
@@ -96,30 +96,24 @@
         out_ref[:, out_ref.shape[1] - LANES :] = terms.astype(BF16)
 
 
-def attend_own_kernel(
-    steps, place_ref, q_ref, k_ref, v_ref, part0_ref, part1_ref, log0_ref, log1_ref, out_ref
-):
+def attend_merge_kernel(place_ref, q_ref, k_ref, v_ref, part_ref, log_ref, _, out_ref):
     rows, width = q_ref.shape
     heads = width // HEAD_DIM
     step = pl.program_id(0)
     row = lax.broadcasted_iota(jnp.int32, (rows, rows), 0)
     col = lax.broadcasted_iota(jnp.int32, (rows, rows), 1)
     own_ok = col <= row
-    lane = lax.broadcasted_iota(jnp.int32, (rows, LANES), 1)
+    lane = lax.broadcasted_iota(jnp.int32, (rows, LANES), 1) & (LOG_LANES - 1)
     has_prev = jnp.broadcast_to(place_ref[0], (rows, 1)) > 0
-    late = step >= steps
     places = places_of(width)
-    terms = jnp.where(late, log1_ref[...].astype(F32), log0_ref[...].astype(F32))
-    first = jnp.where(late, step - steps, step) * heads
+    terms = log_ref[...].astype(F32)
     scores = [
         lax.dot_general(q_ref[:, at], k_ref[:, at], NT, preferred_element_type=F32) * SCALE
         for at in places
     ]
     scores = [jnp.where(own_ok, score, -jnp.inf) for score in scores]
     logs = [
-        jnp.sum(
-            jnp.where((lane & (LOG_LANES - 1)) == first + head, terms, 0.0), axis=1, keepdims=True
-        )
+        jnp.sum(jnp.where(lane == step * heads + head, terms, 0.0), axis=1, keepdims=True)
         for head in range(heads)
     ]
     logs = [jnp.where(has_prev, log, -jnp.inf) for log in logs]
@@ -136,9 +130,39 @@
         jnp.dot(weight, v_ref[:, at], preferred_element_type=F32) for weight, at in zip(weights, places)
     ]
     for head, at in enumerate(places):
-        part = jnp.where(late, part1_ref[:, at].astype(F32), part0_ref[:, at].astype(F32))
-        total = mixed[head] + (prevs[head] * inverses[head]) * part
+        total = mixed[head] + (prevs[head] * inverses[head]) * part_ref[:, at].astype(F32)
         out_ref[:, at] = total.astype(BF16)
+
+
+def attend_whole_kernel(place_ref, q_ref, k_ref, v_ref, kp_ref, vp_ref, out_ref):
+    rows, width = q_ref.shape
+    row = lax.broadcasted_iota(jnp.int32, (rows, rows), 0)
+    col = lax.broadcasted_iota(jnp.int32, (rows, rows), 1)
+    own_ok = col <= row
+    prev_ok = jnp.broadcast_to(place_ref[0], (rows, rows)) > 0
+    places = places_of(width)
+
+    def scores(ref, allowed):
+        products = [
+            lax.dot_general(q_ref[:, at], ref[:, at], NT, preferred_element_type=F32) for at in places
+        ]
+        return [jnp.where(allowed, product * SCALE, -jnp.inf) for product in products]
+
+    own, prev = scores(k_ref, own_ok), scores(kp_ref, prev_ok)
+    largest = [jnp.max(jnp.maximum(o, p), axis=1, keepdims=True) for o, p in zip(own, prev)]
+    own = [jnp.exp(o - top) for o, top in zip(own, largest)]
+    prev = [jnp.exp(p - top) for p, top in zip(prev, largest)]
+    totals = [jnp.sum(o + p, axis=1, keepdims=True) for o, p in zip(own, prev)]
+    inverses = [1.0 / total for total in totals]
+    own = [(o * inverse).astype(BF16) for o, inverse in zip(own, inverses)]
+    prev = [(p * inverse).astype(BF16) for p, inverse in zip(prev, inverses)]
+    mixed = [
+        jnp.dot(o, v_ref[:, at], preferred_element_type=F32)
+        + jnp.dot(p, vp_ref[:, at], preferred_element_type=F32)
+        for o, p, at in zip(own, prev, places)
+    ]
+    for head, at in enumerate(places):
+        out_ref[:, at] = mixed[head].astype(BF16)
 
 
 def attend_cost(rows, channels):
@@ -150,50 +174,63 @@
     )
 
 
-def attend_next(query, key, value, part):
+def attend_next(query, key, value):
     rows, channels = query.shape
     tile = min(512, channels)
-    steps = channels // tile
-    there = pl.BlockSpec((rows, tile), lambda i: (0, part * steps + i))
+    block = pl.BlockSpec((rows, tile), lambda i: (0, i))
     return pl.pallas_call(
         attend_next_kernel,
-        grid=(steps,),
-        in_specs=[pl.BlockSpec((rows, tile), lambda i: (0, i)), there, there],
+        grid=(channels // tile,),
+        in_specs=[block] * 3,
         out_specs=pl.BlockSpec((rows, channels + LANES), lambda i: (0, 0)),
         out_shape=jax.ShapeDtypeStruct((rows, channels + LANES), BF16),
         scratch_shapes=[pltpu.VMEM((rows, LANES), F32)],
-        compiler_params=params(),
+        compiler_params=params(LONG_VMEM),
         cost_estimate=attend_cost(rows, channels),
         name="attend_next",
     )(query, key, value)
 
 
-def attend_own(query, key, value, parts, position):
+def attend(query, key, value, part, previous, position):
     rows, channels = query.shape
-    tile = min(512, channels // 2)
-    steps = channels // 2 // tile
-    block = pl.BlockSpec((rows, tile), lambda i: (0, i))
-    log_at = channels // 2 // LANES
-    log = pl.BlockSpec((rows, LANES), lambda i: (0, log_at))
+    half = channels // 2
+    tile = min(512, half)
+    steps = half // tile
+    place = position.astype(jnp.int32).reshape(1)
+    smem = pl.BlockSpec(memory_space=pltpu.SMEM)
+    first = pl.BlockSpec((rows, tile), lambda i: (0, i))
+    second = pl.BlockSpec((rows, tile), lambda i: (0, steps + i))
+    out = jax.ShapeDtypeStruct((rows, channels), BF16)
+    whole = pl.pallas_call(
+        attend_whole_kernel,
+        grid=(steps,),
+        in_specs=[smem, second, second, second, first, pl.BlockSpec((rows, tile), lambda i: (1, i))],
+        out_specs=second,
+        out_shape=out,
+        compiler_params=params(LONG_VMEM),
+        cost_estimate=attend_cost(rows, channels),
+        name="attend_whole",
+    )(place, query, key, value, previous, previous)
+    log_at = half // LANES
     return pl.pallas_call(
-        functools.partial(attend_own_kernel, steps),
-        grid=(2 * steps,),
+        attend_merge_kernel,
+        grid=(steps,),
         in_specs=[
-            pl.BlockSpec(memory_space=pltpu.SMEM),
-            block,
-            block,
-            block,
-            pl.BlockSpec((rows, tile), lambda i: (0, jnp.minimum(i, steps - 1))),
-            pl.BlockSpec((rows, tile), lambda i: (0, jnp.maximum(i - steps, 0))),
-            log,
-            log,
+            smem,
+            first,
+            first,
+            first,
+            first,
+            pl.BlockSpec((rows, LANES), lambda i: (0, log_at)),
+            pl.BlockSpec(memory_space=pl.ANY),
         ],
-        out_specs=block,
-        out_shape=jax.ShapeDtypeStruct((rows, channels), BF16),
-        compiler_params=params(),
-        cost_estimate=attend_cost(rows, channels),
-        name="attend_own",
-    )(position.astype(jnp.int32).reshape(1), query, key, value, *parts, *parts)
+        out_specs=first,
+        out_shape=out,
+        input_output_aliases={6: 0},
+        compiler_params=params(LONG_VMEM),
+        cost_estimate=attend_cost(rows, half),
+        name="attend_merge",
+    )(place, query, key, value, part, part, whole)
 
 
 def edge_kernel(first, *refs):
@@ -682,20 +719,17 @@
     position = lax.axis_index("ctx")
     tail = shifted(edge_rows((hyena_query, hyena_key, hyena_value), False), "ctx", 1)
     half = channels // 2
-    early, tail = lax.optimization_barrier((query_heads[:, :half], tail))
-    early = shifted(early, "ctx", -1)
     chunks = 2 if gpd % 4 == 0 else 1
     cpd, gpd = cpd // chunks, gpd // chunks
     send = before_exchange(
         hyena_query, hyena_key, hyena_value, output_grad, tail, short_filter, long_filter, n, chunks
     )
-    send, early, late, *sources = lax.optimization_barrier(
-        (send, early, query_heads[:, half:], output_grad, hyena_key, hyena_value)
+    send, query, key, value, *sources = lax.optimization_barrier(
+        (send, query_heads, key_heads, value_heads, output_grad, hyena_key, hyena_value)
     )
     received = lax.all_to_all(send, "ctx", split_axis=0, concat_axis=0, tiled=True)
-    following = shifted(edge_rows(sources, True), "ctx", -1)
-    late = shifted(late, "ctx", -1)
-    parts = [shifted(attend_next(early, key_heads, value_heads, 0), "ctx", 1)]
+    query_next = shifted(query[:, :half], "ctx", -1)
+    previous = shifted(jnp.concatenate([key[:, half:], value[:, half:]], 0), "ctx", 1)
     returned = []
     for chunk in range(chunks):
         raw = ()
@@ -704,14 +738,15 @@
             raw = (raw, total_over(squares, "tp"))
         results = long_convs(received, raw, cpd, gpd, chunk, chunks)
         if chunk == 0:
-            results, received, following, late, parts[0] = lax.optimization_barrier(
-                (results, received, following, late, parts[0])
+            results, received, query_next, previous, *sources = lax.optimization_barrier(
+                (results, received, query_next, previous, *sources)
             )
-            parts.append(shifted(attend_next(late, key_heads, value_heads, 1), "ctx", 1))
+            part = shifted(attend_next(query_next, key_heads, value_heads), "ctx", 1)
+            following = shifted(edge_rows(sources, True), "ctx", -1)
         else:
-            results, parts[1] = lax.optimization_barrier((results, parts[1]))
+            results, part, following = lax.optimization_barrier((results, part, following))
         returned.append(lax.all_to_all(results, "ctx", split_axis=0, concat_axis=0, tiled=True))
-    attention = attend_own(query_heads, key_heads, value_heads, parts, position)
+    attention = attend(query_heads, key_heads, value_heads, part, previous, position)
     bound = math.sqrt(rows * n * groups * tp)
     grads = ()
     for chunk in range(chunks):

time: 165 us -> 167 us (1.012)
  Pallas kernels: 60.9 us -> 57.7 us
  waiting for transfers between devices: 65.7 us -> 67.5 us
    all_to_all x1, waiting for transfers between devices: 36.3 us -> 41.5 us  [on_device(): lax.all_to_all(send, 'ctx', split_axis=0, concat_axis=0, tiled=True)]
    pallas_call x3, Pallas kernels: 17.2 us -> 12.3 us  [the longest x1 4.78 us: attend(): pl.pallas_call(attend_whole_kernel, grid=(steps,), in_specs=[smem, second...]
    ppermute x1, waiting for transfers between devices: 2.29 us -> 0.01 us  [total_over(): lax.ppermute(value, axis, [(i, i ^ distance) for i in range(size)])]
    ppermute x6 -> x5, waiting for transfers between devices: 13.5 us -> 12.1 us  [shifted(): return lax.ppermute(block, axis, route)]
    ppermute x6 -> x5, starting transfers between devices: 14.2 us -> 14.5 us  [shifted(): return lax.ppermute(block, axis, route)]
    unnamed x16 -> x18, local copies, waits for them, and re-layouts: 3.79 us -> 3.57 us
  transfers between devices with their start and end apart: 10 -> 9, of which waited for: 6 -> 5; matrix products, arithmetic and copies ran while one was open for 1% -> 1% of each run, Pallas kernels for 32% -> 25%
where the time goes in v11:
time: 167 us; the launch traced here: 165 us
  waiting for transfers between devices  67.5 us (40%)
  Pallas kernels  57.7 us (35%)
  starting transfers between devices  31.2 us (19%)
  local copies, waits for them, and re-layouts  5.57 us (3%)
  between operations  2.1 us (1%)
    all_to_all x1, waiting for transfers between devices, on_device(): lax.all_to_all(send, 'ctx', split_axis=0, concat_axis=0, tiled=True)  41.5 us
    ppermute x5, starting transfers between devices, shifted(): return lax.ppermute(block, axis, route)  14.5 us
    all_to_all x2, waiting for transfers between devices, on_device(): lax.all_to_all(results, 'ctx', split_axis=0, concat_axis=0, tiled=True)  13.9 us
    pallas_call x2, Pallas kernels, after_exchange(): pl.pallas_call(functools.partial(after_kernel, cpd, gpd, chunks, last, bo...  12.8 us
    ppermute x5, waiting for transfers between devices, shifted(): return lax.ppermute(block, axis, route)  12.1 us
    pallas_call x2, Pallas kernels, long_convs(): pl.pallas_call(functools.partial(conv_kernel, cpd, gpd), grid=(1,), in_sp...  10.6 us
    all_to_all x2, starting transfers between devices, on_device(): lax.all_to_all(results, 'ctx', split_axis=0, concat_axis=0, tiled=True)  9.95 us
    pallas_call x1, Pallas kernels, filter_products(): pl.pallas_call(functools.partial(gram_kernel, cpd, gpd, chunks), in_specs...  9.78 us
  transfers between devices with their start and end apart: 9, of which 5 were waited for; matrix products, arithmetic and copies ran while one was open for 1% of the time, Pallas kernels for 25%

profile of v11, /device:TPU:16, one launch (start us, length us, event | category | flops | bytes accessed | tf_op | source)
XLA Modules:
  0.0 165.2 jit_solution(9328632408732707000)
XLA Ops:
  0.6 1.7 %edge_rows.2 = bf16[24,4096]{1,0:T(8,128)(2,1)} custom-call(bf16[128,4096]{1,0:T(8,128)(2,1)} %q_ref.3, bf16[128,4096]{1,0:T(8,128)(2,1)} %k_ref.11, bf16[128,4096]{1,0:T(8,128)(2,1)} %v_ref.11), custom_call_target="tpu_custom_call" | custom-call | tf_op jit(solution)/shard_map/edge_rows/pallas_call | solution.py:246
  2.4 1.9 %collective-permute-start = (bf16[24,4096]{1,0:T(8,128)(2,1)}, bf16[24,4096]{1,0:T(8,128)(2,1)S(1)}, u32[]{:S(2)}, u32[]{:S(2)}) collective-permute-start(bf16[24,4096]{1,0:T(8,128)(2,1)} %edge_rows.2), channel_id=1, source_target_pairs={{0,2},{2,4},{4,6},{6,8},{8,10},{10,12},{12,14},{14,16},{16,18},{18... | collective-permute-start | bytes 589832 | tf_op jit(solution)/shard_map/ppermute | solution.py:27
  4.3 6.2 %collective-permute-done.tail_ref = bf16[24,4096]{1,0:T(8,128)(2,1)S(1)} collective-permute-done((bf16[24,4096]{1,0:T(8,128)(2,1)}, bf16[24,4096]{1,0:T(8,128)(2,1)S(1)}, u32[]{:S(2)}, u32[]{:S(2)}) %collective-permute-start) | collective-permute-done | bytes 196640 | tf_op jit(solution)/shard_map/ppermute | solution.py:27
  10.4 0.7 copy-done.7
  11.1 8.8 %before_exchange.1 = bf16[16,544,128]{2,1,0:T(8,128)(2,1)} custom-call(bf16[128,4096]{1,0:T(8,128)(2,1)} %q_ref.3, bf16[128,4096]{1,0:T(8,128)(2,1)} %k_ref.11, bf16[128,4096]{1,0:T(8,128)(2,1)} %v_ref.11, bf16[128,4096]{1,0:T(8,128)(2,1)} %og_ref.5, bf16[24,4096]{1,0:T(8,128)(2,1)} %copy-done.7, f32[3,7,4096]{2,1,0:T(8,128)} %taps_ref.5, f32[128,256]{1,0:T(8,128)} %long_ref.1), custom_call_target="tpu_custom_call" | custom-call | flops 26214400 | bytes 6291456 | tf_op jit(solution)/shard_map/before_exchange/pallas_call | solution.py:328
  20.0 5.3 %all-to-all-start = ((bf16[16,544,128]{2,1,0:T(8,128)(2,1)}), bf16[16,544,128]{2,1,0:T(8,128)(2,1)}, u32[]{:S(2)}, u32[]{:S(2)}) async-start(bf16[16,544,128]{2,1,0:T(8,128)(2,1)} %before_exchange.1), calls=%async_computation | async-start | bytes 4456448 | tf_op jit(solution)/shard_map/all_to_all | solution.py:730
  25.3 1.0 slice-done
  26.5 1.0 pad_maximum_fusion
  27.5 2.0 %collective-permute-start.2 = (bf16[256,2048]{1,0:T(8,128)(2,1)}, bf16[256,2048]{1,0:T(8,128)(2,1)}, u32[]{:S(2)}, u32[]{:S(2)}) collective-permute-start(bf16[256,2048]{1,0:T(8,128)(2,1)} %pad_maximum_fusion), channel_id=1, source_target_pairs={{0,2},{2,4},{4,6},{6,8},{8,10},{10,12},{12,14},{14,16},{16,18},{18... | collective-permute-start | bytes 3145736 | tf_op jit(solution)/shard_map/ppermute | solution.py:27
  29.6 0.8 slice.9
  30.4 4.4 %collective-permute-start.1 = (bf16[128,2048]{1,0:T(8,128)(2,1)}, bf16[128,2048]{1,0:T(8,128)(2,1)}, u32[]{:S(2)}, u32[]{:S(2)}) collective-permute-start(bf16[128,2048]{1,0:T(8,128)(2,1)} %slice.9), channel_id=1, source_target_pairs={{2,0},{4,2},{6,4},{8,6},{10,8},{12,10},{14,12},{16,14},{18,16},{20... | collective-permute-start | bytes 1572872 | tf_op jit(solution)/shard_map/ppermute | solution.py:27
  34.8 41.5 %all-to-all-done.in_ref = bf16[16,544,128]{2,1,0:T(8,128)(2,1)} async-done(((bf16[16,544,128]{2,1,0:T(8,128)(2,1)}), bf16[16,544,128]{2,1,0:T(8,128)(2,1)}, u32[]{:S(2)}, u32[]{:S(2)}) %all-to-all-start) | async-done | bytes 2228256 | tf_op jit(solution)/shard_map/all_to_all | solution.py:730
  76.3 5.3 %long_convs.2 = bf16[16,272,128]{2,1,0:T(8,128)(2,1)S(1)} custom-call(bf16[16,544,128]{2,1,0:T(8,128)(2,1)} %all-to-all-done.in_ref), custom_call_target="tpu_custom_call" | custom-call | flops 2147483648 | bytes 2228224 | tf_op jit(solution)/shard_map/long_convs/pallas_call | solution.py:443
  81.6 1.0 copy-done.6
  82.6 4.5 %collective-permute-done.2.kp_ref.vp_ref = bf16[256,2048]{1,0:T(8,128)(2,1)} collective-permute-done((bf16[256,2048]{1,0:T(8,128)(2,1)}, bf16[256,2048]{1,0:T(8,128)(2,1)}, u32[]{:S(2)}, u32[]{:S(2)}) %collective-permute-start.2) | collective-permute-done | bytes 1048608 | tf_op jit(solution)/shard_map/ppermute | solution.py:27
  87.1 4.3 %all-to-all-start.2 = ((bf16[16,272,128]{2,1,0:T(8,128)(2,1)}), bf16[16,272,128]{2,1,0:T(8,128)(2,1)}, u32[]{:S(2)}, u32[]{:S(2)}) async-start(bf16[16,272,128]{2,1,0:T(8,128)(2,1)} %copy-done.6), calls=%async_computation.2 | async-start | bytes 2228224 | tf_op jit(solution)/shard_map/all_to_all | solution.py:748
  91.4 4.3 %attend_next.1 = bf16[128,2176]{1,0:T(8,128)(2,1)} custom-call(bf16[128,2048]{1,0:T(8,128)(2,1)} %collective-permute-done.1.q_ref, bf16[128,4096]{1,0:T(8,128)(2,1)S(1)} %copy-done, bf16[128,4096]{1,0:T(8,128)(2,1)S(1)} %copy-done.1), custom_call_target="tpu_custom_call" | custom-call | flops 134217728 | bytes 2621440 | tf_op jit(solution)/shard_map/attend_next/pallas_call | solution.py:181
  95.7 2.0 %collective-permute-start.4 = (bf16[128,2176]{1,0:T(8,128)(2,1)}, bf16[128,2176]{1,0:T(8,128)(2,1)S(1)}, u32[]{:S(2)}, u32[]{:S(2)}) collective-permute-start(bf16[128,2176]{1,0:T(8,128)(2,1)} %attend_next.1), channel_id=1, source_target_pairs={{0,2},{2,4},{4,6},{6,8},{8,10},{10,12},{12,14},{14,16},{16,18},{18... | collective-permute-start | bytes 1671176 | tf_op jit(solution)/shard_map/ppermute | solution.py:27
  97.7 9.8 %filter_products.1 = (bf16[16,16,128]{2,1,0:T(8,128)(2,1)S(1)}, f32[1,1]{1,0:T(1,128)}) custom-call(bf16[16,544,128]{2,1,0:T(8,128)(2,1)} %all-to-all-done.in_ref), custom_call_target="tpu_custom_call" | custom-call | flops 2147483648 | bytes 2228224 | tf_op jit(solution)/shard_map/filter_products/pallas_call | solution.py:523
  107.5 1.5 collective-permute-start.3
  109.0 1.7 %edge_rows.3 = bf16[24,4096]{1,0:T(8,128)(2,1)} custom-call(bf16[128,4096]{1,0:T(8,128)(2,1)} %og_ref.5, bf16[128,4096]{1,0:T(8,128)(2,1)} %k_ref.11, bf16[128,4096]{1,0:T(8,128)(2,1)} %v_ref.11), custom_call_target="tpu_custom_call" | custom-call | tf_op jit(solution)/shard_map/edge_rows/pallas_call | solution.py:246
  110.7 4.2 %collective-permute-start.5 = (bf16[24,4096]{1,0:T(8,128)(2,1)}, bf16[24,4096]{1,0:T(8,128)(2,1)S(1)}, u32[]{:S(2)}, u32[]{:S(2)}) collective-permute-start(bf16[24,4096]{1,0:T(8,128)(2,1)} %edge_rows.3), channel_id=1, source_target_pairs={{2,0},{4,2},{6,4},{8,6},{10,8},{12,10},{14,12},{16,14},{18,16},{20... | collective-permute-start | bytes 589832 | tf_op jit(solution)/shard_map/ppermute | solution.py:27
  116.2 5.3 %long_convs.3 = bf16[16,288,128]{2,1,0:T(8,128)(2,1)S(1)} custom-call(bf16[16,544,128]{2,1,0:T(8,128)(2,1)} %all-to-all-done.in_ref, bf16[16,16,128]{2,1,0:T(8,128)(2,1)S(1)} %get-tuple-element.44.refs_0_, f32[1,1]{1,0:T(1,128)S(6)} %add.3.refs_1_), custom_call_target="tpu_custom_call" | custom-call | flops 2147483648 | bytes 2359296 | tf_op jit(solution)/shard_map/long_convs/pallas_call | solution.py:443
  121.5 1.0 copy-done.5
  122.6 1.5 collective-permute-done.4.part_ref.log_ref
  124.1 0.8 copy-done.3
  124.9 5.7 %all-to-all-start.1 = ((bf16[16,288,128]{2,1,0:T(8,128)(2,1)}), bf16[16,288,128]{2,1,0:T(8,128)(2,1)}, u32[]{:S(2)}, u32[]{:S(2)}) async-start(bf16[16,288,128]{2,1,0:T(8,128)(2,1)} %copy-done.5), calls=%async_computation.1 | async-start | bytes 2359296 | tf_op jit(solution)/shard_map/all_to_all | solution.py:748
  130.6 4.8 %attend_whole.1._ = bf16[128,4096]{1,0:T(8,128)(2,1)} custom-call(s32[1]{0:T(128)} %bitcast.place_ref, bf16[128,4096]{1,0:T(8,128)(2,1)S(1)} %copy-done.2, bf16[128,4096]{1,0:T(8,128)(2,1)S(1)} %copy-done, bf16[128,4096]{1,0:T(8,128)(2,1)S(1)} %copy-done.1, bf16[256,2048]{1,0:T(8,128)(2,1)} %collective-permute-done.2.kp_ref.vp_ref, ...), custom_call_target="tpu_custom_call" | custom-call | flops 268435456 | bytes 5242880 | tf_op jit(solution)/shard_map/attend_whole/pallas_call | solution.py:204
  135.3 3.2 %attend_merge.1 = bf16[128,4096]{1,0:T(8,128)(2,1)} custom-call(s32[1]{0:T(128)} %bitcast.place_ref, bf16[128,4096]{1,0:T(8,128)(2,1)S(1)} %copy-done.2, bf16[128,4096]{1,0:T(8,128)(2,1)S(1)} %copy-done, bf16[128,4096]{1,0:T(8,128)(2,1)S(1)} %copy-done.1, bf16[128,2176]{1,0:T(8,128)(2,1)S(1)} %copy-done.4, ...), custom_call_target="tpu_custom_call", output_to_operand_aliasing={{}: (6, {})} | custom-call | flops 134217728 | bytes 2621440 | tf_op jit(solution)/shard_map/attend_merge/pallas_call | solution.py:215
  138.5 6.3 %after_exchange.2 = (bf16[128,4096]{1,0:T(8,128)(2,1)}, bf16[128,4096]{1,0:T(8,128)(2,1)}, bf16[128,4096]{1,0:T(8,128)(2,1)}) custom-call(bf16[16,272,128]{2,1,0:T(8,128)(2,1)} %all-to-all-done.2.in_ref, bf16[128,4096]{1,0:T(8,128)(2,1)} %og_ref.5, bf16[128,4096]{1,0:T(8,128)(2,1)} %k_ref.11, bf16[128,4096]{1,0:T(8,128)(2,1)} %v_ref.11, ...), custom_call_target="tpu_custom_call" | custom-call | flops 23592960 | bytes 4718592 | tf_op jit(solution)/shard_map/after_exchange/pallas_call | solution.py:677
  144.8 13.9 %all-to-all-done.1.in_ref = bf16[16,288,128]{2,1,0:T(8,128)(2,1)} async-done(((bf16[16,288,128]{2,1,0:T(8,128)(2,1)}), bf16[16,288,128]{2,1,0:T(8,128)(2,1)}, u32[]{:S(2)}, u32[]{:S(2)}) %all-to-all-start.1) | async-done | bytes 1179680 | tf_op jit(solution)/shard_map/all_to_all | solution.py:748
  158.6 6.6 %after_exchange.3 = (bf16[128,4096]{1,0:T(8,128)(2,1)}, bf16[128,4096]{1,0:T(8,128)(2,1)}, bf16[128,4096]{1,0:T(8,128)(2,1)}, f32[128,256]{1,0:T(8,128)}) custom-call(bf16[16,288,128]{2,1,0:T(8,128)(2,1)} %all-to-all-done.1.in_ref, bf16[128,4096]{1,0:T(8,128)(2,1)} %og_ref.5, ...), custom_call_target="tpu_custom_call", output_to_operand_aliasing={{0}: (7, {}), {1}: (8, {}), {2}: (9, {})} | custom-call | flops 23592960 | bytes 4718592 | tf_op jit(solution)/shard_map/after_exchange/pallas_call | solution.py:677
  (21 shorter events, 0.2 us)
Async XLA Ops:
  2.4 8.1 %collective-permute-start = (bf16[24,4096]{1,0:T(8,128)(2,1)}, bf16[24,4096]{1,0:T(8,128)(2,1)S(1)}, u32[]{:S(2)}, u32[]{:S(2)}) collective-permute-start(bf16[24,4096]{1,0:T(8,128)(2,1)} %edge_rows.2), channel_id=1, source_target_pairs={{0,2},{2,4},{4,6},{6,8},{8,10},{10,12},{12,14},{14,16},{16,18},{18... | collective-permute-start | bytes 589832 | tf_op jit(solution)/shard_map/ppermute | solution.py:27
  10.4 0.7 copy-start.7
  20.0 56.4 %all-to-all-start = ((bf16[16,544,128]{2,1,0:T(8,128)(2,1)}), bf16[16,544,128]{2,1,0:T(8,128)(2,1)}, u32[]{:S(2)}, u32[]{:S(2)}) async-start(bf16[16,544,128]{2,1,0:T(8,128)(2,1)} %before_exchange.1), calls=%async_computation | async-start | bytes 4456448 | tf_op jit(solution)/shard_map/all_to_all | solution.py:730
  25.3 1.0 slice-start
  25.3 1.2 slice-start.1
  25.3 4.3 %copy-start.2 = (bf16[128,4096]{1,0:T(8,128)(2,1)S(1)}, bf16[128,4096]{1,0:T(8,128)(2,1)}, u32[]{:S(2)}) copy-start(bf16[128,4096]{1,0:T(8,128)(2,1)} %q_ref.5) | copy-start | bytes 3145732
  27.5 59.6 %collective-permute-start.2 = (bf16[256,2048]{1,0:T(8,128)(2,1)}, bf16[256,2048]{1,0:T(8,128)(2,1)}, u32[]{:S(2)}, u32[]{:S(2)}) collective-permute-start(bf16[256,2048]{1,0:T(8,128)(2,1)} %pad_maximum_fusion), channel_id=1, source_target_pairs={{0,2},{2,4},{4,6},{6,8},{8,10},{10,12},{12,14},{14,16},{16,18},{18... | collective-permute-start | bytes 3145736 | tf_op jit(solution)/shard_map/ppermute | solution.py:27
  30.4 52.2 %collective-permute-start.1 = (bf16[128,2048]{1,0:T(8,128)(2,1)}, bf16[128,2048]{1,0:T(8,128)(2,1)}, u32[]{:S(2)}, u32[]{:S(2)}) collective-permute-start(bf16[128,2048]{1,0:T(8,128)(2,1)} %slice.9), channel_id=1, source_target_pairs={{2,0},{4,2},{6,4},{8,6},{10,8},{12,10},{14,12},{16,14},{18,16},{20... | collective-permute-start | bytes 1572872 | tf_op jit(solution)/shard_map/ppermute | solution.py:27
  81.6 1.0 copy-start.6
  82.6 8.8 %copy-start = (bf16[128,4096]{1,0:T(8,128)(2,1)S(1)}, bf16[128,4096]{1,0:T(8,128)(2,1)}, u32[]{:S(2)}) copy-start(bf16[128,4096]{1,0:T(8,128)(2,1)} %k_ref.9) | copy-start | bytes 3145732
  82.6 8.8 %copy-start.1 = (bf16[128,4096]{1,0:T(8,128)(2,1)S(1)}, bf16[128,4096]{1,0:T(8,128)(2,1)}, u32[]{:S(2)}) copy-start(bf16[128,4096]{1,0:T(8,128)(2,1)} %v_ref.9) | copy-start | bytes 3145732
  87.1 37.8 %all-to-all-start.2 = ((bf16[16,272,128]{2,1,0:T(8,128)(2,1)}), bf16[16,272,128]{2,1,0:T(8,128)(2,1)}, u32[]{:S(2)}, u32[]{:S(2)}) async-start(bf16[16,272,128]{2,1,0:T(8,128)(2,1)} %copy-done.6), calls=%async_computation.2 | async-start | bytes 2228224 | tf_op jit(solution)/shard_map/all_to_all | solution.py:748
  95.7 28.3 %collective-permute-start.4 = (bf16[128,2176]{1,0:T(8,128)(2,1)}, bf16[128,2176]{1,0:T(8,128)(2,1)S(1)}, u32[]{:S(2)}, u32[]{:S(2)}) collective-permute-start(bf16[128,2176]{1,0:T(8,128)(2,1)} %attend_next.1), channel_id=1, source_target_pairs={{0,2},{2,4},{4,6},{6,8},{8,10},{10,12},{12,14},{14,16},{16,18},{18... | collective-permute-start | bytes 1671176 | tf_op jit(solution)/shard_map/ppermute | solution.py:27
  107.5 7.4 %collective-permute-start.3 = (f32[1,1]{1,0:T(1,128)}, f32[1,1]{1,0:T(1,128)}, u32[]{:S(2)}, u32[]{:S(2)}) collective-permute-start(f32[1,1]{1,0:T(1,128)} %get-tuple-element.45), channel_id=1, source_target_pairs={{0,1},{1,0},{2,3},{3,2},{4,5},{5,4},{6,7},{7,6},{8,9},{9,8},{10,11... | collective-permute-start | bytes 20 | tf_op jit(solution)/shard_map/ppermute | solution.py:34
  110.7 11.9 %collective-permute-start.5 = (bf16[24,4096]{1,0:T(8,128)(2,1)}, bf16[24,4096]{1,0:T(8,128)(2,1)S(1)}, u32[]{:S(2)}, u32[]{:S(2)}) collective-permute-start(bf16[24,4096]{1,0:T(8,128)(2,1)} %edge_rows.3), channel_id=1, source_target_pairs={{2,0},{4,2},{6,4},{8,6},{10,8},{12,10},{14,12},{16,14},{18,16},{20... | collective-permute-start | bytes 589832 | tf_op jit(solution)/shard_map/ppermute | solution.py:27
  121.5 1.0 copy-start.5
  122.6 15.9 %copy-start.8 = (bf16[24,4096]{1,0:T(8,128)(2,1)}, bf16[24,4096]{1,0:T(8,128)(2,1)S(1)}, u32[]{:S(2)}) copy-start(bf16[24,4096]{1,0:T(8,128)(2,1)S(1)} %collective-permute-done.5.next_ref) | copy-start | bytes 589828
  124.1 0.8 copy-start.3
  124.9 33.8 %all-to-all-start.1 = ((bf16[16,288,128]{2,1,0:T(8,128)(2,1)}), bf16[16,288,128]{2,1,0:T(8,128)(2,1)}, u32[]{:S(2)}, u32[]{:S(2)}) async-start(bf16[16,288,128]{2,1,0:T(8,128)(2,1)} %copy-done.5), calls=%async_computation.1 | async-start | bytes 2359296 | tf_op jit(solution)/shard_map/all_to_all | solution.py:748
  130.5 4.8 %copy-start.4 = (bf16[128,2176]{1,0:T(8,128)(2,1)S(1)}, bf16[128,2176]{1,0:T(8,128)(2,1)}, u32[]{:S(2)}) copy-start(bf16[128,2176]{1,0:T(8,128)(2,1)} %copy-done.3) | copy-start | bytes 1671172

commit v12 on v11

--- a/solution.py
+++ b/solution.py
@@ -270,13 +270,32 @@
     return [slice(j * LANES, (j + 1) * LANES) for j in range(width // LANES)]
 
 
-def before_kernel(
-    cpd, gpd, q_ref, k_ref, v_ref, og_ref, tail_ref, taps_ref, long_ref, send_ref,
-    long_rows, ext_q, ext_k, ext_v,
-):
+PAIR = 2
+
+
+def put_pairs(ref, dest, channel, gw, first, second):
+    width = PAIR * gw
+    for piece in range(first.shape[0] // width):
+        at = slice(piece * width, (piece + 1) * width)
+        low = 2 * (channel + piece * width)
+        ref[dest, low : low + width, :] = first[at]
+        ref[dest, low + width : low + 2 * width, :] = second[at]
+
+
+def get_pairs(ref, dest, channel, count, gw, which):
+    width = PAIR * gw
+    lows = [2 * (channel + low) + which * width for low in range(0, count, width)]
+    return jnp.concatenate([ref[dest, low : low + width, :] for low in lows], 0)
+
+
+def before_kernel(cpd, gpd, chunks, *refs):
+    *refs, long_ref, send_ref, long_rows, ext_q, ext_k, ext_v = refs
     step = pl.program_id(0)
     groups = long_ref.shape[1]
-    per_tile, _, rows = send_ref.shape
+    per_tile, send_rows, rows = send_ref.shape
+    gw = cpd // gpd
+    filter_rows = send_rows - 2 * cpd * chunks
+    half = groups // chunks
 
     @pl.when(step == 0)
     def _():
@@ -284,131 +303,136 @@
         long_rows[0:groups, :] = long_ref[...].T
 
     turn = reversal(rows)
-    places = columns_of(q_ref.shape[1])
-    tails = [tail_ref[:, at].astype(F32) for at in places]
-
-    def short(which, ref, ext):
-        return taps_causal(
-            ext,
-            [tail[which * EDGE : (which + 1) * EDGE] for tail in tails],
-            [ref[:, at].astype(F32) for at in places],
-            [taps_ref[which, :, at] for at in places],
-        )
-
-    short_k, short_v = short(1, k_ref, ext_k), short(2, v_ref, ext_v)
-    mixed = [(k * v).T.astype(BF16) for k, v in zip(short_k, short_v)]
-    short_q = short(0, q_ref, ext_q)
-    delta = [(og_ref[:, at].astype(F32) * q).T.astype(BF16) for q, at in zip(short_q, places)]
-    delta = [jnp.dot(d, turn, preferred_element_type=F32).astype(BF16) for d in delta]
-    width = min(cpd, LANES)
-    for j in range(len(places)):
-        for piece in range(LANES // width):
-            channel = j * LANES + piece * width
-            dest, low = channel // cpd, channel % cpd
-            rows_at = slice(piece * width, (piece + 1) * width)
-            send_ref[dest, low : low + width, :] = mixed[j][rows_at]
-            send_ref[dest, cpd + low : cpd + low + width, :] = delta[j][rows_at]
-    filter_rows = send_ref.shape[1] - 2 * cpd
+    for chunk in range(chunks):
+        q_ref, k_ref, v_ref, og_ref, tail_ref, taps_ref = refs[6 * chunk : 6 * chunk + 6]
+        places = columns_of(q_ref.shape[1])
+        tails = [tail_ref[:, at].astype(F32) for at in places]
+
+        def short(which, ref, ext, tails=tails, places=places, taps_ref=taps_ref, chunk=chunk):
+            return taps_causal(
+                ext.at[chunk],
+                [tail[which * EDGE : (which + 1) * EDGE] for tail in tails],
+                [ref[:, at].astype(F32) for at in places],
+                [taps_ref[which, :, at] for at in places],
+            )
+
+        short_k, short_v = short(1, k_ref, ext_k), short(2, v_ref, ext_v)
+        mixed = [(k * v).T.astype(BF16) for k, v in zip(short_k, short_v)]
+        short_q = short(0, q_ref, ext_q)
+        delta = [(og_ref[:, at].astype(F32) * q).T.astype(BF16) for q, at in zip(short_q, places)]
+        delta = [jnp.dot(d, turn, preferred_element_type=F32).astype(BF16) for d in delta]
+        width = min(cpd, LANES)
+        for j in range(len(places)):
+            for piece in range(LANES // width):
+                channel = j * LANES + piece * width
+                dest, low = channel // cpd, channel % cpd
+                at = slice(piece * width, (piece + 1) * width)
+                put_pairs(send_ref, dest, chunk * cpd + low, gw, mixed[j][at], delta[j][at])
     for dest in range(per_tile):
-        first = (step * per_tile + dest) * gpd
-        send_ref[dest, 2 * cpd :, :] = long_rows[pl.ds(first, filter_rows), :].astype(BF16)
+        lines = []
+        for chunk in range(chunks):
+            first = chunk * half + (step * per_tile + dest) * gpd
+            lines.append(long_rows[pl.ds(first, filter_rows if chunks == 1 else gpd), :])
+        send_ref[dest, 2 * cpd * chunks :, :] = jnp.concatenate(lines, 0).astype(BF16)
 
 
 def before_exchange(query, key, value, out_grad, tail, taps, long_filter, n, chunks):
     rows, channels = query.shape
     groups = long_filter.shape[1]
     cpd, gpd = channels // (n * chunks), groups // (n * chunks)
-    tile = min(channels // chunks, max(512, cpd))
+    tile = min(channels // chunks, max(512 // chunks, cpd))
     per_tile = tile // cpd
-    filter_rows = round_up(gpd, 16)
-    send_rows = 2 * cpd + filter_rows
+    filter_rows = round_up(gpd * chunks, 16)
+    send_rows = 2 * cpd * chunks + filter_rows
     steps = n // per_tile
-    block = pl.BlockSpec((rows, tile), lambda i: (0, i))
-    ext = pltpu.VMEM((tile // LANES, rows + EDGE, LANES), F32)
+    specs = []
+    for chunk in range(chunks):
+        first = chunk * steps
+        specs += [pl.BlockSpec((rows, tile), lambda i, f=first: (0, f + i))] * 4
+        specs.append(pl.BlockSpec((3 * EDGE, tile), lambda i, f=first: (0, f + i)))
+        specs.append(pl.BlockSpec((3, taps.shape[1], tile), lambda i, f=first: (0, 0, f + i)))
+    ext = pltpu.VMEM((chunks, tile // LANES, rows + EDGE, LANES), F32)
     return pl.pallas_call(
-        functools.partial(before_kernel, cpd, gpd),
-        grid=(channels // tile,),
-        in_specs=[block] * 4
-        + [
-            pl.BlockSpec((3 * EDGE, tile), lambda i: (0, i)),
-            pl.BlockSpec((3, taps.shape[1], tile), lambda i: (0, 0, i)),
-            pl.BlockSpec((rows, groups), lambda i: (0, 0)),
-        ],
-        out_specs=pl.BlockSpec((per_tile, send_rows, rows), lambda i: (i % steps, i // steps, 0)),
-        out_shape=jax.ShapeDtypeStruct((n, chunks * send_rows, rows), BF16),
+        functools.partial(before_kernel, cpd, gpd, chunks),
+        grid=(steps,),
+        in_specs=specs + [pl.BlockSpec((rows, groups), lambda i: (0, 0))],
+        out_specs=pl.BlockSpec((per_tile, send_rows, rows), lambda i: (i, 0, 0)),
+        out_shape=jax.ShapeDtypeStruct((n, send_rows, rows), BF16),
         scratch_shapes=[pltpu.VMEM((round_up(groups, 8) + filter_rows, rows), F32), ext, ext, ext],
         compiler_params=params(),
         cost_estimate=pl.CostEstimate(
             flops=50 * rows * channels, bytes_accessed=12 * rows * channels, transcendentals=0
         ),
         name="before_exchange",
-    )(query, key, value, out_grad, tail, taps, long_filter)
-
-
-def conv_kernel(cpd, gpd, in_ref, *refs):
+    )(*((query, key, value, out_grad, tail, taps) * chunks), long_filter)
+
+
+def conv_kernel(cpd, gpd, chunk, in_ref, filter_ref, *refs):
     *raw_ref, out_ref, taps, wide = refs
+    step = pl.program_id(0)
+    n, _, rows = in_ref.shape
+    gw = cpd // gpd
+    span = n * rows
+    slots = range(PAIR)
+
+    @pl.when(step == 0)
+    def _():
+        taps[:, 0:rows] = jnp.zeros((taps.shape[0], rows), F32)
+        for a in range(n):
+            taps[:, (a + 1) * rows : (a + 2) * rows] = filter_ref[a].astype(F32)
+        for slot in slots:
+            wide[slot, :, 0:rows] = jnp.zeros((rows, rows), BF16)
+
+    bases = []
+    for slot in slots:
+        line = taps[pl.ds(chunk * gpd + PAIR * step + slot, 1), :]
+        line = jnp.broadcast_to(line, (16, span + rows))
+        bases.append(pltpu.roll(line, 0, 1, stride=1, stride_axis=0).astype(BF16))
+    for m in range(rows // 16):
+        for slot in slots:
+            moved = bases[slot] if m == 0 else pltpu.roll(bases[slot], 16 * m, 1)
+            wide[slot, 16 * m : 16 * m + 16, rows:] = moved[:, rows:]
+    stacks = []
+    for slot in slots:
+        x = in_ref[:, slot * gw : (slot + 1) * gw, :]
+        d = in_ref[:, (PAIR + slot) * gw : (PAIR + slot + 1) * gw, :]
+        both = [jnp.concatenate([x[a], d[n - 1 - a]], 0) for a in range(n)]
+        stacks.append(
+            jnp.concatenate([jnp.concatenate([both[a], both[a + 1]], 1) for a in range(0, n, 2)], 0)
+        )
+    totals = [None] * PAIR
+    for k in range(n // 2):
+        skip = 2 * gw * k
+        low = 2 * rows * k
+        for slot in slots:
+            tile = jnp.concatenate(
+                [wide[slot, :, low + rows : low + 3 * rows], wide[slot, :, low : low + 2 * rows]], 0
+            )
+            part = jnp.dot(stacks[slot][: n * gw - skip], tile, preferred_element_type=F32)
+            total = totals[slot]
+            totals[slot] = part if k == 0 else jnp.concatenate([total[:skip], total[skip:] + part], 0)
+    for slot in slots:
+        total = totals[slot]
+        first = pl.multiple_of(2 * PAIR * gw * step + slot * gw, gw)
+        second = pl.multiple_of(2 * PAIR * gw * step + (PAIR + slot) * gw, gw)
+        for a in range(n):
+            at = slice(a % 2 * rows, (a % 2 + 1) * rows)
+            top = a // 2 * 2 * gw
+            out_ref[a, pl.ds(first, gw), :] = total[top : top + gw, at].astype(BF16)
+            out_ref[n - 1 - a, pl.ds(second, gw), :] = total[top + gw : top + 2 * gw, at].astype(BF16)
+
+    @pl.when(step == pl.num_programs(0) - 1)
+    def _():
+        finish_conv(cpd, gw, out_ref, raw_ref)
+
+
+def finish_conv(cpd, gw, out_ref, raw_ref):
+    n, _, rows = out_ref.shape
     upper = lower = 0.0
     if raw_ref:
         *raw_ref, squares_ref = raw_ref
         upper = squares_ref[...].astype(BF16).astype(F32)
         lower = squares_ref[...] - upper
-    n, send_rows, rows = in_ref.shape
-    gw = cpd // gpd
-    span = n * rows
-    filter_rows = send_rows - 2 * cpd
-    taps[:, 0:rows] = jnp.zeros((filter_rows, rows), F32)
-    for a in range(n):
-        taps[:, (a + 1) * rows : (a + 2) * rows] = in_ref[a, 2 * cpd :, :].astype(F32)
-    for slot in range(2):
-        wide[slot, :, 0:rows] = jnp.zeros((rows, rows), BF16)
-
-    def body(i, carry):
-        slots = range(2)
-        firsts = [pl.multiple_of((2 * i + slot) * gw, gw) for slot in slots]
-        seconds = [pl.multiple_of(cpd + (2 * i + slot) * gw, gw) for slot in slots]
-        bases = []
-        for slot in slots:
-            line = jnp.broadcast_to(taps[pl.ds(2 * i + slot, 1), :], (16, span + rows))
-            bases.append(pltpu.roll(line, 0, 1, stride=1, stride_axis=0).astype(BF16))
-        for m in range(rows // 16):
-            for slot in slots:
-                moved = bases[slot] if m == 0 else pltpu.roll(bases[slot], 16 * m, 1)
-                wide[slot, 16 * m : 16 * m + 16, rows:] = moved[:, rows:]
-        stacks = []
-        for slot in slots:
-            x = in_ref[:, pl.ds(firsts[slot], gw), :]
-            d = in_ref[:, pl.ds(seconds[slot], gw), :]
-            both = [jnp.concatenate([x[a], d[n - 1 - a]], 0) for a in range(n)]
-            stacks.append(
-                jnp.concatenate(
-                    [jnp.concatenate([both[a], both[a + 1]], 1) for a in range(0, n, 2)], 0
-                )
-            )
-        totals = [None, None]
-        for k in range(n // 2):
-            skip = 2 * gw * k
-            low = 2 * rows * k
-            for slot in slots:
-                tile = jnp.concatenate(
-                    [wide[slot, :, low + rows : low + 3 * rows], wide[slot, :, low : low + 2 * rows]], 0
-                )
-                part = jnp.dot(stacks[slot][: n * gw - skip], tile, preferred_element_type=F32)
-                total = totals[slot]
-                totals[slot] = (
-                    part if k == 0 else jnp.concatenate([total[:skip], total[skip:] + part], 0)
-                )
-        for slot in slots:
-            total = totals[slot]
-            for a in range(n):
-                at = slice(a % 2 * rows, (a % 2 + 1) * rows)
-                top = a // 2 * 2 * gw
-                out_ref[a, pl.ds(firsts[slot], gw), :] = total[top : top + gw, at].astype(BF16)
-                out_ref[n - 1 - a, pl.ds(seconds[slot], gw), :] = total[
-                    top + gw : top + 2 * gw, at
-                ].astype(BF16)
-        return carry
-
-    lax.fori_loop(0, gpd // 2, body, 0)
     halo_at = 2 * cpd
     row = lax.broadcasted_iota(jnp.int32, (2 * EDGE, 2 * rows), 0)
     lane = lax.broadcasted_iota(jnp.int32, (2 * EDGE, 2 * rows), 1)
@@ -417,7 +441,8 @@
     row_out = lax.broadcasted_iota(jnp.int32, (2 * EDGE, rows), 0)
     for a in range(n):
         if a + 1 < n:
-            results = jnp.concatenate([out_ref[a + 1, 0:cpd, :], out_ref[a + 1, cpd : 2 * cpd, :]], 1)
+            results = [get_pairs(out_ref, a + 1, 0, cpd, gw, which) for which in range(2)]
+            results = jnp.concatenate(results, 1)
             halo = lax.dot_general(
                 pick, results, (((1,), (1,)), ((), ())), preferred_element_type=F32
             )
@@ -436,38 +461,47 @@
 
 def long_convs(received, raw, cpd, gpd, chunk, chunks):
     n, send_rows, rows = received.shape
-    send_rows = send_rows // chunks
-    filter_rows = send_rows - 2 * cpd
+    filter_rows = send_rows - 2 * cpd * chunks
     out_rows = 2 * cpd + 2 * EDGE * max(1, cpd // LANES) + sum(r.shape[1] for r in raw[:1])
     span = n * rows
+    pairs = gpd // PAIR
+    pair_rows = 2 * cpd // pairs
+    filter_at = 2 * cpd * chunks // filter_rows
     return pl.pallas_call(
-        functools.partial(conv_kernel, cpd, gpd),
-        grid=(1,),
-        in_specs=[pl.BlockSpec((n, send_rows, rows), lambda i: (0, chunk, 0))]
+        functools.partial(conv_kernel, cpd, gpd, chunk),
+        grid=(pairs,),
+        in_specs=[
+            pl.BlockSpec((n, pair_rows, rows), lambda i: (0, chunk * pairs + i, 0)),
+            pl.BlockSpec((n, filter_rows, rows), lambda i: (0, filter_at, 0)),
+        ]
         + [pl.BlockSpec(r.shape, lambda i, r=r: (0,) * r.ndim) for r in raw],
         out_specs=pl.BlockSpec((n, out_rows, rows), lambda i: (0, 0, 0)),
         out_shape=jax.ShapeDtypeStruct((n, out_rows, rows), BF16),
         scratch_shapes=[
             pltpu.VMEM((filter_rows, span + rows), F32),
-            pltpu.VMEM((2, rows, span + rows), BF16),
+            pltpu.VMEM((PAIR, rows, span + rows), BF16),
         ],
-        compiler_params=params(LONG_VMEM),
+        compiler_params=params(),
         cost_estimate=pl.CostEstimate(
             flops=4 * cpd * span * span, bytes_accessed=4 * n * out_rows * rows, transcendentals=0
         ),
         name="long_convs",
-    )(received, *raw)
-
-
-def gram_kernel(cpd, gpd, chunks, in_ref, out_ref, squares_ref, gram, raw):
-    n, send_rows, rows = in_ref.shape
-    send_rows = send_rows // chunks
-    gw = cpd // gpd
+    )(received, received, *raw)
+
+
+def gram_kernel(gw, in_ref, out_ref, squares_ref, gram, raw, total_ref):
+    step = pl.program_id(0)
+    n, _, rows = in_ref.shape
     span = n * rows
-    for slot in range(2):
-        gram[slot, :, span:] = jnp.zeros((rows, rows), F32)
-    if gpd * chunks < raw.shape[0]:
+    slots = range(PAIR)
+
+    @pl.when(step == 0)
+    def _():
+        for slot in slots:
+            gram[slot, :, span:] = jnp.zeros((rows, rows), F32)
         raw[...] = jnp.zeros_like(raw)
+        total_ref[...] = jnp.zeros_like(total_ref)
+
     no_rows = jnp.zeros((n * gw, rows), BF16)
 
     def offset(d, k):
@@ -476,63 +510,62 @@
             return d
         return jnp.concatenate([d[n * gw - held :], no_rows[held:]], 0)
 
-    squares = jnp.zeros((1, span), F32)
-    for chunk in range(chunks):
-        base = chunk * send_rows
-
-        def body(i, squares, chunk=chunk, base=base):
-            slots = range(2)
-            turned, shifting = [], []
-            for slot in slots:
-                first = pl.multiple_of(base + (2 * i + slot) * gw, gw)
-                second = pl.multiple_of(base + cpd + (2 * i + slot) * gw, gw)
-                x = in_ref[:, pl.ds(first, gw), :].reshape(n * gw, rows)
-                shifting.append(in_ref[:, pl.ds(second, gw), :].reshape(n * gw, rows))
-                turned.append(x.astype(F32).T.astype(BF16))
-            for k in range(0, n, 2):
-                for slot in slots:
-                    d = shifting[slot]
-                    pairs = jnp.concatenate([offset(d, k), offset(d, k + 1)], 1)
-                    gram[slot, :, k * rows : (k + 2) * rows] = jnp.dot(
-                        turned[slot], pairs, preferred_element_type=F32
-                    )
-            sums = [gram[slot, 0:8, :] for slot in slots]
-            for m in range(1, rows // 8):
-                for slot in slots:
-                    block = gram[slot, 8 * m : 8 * m + 8, :]
-                    sums[slot] = sums[slot] + pltpu.roll(block, 8 * m, 1)
-            sums = [pltpu.roll(total, 0, 1, stride=1, stride_axis=0) for total in sums]
-            for slot in slots:
-                line = jnp.sum(sums[slot], axis=0, keepdims=True)[:, :span]
-                raw[pl.ds(chunk * gpd + 2 * i + slot, 1), :] = line
-                squares = squares + line * line
-            return squares
-
-        squares = lax.fori_loop(0, gpd // 2, body, squares)
-    squares_ref[...] = jnp.sum(squares, axis=1, keepdims=True)
-    turn = reversal(rows)
-    for a in range(n):
-        tile = raw[:, (n - 1 - a) * rows : (n - a) * rows].astype(BF16)
-        out_ref[a] = jnp.dot(tile, turn, preferred_element_type=F32).astype(BF16)
+    turned, shifting = [], []
+    for slot in slots:
+        x = in_ref[:, slot * gw : (slot + 1) * gw, :].reshape(n * gw, rows)
+        d = in_ref[:, (PAIR + slot) * gw : (PAIR + slot + 1) * gw, :]
+        shifting.append(d.reshape(n * gw, rows))
+        turned.append(x.astype(F32).T.astype(BF16))
+    for k in range(0, n, 2):
+        for slot in slots:
+            d = shifting[slot]
+            pairs = jnp.concatenate([offset(d, k), offset(d, k + 1)], 1)
+            gram[slot, :, k * rows : (k + 2) * rows] = jnp.dot(
+                turned[slot], pairs, preferred_element_type=F32
+            )
+    sums = [gram[slot, 0:8, :] for slot in slots]
+    for m in range(1, rows // 8):
+        for slot in slots:
+            sums[slot] = sums[slot] + pltpu.roll(gram[slot, 8 * m : 8 * m + 8, :], 8 * m, 1)
+    sums = [pltpu.roll(total, 0, 1, stride=1, stride_axis=0) for total in sums]
+    for slot in slots:
+        line = jnp.sum(sums[slot], axis=0, keepdims=True)[:, :span]
+        raw[pl.ds(PAIR * step + slot, 1), :] = line
+        total_ref[...] = total_ref[...] + line * line
+
+    @pl.when(step == pl.num_programs(0) - 1)
+    def _():
+        squares_ref[...] = jnp.sum(total_ref[...], axis=1, keepdims=True)
+        turn = reversal(rows)
+        for a in range(n):
+            tile = raw[:, (n - 1 - a) * rows : (n - a) * rows].astype(BF16)
+            out_ref[a] = jnp.dot(tile, turn, preferred_element_type=F32).astype(BF16)
 
 
 def filter_products(received, cpd, gpd, chunks):
     n, _, rows = received.shape
     span = n * rows
     raw_rows = round_up(gpd * chunks, 16)
+    pairs = gpd * chunks // PAIR
+    pair_rows = 2 * cpd * chunks // pairs
     return pl.pallas_call(
-        functools.partial(gram_kernel, cpd, gpd, chunks),
-        in_specs=[pl.BlockSpec(memory_space=pltpu.VMEM)],
-        out_specs=[pl.BlockSpec(memory_space=pltpu.VMEM)] * 2,
+        functools.partial(gram_kernel, cpd // gpd),
+        grid=(pairs,),
+        in_specs=[pl.BlockSpec((n, pair_rows, rows), lambda i: (0, i, 0))],
+        out_specs=[
+            pl.BlockSpec((n, raw_rows, rows), lambda i: (0, 0, 0)),
+            pl.BlockSpec((1, 1), lambda i: (0, 0)),
+        ],
         out_shape=[
             jax.ShapeDtypeStruct((n, raw_rows, rows), BF16),
             jax.ShapeDtypeStruct((1, 1), F32),
         ],
         scratch_shapes=[
-            pltpu.VMEM((2, rows, span + rows), F32),
+            pltpu.VMEM((PAIR, rows, span + rows), F32),
             pltpu.VMEM((raw_rows, span), F32),
+            pltpu.VMEM((1, span), F32),
         ],
-        compiler_params=params(LONG_VMEM),
+        compiler_params=params(),
         cost_estimate=pl.CostEstimate(
             flops=2 * cpd * chunks * span * span,
             bytes_accessed=2 * received.size,
@@ -581,14 +614,14 @@
     for j in range(len(places)):
         if cpd >= LANES:
             dest, low = j * LANES // cpd, j * LANES % cpd
-            conv = in_ref[dest, low : low + LANES, :]
-            back = in_ref[dest, cpd + low : cpd + low + LANES, :]
+            conv = get_pairs(in_ref, dest, low, LANES, cpd // gpd, 0)
+            back = get_pairs(in_ref, dest, low, LANES, cpd // gpd, 1)
             edge = halo_at + 2 * EDGE * (low // LANES)
             halo = in_ref[dest, edge : edge + 2 * EDGE, :].astype(F32)
         else:
             dests = range(j * LANES // cpd, (j + 1) * LANES // cpd)
-            conv = jnp.concatenate([in_ref[d, 0:cpd, :] for d in dests], 0)
-            back = jnp.concatenate([in_ref[d, cpd : 2 * cpd, :] for d in dests], 0)
+            conv = jnp.concatenate([get_pairs(in_ref, d, 0, cpd, cpd // gpd, 0) for d in dests], 0)
+            back = jnp.concatenate([get_pairs(in_ref, d, 0, cpd, cpd // gpd, 1) for d in dests], 0)
             halo = jnp.concatenate(
                 [in_ref[d, halo_at : halo_at + halo_rows, :].astype(F32)[:, :cpd] for d in dests], 1
             )

time: 167 us -> 165 us (0.988)
  local copies, waits for them, and re-layouts: 5.57 us -> 3.5 us
    unnamed x18 -> x14, local copies, waits for them, and re-layouts: 3.57 us -> 1.5 us
  transfers between devices with their start and end apart: 9 -> 9, of which waited for: 5 -> 5; matrix products, arithmetic and copies ran while one was open for 1% -> 1% of each run, Pallas kernels for 25% -> 26%
where the time goes in v12:
time: 165 us; the launch traced here: 164 us
  waiting for transfers between devices  67 us (41%)
  Pallas kernels  59.1 us (36%)
  starting transfers between devices  31.1 us (19%)
  local copies, waits for them, and re-layouts  3.5 us (2%)
  between operations  1.97 us (1%)
    all_to_all x1, waiting for transfers between devices, on_device(): lax.all_to_all(send, 'ctx', split_axis=0, concat_axis=0, tiled=True)  40.1 us
    ppermute x5, starting transfers between devices, shifted(): return lax.ppermute(block, axis, route)  14.5 us
    all_to_all x2, waiting for transfers between devices, on_device(): lax.all_to_all(results, 'ctx', split_axis=0, concat_axis=0, tiled=True)  13.9 us
    ppermute x5, waiting for transfers between devices, shifted(): return lax.ppermute(block, axis, route)  13 us
    pallas_call x2, Pallas kernels, after_exchange(): pl.pallas_call(functools.partial(after_kernel, cpd, gpd, chunks, last, bo...  12.9 us
    pallas_call x2, Pallas kernels, long_convs(): pl.pallas_call(functools.partial(conv_kernel, cpd, gpd, chunk), grid=(pai...  12.3 us
    all_to_all x2, starting transfers between devices, on_device(): lax.all_to_all(results, 'ctx', split_axis=0, concat_axis=0, tiled=True)  9.8 us
    pallas_call x1, Pallas kernels, filter_products(): pl.pallas_call(functools.partial(gram_kernel, cpd // gpd), grid=(pairs,),...  9.35 us
  transfers between devices with their start and end apart: 9, of which 5 were waited for; matrix products, arithmetic and copies ran while one was open for 1% of the time, Pallas kernels for 26%

profile of v12, /device:TPU:16, one launch (start us, length us, event | category | flops | bytes accessed | tf_op | source)
XLA Modules:
  0.0 163.7 jit_solution(15149881569548156980)
XLA Ops:
  0.6 1.7 %edge_rows.2 = bf16[24,4096]{1,0:T(8,128)(2,1)} custom-call(bf16[128,4096]{1,0:T(8,128)(2,1)} %refs_6_.1, bf16[128,4096]{1,0:T(8,128)(2,1)} %k_ref.9, bf16[128,4096]{1,0:T(8,128)(2,1)} %v_ref.9), custom_call_target="tpu_custom_call" | custom-call | tf_op jit(solution)/shard_map/edge_rows/pallas_call | solution.py:246
  2.4 1.9 %collective-permute-start = (bf16[24,4096]{1,0:T(8,128)(2,1)}, bf16[24,4096]{1,0:T(8,128)(2,1)S(1)}, u32[]{:S(2)}, u32[]{:S(2)}) collective-permute-start(bf16[24,4096]{1,0:T(8,128)(2,1)} %edge_rows.2), channel_id=1, source_target_pairs={{0,2},{2,4},{4,6},{6,8},{8,10},{10,12},{12,14},{14,16},{16,18},{18... | collective-permute-start | bytes 589832 | tf_op jit(solution)/shard_map/ppermute | solution.py:27
  4.3 6.2 %collective-permute-done.refs_4_.refs_10_.tail_ref = bf16[24,4096]{1,0:T(8,128)(2,1)S(1)} collective-permute-done((bf16[24,4096]{1,0:T(8,128)(2,1)}, bf16[24,4096]{1,0:T(8,128)(2,1)S(1)}, u32[]{:S(2)}, u32[]{:S(2)}) %collective-permute-start) | collective-permute-done | bytes 196640 | tf_op jit(solution)/shard_map/ppermute | solution.py:27
  10.4 0.7 copy-done.5
  11.1 8.9 %before_exchange.1 = bf16[16,528,128]{2,1,0:T(8,128)(2,1)} custom-call(bf16[128,4096]{1,0:T(8,128)(2,1)} %refs_6_.1, bf16[128,4096]{1,0:T(8,128)(2,1)} %k_ref.9, bf16[128,4096]{1,0:T(8,128)(2,1)} %v_ref.9, bf16[128,4096]{1,0:T(8,128)(2,1)} %og_ref.3, bf16[24,4096]{1,0:T(8,128)(2,1)} %copy-done.5, f32[3,7,4096]{2,1,0:T(8,128)} %taps_ref.3, ...), custom_call_target="tpu_custom_call" | custom-call | flops 26214400 | bytes 6291456 | tf_op jit(solution)/shard_map/before_exchange/pallas_call | solution.py:355
  20.0 5.3 %all-to-all-start = ((bf16[16,528,128]{2,1,0:T(8,128)(2,1)}), bf16[16,528,128]{2,1,0:T(8,128)(2,1)}, u32[]{:S(2)}, u32[]{:S(2)}) async-start(bf16[16,528,128]{2,1,0:T(8,128)(2,1)} %before_exchange.1), calls=%async_computation | async-start | bytes 4325376 | tf_op jit(solution)/shard_map/all_to_all | solution.py:763
  25.3 0.0 slice-start.1
  25.3 1.0 slice-done
  26.3 0.2 slice-done.1
  26.5 1.0 pad_maximum_fusion
  27.5 2.0 %collective-permute-start.2 = (bf16[256,2048]{1,0:T(8,128)(2,1)}, bf16[256,2048]{1,0:T(8,128)(2,1)}, u32[]{:S(2)}, u32[]{:S(2)}) collective-permute-start(bf16[256,2048]{1,0:T(8,128)(2,1)} %pad_maximum_fusion), channel_id=1, source_target_pairs={{0,2},{2,4},{4,6},{6,8},{8,10},{10,12},{12,14},{14,16},{16,18},{18... | collective-permute-start | bytes 3145736 | tf_op jit(solution)/shard_map/ppermute | solution.py:27
  29.6 0.8 slice.9
  30.4 4.4 %collective-permute-start.1 = (bf16[128,2048]{1,0:T(8,128)(2,1)}, bf16[128,2048]{1,0:T(8,128)(2,1)}, u32[]{:S(2)}, u32[]{:S(2)}) collective-permute-start(bf16[128,2048]{1,0:T(8,128)(2,1)} %slice.9), channel_id=1, source_target_pairs={{2,0},{4,2},{6,4},{8,6},{10,8},{12,10},{14,12},{16,14},{18,16},{20... | collective-permute-start | bytes 1572872 | tf_op jit(solution)/shard_map/ppermute | solution.py:27
  34.8 40.1 %all-to-all-done.in_ref.filter_ref = bf16[16,528,128]{2,1,0:T(8,128)(2,1)} async-done(((bf16[16,528,128]{2,1,0:T(8,128)(2,1)}), bf16[16,528,128]{2,1,0:T(8,128)(2,1)}, u32[]{:S(2)}, u32[]{:S(2)}) %all-to-all-start) | async-done | bytes 2162720 | tf_op jit(solution)/shard_map/all_to_all | solution.py:763
  75.0 6.1 %long_convs.2 = bf16[16,272,128]{2,1,0:T(8,128)(2,1)} custom-call(bf16[16,528,128]{2,1,0:T(8,128)(2,1)} %all-to-all-done.in_ref.filter_ref, bf16[16,528,128]{2,1,0:T(8,128)(2,1)} %all-to-all-done.in_ref.filter_ref), custom_call_target="tpu_custom_call" | custom-call | flops 2147483648 | bytes 2228224 | tf_op jit(solution)/shard_map/long_convs/pallas_call | solution.py:470
  81.1 4.6 %collective-permute-done.2.kp_ref.vp_ref = bf16[256,2048]{1,0:T(8,128)(2,1)} collective-permute-done((bf16[256,2048]{1,0:T(8,128)(2,1)}, bf16[256,2048]{1,0:T(8,128)(2,1)}, u32[]{:S(2)}, u32[]{:S(2)}) %collective-permute-start.2) | collective-permute-done | bytes 1048608 | tf_op jit(solution)/shard_map/ppermute | solution.py:27
  85.7 4.3 %all-to-all-start.2 = ((bf16[16,272,128]{2,1,0:T(8,128)(2,1)}), bf16[16,272,128]{2,1,0:T(8,128)(2,1)}, u32[]{:S(2)}, u32[]{:S(2)}) async-start(bf16[16,272,128]{2,1,0:T(8,128)(2,1)} %long_convs.2), calls=%async_computation.2 | async-start | bytes 2228224 | tf_op jit(solution)/shard_map/all_to_all | solution.py:781
  90.0 4.3 %attend_next.1 = bf16[128,2176]{1,0:T(8,128)(2,1)} custom-call(bf16[128,2048]{1,0:T(8,128)(2,1)} %collective-permute-done.1.q_ref, bf16[128,4096]{1,0:T(8,128)(2,1)S(1)} %copy-done, bf16[128,4096]{1,0:T(8,128)(2,1)S(1)} %copy-done.1), custom_call_target="tpu_custom_call" | custom-call | flops 134217728 | bytes 2621440 | tf_op jit(solution)/shard_map/attend_next/pallas_call | solution.py:181
  94.4 2.0 %collective-permute-start.4 = (bf16[128,2176]{1,0:T(8,128)(2,1)}, bf16[128,2176]{1,0:T(8,128)(2,1)S(1)}, u32[]{:S(2)}, u32[]{:S(2)}) collective-permute-start(bf16[128,2176]{1,0:T(8,128)(2,1)} %attend_next.1), channel_id=1, source_target_pairs={{0,2},{2,4},{4,6},{6,8},{8,10},{10,12},{12,14},{14,16},{16,18},{18... | collective-permute-start | bytes 1671176 | tf_op jit(solution)/shard_map/ppermute | solution.py:27
  96.3 9.4 %filter_products.1 = (bf16[16,16,128]{2,1,0:T(8,128)(2,1)}, f32[1,1]{1,0:T(1,128)}) custom-call(bf16[16,528,128]{2,1,0:T(8,128)(2,1)} %all-to-all-done.in_ref.filter_ref), custom_call_target="tpu_custom_call" | custom-call | flops 2147483648 | bytes 2162688 | tf_op jit(solution)/shard_map/filter_products/pallas_call | solution.py:551
  105.7 1.5 collective-permute-start.3
  107.2 1.7 %edge_rows.3 = bf16[24,4096]{1,0:T(8,128)(2,1)} custom-call(bf16[128,4096]{1,0:T(8,128)(2,1)} %og_ref.3, bf16[128,4096]{1,0:T(8,128)(2,1)} %k_ref.9, bf16[128,4096]{1,0:T(8,128)(2,1)} %v_ref.9), custom_call_target="tpu_custom_call" | custom-call | tf_op jit(solution)/shard_map/edge_rows/pallas_call | solution.py:246
  108.9 4.2 %collective-permute-start.5 = (bf16[24,4096]{1,0:T(8,128)(2,1)}, bf16[24,4096]{1,0:T(8,128)(2,1)S(1)}, u32[]{:S(2)}, u32[]{:S(2)}) collective-permute-start(bf16[24,4096]{1,0:T(8,128)(2,1)} %edge_rows.3), channel_id=1, source_target_pairs={{2,0},{4,2},{6,4},{8,6},{10,8},{12,10},{14,12},{16,14},{18,16},{20... | collective-permute-start | bytes 589832 | tf_op jit(solution)/shard_map/ppermute | solution.py:27
  114.3 6.2 %long_convs.3 = bf16[16,288,128]{2,1,0:T(8,128)(2,1)} custom-call(bf16[16,528,128]{2,1,0:T(8,128)(2,1)} %all-to-all-done.in_ref.filter_ref, bf16[16,528,128]{2,1,0:T(8,128)(2,1)} %all-to-all-done.in_ref.filter_ref, bf16[16,16,128]{2,1,0:T(8,128)(2,1)} %get-tuple-element.44.refs_0_, f32[1,1]{1,0:T(1,128)S(6)} %add.3.refs_1_), custom_call_target="tpu_custom_call" | custom-call | flops 2147483648 | bytes 2359296 | tf_op jit(solution)/shard_map/long_convs/pallas_call | solution.py:470
  120.5 2.2 %collective-permute-done.4.part_ref.log_ref = bf16[128,2176]{1,0:T(8,128)(2,1)S(1)} collective-permute-done((bf16[128,2176]{1,0:T(8,128)(2,1)}, bf16[128,2176]{1,0:T(8,128)(2,1)S(1)}, u32[]{:S(2)}, u32[]{:S(2)}) %collective-permute-start.4) | collective-permute-done | bytes 557088 | tf_op jit(solution)/shard_map/ppermute | solution.py:27
  122.7 0.8 copy-done.3
  123.5 5.5 %all-to-all-start.1 = ((bf16[16,288,128]{2,1,0:T(8,128)(2,1)}), bf16[16,288,128]{2,1,0:T(8,128)(2,1)}, u32[]{:S(2)}, u32[]{:S(2)}) async-start(bf16[16,288,128]{2,1,0:T(8,128)(2,1)} %long_convs.3), calls=%async_computation.1 | async-start | bytes 2359296 | tf_op jit(solution)/shard_map/all_to_all | solution.py:781
  129.0 4.7 %attend_whole.1._ = bf16[128,4096]{1,0:T(8,128)(2,1)} custom-call(s32[1]{0:T(128)} %bitcast.place_ref, bf16[128,4096]{1,0:T(8,128)(2,1)S(1)} %copy-done.2, bf16[128,4096]{1,0:T(8,128)(2,1)S(1)} %copy-done, bf16[128,4096]{1,0:T(8,128)(2,1)S(1)} %copy-done.1, bf16[256,2048]{1,0:T(8,128)(2,1)} %collective-permute-done.2.kp_ref.vp_ref, ...), custom_call_target="tpu_custom_call" | custom-call | flops 268435456 | bytes 5242880 | tf_op jit(solution)/shard_map/attend_whole/pallas_call | solution.py:204
  133.8 3.2 %attend_merge.1 = bf16[128,4096]{1,0:T(8,128)(2,1)} custom-call(s32[1]{0:T(128)} %bitcast.place_ref, bf16[128,4096]{1,0:T(8,128)(2,1)S(1)} %copy-done.2, bf16[128,4096]{1,0:T(8,128)(2,1)S(1)} %copy-done, bf16[128,4096]{1,0:T(8,128)(2,1)S(1)} %copy-done.1, bf16[128,2176]{1,0:T(8,128)(2,1)S(1)} %copy-done.4, ...), custom_call_target="tpu_custom_call", output_to_operand_aliasing={{}: (6, {})} | custom-call | flops 134217728 | bytes 2621440 | tf_op jit(solution)/shard_map/attend_merge/pallas_call | solution.py:215
  137.0 6.3 %after_exchange.2 = (bf16[128,4096]{1,0:T(8,128)(2,1)}, bf16[128,4096]{1,0:T(8,128)(2,1)}, bf16[128,4096]{1,0:T(8,128)(2,1)}) custom-call(bf16[16,272,128]{2,1,0:T(8,128)(2,1)} %all-to-all-done.2.in_ref, bf16[128,4096]{1,0:T(8,128)(2,1)} %og_ref.3, bf16[128,4096]{1,0:T(8,128)(2,1)} %k_ref.9, bf16[128,4096]{1,0:T(8,128)(2,1)} %v_ref.9, ...), custom_call_target="tpu_custom_call" | custom-call | flops 23592960 | bytes 4718592 | tf_op jit(solution)/shard_map/after_exchange/pallas_call | solution.py:710
  143.2 13.9 %all-to-all-done.1.in_ref = bf16[16,288,128]{2,1,0:T(8,128)(2,1)} async-done(((bf16[16,288,128]{2,1,0:T(8,128)(2,1)}), bf16[16,288,128]{2,1,0:T(8,128)(2,1)}, u32[]{:S(2)}, u32[]{:S(2)}) %all-to-all-start.1) | async-done | bytes 1179680 | tf_op jit(solution)/shard_map/all_to_all | solution.py:781
  157.1 6.6 %after_exchange.3 = (bf16[128,4096]{1,0:T(8,128)(2,1)}, bf16[128,4096]{1,0:T(8,128)(2,1)}, bf16[128,4096]{1,0:T(8,128)(2,1)}, f32[128,256]{1,0:T(8,128)}) custom-call(bf16[16,288,128]{2,1,0:T(8,128)(2,1)} %all-to-all-done.1.in_ref, bf16[128,4096]{1,0:T(8,128)(2,1)} %og_ref.3, ...), custom_call_target="tpu_custom_call", output_to_operand_aliasing={{0}: (7, {}), {1}: (8, {}), {2}: (9, {})} | custom-call | flops 23592960 | bytes 4718592 | tf_op jit(solution)/shard_map/after_exchange/pallas_call | solution.py:710
  (17 shorter events, 0.0 us)
Async XLA Ops:
  2.4 8.1 %collective-permute-start = (bf16[24,4096]{1,0:T(8,128)(2,1)}, bf16[24,4096]{1,0:T(8,128)(2,1)S(1)}, u32[]{:S(2)}, u32[]{:S(2)}) collective-permute-start(bf16[24,4096]{1,0:T(8,128)(2,1)} %edge_rows.2), channel_id=1, source_target_pairs={{0,2},{2,4},{4,6},{6,8},{8,10},{10,12},{12,14},{14,16},{16,18},{18... | collective-permute-start | bytes 589832 | tf_op jit(solution)/shard_map/ppermute | solution.py:27
  10.4 0.7 copy-start.5
  20.0 55.0 %all-to-all-start = ((bf16[16,528,128]{2,1,0:T(8,128)(2,1)}), bf16[16,528,128]{2,1,0:T(8,128)(2,1)}, u32[]{:S(2)}, u32[]{:S(2)}) async-start(bf16[16,528,128]{2,1,0:T(8,128)(2,1)} %before_exchange.1), calls=%async_computation | async-start | bytes 4325376 | tf_op jit(solution)/shard_map/all_to_all | solution.py:763
  25.3 1.0 slice-start
  25.3 1.2 slice-start.1
  25.3 4.3 %copy-start.2 = (bf16[128,4096]{1,0:T(8,128)(2,1)S(1)}, bf16[128,4096]{1,0:T(8,128)(2,1)}, u32[]{:S(2)}) copy-start(bf16[128,4096]{1,0:T(8,128)(2,1)} %q_ref.3) | copy-start | bytes 3145732
  27.5 58.2 %collective-permute-start.2 = (bf16[256,2048]{1,0:T(8,128)(2,1)}, bf16[256,2048]{1,0:T(8,128)(2,1)}, u32[]{:S(2)}, u32[]{:S(2)}) collective-permute-start(bf16[256,2048]{1,0:T(8,128)(2,1)} %pad_maximum_fusion), channel_id=1, source_target_pairs={{0,2},{2,4},{4,6},{6,8},{8,10},{10,12},{12,14},{14,16},{16,18},{18... | collective-permute-start | bytes 3145736 | tf_op jit(solution)/shard_map/ppermute | solution.py:27
  30.4 50.7 %collective-permute-start.1 = (bf16[128,2048]{1,0:T(8,128)(2,1)}, bf16[128,2048]{1,0:T(8,128)(2,1)}, u32[]{:S(2)}, u32[]{:S(2)}) collective-permute-start(bf16[128,2048]{1,0:T(8,128)(2,1)} %slice.9), channel_id=1, source_target_pairs={{2,0},{4,2},{6,4},{8,6},{10,8},{12,10},{14,12},{16,14},{18,16},{20... | collective-permute-start | bytes 1572872 | tf_op jit(solution)/shard_map/ppermute | solution.py:27
  81.1 8.9 %copy-start = (bf16[128,4096]{1,0:T(8,128)(2,1)S(1)}, bf16[128,4096]{1,0:T(8,128)(2,1)}, u32[]{:S(2)}) copy-start(bf16[128,4096]{1,0:T(8,128)(2,1)} %k_ref.7) | copy-start | bytes 3145732
  81.1 8.9 %copy-start.1 = (bf16[128,4096]{1,0:T(8,128)(2,1)S(1)}, bf16[128,4096]{1,0:T(8,128)(2,1)}, u32[]{:S(2)}) copy-start(bf16[128,4096]{1,0:T(8,128)(2,1)} %v_ref.7) | copy-start | bytes 3145732
  85.7 37.8 %all-to-all-start.2 = ((bf16[16,272,128]{2,1,0:T(8,128)(2,1)}), bf16[16,272,128]{2,1,0:T(8,128)(2,1)}, u32[]{:S(2)}, u32[]{:S(2)}) async-start(bf16[16,272,128]{2,1,0:T(8,128)(2,1)} %long_convs.2), calls=%async_computation.2 | async-start | bytes 2228224 | tf_op jit(solution)/shard_map/all_to_all | solution.py:781
  94.4 28.3 %collective-permute-start.4 = (bf16[128,2176]{1,0:T(8,128)(2,1)}, bf16[128,2176]{1,0:T(8,128)(2,1)S(1)}, u32[]{:S(2)}, u32[]{:S(2)}) collective-permute-start(bf16[128,2176]{1,0:T(8,128)(2,1)} %attend_next.1), channel_id=1, source_target_pairs={{0,2},{2,4},{4,6},{6,8},{8,10},{10,12},{12,14},{14,16},{16,18},{18... | collective-permute-start | bytes 1671176 | tf_op jit(solution)/shard_map/ppermute | solution.py:27
  105.7 7.4 %collective-permute-start.3 = (f32[1,1]{1,0:T(1,128)}, f32[1,1]{1,0:T(1,128)}, u32[]{:S(2)}, u32[]{:S(2)}) collective-permute-start(f32[1,1]{1,0:T(1,128)} %get-tuple-element.45), channel_id=1, source_target_pairs={{0,1},{1,0},{2,3},{3,2},{4,5},{5,4},{6,7},{7,6},{8,9},{9,8},{10,11... | collective-permute-start | bytes 20 | tf_op jit(solution)/shard_map/ppermute | solution.py:34
  108.9 11.6 %collective-permute-start.5 = (bf16[24,4096]{1,0:T(8,128)(2,1)}, bf16[24,4096]{1,0:T(8,128)(2,1)S(1)}, u32[]{:S(2)}, u32[]{:S(2)}) collective-permute-start(bf16[24,4096]{1,0:T(8,128)(2,1)} %edge_rows.3), channel_id=1, source_target_pairs={{2,0},{4,2},{6,4},{8,6},{10,8},{12,10},{14,12},{16,14},{18,16},{20... | collective-permute-start | bytes 589832 | tf_op jit(solution)/shard_map/ppermute | solution.py:27
  120.5 16.4 %copy-start.6 = (bf16[24,4096]{1,0:T(8,128)(2,1)}, bf16[24,4096]{1,0:T(8,128)(2,1)S(1)}, u32[]{:S(2)}) copy-start(bf16[24,4096]{1,0:T(8,128)(2,1)S(1)} %collective-permute-done.5.next_ref) | copy-start | bytes 589828
  122.7 0.8 copy-start.3
  123.5 33.6 %all-to-all-start.1 = ((bf16[16,288,128]{2,1,0:T(8,128)(2,1)}), bf16[16,288,128]{2,1,0:T(8,128)(2,1)}, u32[]{:S(2)}, u32[]{:S(2)}) async-start(bf16[16,288,128]{2,1,0:T(8,128)(2,1)} %long_convs.3), calls=%async_computation.1 | async-start | bytes 2359296 | tf_op jit(solution)/shard_map/all_to_all | solution.py:781
  129.0 4.8 %copy-start.4 = (bf16[128,2176]{1,0:T(8,128)(2,1)S(1)}, bf16[128,2176]{1,0:T(8,128)(2,1)}, u32[]{:S(2)}) copy-start(bf16[128,2176]{1,0:T(8,128)(2,1)} %copy-done.3) | copy-start | bytes 1671172

commit v13 on v12

--- a/solution.py
+++ b/solution.py
@@ -14,7 +14,7 @@
 F32 = jnp.float32
 BF16 = jnp.bfloat16
 VMEM_BYTES = 60 * 1024 * 1024
-LONG_VMEM = 20 * 1024 * 1024
+LONG_VMEM = 24 * 1024 * 1024
 
 
 def params(size=VMEM_BYTES):
@@ -249,7 +249,7 @@
         in_specs=[block] * len(arrays),
         out_specs=pl.BlockSpec((len(arrays) * EDGE, channels), lambda i: (0, 0)),
         out_shape=jax.ShapeDtypeStruct((len(arrays) * EDGE, channels), BF16),
-        compiler_params=params(),
+        compiler_params=params(LONG_VMEM if first else VMEM_BYTES),
         name="edge_rows",
     )(*arrays)
 
@@ -481,7 +481,7 @@
             pltpu.VMEM((filter_rows, span + rows), F32),
             pltpu.VMEM((PAIR, rows, span + rows), BF16),
         ],
-        compiler_params=params(),
+        compiler_params=params(LONG_VMEM),
         cost_estimate=pl.CostEstimate(
             flops=4 * cpd * span * span, bytes_accessed=4 * n * out_rows * rows, transcendentals=0
         ),
@@ -565,7 +565,7 @@
             pltpu.VMEM((raw_rows, span), F32),
             pltpu.VMEM((1, span), F32),
         ],
-        compiler_params=params(),
+        compiler_params=params(LONG_VMEM),
         cost_estimate=pl.CostEstimate(
             flops=2 * cpd * chunks * span * span,
             bytes_accessed=2 * received.size,
@@ -725,7 +725,7 @@
         out_shape=[grad] * 3 + [jax.ShapeDtypeStruct((rows, groups), F32)] * last,
         scratch_shapes=[pltpu.VMEM((groups, rows), F32), pltpu.VMEM((1, LANES), F32)] * last
         + [ext] * 5,
-        compiler_params=params(),
+        compiler_params=params(LONG_VMEM),
         cost_estimate=pl.CostEstimate(
             flops=90 * rows * channels, bytes_accessed=18 * rows * channels, transcendentals=0
         ),
@@ -761,6 +761,7 @@
         (send, query_heads, key_heads, value_heads, output_grad, hyena_key, hyena_value)
     )
     received = lax.all_to_all(send, "ctx", split_axis=0, concat_axis=0, tiled=True)
+    following = shifted(edge_rows(sources, True), "ctx", -1)
     query_next = shifted(query[:, :half], "ctx", -1)
     previous = shifted(jnp.concatenate([key[:, half:], value[:, half:]], 0), "ctx", 1)
     returned = []
@@ -768,16 +769,17 @@
         raw = ()
         if chunk + 1 == chunks:
             raw, squares = filter_products(received, cpd, gpd, chunks)
+            query_next, raw, squares = lax.optimization_barrier((query_next, raw, squares))
             raw = (raw, total_over(squares, "tp"))
         results = long_convs(received, raw, cpd, gpd, chunk, chunks)
+        if chunk + 1 == chunks:
+            part = shifted(attend_next(query_next, key_heads, value_heads), "ctx", 1)
         if chunk == 0:
-            results, received, query_next, previous, *sources = lax.optimization_barrier(
-                (results, received, query_next, previous, *sources)
+            results, received, query_next, previous, following = lax.optimization_barrier(
+                (results, received, query_next, previous, following)
             )
-            part = shifted(attend_next(query_next, key_heads, value_heads), "ctx", 1)
-            following = shifted(edge_rows(sources, True), "ctx", -1)
         else:
-            results, part, following = lax.optimization_barrier((results, part, following))
+            results, part = lax.optimization_barrier((results, part))
         returned.append(lax.all_to_all(results, "ctx", split_axis=0, concat_axis=0, tiled=True))
     attention = attend(query_heads, key_heads, value_heads, part, previous, position)
     bound = math.sqrt(rows * n * groups * tp)

time: 165 us -> 165 us (level)
  local copies, waits for them, and re-layouts: 3.5 us -> 11.1 us
  Pallas kernels: 59.1 us -> 53.9 us
  starting transfers between devices: 31.1 us -> 27.7 us
    unnamed x14 -> x40, local copies, waits for them, and re-layouts: 1.5 us -> 9.12 us
    ppermute x5, waiting for transfers between devices: 13 us -> 17.2 us  [shifted(): return lax.ppermute(block, axis, route)]
    all_to_all x2, waiting for transfers between devices: 13.9 us -> 10.4 us  [on_device(): lax.all_to_all(results, 'ctx', split_axis=0, concat_axis=0, tiled=True)]
    ppermute x1, waiting for transfers between devices: 0.01 us -> 2.29 us  [total_over(): lax.ppermute(value, axis, [(i, i ^ distance) for i in range(size)])]
    ppermute x5, starting transfers between devices: 14.5 us -> 12.2 us  [shifted(): return lax.ppermute(block, axis, route)]
    pallas_call x2, Pallas kernels: 12.3 us -> 10.2 us  [long_convs(): pl.pallas_call(functools.partial(conv_kernel, cpd, gpd, chunk), grid=(pai...]
    all_to_all x1, waiting for transfers between devices: 40.1 us -> 38.1 us  [on_device(): lax.all_to_all(send, 'ctx', split_axis=0, concat_axis=0, tiled=True)]
    pallas_call x2, Pallas kernels: 3.44 us -> 1.74 us  [edge_rows(): pl.pallas_call(functools.partial(edge_kernel, first), grid=(1,), in_specs...]
  transfers between devices with their start and end apart: 9 -> 9, of which waited for: 5 -> 6; matrix products, arithmetic and copies ran while one was open for 1% -> 1% of each run, Pallas kernels for 26% -> 23%
where the time goes in v13:
time: 165 us; the launch traced here: 164 us
  waiting for transfers between devices  68 us (41%)
  Pallas kernels  53.9 us (33%)
  starting transfers between devices  27.7 us (17%)
  local copies, waits for them, and re-layouts  11.1 us (7%)
  between operations  2.08 us (1%)
    all_to_all x1, waiting for transfers between devices, on_device(): lax.all_to_all(send, 'ctx', split_axis=0, concat_axis=0, tiled=True)  38.1 us
    ppermute x5, waiting for transfers between devices, shifted(): return lax.ppermute(block, axis, route)  17.2 us
    pallas_call x2, Pallas kernels, after_exchange(): pl.pallas_call(functools.partial(after_kernel, cpd, gpd, chunks, last, bo...  12.3 us
    ppermute x5, starting transfers between devices, shifted(): return lax.ppermute(block, axis, route)  12.2 us
    all_to_all x2, waiting for transfers between devices, on_device(): lax.all_to_all(results, 'ctx', split_axis=0, concat_axis=0, tiled=True)  10.4 us
    pallas_call x2, Pallas kernels, long_convs(): pl.pallas_call(functools.partial(conv_kernel, cpd, gpd, chunk), grid=(pai...  10.2 us
    pallas_call x1, Pallas kernels, filter_products(): pl.pallas_call(functools.partial(gram_kernel, cpd // gpd), grid=(pairs,),...  9.36 us
    unnamed x40, local copies, waits for them, and re-layouts  9.12 us
  transfers between devices with their start and end apart: 9, of which 6 were waited for; matrix products, arithmetic and copies ran while one was open for 1% of the time, Pallas kernels for 23%

profile of v13, /device:TPU:16, one launch (start us, length us, event | category | flops | bytes accessed | tf_op | source)
XLA Modules:
  0.0 163.8 jit_solution(16811468639605291861)
XLA Ops:
  0.6 1.7 %edge_rows.2 = bf16[24,4096]{1,0:T(8,128)(2,1)} custom-call(bf16[128,4096]{1,0:T(8,128)(2,1)} %refs_6_.1, bf16[128,4096]{1,0:T(8,128)(2,1)} %k_ref.9, bf16[128,4096]{1,0:T(8,128)(2,1)} %v_ref.9), custom_call_target="tpu_custom_call" | custom-call | tf_op jit(solution)/shard_map/edge_rows/pallas_call | solution.py:246
  2.4 1.9 %collective-permute-start = (bf16[24,4096]{1,0:T(8,128)(2,1)}, bf16[24,4096]{1,0:T(8,128)(2,1)S(1)}, u32[]{:S(2)}, u32[]{:S(2)}) collective-permute-start(bf16[24,4096]{1,0:T(8,128)(2,1)} %edge_rows.2), channel_id=1, source_target_pairs={{0,2},{2,4},{4,6},{6,8},{8,10},{10,12},{12,14},{14,16},{16,18},{18... | collective-permute-start | bytes 589832 | tf_op jit(solution)/shard_map/ppermute | solution.py:27
  4.3 6.2 %collective-permute-done.refs_4_.refs_10_.tail_ref = bf16[24,4096]{1,0:T(8,128)(2,1)S(1)} collective-permute-done((bf16[24,4096]{1,0:T(8,128)(2,1)}, bf16[24,4096]{1,0:T(8,128)(2,1)S(1)}, u32[]{:S(2)}, u32[]{:S(2)}) %collective-permute-start) | collective-permute-done | bytes 196640 | tf_op jit(solution)/shard_map/ppermute | solution.py:27
  11.1 8.9 %before_exchange.1 = bf16[16,528,128]{2,1,0:T(8,128)(2,1)} custom-call(bf16[128,4096]{1,0:T(8,128)(2,1)} %refs_6_.1, bf16[128,4096]{1,0:T(8,128)(2,1)} %k_ref.9, bf16[128,4096]{1,0:T(8,128)(2,1)} %v_ref.9, bf16[128,4096]{1,0:T(8,128)(2,1)} %og_ref.3, bf16[24,4096]{1,0:T(8,128)(2,1)} %copy-done.10, f32[3,7,4096]{2,1,0:T(8,128)} %taps_ref.3, ...), custom_call_target="tpu_custom_call" | custom-call | flops 26214400 | bytes 6291456 | tf_op jit(solution)/shard_map/before_exchange/pallas_call | solution.py:355
  20.0 5.3 %all-to-all-start = ((bf16[16,528,128]{2,1,0:T(8,128)(2,1)}), bf16[16,528,128]{2,1,0:T(8,128)(2,1)}, u32[]{:S(2)}, u32[]{:S(2)}) async-start(bf16[16,528,128]{2,1,0:T(8,128)(2,1)} %before_exchange.1), calls=%async_computation | async-start | bytes 4325376 | tf_op jit(solution)/shard_map/all_to_all | solution.py:763
  25.4 1.0 slice-done
  26.5 1.1 pad_maximum_fusion
  27.6 2.0 %collective-permute-start.2 = (bf16[256,2048]{1,0:T(8,128)(2,1)}, bf16[256,2048]{1,0:T(8,128)(2,1)}, u32[]{:S(2)}, u32[]{:S(2)}) collective-permute-start(bf16[256,2048]{1,0:T(8,128)(2,1)} %pad_maximum_fusion), channel_id=1, source_target_pairs={{0,2},{2,4},{4,6},{6,8},{8,10},{10,12},{12,14},{14,16},{16,18},{18... | collective-permute-start | bytes 3145736 | tf_op jit(solution)/shard_map/ppermute | solution.py:27
  30.5 4.4 %collective-permute-start.1 = (bf16[128,2048]{1,0:T(8,128)(2,1)}, bf16[128,2048]{1,0:T(8,128)(2,1)}, u32[]{:S(2)}, u32[]{:S(2)}) collective-permute-start(bf16[128,2048]{1,0:T(8,128)(2,1)} %slice.9), channel_id=1, source_target_pairs={{2,0},{4,2},{6,4},{8,6},{10,8},{12,10},{14,12},{16,14},{18,16},{20... | collective-permute-start | bytes 1572872 | tf_op jit(solution)/shard_map/ppermute | solution.py:27
  34.9 1.9 %collective-permute-start.3 = (bf16[24,4096]{1,0:T(8,128)(2,1)S(1)}, bf16[24,4096]{1,0:T(8,128)(2,1)S(1)}, u32[]{:S(2)}, u32[]{:S(2)}) collective-permute-start(bf16[24,4096]{1,0:T(8,128)(2,1)S(1)} %edge_rows.3), channel_id=1, source_target_pairs={{2,0},{4,2},{6,4},{8,6},{10,8},{12,10},{14,12},{16,14},{18,16},{20... | collective-permute-start | bytes 589832 | tf_op jit(solution)/shard_map/ppermute | solution.py:27
  36.9 38.1 %all-to-all-done.in_ref.filter_ref = bf16[16,528,128]{2,1,0:T(8,128)(2,1)} async-done(((bf16[16,528,128]{2,1,0:T(8,128)(2,1)}), bf16[16,528,128]{2,1,0:T(8,128)(2,1)}, u32[]{:S(2)}, u32[]{:S(2)}) %all-to-all-start) | async-done | bytes 2162720 | tf_op jit(solution)/shard_map/all_to_all | solution.py:763
  75.0 5.1 %long_convs.2 = bf16[16,272,128]{2,1,0:T(8,128)(2,1)S(1)} custom-call(bf16[16,528,128]{2,1,0:T(8,128)(2,1)} %all-to-all-done.in_ref.filter_ref, bf16[16,528,128]{2,1,0:T(8,128)(2,1)} %all-to-all-done.in_ref.filter_ref), custom_call_target="tpu_custom_call" | custom-call | flops 2147483648 | bytes 2228224 | tf_op jit(solution)/shard_map/long_convs/pallas_call | solution.py:470
  80.0 1.0 copy-done.16
  81.1 4.7 %collective-permute-done.2.kp_ref.vp_ref = bf16[256,2048]{1,0:T(8,128)(2,1)} collective-permute-done((bf16[256,2048]{1,0:T(8,128)(2,1)}, bf16[256,2048]{1,0:T(8,128)(2,1)}, u32[]{:S(2)}, u32[]{:S(2)}) %collective-permute-start.2) | collective-permute-done | bytes 1048608 | tf_op jit(solution)/shard_map/ppermute | solution.py:27
  85.7 4.3 %all-to-all-start.2 = ((bf16[16,272,128]{2,1,0:T(8,128)(2,1)}), bf16[16,272,128]{2,1,0:T(8,128)(2,1)}, u32[]{:S(2)}, u32[]{:S(2)}) async-start(bf16[16,272,128]{2,1,0:T(8,128)(2,1)} %copy-done.16), calls=%async_computation.2 | async-start | bytes 2228224 | tf_op jit(solution)/shard_map/all_to_all | solution.py:783
  90.1 9.4 %filter_products.1 = (bf16[16,16,128]{2,1,0:T(8,128)(2,1)S(1)}, f32[1,1]{1,0:T(1,128)}) custom-call(bf16[16,528,128]{2,1,0:T(8,128)(2,1)} %all-to-all-done.in_ref.filter_ref), custom_call_target="tpu_custom_call" | custom-call | flops 2147483648 | bytes 2162688 | tf_op jit(solution)/shard_map/filter_products/pallas_call | solution.py:551
  99.4 3.5 %attend_next.1 = bf16[128,2176]{1,0:T(8,128)(2,1)S(1)} custom-call(bf16[128,2048]{1,0:T(8,128)(2,1)} %collective-permute-done.1.q_ref, bf16[128,4096]{1,0:T(8,128)(2,1)S(1)} %copy-done.3, bf16[128,4096]{1,0:T(8,128)(2,1)S(1)} %copy-done.5), custom_call_target="tpu_custom_call" | custom-call | flops 134217728 | bytes 2621440 | tf_op jit(solution)/shard_map/attend_next/pallas_call | solution.py:181
  103.0 2.0 %collective-permute-start.5 = (bf16[128,2176]{1,0:T(8,128)(2,1)S(1)}, bf16[128,2176]{1,0:T(8,128)(2,1)S(1)}, u32[]{:S(2)}, u32[]{:S(2)}) collective-permute-start(bf16[128,2176]{1,0:T(8,128)(2,1)S(1)} %attend_next.1), channel_id=1, source_target_pairs={{0,2},{2,4},{4,6},{6,8},{8,10},{10,12},{12,14},{14,16},{16,18},{18... | collective-permute-start | bytes 1671176 | tf_op jit(solution)/shard_map/ppermute | solution.py:27
  105.0 1.6 collective-permute-start.4
  106.5 2.3 %collective-permute-done.4 = f32[1,1]{1,0:T(1,128)} collective-permute-done((f32[1,1]{1,0:T(1,128)}, f32[1,1]{1,0:T(1,128)}, u32[]{:S(2)}, u32[]{:S(2)}) %collective-permute-start.4) | collective-permute-done | bytes 36 | tf_op jit(solution)/shard_map/ppermute | solution.py:34
  110.0 5.1 %long_convs.3 = bf16[16,288,128]{2,1,0:T(8,128)(2,1)S(1)} custom-call(bf16[16,528,128]{2,1,0:T(8,128)(2,1)} %all-to-all-done.in_ref.filter_ref, bf16[16,528,128]{2,1,0:T(8,128)(2,1)} %all-to-all-done.in_ref.filter_ref, bf16[16,16,128]{2,1,0:T(8,128)(2,1)S(1)} %get-tuple-element.47.refs_0_, f32[1,1]{1,0:T(1,128)S(6)} %add.3.refs_1_), custom_call_target="tpu_custom_call" | custom-call | flops 2147483648 | bytes 2359296 | tf_op jit(solution)/shard_map/long_convs/pallas_call | solution.py:470
  115.1 1.0 copy-done.15
  116.2 6.4 %collective-permute-done.5.part_ref.log_ref = bf16[128,2176]{1,0:T(8,128)(2,1)S(1)} collective-permute-done((bf16[128,2176]{1,0:T(8,128)(2,1)S(1)}, bf16[128,2176]{1,0:T(8,128)(2,1)S(1)}, u32[]{:S(2)}, u32[]{:S(2)}) %collective-permute-start.5) | collective-permute-done | bytes 557088 | tf_op jit(solution)/shard_map/ppermute | solution.py:27
  123.4 4.3 %all-to-all-start.1 = ((bf16[16,288,128]{2,1,0:T(8,128)(2,1)}), bf16[16,288,128]{2,1,0:T(8,128)(2,1)}, u32[]{:S(2)}, u32[]{:S(2)}) async-start(bf16[16,288,128]{2,1,0:T(8,128)(2,1)} %copy-done.15), calls=%async_computation.1 | async-start | bytes 2359296 | tf_op jit(solution)/shard_map/all_to_all | solution.py:783
  127.7 1.2 copy-done.4
  128.9 1.2 copy-done.6
  130.1 1.2 copy-done.8
  131.3 4.7 %attend_whole.1._ = bf16[128,4096]{1,0:T(8,128)(2,1)} custom-call(s32[1]{0:T(128)} %bitcast.place_ref, bf16[128,4096]{1,0:T(8,128)(2,1)S(1)} %copy-done.8, bf16[128,4096]{1,0:T(8,128)(2,1)S(1)} %copy-done.4, bf16[128,4096]{1,0:T(8,128)(2,1)S(1)} %copy-done.6, bf16[256,2048]{1,0:T(8,128)(2,1)} %collective-permute-done.2.kp_ref.vp_ref, ...), custom_call_target="tpu_custom_call" | custom-call | flops 268435456 | bytes 5242880 | tf_op jit(solution)/shard_map/attend_whole/pallas_call | solution.py:204
  136.1 3.2 %attend_merge.1 = bf16[128,4096]{1,0:T(8,128)(2,1)} custom-call(s32[1]{0:T(128)} %bitcast.place_ref, bf16[128,4096]{1,0:T(8,128)(2,1)S(1)} %copy-done.8, bf16[128,4096]{1,0:T(8,128)(2,1)S(1)} %copy-done.4, bf16[128,4096]{1,0:T(8,128)(2,1)S(1)} %copy-done.6, bf16[128,2176]{1,0:T(8,128)(2,1)S(1)} %copy-done.14, ...), custom_call_target="tpu_custom_call", output_to_operand_aliasing={{}: (6, {})} | custom-call | flops 134217728 | bytes 2621440 | tf_op jit(solution)/shard_map/attend_merge/pallas_call | solution.py:215
  139.3 6.0 %after_exchange.2 = (bf16[128,4096]{1,0:T(8,128)(2,1)}, bf16[128,4096]{1,0:T(8,128)(2,1)}, bf16[128,4096]{1,0:T(8,128)(2,1)}) custom-call(bf16[16,272,128]{2,1,0:T(8,128)(2,1)} %all-to-all-done.2.in_ref, bf16[128,4096]{1,0:T(8,128)(2,1)S(1)} %copy-done.2, bf16[128,4096]{1,0:T(8,128)(2,1)S(1)} %copy-done, bf16[128,4096]{1,0:T(8,128)(2,1)S(1)} %copy-done.1, ...), custom_call_target="tpu_custom_call" | custom-call | flops 23592960 | bytes 4718592 | tf_op jit(solution)/shard_map/after_exchange/pallas_call | solution.py:710
  145.3 10.4 %all-to-all-done.1.in_ref = bf16[16,288,128]{2,1,0:T(8,128)(2,1)} async-done(((bf16[16,288,128]{2,1,0:T(8,128)(2,1)}), bf16[16,288,128]{2,1,0:T(8,128)(2,1)}, u32[]{:S(2)}, u32[]{:S(2)}) %all-to-all-start.1) | async-done | bytes 1179680 | tf_op jit(solution)/shard_map/all_to_all | solution.py:783
  157.5 6.3 %after_exchange.3 = (bf16[128,4096]{1,0:T(8,128)(2,1)}, bf16[128,4096]{1,0:T(8,128)(2,1)}, bf16[128,4096]{1,0:T(8,128)(2,1)}, f32[128,256]{1,0:T(8,128)}) custom-call(bf16[16,288,128]{2,1,0:T(8,128)(2,1)} %all-to-all-done.1.in_ref, bf16[128,4096]{1,0:T(8,128)(2,1)S(1)} %copy-done.2, ...), custom_call_target="tpu_custom_call", output_to_operand_aliasing={{0}: (7, {}), {1}: (8, {}), {2}: (9, {})} | custom-call | flops 23592960 | bytes 4718592 | tf_op jit(solution)/shard_map/after_exchange/pallas_call | solution.py:710
  (43 shorter events, 4.4 us)
Async XLA Ops:
  2.4 8.1 %collective-permute-start = (bf16[24,4096]{1,0:T(8,128)(2,1)}, bf16[24,4096]{1,0:T(8,128)(2,1)S(1)}, u32[]{:S(2)}, u32[]{:S(2)}) collective-permute-start(bf16[24,4096]{1,0:T(8,128)(2,1)} %edge_rows.2), channel_id=1, source_target_pairs={{0,2},{2,4},{4,6},{6,8},{8,10},{10,12},{12,14},{14,16},{16,18},{18... | collective-permute-start | bytes 589832 | tf_op jit(solution)/shard_map/ppermute | solution.py:27
  10.4 0.7 copy-start.10
  20.0 55.0 %all-to-all-start = ((bf16[16,528,128]{2,1,0:T(8,128)(2,1)}), bf16[16,528,128]{2,1,0:T(8,128)(2,1)}, u32[]{:S(2)}, u32[]{:S(2)}) async-start(bf16[16,528,128]{2,1,0:T(8,128)(2,1)} %before_exchange.1), calls=%async_computation | async-start | bytes 4325376 | tf_op jit(solution)/shard_map/all_to_all | solution.py:763
  25.3 1.0 slice-start
  25.3 1.2 slice-start.1
  25.3 4.3 %copy-start.7 = (bf16[128,4096]{1,0:T(8,128)(2,1)S(1)}, bf16[128,4096]{1,0:T(8,128)(2,1)}, u32[]{:S(2)}) copy-start(bf16[128,4096]{1,0:T(8,128)(2,1)} %q_ref.3) | copy-start | bytes 3145732
  25.3 9.6 %copy-start = (bf16[128,4096]{1,0:T(8,128)(2,1)S(1)}, bf16[128,4096]{1,0:T(8,128)(2,1)}, u32[]{:S(2)}) copy-start(bf16[128,4096]{1,0:T(8,128)(2,1)} %k_ref.9) | copy-start | bytes 3145732
  25.3 9.6 %copy-start.1 = (bf16[128,4096]{1,0:T(8,128)(2,1)S(1)}, bf16[128,4096]{1,0:T(8,128)(2,1)}, u32[]{:S(2)}) copy-start(bf16[128,4096]{1,0:T(8,128)(2,1)} %v_ref.9) | copy-start | bytes 3145732
  25.4 9.6 %copy-start.2 = (bf16[128,4096]{1,0:T(8,128)(2,1)S(1)}, bf16[128,4096]{1,0:T(8,128)(2,1)}, u32[]{:S(2)}) copy-start(bf16[128,4096]{1,0:T(8,128)(2,1)} %og_ref.3) | copy-start | bytes 3145732
  27.6 58.2 %collective-permute-start.2 = (bf16[256,2048]{1,0:T(8,128)(2,1)}, bf16[256,2048]{1,0:T(8,128)(2,1)}, u32[]{:S(2)}, u32[]{:S(2)}) collective-permute-start(bf16[256,2048]{1,0:T(8,128)(2,1)} %pad_maximum_fusion), channel_id=1, source_target_pairs={{0,2},{2,4},{4,6},{6,8},{8,10},{10,12},{12,14},{14,16},{16,18},{18... | collective-permute-start | bytes 3145736 | tf_op jit(solution)/shard_map/ppermute | solution.py:27
  30.5 50.6 %collective-permute-start.1 = (bf16[128,2048]{1,0:T(8,128)(2,1)}, bf16[128,2048]{1,0:T(8,128)(2,1)}, u32[]{:S(2)}, u32[]{:S(2)}) collective-permute-start(bf16[128,2048]{1,0:T(8,128)(2,1)} %slice.9), channel_id=1, source_target_pairs={{2,0},{4,2},{6,4},{8,6},{10,8},{12,10},{14,12},{16,14},{18,16},{20... | collective-permute-start | bytes 1572872 | tf_op jit(solution)/shard_map/ppermute | solution.py:27
  34.9 46.1 %collective-permute-start.3 = (bf16[24,4096]{1,0:T(8,128)(2,1)S(1)}, bf16[24,4096]{1,0:T(8,128)(2,1)S(1)}, u32[]{:S(2)}, u32[]{:S(2)}) collective-permute-start(bf16[24,4096]{1,0:T(8,128)(2,1)S(1)} %edge_rows.3), channel_id=1, source_target_pairs={{2,0},{4,2},{6,4},{8,6},{10,8},{12,10},{14,12},{16,14},{18,16},{20... | collective-permute-start | bytes 589832 | tf_op jit(solution)/shard_map/ppermute | solution.py:27
  80.0 1.0 copy-start.16
  81.1 18.4 %copy-start.17 = (bf16[24,4096]{1,0:T(8,128)(2,1)}, bf16[24,4096]{1,0:T(8,128)(2,1)S(1)}, u32[]{:S(2)}) copy-start(bf16[24,4096]{1,0:T(8,128)(2,1)S(1)} %collective-permute-done.3.next_ref) | copy-start | bytes 589828
  85.7 37.6 %all-to-all-start.2 = ((bf16[16,272,128]{2,1,0:T(8,128)(2,1)}), bf16[16,272,128]{2,1,0:T(8,128)(2,1)}, u32[]{:S(2)}, u32[]{:S(2)}) async-start(bf16[16,272,128]{2,1,0:T(8,128)(2,1)} %copy-done.16), calls=%async_computation.2 | async-start | bytes 2228224 | tf_op jit(solution)/shard_map/all_to_all | solution.py:783
  90.0 9.4 %copy-start.3 = (bf16[128,4096]{1,0:T(8,128)(2,1)S(1)}, bf16[128,4096]{1,0:T(8,128)(2,1)}, u32[]{:S(2)}) copy-start(bf16[128,4096]{1,0:T(8,128)(2,1)} %k_ref.7) | copy-start | bytes 3145732
  90.0 9.4 %copy-start.5 = (bf16[128,4096]{1,0:T(8,128)(2,1)S(1)}, bf16[128,4096]{1,0:T(8,128)(2,1)}, u32[]{:S(2)}) copy-start(bf16[128,4096]{1,0:T(8,128)(2,1)} %v_ref.7) | copy-start | bytes 3145732
  103.0 19.6 %collective-permute-start.5 = (bf16[128,2176]{1,0:T(8,128)(2,1)S(1)}, bf16[128,2176]{1,0:T(8,128)(2,1)S(1)}, u32[]{:S(2)}, u32[]{:S(2)}) collective-permute-start(bf16[128,2176]{1,0:T(8,128)(2,1)S(1)} %attend_next.1), channel_id=1, source_target_pairs={{0,2},{2,4},{4,6},{6,8},{8,10},{10,12},{12,14},{14,16},{16,18},{18... | collective-permute-start | bytes 1671176 | tf_op jit(solution)/shard_map/ppermute | solution.py:27
  105.0 3.8 %collective-permute-start.4 = (f32[1,1]{1,0:T(1,128)}, f32[1,1]{1,0:T(1,128)}, u32[]{:S(2)}, u32[]{:S(2)}) collective-permute-start(f32[1,1]{1,0:T(1,128)} %get-tuple-element.48), channel_id=1, source_target_pairs={{0,1},{1,0},{2,3},{3,2},{4,5},{5,4},{6,7},{7,6},{8,9},{9,8},{10,11... | collective-permute-start | bytes 20 | tf_op jit(solution)/shard_map/ppermute | solution.py:34
  115.1 1.0 copy-start.15
  122.5 0.8 copy-start.13
  123.4 32.3 %all-to-all-start.1 = ((bf16[16,288,128]{2,1,0:T(8,128)(2,1)}), bf16[16,288,128]{2,1,0:T(8,128)(2,1)}, u32[]{:S(2)}, u32[]{:S(2)}) async-start(bf16[16,288,128]{2,1,0:T(8,128)(2,1)} %copy-done.15), calls=%async_computation.1 | async-start | bytes 2359296 | tf_op jit(solution)/shard_map/all_to_all | solution.py:783
  127.7 1.2 copy-start.4
  128.9 1.2 copy-start.6
  130.1 1.2 copy-start.8
  131.3 4.7 %copy-start.14 = (bf16[128,2176]{1,0:T(8,128)(2,1)S(1)}, bf16[128,2176]{1,0:T(8,128)(2,1)}, u32[]{:S(2)}) copy-start(bf16[128,2176]{1,0:T(8,128)(2,1)} %copy-done.13) | copy-start | bytes 1671172
  136.1 3.2 %copy-start.9 = (f32[3,7,4096]{2,1,0:T(8,128)S(1)}, f32[3,7,4096]{2,1,0:T(8,128)}, u32[]{:S(2)}) copy-start(f32[3,7,4096]{2,1,0:T(8,128)} %taps_ref.3) | copy-start | bytes 1032196
  136.1 3.2 %copy-start.11 = (bf16[24,4096]{1,0:T(8,128)(2,1)S(1)}, bf16[24,4096]{1,0:T(8,128)(2,1)}, u32[]{:S(2)}) copy-start(bf16[24,4096]{1,0:T(8,128)(2,1)} %copy-done.10) | copy-start | bytes 589828
  136.1 3.2 %copy-start.18 = (bf16[24,4096]{1,0:T(8,128)(2,1)S(1)}, bf16[24,4096]{1,0:T(8,128)(2,1)}, u32[]{:S(2)}) copy-start(bf16[24,4096]{1,0:T(8,128)(2,1)} %copy-done.17) | copy-start | bytes 589828
  155.7 0.9 copy-start.12
  156.6 0.9 copy-start.19

commit v14 on v13

--- a/solution.py
+++ b/solution.py
@@ -57,10 +57,12 @@
     return [slice(head * HEAD_DIM, (head + 1) * HEAD_DIM) for head in range(width // HEAD_DIM)]
 
 
-def attend_next_kernel(q_ref, k_ref, v_ref, out_ref, logs_ref):
+def attend_part_kernel(causal, q_ref, k_ref, v_ref, out_ref, logs_ref):
     rows, width = q_ref.shape
     heads = width // HEAD_DIM
     step = pl.program_id(0)
+    row = lax.broadcasted_iota(jnp.int32, (rows, rows), 0)
+    col = lax.broadcasted_iota(jnp.int32, (rows, rows), 1)
     lane = lax.broadcasted_iota(jnp.int32, (rows, LANES), 1)
 
     @pl.when(step == 0)
@@ -72,6 +74,8 @@
         lax.dot_general(q_ref[:, at], k_ref[:, at], NT, preferred_element_type=F32) * SCALE
         for at in places
     ]
+    if causal:
+        scores = [jnp.where(col <= row, score, -jnp.inf) for score in scores]
     largest = [jnp.max(score, axis=1, keepdims=True) for score in scores]
     raised = [jnp.exp(score - top) for score, top in zip(scores, largest)]
     totals = [jnp.sum(r, axis=1, keepdims=True) for r in raised]
@@ -96,41 +100,35 @@
         out_ref[:, out_ref.shape[1] - LANES :] = terms.astype(BF16)
 
 
-def attend_merge_kernel(place_ref, q_ref, k_ref, v_ref, part_ref, log_ref, _, out_ref):
-    rows, width = q_ref.shape
+def combine_kernel(place_ref, own_ref, prev_ref, own_log_ref, prev_log_ref, _, out_ref, own_share, prev_share):
+    rows, width = own_ref.shape
     heads = width // HEAD_DIM
     step = pl.program_id(0)
-    row = lax.broadcasted_iota(jnp.int32, (rows, rows), 0)
-    col = lax.broadcasted_iota(jnp.int32, (rows, rows), 1)
-    own_ok = col <= row
-    lane = lax.broadcasted_iota(jnp.int32, (rows, LANES), 1) & (LOG_LANES - 1)
-    has_prev = jnp.broadcast_to(place_ref[0], (rows, 1)) > 0
-    places = places_of(width)
-    terms = log_ref[...].astype(F32)
-    scores = [
-        lax.dot_general(q_ref[:, at], k_ref[:, at], NT, preferred_element_type=F32) * SCALE
-        for at in places
-    ]
-    scores = [jnp.where(own_ok, score, -jnp.inf) for score in scores]
-    logs = [
-        jnp.sum(jnp.where(lane == step * heads + head, terms, 0.0), axis=1, keepdims=True)
-        for head in range(heads)
-    ]
-    logs = [jnp.where(has_prev, log, -jnp.inf) for log in logs]
-    largest = [
-        jnp.maximum(jnp.max(score, axis=1, keepdims=True), log) for score, log in zip(scores, logs)
-    ]
-    raised = [jnp.exp(score - top) for score, top in zip(scores, largest)]
-    prevs = [jnp.exp(log - top) for log, top in zip(logs, largest)]
-    inverses = [
-        1.0 / (jnp.sum(r, axis=1, keepdims=True) + prev) for r, prev in zip(raised, prevs)
-    ]
-    weights = [(r * inverse).astype(BF16) for r, inverse in zip(raised, inverses)]
-    mixed = [
-        jnp.dot(weight, v_ref[:, at], preferred_element_type=F32) for weight, at in zip(weights, places)
-    ]
-    for head, at in enumerate(places):
-        total = mixed[head] + (prevs[head] * inverses[head]) * part_ref[:, at].astype(F32)
+    lane = lax.broadcasted_iota(jnp.int32, (rows, LANES), 1)
+
+    @pl.when(step == 0)
+    def _():
+        def joined(ref):
+            terms = ref[...].astype(F32)
+            middle = pltpu.roll(terms, LANES - LOG_LANES, 1)
+            return terms + (middle + pltpu.roll(terms, LANES - 2 * LOG_LANES, 1))
+
+        own = joined(own_log_ref)
+        has_prev = jnp.broadcast_to(place_ref[0], (rows, LANES)) > 0
+        prev = jnp.where(has_prev, joined(prev_log_ref), -jnp.inf)
+        largest = jnp.maximum(own, prev)
+        own, prev = jnp.exp(own - largest), jnp.exp(prev - largest)
+        inverse = 1.0 / (own + prev)
+        own_share[...] = own * inverse
+        prev_share[...] = prev * inverse
+
+    def column(ref, head):
+        return jnp.sum(jnp.where(lane == step * heads + head, ref[...], 0.0), axis=1, keepdims=True)
+
+    owns = [column(own_share, head) for head in range(heads)]
+    prevs = [column(prev_share, head) for head in range(heads)]
+    for head, at in enumerate(places_of(width)):
+        total = owns[head] * own_ref[:, at].astype(F32) + prevs[head] * prev_ref[:, at].astype(F32)
         out_ref[:, at] = total.astype(BF16)
 
 
@@ -174,12 +172,12 @@
     )
 
 
-def attend_next(query, key, value):
-    rows, channels = query.shape
+def attend_part(query, key, value, channels, causal):
+    rows = query.shape[0]
     tile = min(512, channels)
     block = pl.BlockSpec((rows, tile), lambda i: (0, i))
     return pl.pallas_call(
-        attend_next_kernel,
+        functools.partial(attend_part_kernel, causal),
         grid=(channels // tile,),
         in_specs=[block] * 3,
         out_specs=pl.BlockSpec((rows, channels + LANES), lambda i: (0, 0)),
@@ -187,50 +185,57 @@
         scratch_shapes=[pltpu.VMEM((rows, LANES), F32)],
         compiler_params=params(LONG_VMEM),
         cost_estimate=attend_cost(rows, channels),
-        name="attend_next",
+        name="attend_part",
     )(query, key, value)
 
 
-def attend(query, key, value, part, previous, position):
+def attend_whole(query, key, value, previous, place):
     rows, channels = query.shape
     half = channels // 2
     tile = min(512, half)
     steps = half // tile
-    place = position.astype(jnp.int32).reshape(1)
-    smem = pl.BlockSpec(memory_space=pltpu.SMEM)
     first = pl.BlockSpec((rows, tile), lambda i: (0, i))
     second = pl.BlockSpec((rows, tile), lambda i: (0, steps + i))
-    out = jax.ShapeDtypeStruct((rows, channels), BF16)
-    whole = pl.pallas_call(
+    return pl.pallas_call(
         attend_whole_kernel,
         grid=(steps,),
-        in_specs=[smem, second, second, second, first, pl.BlockSpec((rows, tile), lambda i: (1, i))],
+        in_specs=[
+            pl.BlockSpec(memory_space=pltpu.SMEM),
+            second,
+            second,
+            second,
+            first,
+            pl.BlockSpec((rows, tile), lambda i: (1, i)),
+        ],
         out_specs=second,
-        out_shape=out,
+        out_shape=jax.ShapeDtypeStruct((rows, channels), BF16),
         compiler_params=params(LONG_VMEM),
         cost_estimate=attend_cost(rows, channels),
         name="attend_whole",
     )(place, query, key, value, previous, previous)
+
+
+def combine(own, prev, whole, place):
+    rows, channels = whole.shape
+    half = channels // 2
+    tile = min(512, half)
+    block = pl.BlockSpec((rows, tile), lambda i: (0, i))
     log_at = half // LANES
+    log = pl.BlockSpec((rows, LANES), lambda i: (0, log_at))
+    share = pltpu.VMEM((rows, LANES), F32)
     return pl.pallas_call(
-        attend_merge_kernel,
-        grid=(steps,),
-        in_specs=[
-            smem,
-            first,
-            first,
-            first,
-            first,
-            pl.BlockSpec((rows, LANES), lambda i: (0, log_at)),
-            pl.BlockSpec(memory_space=pl.ANY),
-        ],
-        out_specs=first,
-        out_shape=out,
-        input_output_aliases={6: 0},
-        compiler_params=params(LONG_VMEM),
-        cost_estimate=attend_cost(rows, half),
-        name="attend_merge",
-    )(place, query, key, value, part, part, whole)
+        combine_kernel,
+        grid=(half // tile,),
+        in_specs=[pl.BlockSpec(memory_space=pltpu.SMEM), block, block, log, log]
+        + [pl.BlockSpec(memory_space=pl.ANY)],
+        out_specs=block,
+        out_shape=jax.ShapeDtypeStruct((rows, channels), BF16),
+        input_output_aliases={5: 0},
+        scratch_shapes=[share, share],
+        compiler_params=params(),
+        cost_estimate=attend_cost(rows, half // 4),
+        name="combine",
+    )(place, own, prev, own, prev, whole)
 
 
 def edge_kernel(first, *refs):
@@ -725,7 +730,7 @@
         out_shape=[grad] * 3 + [jax.ShapeDtypeStruct((rows, groups), F32)] * last,
         scratch_shapes=[pltpu.VMEM((groups, rows), F32), pltpu.VMEM((1, LANES), F32)] * last
         + [ext] * 5,
-        compiler_params=params(LONG_VMEM),
+        compiler_params=params(),
         cost_estimate=pl.CostEstimate(
             flops=90 * rows * channels, bytes_accessed=18 * rows * channels, transcendentals=0
         ),
@@ -773,27 +778,30 @@
             raw = (raw, total_over(squares, "tp"))
         results = long_convs(received, raw, cpd, gpd, chunk, chunks)
         if chunk + 1 == chunks:
-            part = shifted(attend_next(query_next, key_heads, value_heads), "ctx", 1)
+            part = attend_part(query_next, key_heads, value_heads, half, False)
+            results, part = lax.optimization_barrier((results, part))
         if chunk == 0:
             results, received, query_next, previous, following = lax.optimization_barrier(
                 (results, received, query_next, previous, following)
             )
-        else:
-            results, part = lax.optimization_barrier((results, part))
         returned.append(lax.all_to_all(results, "ctx", split_axis=0, concat_axis=0, tiled=True))
-    attention = attend(query_heads, key_heads, value_heads, part, previous, position)
+    part = shifted(part, "ctx", 1)
+    place = position.astype(jnp.int32).reshape(1)
+    whole = attend_whole(query_heads, key_heads, value_heads, previous, place)
+    own = attend_part(query_heads, key_heads, value_heads, half, True)
     bound = math.sqrt(rows * n * groups * tp)
     grads = ()
     for chunk in range(chunks):
         if chunk > 0:
-            returned[chunk], attention, *grads = lax.optimization_barrier(
-                (returned[chunk], attention, *grads)
+            returned[chunk], whole, own, *grads = lax.optimization_barrier(
+                (returned[chunk], whole, own, *grads)
             )
         grads = after_exchange(
             returned[chunk], output_grad, hyena_key, hyena_value, tail, following, short_filter, groups,
             chunk, chunks, grads, bound,
         )
-    return (attention, *grads)
+    part, *grads = lax.optimization_barrier((part, *grads))
+    return (combine(own, part, whole, place), *grads)
 
 
 def solution(mesh):

time: 165 us -> 162 us (0.982)
  local copies, waits for them, and re-layouts: 11.1 us -> 5.35 us
  Pallas kernels: 53.9 us -> 58.5 us
  waiting for transfers between devices: 68 us -> 65.3 us
    ppermute x5, waiting for transfers between devices: 17.2 us -> 10.8 us  [shifted(): return lax.ppermute(block, axis, route)]
    all_to_all x2, waiting for transfers between devices: 10.4 us -> 16.4 us  [on_device(): lax.all_to_all(results, 'ctx', split_axis=0, concat_axis=0, tiled=True)]
    unnamed x40 -> x24, local copies, waits for them, and re-layouts: 9.12 us -> 3.37 us
    pallas_call x3 -> x4, Pallas kernels: 11.5 us -> 14.4 us  [the longest x2 5.88 us: attend_part(): pl.pallas_call(functools.partial(attend_part_kernel, causal), grid=(chann...]
    ppermute x1, waiting for transfers between devices: 2.29 us -> 0.01 us  [total_over(): lax.ppermute(value, axis, [(i, i ^ distance) for i in range(size)])]
  transfers between devices with their start and end apart: 9 -> 9, of which waited for: 6 -> 5; matrix products, arithmetic and copies ran while one was open for 1% -> 1% of each run, Pallas kernels for 23% -> 27%
where the time goes in v14:
time: 162 us; the launch traced here: 160 us
  waiting for transfers between devices  65.3 us (40%)
  Pallas kernels  58.5 us (36%)
  starting transfers between devices  28 us (17%)
  local copies, waits for them, and re-layouts  5.35 us (3%)
  between operations  2.18 us (1%)
    all_to_all x1, waiting for transfers between devices, on_device(): lax.all_to_all(send, 'ctx', split_axis=0, concat_axis=0, tiled=True)  38.1 us
    all_to_all x2, waiting for transfers between devices, on_device(): lax.all_to_all(results, 'ctx', split_axis=0, concat_axis=0, tiled=True)  16.4 us
    pallas_call x2, Pallas kernels, after_exchange(): pl.pallas_call(functools.partial(after_kernel, cpd, gpd, chunks, last, bo...  12.9 us
    ppermute x5, starting transfers between devices, shifted(): return lax.ppermute(block, axis, route)  12.3 us
    pallas_call x2, Pallas kernels, long_convs(): pl.pallas_call(functools.partial(conv_kernel, cpd, gpd, chunk), grid=(pai...  11.2 us
    ppermute x5, waiting for transfers between devices, shifted(): return lax.ppermute(block, axis, route)  10.8 us
    pallas_call x1, Pallas kernels, filter_products(): pl.pallas_call(functools.partial(gram_kernel, cpd // gpd), grid=(pairs,),...  9.37 us
    all_to_all x2, starting transfers between devices, on_device(): lax.all_to_all(results, 'ctx', split_axis=0, concat_axis=0, tiled=True)  8.92 us
  transfers between devices with their start and end apart: 9, of which 5 were waited for; matrix products, arithmetic and copies ran while one was open for 1% of the time, Pallas kernels for 27%

profile of v14, /device:TPU:16, one launch (start us, length us, event | category | flops | bytes accessed | tf_op | source)
XLA Modules:
  0.0 160.4 jit_solution(17829616544497702481)
XLA Ops:
  0.6 1.7 %edge_rows.2 = bf16[24,4096]{1,0:T(8,128)(2,1)} custom-call(bf16[128,4096]{1,0:T(8,128)(2,1)} %refs_6_.1, bf16[128,4096]{1,0:T(8,128)(2,1)} %k_ref.9, bf16[128,4096]{1,0:T(8,128)(2,1)} %v_ref.9), custom_call_target="tpu_custom_call" | custom-call | tf_op jit(solution)/shard_map/edge_rows/pallas_call | solution.py:251
  2.4 1.9 %collective-permute-start = (bf16[24,4096]{1,0:T(8,128)(2,1)}, bf16[24,4096]{1,0:T(8,128)(2,1)S(1)}, u32[]{:S(2)}, u32[]{:S(2)}) collective-permute-start(bf16[24,4096]{1,0:T(8,128)(2,1)} %edge_rows.2), channel_id=1, source_target_pairs={{0,2},{2,4},{4,6},{6,8},{8,10},{10,12},{12,14},{14,16},{16,18},{18... | collective-permute-start | bytes 589832 | tf_op jit(solution)/shard_map/ppermute | solution.py:27
  4.3 6.2 %collective-permute-done.refs_4_.refs_10_.tail_ref = bf16[24,4096]{1,0:T(8,128)(2,1)S(1)} collective-permute-done((bf16[24,4096]{1,0:T(8,128)(2,1)}, bf16[24,4096]{1,0:T(8,128)(2,1)S(1)}, u32[]{:S(2)}, u32[]{:S(2)}) %collective-permute-start) | collective-permute-done | bytes 196640 | tf_op jit(solution)/shard_map/ppermute | solution.py:27
  10.4 0.7 copy-done.10
  11.1 8.9 %before_exchange.1 = bf16[16,528,128]{2,1,0:T(8,128)(2,1)} custom-call(bf16[128,4096]{1,0:T(8,128)(2,1)} %refs_6_.1, bf16[128,4096]{1,0:T(8,128)(2,1)} %k_ref.9, bf16[128,4096]{1,0:T(8,128)(2,1)} %v_ref.9, bf16[128,4096]{1,0:T(8,128)(2,1)} %og_ref.3, bf16[24,4096]{1,0:T(8,128)(2,1)} %copy-done.10, f32[3,7,4096]{2,1,0:T(8,128)} %taps_ref.3, ...), custom_call_target="tpu_custom_call" | custom-call | flops 26214400 | bytes 6291456 | tf_op jit(solution)/shard_map/before_exchange/pallas_call | solution.py:360
  20.0 5.3 %all-to-all-start = ((bf16[16,528,128]{2,1,0:T(8,128)(2,1)}), bf16[16,528,128]{2,1,0:T(8,128)(2,1)}, u32[]{:S(2)}, u32[]{:S(2)}) async-start(bf16[16,528,128]{2,1,0:T(8,128)(2,1)} %before_exchange.1), calls=%async_computation | async-start | bytes 4325376 | tf_op jit(solution)/shard_map/all_to_all | solution.py:768
  25.4 1.0 slice-done
  26.5 1.1 pad_maximum_fusion
  27.6 2.0 %collective-permute-start.2 = (bf16[256,2048]{1,0:T(8,128)(2,1)}, bf16[256,2048]{1,0:T(8,128)(2,1)}, u32[]{:S(2)}, u32[]{:S(2)}) collective-permute-start(bf16[256,2048]{1,0:T(8,128)(2,1)} %pad_maximum_fusion), channel_id=1, source_target_pairs={{0,2},{2,4},{4,6},{6,8},{8,10},{10,12},{12,14},{14,16},{16,18},{18... | collective-permute-start | bytes 3145736 | tf_op jit(solution)/shard_map/ppermute | solution.py:27
  29.6 0.8 slice.9
  30.5 4.4 %collective-permute-start.1 = (bf16[128,2048]{1,0:T(8,128)(2,1)}, bf16[128,2048]{1,0:T(8,128)(2,1)}, u32[]{:S(2)}, u32[]{:S(2)}) collective-permute-start(bf16[128,2048]{1,0:T(8,128)(2,1)} %slice.9), channel_id=1, source_target_pairs={{2,0},{4,2},{6,4},{8,6},{10,8},{12,10},{14,12},{16,14},{18,16},{20... | collective-permute-start | bytes 1572872 | tf_op jit(solution)/shard_map/ppermute | solution.py:27
  34.9 1.9 %collective-permute-start.3 = (bf16[24,4096]{1,0:T(8,128)(2,1)S(1)}, bf16[24,4096]{1,0:T(8,128)(2,1)S(1)}, u32[]{:S(2)}, u32[]{:S(2)}) collective-permute-start(bf16[24,4096]{1,0:T(8,128)(2,1)S(1)} %edge_rows.3), channel_id=1, source_target_pairs={{2,0},{4,2},{6,4},{8,6},{10,8},{12,10},{14,12},{16,14},{18,16},{20... | collective-permute-start | bytes 589832 | tf_op jit(solution)/shard_map/ppermute | solution.py:27
  36.9 38.1 %all-to-all-done.in_ref.filter_ref = bf16[16,528,128]{2,1,0:T(8,128)(2,1)} async-done(((bf16[16,528,128]{2,1,0:T(8,128)(2,1)}), bf16[16,528,128]{2,1,0:T(8,128)(2,1)}, u32[]{:S(2)}, u32[]{:S(2)}) %all-to-all-start) | async-done | bytes 2162720 | tf_op jit(solution)/shard_map/all_to_all | solution.py:768
  75.0 6.1 %long_convs.2 = bf16[16,272,128]{2,1,0:T(8,128)(2,1)} custom-call(bf16[16,528,128]{2,1,0:T(8,128)(2,1)} %all-to-all-done.in_ref.filter_ref, bf16[16,528,128]{2,1,0:T(8,128)(2,1)} %all-to-all-done.in_ref.filter_ref), custom_call_target="tpu_custom_call" | custom-call | flops 2147483648 | bytes 2228224 | tf_op jit(solution)/shard_map/long_convs/pallas_call | solution.py:475
  81.1 4.7 %collective-permute-done.2.kp_ref.vp_ref = bf16[256,2048]{1,0:T(8,128)(2,1)} collective-permute-done((bf16[256,2048]{1,0:T(8,128)(2,1)}, bf16[256,2048]{1,0:T(8,128)(2,1)}, u32[]{:S(2)}, u32[]{:S(2)}) %collective-permute-start.2) | collective-permute-done | bytes 1048608 | tf_op jit(solution)/shard_map/ppermute | solution.py:27
  85.7 4.3 %all-to-all-start.2 = ((bf16[16,272,128]{2,1,0:T(8,128)(2,1)}), bf16[16,272,128]{2,1,0:T(8,128)(2,1)}, u32[]{:S(2)}, u32[]{:S(2)}) async-start(bf16[16,272,128]{2,1,0:T(8,128)(2,1)} %long_convs.2), calls=%async_computation.2 | async-start | bytes 2228224 | tf_op jit(solution)/shard_map/all_to_all | solution.py:787
  90.1 9.4 %filter_products.1 = (bf16[16,16,128]{2,1,0:T(8,128)(2,1)S(1)}, f32[1,1]{1,0:T(1,128)}) custom-call(bf16[16,528,128]{2,1,0:T(8,128)(2,1)} %all-to-all-done.in_ref.filter_ref), custom_call_target="tpu_custom_call" | custom-call | flops 2147483648 | bytes 2162688 | tf_op jit(solution)/shard_map/filter_products/pallas_call | solution.py:556
  99.4 1.5 collective-permute-start.4
  100.9 3.5 %attend_part.2 = bf16[128,2176]{1,0:T(8,128)(2,1)S(1)} custom-call(bf16[128,2048]{1,0:T(8,128)(2,1)} %collective-permute-done.1.q_ref, bf16[128,4096]{1,0:T(8,128)(2,1)S(1)} %copy-done.3, bf16[128,4096]{1,0:T(8,128)(2,1)S(1)} %copy-done.4), custom_call_target="tpu_custom_call" | custom-call | flops 134217728 | bytes 2621440 | tf_op jit(solution)/shard_map/attend_part/pallas_call | solution.py:179
  104.5 0.8 copy-done.9
  106.6 5.1 %long_convs.3 = bf16[16,288,128]{2,1,0:T(8,128)(2,1)S(1)} custom-call(bf16[16,528,128]{2,1,0:T(8,128)(2,1)} %all-to-all-done.in_ref.filter_ref, bf16[16,528,128]{2,1,0:T(8,128)(2,1)} %all-to-all-done.in_ref.filter_ref, bf16[16,16,128]{2,1,0:T(8,128)(2,1)S(1)} %get-tuple-element.53.refs_0_, f32[1,1]{1,0:T(1,128)S(6)} %add.3.refs_1_), custom_call_target="tpu_custom_call" | custom-call | flops 2147483648 | bytes 2359296 | tf_op jit(solution)/shard_map/long_convs/pallas_call | solution.py:475
  111.7 1.0 copy-done.8
  112.7 3.9 %all-to-all-done.2.in_ref = bf16[16,272,128]{2,1,0:T(8,128)(2,1)} async-done(((bf16[16,272,128]{2,1,0:T(8,128)(2,1)}), bf16[16,272,128]{2,1,0:T(8,128)(2,1)}, u32[]{:S(2)}, u32[]{:S(2)}) %all-to-all-start.2) | async-done | bytes 1114144 | tf_op jit(solution)/shard_map/all_to_all | solution.py:787
  116.6 4.6 %all-to-all-start.1 = ((bf16[16,288,128]{2,1,0:T(8,128)(2,1)}), bf16[16,288,128]{2,1,0:T(8,128)(2,1)}, u32[]{:S(2)}, u32[]{:S(2)}) async-start(bf16[16,288,128]{2,1,0:T(8,128)(2,1)} %copy-done.8), calls=%async_computation.1 | async-start | bytes 2359296 | tf_op jit(solution)/shard_map/all_to_all | solution.py:787
  121.3 2.0 %collective-permute-start.5 = (bf16[128,2176]{1,0:T(8,128)(2,1)}, bf16[128,2176]{1,0:T(8,128)(2,1)}, u32[]{:S(2)}, u32[]{:S(2)}) collective-permute-start(bf16[128,2176]{1,0:T(8,128)(2,1)} %copy-done.9), channel_id=1, source_target_pairs={{0,2},{2,4},{4,6},{6,8},{8,10},{10,12},{12,14},{14,16},{16,18},{18... | collective-permute-start | bytes 1671176 | tf_op jit(solution)/shard_map/ppermute | solution.py:27
  123.3 2.4 %attend_part.3.own_ref.own_log_ref = bf16[128,2176]{1,0:T(8,128)(2,1)S(1)} custom-call(bf16[128,4096]{1,0:T(8,128)(2,1)S(1)} %copy-done.6, bf16[128,4096]{1,0:T(8,128)(2,1)S(1)} %copy-done.3, bf16[128,4096]{1,0:T(8,128)(2,1)S(1)} %copy-done.4), custom_call_target="tpu_custom_call" | custom-call | flops 134217728 | bytes 2621440 | tf_op jit(solution)/shard_map/attend_part/pallas_call | solution.py:179
  125.7 0.8 copy-done.7
  126.5 4.7 %attend_whole.1._ = bf16[128,4096]{1,0:T(8,128)(2,1)} custom-call(s32[1]{0:T(128)} %bitcast.place_ref, bf16[128,4096]{1,0:T(8,128)(2,1)S(1)} %copy-done.6, bf16[128,4096]{1,0:T(8,128)(2,1)S(1)} %copy-done.3, bf16[128,4096]{1,0:T(8,128)(2,1)S(1)} %copy-done.4, bf16[256,2048]{1,0:T(8,128)(2,1)} %collective-permute-done.2.kp_ref.vp_ref, ...), custom_call_target="tpu_custom_call" | custom-call | flops 268435456 | bytes 5242880 | tf_op jit(solution)/shard_map/attend_whole/pallas_call | solution.py:199
  131.2 6.3 %after_exchange.2 = (bf16[128,4096]{1,0:T(8,128)(2,1)}, bf16[128,4096]{1,0:T(8,128)(2,1)}, bf16[128,4096]{1,0:T(8,128)(2,1)}) custom-call(bf16[16,272,128]{2,1,0:T(8,128)(2,1)} %all-to-all-done.2.in_ref, bf16[128,4096]{1,0:T(8,128)(2,1)} %og_ref.3, bf16[128,4096]{1,0:T(8,128)(2,1)} %k_ref.9, bf16[128,4096]{1,0:T(8,128)(2,1)} %v_ref.9, ...), custom_call_target="tpu_custom_call" | custom-call | flops 23592960 | bytes 4718592 | tf_op jit(solution)/shard_map/after_exchange/pallas_call | solution.py:715
  137.5 12.5 %all-to-all-done.1.in_ref = bf16[16,288,128]{2,1,0:T(8,128)(2,1)} async-done(((bf16[16,288,128]{2,1,0:T(8,128)(2,1)}), bf16[16,288,128]{2,1,0:T(8,128)(2,1)}, u32[]{:S(2)}, u32[]{:S(2)}) %all-to-all-start.1) | async-done | bytes 1179680 | tf_op jit(solution)/shard_map/all_to_all | solution.py:787
  149.9 6.6 %after_exchange.3 = (bf16[128,4096]{1,0:T(8,128)(2,1)}, bf16[128,4096]{1,0:T(8,128)(2,1)}, bf16[128,4096]{1,0:T(8,128)(2,1)}, f32[128,256]{1,0:T(8,128)}) custom-call(bf16[16,288,128]{2,1,0:T(8,128)(2,1)} %all-to-all-done.1.in_ref, bf16[128,4096]{1,0:T(8,128)(2,1)} %og_ref.3, ...), custom_call_target="tpu_custom_call", output_to_operand_aliasing={{0}: (7, {}), {1}: (8, {}), {2}: (9, {})} | custom-call | flops 23592960 | bytes 4718592 | tf_op jit(solution)/shard_map/after_exchange/pallas_call | solution.py:715
  156.5 3.9 %combine.1 = bf16[128,4096]{1,0:T(8,128)(2,1)} custom-call(s32[1]{0:T(128)} %bitcast.place_ref, bf16[128,2176]{1,0:T(8,128)(2,1)} %copy-done.7, bf16[128,2176]{1,0:T(8,128)(2,1)} %collective-permute-done.5.prev_ref.prev_log_ref, bf16[128,2176]{1,0:T(8,128)(2,1)} %copy-done.7, ...), custom_call_target="tpu_custom_call", output_to_operand_aliasing={{}: (5, {})} | custom-call | flops 33554432 | bytes 655360 | tf_op jit(solution)/shard_map/combine/pallas_call | solution.py:226
  (28 shorter events, 0.2 us)
Async XLA Ops:
  2.4 8.1 %collective-permute-start = (bf16[24,4096]{1,0:T(8,128)(2,1)}, bf16[24,4096]{1,0:T(8,128)(2,1)S(1)}, u32[]{:S(2)}, u32[]{:S(2)}) collective-permute-start(bf16[24,4096]{1,0:T(8,128)(2,1)} %edge_rows.2), channel_id=1, source_target_pairs={{0,2},{2,4},{4,6},{6,8},{8,10},{10,12},{12,14},{14,16},{16,18},{18... | collective-permute-start | bytes 589832 | tf_op jit(solution)/shard_map/ppermute | solution.py:27
  10.4 0.7 copy-start.10
  20.0 55.0 %all-to-all-start = ((bf16[16,528,128]{2,1,0:T(8,128)(2,1)}), bf16[16,528,128]{2,1,0:T(8,128)(2,1)}, u32[]{:S(2)}, u32[]{:S(2)}) async-start(bf16[16,528,128]{2,1,0:T(8,128)(2,1)} %before_exchange.1), calls=%async_computation | async-start | bytes 4325376 | tf_op jit(solution)/shard_map/all_to_all | solution.py:768
  25.3 1.0 slice-start
  25.3 1.2 slice-start.1
  25.3 4.3 %copy-start.5 = (bf16[128,4096]{1,0:T(8,128)(2,1)S(1)}, bf16[128,4096]{1,0:T(8,128)(2,1)}, u32[]{:S(2)}) copy-start(bf16[128,4096]{1,0:T(8,128)(2,1)} %q_ref.3) | copy-start | bytes 3145732
  25.3 9.6 %copy-start = (bf16[128,4096]{1,0:T(8,128)(2,1)S(1)}, bf16[128,4096]{1,0:T(8,128)(2,1)}, u32[]{:S(2)}) copy-start(bf16[128,4096]{1,0:T(8,128)(2,1)} %k_ref.9) | copy-start | bytes 3145732
  25.3 9.6 %copy-start.1 = (bf16[128,4096]{1,0:T(8,128)(2,1)S(1)}, bf16[128,4096]{1,0:T(8,128)(2,1)}, u32[]{:S(2)}) copy-start(bf16[128,4096]{1,0:T(8,128)(2,1)} %v_ref.9) | copy-start | bytes 3145732
  25.4 9.6 %copy-start.2 = (bf16[128,4096]{1,0:T(8,128)(2,1)S(1)}, bf16[128,4096]{1,0:T(8,128)(2,1)}, u32[]{:S(2)}) copy-start(bf16[128,4096]{1,0:T(8,128)(2,1)} %og_ref.3) | copy-start | bytes 3145732
  27.6 58.2 %collective-permute-start.2 = (bf16[256,2048]{1,0:T(8,128)(2,1)}, bf16[256,2048]{1,0:T(8,128)(2,1)}, u32[]{:S(2)}, u32[]{:S(2)}) collective-permute-start(bf16[256,2048]{1,0:T(8,128)(2,1)} %pad_maximum_fusion), channel_id=1, source_target_pairs={{0,2},{2,4},{4,6},{6,8},{8,10},{10,12},{12,14},{14,16},{16,18},{18... | collective-permute-start | bytes 3145736 | tf_op jit(solution)/shard_map/ppermute | solution.py:27
  30.5 50.6 %collective-permute-start.1 = (bf16[128,2048]{1,0:T(8,128)(2,1)}, bf16[128,2048]{1,0:T(8,128)(2,1)}, u32[]{:S(2)}, u32[]{:S(2)}) collective-permute-start(bf16[128,2048]{1,0:T(8,128)(2,1)} %slice.9), channel_id=1, source_target_pairs={{2,0},{4,2},{6,4},{8,6},{10,8},{12,10},{14,12},{16,14},{18,16},{20... | collective-permute-start | bytes 1572872 | tf_op jit(solution)/shard_map/ppermute | solution.py:27
  34.9 46.1 %collective-permute-start.3 = (bf16[24,4096]{1,0:T(8,128)(2,1)S(1)}, bf16[24,4096]{1,0:T(8,128)(2,1)S(1)}, u32[]{:S(2)}, u32[]{:S(2)}) collective-permute-start(bf16[24,4096]{1,0:T(8,128)(2,1)S(1)} %edge_rows.3), channel_id=1, source_target_pairs={{2,0},{4,2},{6,4},{8,6},{10,8},{12,10},{14,12},{16,14},{18,16},{20... | collective-permute-start | bytes 589832 | tf_op jit(solution)/shard_map/ppermute | solution.py:27
  81.1 18.4 %copy-start.11 = (bf16[24,4096]{1,0:T(8,128)(2,1)}, bf16[24,4096]{1,0:T(8,128)(2,1)S(1)}, u32[]{:S(2)}) copy-start(bf16[24,4096]{1,0:T(8,128)(2,1)S(1)} %collective-permute-done.3.next_ref) | copy-start | bytes 589828
  85.7 30.9 %all-to-all-start.2 = ((bf16[16,272,128]{2,1,0:T(8,128)(2,1)}), bf16[16,272,128]{2,1,0:T(8,128)(2,1)}, u32[]{:S(2)}, u32[]{:S(2)}) async-start(bf16[16,272,128]{2,1,0:T(8,128)(2,1)} %long_convs.2), calls=%async_computation.2 | async-start | bytes 2228224 | tf_op jit(solution)/shard_map/all_to_all | solution.py:787
  90.0 10.9 %copy-start.3 = (bf16[128,4096]{1,0:T(8,128)(2,1)S(1)}, bf16[128,4096]{1,0:T(8,128)(2,1)}, u32[]{:S(2)}) copy-start(bf16[128,4096]{1,0:T(8,128)(2,1)} %k_ref.7) | copy-start | bytes 3145732
  90.0 10.9 %copy-start.4 = (bf16[128,4096]{1,0:T(8,128)(2,1)S(1)}, bf16[128,4096]{1,0:T(8,128)(2,1)}, u32[]{:S(2)}) copy-start(bf16[128,4096]{1,0:T(8,128)(2,1)} %v_ref.7) | copy-start | bytes 3145732
  99.4 5.9 %collective-permute-start.4 = (f32[1,1]{1,0:T(1,128)}, f32[1,1]{1,0:T(1,128)}, u32[]{:S(2)}, u32[]{:S(2)}) collective-permute-start(f32[1,1]{1,0:T(1,128)} %get-tuple-element.54), channel_id=1, source_target_pairs={{0,1},{1,0},{2,3},{3,2},{4,5},{5,4},{6,7},{7,6},{8,9},{9,8},{10,11... | collective-permute-start | bytes 20 | tf_op jit(solution)/shard_map/ppermute | solution.py:34
  104.5 0.8 copy-start.9
  111.7 1.0 copy-start.8
  112.7 10.6 %copy-start.6 = (bf16[128,4096]{1,0:T(8,128)(2,1)S(1)}, bf16[128,4096]{1,0:T(8,128)(2,1)}, u32[]{:S(2)}) copy-start(bf16[128,4096]{1,0:T(8,128)(2,1)} %q_ref.3) | copy-start | bytes 3145732
  116.6 33.3 %all-to-all-start.1 = ((bf16[16,288,128]{2,1,0:T(8,128)(2,1)}), bf16[16,288,128]{2,1,0:T(8,128)(2,1)}, u32[]{:S(2)}, u32[]{:S(2)}) async-start(bf16[16,288,128]{2,1,0:T(8,128)(2,1)} %copy-done.8), calls=%async_computation.1 | async-start | bytes 2359296 | tf_op jit(solution)/shard_map/all_to_all | solution.py:787
  121.3 35.2 %collective-permute-start.5 = (bf16[128,2176]{1,0:T(8,128)(2,1)}, bf16[128,2176]{1,0:T(8,128)(2,1)}, u32[]{:S(2)}, u32[]{:S(2)}) collective-permute-start(bf16[128,2176]{1,0:T(8,128)(2,1)} %copy-done.9), channel_id=1, source_target_pairs={{0,2},{2,4},{4,6},{6,8},{8,10},{10,12},{12,14},{14,16},{16,18},{18... | collective-permute-start | bytes 1671176 | tf_op jit(solution)/shard_map/ppermute | solution.py:27
  125.7 0.8 copy-start.7

commit v15 on v14

--- a/solution.py
+++ b/solution.py
@@ -104,8 +104,6 @@
     rows, width = own_ref.shape
     heads = width // HEAD_DIM
     step = pl.program_id(0)
-    lane = lax.broadcasted_iota(jnp.int32, (rows, LANES), 1)
-
     @pl.when(step == 0)
     def _():
         def joined(ref):
@@ -122,14 +120,20 @@
         own_share[...] = own * inverse
         prev_share[...] = prev * inverse
 
-    def column(ref, head):
-        return jnp.sum(jnp.where(lane == step * heads + head, ref[...], 0.0), axis=1, keepdims=True)
-
-    owns = [column(own_share, head) for head in range(heads)]
-    prevs = [column(prev_share, head) for head in range(heads)]
-    for head, at in enumerate(places_of(width)):
-        total = owns[head] * own_ref[:, at].astype(F32) + prevs[head] * prev_ref[:, at].astype(F32)
-        out_ref[:, at] = total.astype(BF16)
+    row = lax.broadcasted_iota(jnp.int32, (LANES, width), 0)
+    col = lax.broadcasted_iota(jnp.int32, (LANES, width), 1)
+    spread = jnp.where(row == step * heads + col // HEAD_DIM, 1.0, 0.0).astype(BF16)
+
+    def spread_out(ref):
+        upper = ref[...].astype(BF16)
+        lower = (ref[...] - upper.astype(F32)).astype(BF16)
+        return jnp.dot(upper, spread, preferred_element_type=F32) + jnp.dot(
+            lower, spread, preferred_element_type=F32
+        )
+
+    total = spread_out(own_share) * own_ref[...].astype(F32)
+    total = total + spread_out(prev_share) * prev_ref[...].astype(F32)
+    out_ref[...] = total.astype(BF16)
 
 
 def attend_whole_kernel(place_ref, q_ref, k_ref, v_ref, kp_ref, vp_ref, out_ref):
@@ -189,7 +193,7 @@
     )(query, key, value)
 
 
-def attend_whole(query, key, value, previous, place):
+def attend_whole(query, key, value, key_prev, value_prev, place):
     rows, channels = query.shape
     half = channels // 2
     tile = min(512, half)
@@ -205,20 +209,20 @@
             second,
             second,
             first,
-            pl.BlockSpec((rows, tile), lambda i: (1, i)),
+            first,
         ],
         out_specs=second,
         out_shape=jax.ShapeDtypeStruct((rows, channels), BF16),
         compiler_params=params(LONG_VMEM),
         cost_estimate=attend_cost(rows, channels),
         name="attend_whole",
-    )(place, query, key, value, previous, previous)
+    )(place, query, key, value, key_prev, value_prev)
 
 
 def combine(own, prev, whole, place):
     rows, channels = whole.shape
     half = channels // 2
-    tile = min(512, half)
+    tile = min(1024, half)
     block = pl.BlockSpec((rows, tile), lambda i: (0, i))
     log_at = half // LANES
     log = pl.BlockSpec((rows, LANES), lambda i: (0, log_at))
@@ -706,7 +710,7 @@
     channels = out_grad.shape[1] // chunks
     cpd, gpd = channels // n, groups // (n * chunks)
     last = chunk + 1 == chunks
-    tile = min(channels, max(512, cpd))
+    tile = min(channels, max(256, cpd))
     per_tile = tile // cpd
     first = chunk * channels // tile
     block = pl.BlockSpec((rows, tile), lambda i: (0, first + i))
@@ -768,7 +772,8 @@
     received = lax.all_to_all(send, "ctx", split_axis=0, concat_axis=0, tiled=True)
     following = shifted(edge_rows(sources, True), "ctx", -1)
     query_next = shifted(query[:, :half], "ctx", -1)
-    previous = shifted(jnp.concatenate([key[:, half:], value[:, half:]], 0), "ctx", 1)
+    key_prev = shifted(key[:, half:], "ctx", 1)
+    value_prev = value[:, half:]
     returned = []
     for chunk in range(chunks):
         raw = ()
@@ -777,17 +782,21 @@
             query_next, raw, squares = lax.optimization_barrier((query_next, raw, squares))
             raw = (raw, total_over(squares, "tp"))
         results = long_convs(received, raw, cpd, gpd, chunk, chunks)
+        if chunks == 1:
+            value_prev = shifted(value_prev, "ctx", 1)
         if chunk + 1 == chunks:
             part = attend_part(query_next, key_heads, value_heads, half, False)
-            results, part = lax.optimization_barrier((results, part))
+            results, part, value_prev = lax.optimization_barrier((results, part, value_prev))
         if chunk == 0:
-            results, received, query_next, previous, following = lax.optimization_barrier(
-                (results, received, query_next, previous, following)
+            results, received, query_next, key_prev, value_prev, following = lax.optimization_barrier(
+                (results, received, query_next, key_prev, value_prev, following)
             )
+            if chunks > 1:
+                value_prev = shifted(value_prev, "ctx", 1)
         returned.append(lax.all_to_all(results, "ctx", split_axis=0, concat_axis=0, tiled=True))
     part = shifted(part, "ctx", 1)
     place = position.astype(jnp.int32).reshape(1)
-    whole = attend_whole(query_heads, key_heads, value_heads, previous, place)
+    whole = attend_whole(query_heads, key_heads, value_heads, key_prev, value_prev, place)
     own = attend_part(query_heads, key_heads, value_heads, half, True)
     bound = math.sqrt(rows * n * groups * tp)
     grads = ()

time: 162 us -> 166 us (1.025)
  starting transfers between devices: 28 us -> 31.5 us
  waiting for transfers between devices: 65.3 us -> 63.5 us
  Pallas kernels: 58.5 us -> 60.2 us
    all_to_all x2, waiting for transfers between devices: 16.4 us -> 11.1 us  [on_device(): lax.all_to_all(results, 'ctx', split_axis=0, concat_axis=0, tiled=True)]
    ppermute x5 -> x6, waiting for transfers between devices: 10.8 us -> 14 us  [shifted(): return lax.ppermute(block, axis, route)]
    pallas_call x2, Pallas kernels: 12.9 us -> 15.9 us  [after_exchange(): pl.pallas_call(functools.partial(after_kernel, cpd, gpd, chunks, last, bo...]
    ppermute x5 -> x6, starting transfers between devices: 12.3 us -> 14.4 us  [shifted(): return lax.ppermute(block, axis, route)]
    unnamed x24 -> x28, local copies, waits for them, and re-layouts: 3.37 us -> 4.14 us
  transfers between devices with their start and end apart: 9 -> 10, of which waited for: 5 -> 4; matrix products, arithmetic and copies ran while one was open for 1% -> 2% of each run, Pallas kernels for 27% -> 29%
where the time goes in v15:
time: 166 us; the launch traced here: 164 us
  waiting for transfers between devices  63.5 us (38%)
  Pallas kernels  60.2 us (36%)
  starting transfers between devices  31.5 us (19%)
  local copies, waits for them, and re-layouts  6.66 us (4%)
  between operations  2.08 us (1%)
    all_to_all x1, waiting for transfers between devices, on_device(): lax.all_to_all(send, 'ctx', split_axis=0, concat_axis=0, tiled=True)  38.5 us
    pallas_call x2, Pallas kernels, after_exchange(): pl.pallas_call(functools.partial(after_kernel, cpd, gpd, chunks, last, bo...  15.9 us
    ppermute x6, starting transfers between devices, shifted(): return lax.ppermute(block, axis, route)  14.4 us
    ppermute x6, waiting for transfers between devices, shifted(): return lax.ppermute(block, axis, route)  14 us
    pallas_call x2, Pallas kernels, long_convs(): pl.pallas_call(functools.partial(conv_kernel, cpd, gpd, chunk), grid=(pai...  11.2 us
    all_to_all x2, waiting for transfers between devices, on_device(): lax.all_to_all(results, 'ctx', split_axis=0, concat_axis=0, tiled=True)  11.1 us
    all_to_all x2, starting transfers between devices, on_device(): lax.all_to_all(results, 'ctx', split_axis=0, concat_axis=0, tiled=True)  10 us
    pallas_call x1, Pallas kernels, filter_products(): pl.pallas_call(functools.partial(gram_kernel, cpd // gpd), grid=(pairs,),...  9.22 us
  transfers between devices with their start and end apart: 10, of which 4 were waited for; matrix products, arithmetic and copies ran while one was open for 2% of the time, Pallas kernels for 29%

profile of v15, /device:TPU:16, one launch (start us, length us, event | category | flops | bytes accessed | tf_op | source)
XLA Modules:
  0.0 164.0 jit_solution(627211167207579646)
XLA Ops:
  0.6 1.7 %edge_rows.2 = bf16[24,4096]{1,0:T(8,128)(2,1)} custom-call(bf16[128,4096]{1,0:T(8,128)(2,1)} %refs_6_.1, bf16[128,4096]{1,0:T(8,128)(2,1)} %k_ref.9, bf16[128,4096]{1,0:T(8,128)(2,1)} %v_ref.9), custom_call_target="tpu_custom_call" | custom-call | tf_op jit(solution)/shard_map/edge_rows/pallas_call | solution.py:255
  2.4 1.9 %collective-permute-start = (bf16[24,4096]{1,0:T(8,128)(2,1)}, bf16[24,4096]{1,0:T(8,128)(2,1)S(1)}, u32[]{:S(2)}, u32[]{:S(2)}) collective-permute-start(bf16[24,4096]{1,0:T(8,128)(2,1)} %edge_rows.2), channel_id=1, source_target_pairs={{0,2},{2,4},{4,6},{6,8},{8,10},{10,12},{12,14},{14,16},{16,18},{18... | collective-permute-start | bytes 589832 | tf_op jit(solution)/shard_map/ppermute | solution.py:27
  4.3 6.2 %collective-permute-done.refs_4_.refs_10_.tail_ref = bf16[24,4096]{1,0:T(8,128)(2,1)S(1)} collective-permute-done((bf16[24,4096]{1,0:T(8,128)(2,1)}, bf16[24,4096]{1,0:T(8,128)(2,1)S(1)}, u32[]{:S(2)}, u32[]{:S(2)}) %collective-permute-start) | collective-permute-done | bytes 196640 | tf_op jit(solution)/shard_map/ppermute | solution.py:27
  11.1 8.9 %before_exchange.1 = bf16[16,528,128]{2,1,0:T(8,128)(2,1)} custom-call(bf16[128,4096]{1,0:T(8,128)(2,1)} %refs_6_.1, bf16[128,4096]{1,0:T(8,128)(2,1)} %k_ref.9, bf16[128,4096]{1,0:T(8,128)(2,1)} %v_ref.9, bf16[128,4096]{1,0:T(8,128)(2,1)} %og_ref.3, bf16[24,4096]{1,0:T(8,128)(2,1)} %copy-done.12, f32[3,7,4096]{2,1,0:T(8,128)} %taps_ref.3, ...), custom_call_target="tpu_custom_call" | custom-call | flops 26214400 | bytes 6291456 | tf_op jit(solution)/shard_map/before_exchange/pallas_call | solution.py:364
  20.0 5.6 %all-to-all-start = ((bf16[16,528,128]{2,1,0:T(8,128)(2,1)}), bf16[16,528,128]{2,1,0:T(8,128)(2,1)}, u32[]{:S(2)}, u32[]{:S(2)}) async-start(bf16[16,528,128]{2,1,0:T(8,128)(2,1)} %before_exchange.1), calls=%async_computation | async-start | bytes 4325376 | tf_op jit(solution)/shard_map/all_to_all | solution.py:772
  25.6 0.8 slice.9
  26.5 0.8 slice.10
  27.3 2.2 %collective-permute-start.2 = (bf16[128,2048]{1,0:T(8,128)(2,1)}, bf16[128,2048]{1,0:T(8,128)(2,1)}, u32[]{:S(2)}, u32[]{:S(2)}) collective-permute-start(bf16[128,2048]{1,0:T(8,128)(2,1)} %slice.10), channel_id=1, source_target_pairs={{0,2},{2,4},{4,6},{6,8},{8,10},{10,12},{12,14},{14,16},{16,18},{18... | collective-permute-start | bytes 1572872 | tf_op jit(solution)/shard_map/ppermute | solution.py:27
  29.5 4.4 %collective-permute-start.1 = (bf16[128,2048]{1,0:T(8,128)(2,1)}, bf16[128,2048]{1,0:T(8,128)(2,1)}, u32[]{:S(2)}, u32[]{:S(2)}) collective-permute-start(bf16[128,2048]{1,0:T(8,128)(2,1)} %slice.9), channel_id=1, source_target_pairs={{2,0},{4,2},{6,4},{8,6},{10,8},{12,10},{14,12},{16,14},{18,16},{20... | collective-permute-start | bytes 1572872 | tf_op jit(solution)/shard_map/ppermute | solution.py:27
  34.0 1.9 %collective-permute-start.3 = (bf16[24,4096]{1,0:T(8,128)(2,1)S(1)}, bf16[24,4096]{1,0:T(8,128)(2,1)S(1)}, u32[]{:S(2)}, u32[]{:S(2)}) collective-permute-start(bf16[24,4096]{1,0:T(8,128)(2,1)S(1)} %edge_rows.3), channel_id=1, source_target_pairs={{2,0},{4,2},{6,4},{8,6},{10,8},{12,10},{14,12},{16,14},{18,16},{20... | collective-permute-start | bytes 589832 | tf_op jit(solution)/shard_map/ppermute | solution.py:27
  35.9 0.8 slice.11
  36.7 38.5 %all-to-all-done.in_ref.filter_ref = bf16[16,528,128]{2,1,0:T(8,128)(2,1)} async-done(((bf16[16,528,128]{2,1,0:T(8,128)(2,1)}), bf16[16,528,128]{2,1,0:T(8,128)(2,1)}, u32[]{:S(2)}, u32[]{:S(2)}) %all-to-all-start) | async-done | bytes 2162720 | tf_op jit(solution)/shard_map/all_to_all | solution.py:772
  75.2 6.1 %long_convs.2 = bf16[16,272,128]{2,1,0:T(8,128)(2,1)} custom-call(bf16[16,528,128]{2,1,0:T(8,128)(2,1)} %all-to-all-done.in_ref.filter_ref, bf16[16,528,128]{2,1,0:T(8,128)(2,1)} %all-to-all-done.in_ref.filter_ref), custom_call_target="tpu_custom_call" | custom-call | flops 2147483648 | bytes 2228224 | tf_op jit(solution)/shard_map/long_convs/pallas_call | solution.py:479
  81.3 5.7 %all-to-all-start.2 = ((bf16[16,272,128]{2,1,0:T(8,128)(2,1)}), bf16[16,272,128]{2,1,0:T(8,128)(2,1)}, u32[]{:S(2)}, u32[]{:S(2)}) async-start(bf16[16,272,128]{2,1,0:T(8,128)(2,1)} %long_convs.2), calls=%async_computation.2 | async-start | bytes 2228224 | tf_op jit(solution)/shard_map/all_to_all | solution.py:796
  87.1 2.0 %collective-permute-start.5 = (bf16[128,2048]{1,0:T(8,128)(2,1)}, bf16[128,2048]{1,0:T(8,128)(2,1)S(1)}, u32[]{:S(2)}, u32[]{:S(2)}) collective-permute-start(bf16[128,2048]{1,0:T(8,128)(2,1)} %slice.11), channel_id=1, source_target_pairs={{0,2},{2,4},{4,6},{6,8},{8,10},{10,12},{12,14},{14,16},{16,18},{18... | collective-permute-start | bytes 1572872 | tf_op jit(solution)/shard_map/ppermute | solution.py:27
  89.1 9.2 %filter_products.1 = (bf16[16,16,128]{2,1,0:T(8,128)(2,1)S(1)}, f32[1,1]{1,0:T(1,128)}) custom-call(bf16[16,528,128]{2,1,0:T(8,128)(2,1)} %all-to-all-done.in_ref.filter_ref), custom_call_target="tpu_custom_call" | custom-call | flops 2147483648 | bytes 2162688 | tf_op jit(solution)/shard_map/filter_products/pallas_call | solution.py:560
  98.3 1.5 collective-permute-start.4
  99.8 3.5 %attend_part.2 = bf16[128,2176]{1,0:T(8,128)(2,1)S(1)} custom-call(bf16[128,2048]{1,0:T(8,128)(2,1)} %collective-permute-done.1.q_ref, bf16[128,4096]{1,0:T(8,128)(2,1)S(1)} %copy-done.3, bf16[128,4096]{1,0:T(8,128)(2,1)S(1)} %copy-done.4), custom_call_target="tpu_custom_call" | custom-call | flops 134217728 | bytes 2621440 | tf_op jit(solution)/shard_map/attend_part/pallas_call | solution.py:183
  103.4 0.8 copy-done.9
  105.4 5.1 %long_convs.3 = bf16[16,288,128]{2,1,0:T(8,128)(2,1)S(1)} custom-call(bf16[16,528,128]{2,1,0:T(8,128)(2,1)} %all-to-all-done.in_ref.filter_ref, bf16[16,528,128]{2,1,0:T(8,128)(2,1)} %all-to-all-done.in_ref.filter_ref, bf16[16,16,128]{2,1,0:T(8,128)(2,1)S(1)} %get-tuple-element.55.refs_0_, f32[1,1]{1,0:T(1,128)S(6)} %add.3.refs_1_), custom_call_target="tpu_custom_call" | custom-call | flops 2147483648 | bytes 2359296 | tf_op jit(solution)/shard_map/long_convs/pallas_call | solution.py:479
  110.5 1.0 copy-done.8
  111.5 7.8 %collective-permute-done.5.vp_ref = bf16[128,2048]{1,0:T(8,128)(2,1)S(1)} collective-permute-done((bf16[128,2048]{1,0:T(8,128)(2,1)}, bf16[128,2048]{1,0:T(8,128)(2,1)S(1)}, u32[]{:S(2)}, u32[]{:S(2)}) %collective-permute-start.5) | collective-permute-done | bytes 524320 | tf_op jit(solution)/shard_map/ppermute | solution.py:27
  119.3 0.8 copy-done.10
  120.1 4.3 %all-to-all-start.1 = ((bf16[16,288,128]{2,1,0:T(8,128)(2,1)}), bf16[16,288,128]{2,1,0:T(8,128)(2,1)}, u32[]{:S(2)}, u32[]{:S(2)}) async-start(bf16[16,288,128]{2,1,0:T(8,128)(2,1)} %copy-done.8), calls=%async_computation.1 | async-start | bytes 2359296 | tf_op jit(solution)/shard_map/all_to_all | solution.py:796
  124.4 2.0 %collective-permute-start.6 = (bf16[128,2176]{1,0:T(8,128)(2,1)}, bf16[128,2176]{1,0:T(8,128)(2,1)}, u32[]{:S(2)}, u32[]{:S(2)}) collective-permute-start(bf16[128,2176]{1,0:T(8,128)(2,1)} %copy-done.9), channel_id=1, source_target_pairs={{0,2},{2,4},{4,6},{6,8},{8,10},{10,12},{12,14},{14,16},{16,18},{18... | collective-permute-start | bytes 1671176 | tf_op jit(solution)/shard_map/ppermute | solution.py:27
  126.4 2.4 %attend_part.3.own_ref.own_log_ref = bf16[128,2176]{1,0:T(8,128)(2,1)S(1)} custom-call(bf16[128,4096]{1,0:T(8,128)(2,1)S(1)} %copy-done.6, bf16[128,4096]{1,0:T(8,128)(2,1)S(1)} %copy-done.3, bf16[128,4096]{1,0:T(8,128)(2,1)S(1)} %copy-done.4), custom_call_target="tpu_custom_call" | custom-call | flops 134217728 | bytes 2621440 | tf_op jit(solution)/shard_map/attend_part/pallas_call | solution.py:183
  128.8 0.8 copy-done.7
  129.6 4.5 %attend_whole.1._ = bf16[128,4096]{1,0:T(8,128)(2,1)} custom-call(s32[1]{0:T(128)} %bitcast.place_ref, bf16[128,4096]{1,0:T(8,128)(2,1)S(1)} %copy-done.6, bf16[128,4096]{1,0:T(8,128)(2,1)S(1)} %copy-done.3, bf16[128,4096]{1,0:T(8,128)(2,1)S(1)} %copy-done.4, bf16[128,2048]{1,0:T(8,128)(2,1)} %collective-permute-done.2.kp_ref, bf16[128,2048]{1,0:T(8,128)(2,1)S(1)} %copy-done.11), custom_call_target="tpu_custom_call" | custom-call | flops 268435456 | bytes 5242880 | tf_op jit(solution)/shard_map/attend_whole/pallas_call | solution.py:203
  134.1 7.8 %after_exchange.2 = (bf16[128,4096]{1,0:T(8,128)(2,1)}, bf16[128,4096]{1,0:T(8,128)(2,1)}, bf16[128,4096]{1,0:T(8,128)(2,1)}) custom-call(bf16[16,272,128]{2,1,0:T(8,128)(2,1)} %all-to-all-done.2.in_ref, bf16[128,4096]{1,0:T(8,128)(2,1)} %og_ref.3, bf16[128,4096]{1,0:T(8,128)(2,1)} %k_ref.9, bf16[128,4096]{1,0:T(8,128)(2,1)} %v_ref.9, ...), custom_call_target="tpu_custom_call" | custom-call | flops 23592960 | bytes 4718592 | tf_op jit(solution)/shard_map/after_exchange/pallas_call | solution.py:719
  141.9 11.1 %all-to-all-done.1.in_ref = bf16[16,288,128]{2,1,0:T(8,128)(2,1)} async-done(((bf16[16,288,128]{2,1,0:T(8,128)(2,1)}), bf16[16,288,128]{2,1,0:T(8,128)(2,1)}, u32[]{:S(2)}, u32[]{:S(2)}) %all-to-all-start.1) | async-done | bytes 1179680 | tf_op jit(solution)/shard_map/all_to_all | solution.py:796
  153.0 8.1 %after_exchange.3 = (bf16[128,4096]{1,0:T(8,128)(2,1)}, bf16[128,4096]{1,0:T(8,128)(2,1)}, bf16[128,4096]{1,0:T(8,128)(2,1)}, f32[128,256]{1,0:T(8,128)}) custom-call(bf16[16,288,128]{2,1,0:T(8,128)(2,1)} %all-to-all-done.1.in_ref, bf16[128,4096]{1,0:T(8,128)(2,1)} %og_ref.3, ...), custom_call_target="tpu_custom_call", output_to_operand_aliasing={{0}: (7, {}), {1}: (8, {}), {2}: (9, {})} | custom-call | flops 23592960 | bytes 4718592 | tf_op jit(solution)/shard_map/after_exchange/pallas_call | solution.py:719
  161.1 2.8 %combine.1 = bf16[128,4096]{1,0:T(8,128)(2,1)} custom-call(s32[1]{0:T(128)} %bitcast.place_ref, bf16[128,2176]{1,0:T(8,128)(2,1)} %copy-done.7, bf16[128,2176]{1,0:T(8,128)(2,1)} %collective-permute-done.6.prev_ref.prev_log_ref, bf16[128,2176]{1,0:T(8,128)(2,1)} %copy-done.7, ...), custom_call_target="tpu_custom_call", output_to_operand_aliasing={{}: (5, {})} | custom-call | flops 33554432 | bytes 655360 | tf_op jit(solution)/shard_map/combine/pallas_call | solution.py:230
  (31 shorter events, 0.8 us)
Async XLA Ops:
  2.4 8.1 %collective-permute-start = (bf16[24,4096]{1,0:T(8,128)(2,1)}, bf16[24,4096]{1,0:T(8,128)(2,1)S(1)}, u32[]{:S(2)}, u32[]{:S(2)}) collective-permute-start(bf16[24,4096]{1,0:T(8,128)(2,1)} %edge_rows.2), channel_id=1, source_target_pairs={{0,2},{2,4},{4,6},{6,8},{8,10},{10,12},{12,14},{14,16},{16,18},{18... | collective-permute-start | bytes 589832 | tf_op jit(solution)/shard_map/ppermute | solution.py:27
  10.4 0.7 copy-start.12
  20.0 5.6 %copy-start.5 = (bf16[128,4096]{1,0:T(8,128)(2,1)S(1)}, bf16[128,4096]{1,0:T(8,128)(2,1)}, u32[]{:S(2)}) copy-start(bf16[128,4096]{1,0:T(8,128)(2,1)} %q_ref.3) | copy-start | bytes 3145732
  20.0 6.5 %copy-start.3 = (bf16[128,4096]{1,0:T(8,128)(2,1)S(1)}, bf16[128,4096]{1,0:T(8,128)(2,1)}, u32[]{:S(2)}) copy-start(bf16[128,4096]{1,0:T(8,128)(2,1)} %k_ref.7) | copy-start | bytes 3145732
  20.0 13.9 %copy-start.2 = (bf16[128,4096]{1,0:T(8,128)(2,1)S(1)}, bf16[128,4096]{1,0:T(8,128)(2,1)}, u32[]{:S(2)}) copy-start(bf16[128,4096]{1,0:T(8,128)(2,1)} %og_ref.3) | copy-start | bytes 3145732
  20.0 55.2 %all-to-all-start = ((bf16[16,528,128]{2,1,0:T(8,128)(2,1)}), bf16[16,528,128]{2,1,0:T(8,128)(2,1)}, u32[]{:S(2)}, u32[]{:S(2)}) async-start(bf16[16,528,128]{2,1,0:T(8,128)(2,1)} %before_exchange.1), calls=%async_computation | async-start | bytes 4325376 | tf_op jit(solution)/shard_map/all_to_all | solution.py:772
  25.6 8.3 %copy-start = (bf16[128,4096]{1,0:T(8,128)(2,1)S(1)}, bf16[128,4096]{1,0:T(8,128)(2,1)}, u32[]{:S(2)}) copy-start(bf16[128,4096]{1,0:T(8,128)(2,1)} %k_ref.9) | copy-start | bytes 3145732
  25.6 8.3 %copy-start.1 = (bf16[128,4096]{1,0:T(8,128)(2,1)S(1)}, bf16[128,4096]{1,0:T(8,128)(2,1)}, u32[]{:S(2)}) copy-start(bf16[128,4096]{1,0:T(8,128)(2,1)} %v_ref.9) | copy-start | bytes 3145732
  27.3 8.6 %copy-start.4 = (bf16[128,4096]{1,0:T(8,128)(2,1)S(1)}, bf16[128,4096]{1,0:T(8,128)(2,1)}, u32[]{:S(2)}) copy-start(bf16[128,4096]{1,0:T(8,128)(2,1)} %v_ref.7) | copy-start | bytes 3145732
  27.3 54.0 %collective-permute-start.2 = (bf16[128,2048]{1,0:T(8,128)(2,1)}, bf16[128,2048]{1,0:T(8,128)(2,1)}, u32[]{:S(2)}, u32[]{:S(2)}) collective-permute-start(bf16[128,2048]{1,0:T(8,128)(2,1)} %slice.10), channel_id=1, source_target_pairs={{0,2},{2,4},{4,6},{6,8},{8,10},{10,12},{12,14},{14,16},{16,18},{18... | collective-permute-start | bytes 1572872 | tf_op jit(solution)/shard_map/ppermute | solution.py:27
  29.5 51.8 %collective-permute-start.1 = (bf16[128,2048]{1,0:T(8,128)(2,1)}, bf16[128,2048]{1,0:T(8,128)(2,1)}, u32[]{:S(2)}, u32[]{:S(2)}) collective-permute-start(bf16[128,2048]{1,0:T(8,128)(2,1)} %slice.9), channel_id=1, source_target_pairs={{2,0},{4,2},{6,4},{8,6},{10,8},{12,10},{14,12},{16,14},{18,16},{20... | collective-permute-start | bytes 1572872 | tf_op jit(solution)/shard_map/ppermute | solution.py:27
  34.0 47.4 %collective-permute-start.3 = (bf16[24,4096]{1,0:T(8,128)(2,1)S(1)}, bf16[24,4096]{1,0:T(8,128)(2,1)S(1)}, u32[]{:S(2)}, u32[]{:S(2)}) collective-permute-start(bf16[24,4096]{1,0:T(8,128)(2,1)S(1)} %edge_rows.3), channel_id=1, source_target_pairs={{2,0},{4,2},{6,4},{8,6},{10,8},{12,10},{14,12},{16,14},{18,16},{20... | collective-permute-start | bytes 589832 | tf_op jit(solution)/shard_map/ppermute | solution.py:27
  81.3 17.0 %copy-start.13 = (bf16[24,4096]{1,0:T(8,128)(2,1)}, bf16[24,4096]{1,0:T(8,128)(2,1)S(1)}, u32[]{:S(2)}) copy-start(bf16[24,4096]{1,0:T(8,128)(2,1)S(1)} %collective-permute-done.3.next_ref) | copy-start | bytes 589828
  81.3 38.8 %all-to-all-start.2 = ((bf16[16,272,128]{2,1,0:T(8,128)(2,1)}), bf16[16,272,128]{2,1,0:T(8,128)(2,1)}, u32[]{:S(2)}, u32[]{:S(2)}) async-start(bf16[16,272,128]{2,1,0:T(8,128)(2,1)} %long_convs.2), calls=%async_computation.2 | async-start | bytes 2228224 | tf_op jit(solution)/shard_map/all_to_all | solution.py:796
  87.1 32.3 %collective-permute-start.5 = (bf16[128,2048]{1,0:T(8,128)(2,1)}, bf16[128,2048]{1,0:T(8,128)(2,1)S(1)}, u32[]{:S(2)}, u32[]{:S(2)}) collective-permute-start(bf16[128,2048]{1,0:T(8,128)(2,1)} %slice.11), channel_id=1, source_target_pairs={{0,2},{2,4},{4,6},{6,8},{8,10},{10,12},{12,14},{14,16},{16,18},{18... | collective-permute-start | bytes 1572872 | tf_op jit(solution)/shard_map/ppermute | solution.py:27
  98.3 5.8 %collective-permute-start.4 = (f32[1,1]{1,0:T(1,128)}, f32[1,1]{1,0:T(1,128)}, u32[]{:S(2)}, u32[]{:S(2)}) collective-permute-start(f32[1,1]{1,0:T(1,128)} %get-tuple-element.56), channel_id=1, source_target_pairs={{0,1},{1,0},{2,3},{3,2},{4,5},{5,4},{6,7},{7,6},{8,9},{9,8},{10,11... | collective-permute-start | bytes 20 | tf_op jit(solution)/shard_map/ppermute | solution.py:34
  103.4 0.8 copy-start.9
  110.5 1.0 copy-start.8
  111.5 14.9 %copy-start.6 = (bf16[128,4096]{1,0:T(8,128)(2,1)S(1)}, bf16[128,4096]{1,0:T(8,128)(2,1)}, u32[]{:S(2)}) copy-start(bf16[128,4096]{1,0:T(8,128)(2,1)} %q_ref.3) | copy-start | bytes 3145732
  119.3 0.8 copy-start.10
  120.1 32.9 %all-to-all-start.1 = ((bf16[16,288,128]{2,1,0:T(8,128)(2,1)}), bf16[16,288,128]{2,1,0:T(8,128)(2,1)}, u32[]{:S(2)}, u32[]{:S(2)}) async-start(bf16[16,288,128]{2,1,0:T(8,128)(2,1)} %copy-done.8), calls=%async_computation.1 | async-start | bytes 2359296 | tf_op jit(solution)/shard_map/all_to_all | solution.py:796
  124.4 36.7 %collective-permute-start.6 = (bf16[128,2176]{1,0:T(8,128)(2,1)}, bf16[128,2176]{1,0:T(8,128)(2,1)}, u32[]{:S(2)}, u32[]{:S(2)}) collective-permute-start(bf16[128,2176]{1,0:T(8,128)(2,1)} %copy-done.9), channel_id=1, source_target_pairs={{0,2},{2,4},{4,6},{6,8},{8,10},{10,12},{12,14},{14,16},{16,18},{18... | collective-permute-start | bytes 1671176 | tf_op jit(solution)/shard_map/ppermute | solution.py:27
  126.4 3.2 %copy-start.11 = (bf16[128,2048]{1,0:T(8,128)(2,1)S(1)}, bf16[128,2048]{1,0:T(8,128)(2,1)}, u32[]{:S(2)}) copy-start(bf16[128,2048]{1,0:T(8,128)(2,1)} %copy-done.10) | copy-start | bytes 1572868
  128.8 0.8 copy-start.7

commit v16 on v14

--- a/solution.py
+++ b/solution.py
@@ -104,8 +104,6 @@
     rows, width = own_ref.shape
     heads = width // HEAD_DIM
     step = pl.program_id(0)
-    lane = lax.broadcasted_iota(jnp.int32, (rows, LANES), 1)
-
     @pl.when(step == 0)
     def _():
         def joined(ref):
@@ -122,14 +120,20 @@
         own_share[...] = own * inverse
         prev_share[...] = prev * inverse
 
-    def column(ref, head):
-        return jnp.sum(jnp.where(lane == step * heads + head, ref[...], 0.0), axis=1, keepdims=True)
-
-    owns = [column(own_share, head) for head in range(heads)]
-    prevs = [column(prev_share, head) for head in range(heads)]
-    for head, at in enumerate(places_of(width)):
-        total = owns[head] * own_ref[:, at].astype(F32) + prevs[head] * prev_ref[:, at].astype(F32)
-        out_ref[:, at] = total.astype(BF16)
+    row = lax.broadcasted_iota(jnp.int32, (LANES, width), 0)
+    col = lax.broadcasted_iota(jnp.int32, (LANES, width), 1)
+    spread = jnp.where(row == step * heads + col // HEAD_DIM, 1.0, 0.0).astype(BF16)
+
+    def spread_out(ref):
+        upper = ref[...].astype(BF16)
+        lower = (ref[...] - upper.astype(F32)).astype(BF16)
+        return jnp.dot(upper, spread, preferred_element_type=F32) + jnp.dot(
+            lower, spread, preferred_element_type=F32
+        )
+
+    total = spread_out(own_share) * own_ref[...].astype(F32)
+    total = total + spread_out(prev_share) * prev_ref[...].astype(F32)
+    out_ref[...] = total.astype(BF16)
 
 
 def attend_whole_kernel(place_ref, q_ref, k_ref, v_ref, kp_ref, vp_ref, out_ref):
@@ -218,7 +222,7 @@
 def combine(own, prev, whole, place):
     rows, channels = whole.shape
     half = channels // 2
-    tile = min(512, half)
+    tile = min(1024, half)
     block = pl.BlockSpec((rows, tile), lambda i: (0, i))
     log_at = half // LANES
     log = pl.BlockSpec((rows, LANES), lambda i: (0, log_at))
@@ -345,7 +349,7 @@
     rows, channels = query.shape
     groups = long_filter.shape[1]
     cpd, gpd = channels // (n * chunks), groups // (n * chunks)
-    tile = min(channels // chunks, max(512 // chunks, cpd))
+    tile = min(channels // chunks, max(1024 // chunks, cpd))
     per_tile = tile // cpd
     filter_rows = round_up(gpd * chunks, 16)
     send_rows = 2 * cpd * chunks + filter_rows

time: 162 us -> 160 us (0.988)
  Pallas kernels: 58.5 us -> 56.2 us
  transfers between devices with their start and end apart: 9 -> 9, of which waited for: 5 -> 5; matrix products, arithmetic and copies ran while one was open for 1% -> 1% of each run, Pallas kernels for 27% -> 28%
where the time goes in v16:
time: 160 us; the launch traced here: 158 us
  waiting for transfers between devices  65.3 us (41%)
  Pallas kernels  56.2 us (35%)
  starting transfers between devices  28 us (18%)
  local copies, waits for them, and re-layouts  5.35 us (3%)
  between operations  2.18 us (1%)
    all_to_all x1, waiting for transfers between devices, on_device(): lax.all_to_all(send, 'ctx', split_axis=0, concat_axis=0, tiled=True)  38.1 us
    all_to_all x2, waiting for transfers between devices, on_device(): lax.all_to_all(results, 'ctx', split_axis=0, concat_axis=0, tiled=True)  16.4 us
    pallas_call x2, Pallas kernels, after_exchange(): pl.pallas_call(functools.partial(after_kernel, cpd, gpd, chunks, last, bo...  12.9 us
    ppermute x5, starting transfers between devices, shifted(): return lax.ppermute(block, axis, route)  12.3 us
    pallas_call x2, Pallas kernels, long_convs(): pl.pallas_call(functools.partial(conv_kernel, cpd, gpd, chunk), grid=(pai...  11.2 us
    ppermute x5, waiting for transfers between devices, shifted(): return lax.ppermute(block, axis, route)  10.8 us
    pallas_call x1, Pallas kernels, filter_products(): pl.pallas_call(functools.partial(gram_kernel, cpd // gpd), grid=(pairs,),...  9.36 us
    all_to_all x2, starting transfers between devices, on_device(): lax.all_to_all(results, 'ctx', split_axis=0, concat_axis=0, tiled=True)  8.92 us
  transfers between devices with their start and end apart: 9, of which 5 were waited for; matrix products, arithmetic and copies ran while one was open for 1% of the time, Pallas kernels for 28%

profile of v16, /device:TPU:16, one launch (start us, length us, event | category | flops | bytes accessed | tf_op | source)
XLA Modules:
  0.0 158.1 jit_solution(244812632242998564)
XLA Ops:
  0.6 1.7 %edge_rows.2 = bf16[24,4096]{1,0:T(8,128)(2,1)} custom-call(bf16[128,4096]{1,0:T(8,128)(2,1)} %refs_6_.1, bf16[128,4096]{1,0:T(8,128)(2,1)} %k_ref.9, bf16[128,4096]{1,0:T(8,128)(2,1)} %v_ref.9), custom_call_target="tpu_custom_call" | custom-call | tf_op jit(solution)/shard_map/edge_rows/pallas_call | solution.py:255
  2.4 1.9 %collective-permute-start = (bf16[24,4096]{1,0:T(8,128)(2,1)}, bf16[24,4096]{1,0:T(8,128)(2,1)S(1)}, u32[]{:S(2)}, u32[]{:S(2)}) collective-permute-start(bf16[24,4096]{1,0:T(8,128)(2,1)} %edge_rows.2), channel_id=1, source_target_pairs={{0,2},{2,4},{4,6},{6,8},{8,10},{10,12},{12,14},{14,16},{16,18},{18... | collective-permute-start | bytes 589832 | tf_op jit(solution)/shard_map/ppermute | solution.py:27
  4.3 6.2 %collective-permute-done.refs_4_.refs_10_.tail_ref = bf16[24,4096]{1,0:T(8,128)(2,1)S(1)} collective-permute-done((bf16[24,4096]{1,0:T(8,128)(2,1)}, bf16[24,4096]{1,0:T(8,128)(2,1)S(1)}, u32[]{:S(2)}, u32[]{:S(2)}) %collective-permute-start) | collective-permute-done | bytes 196640 | tf_op jit(solution)/shard_map/ppermute | solution.py:27
  10.4 0.7 copy-done.10
  11.1 7.6 %before_exchange.1 = bf16[16,528,128]{2,1,0:T(8,128)(2,1)} custom-call(bf16[128,4096]{1,0:T(8,128)(2,1)} %refs_6_.1, bf16[128,4096]{1,0:T(8,128)(2,1)} %k_ref.9, bf16[128,4096]{1,0:T(8,128)(2,1)} %v_ref.9, bf16[128,4096]{1,0:T(8,128)(2,1)} %og_ref.3, bf16[24,4096]{1,0:T(8,128)(2,1)} %copy-done.10, f32[3,7,4096]{2,1,0:T(8,128)} %taps_ref.3, ...), custom_call_target="tpu_custom_call" | custom-call | flops 26214400 | bytes 6291456 | tf_op jit(solution)/shard_map/before_exchange/pallas_call | solution.py:364
  18.8 5.3 %all-to-all-start = ((bf16[16,528,128]{2,1,0:T(8,128)(2,1)}), bf16[16,528,128]{2,1,0:T(8,128)(2,1)}, u32[]{:S(2)}, u32[]{:S(2)}) async-start(bf16[16,528,128]{2,1,0:T(8,128)(2,1)} %before_exchange.1), calls=%async_computation | async-start | bytes 4325376 | tf_op jit(solution)/shard_map/all_to_all | solution.py:772
  24.1 1.0 slice-done
  25.3 1.1 pad_maximum_fusion
  26.3 2.0 %collective-permute-start.2 = (bf16[256,2048]{1,0:T(8,128)(2,1)}, bf16[256,2048]{1,0:T(8,128)(2,1)}, u32[]{:S(2)}, u32[]{:S(2)}) collective-permute-start(bf16[256,2048]{1,0:T(8,128)(2,1)} %pad_maximum_fusion), channel_id=1, source_target_pairs={{0,2},{2,4},{4,6},{6,8},{8,10},{10,12},{12,14},{14,16},{16,18},{18... | collective-permute-start | bytes 3145736 | tf_op jit(solution)/shard_map/ppermute | solution.py:27
  28.4 0.8 slice.9
  29.2 4.4 %collective-permute-start.1 = (bf16[128,2048]{1,0:T(8,128)(2,1)}, bf16[128,2048]{1,0:T(8,128)(2,1)}, u32[]{:S(2)}, u32[]{:S(2)}) collective-permute-start(bf16[128,2048]{1,0:T(8,128)(2,1)} %slice.9), channel_id=1, source_target_pairs={{2,0},{4,2},{6,4},{8,6},{10,8},{12,10},{14,12},{16,14},{18,16},{20... | collective-permute-start | bytes 1572872 | tf_op jit(solution)/shard_map/ppermute | solution.py:27
  33.7 1.9 %collective-permute-start.3 = (bf16[24,4096]{1,0:T(8,128)(2,1)S(1)}, bf16[24,4096]{1,0:T(8,128)(2,1)S(1)}, u32[]{:S(2)}, u32[]{:S(2)}) collective-permute-start(bf16[24,4096]{1,0:T(8,128)(2,1)S(1)} %edge_rows.3), channel_id=1, source_target_pairs={{2,0},{4,2},{6,4},{8,6},{10,8},{12,10},{14,12},{16,14},{18,16},{20... | collective-permute-start | bytes 589832 | tf_op jit(solution)/shard_map/ppermute | solution.py:27
  35.6 38.1 %all-to-all-done.in_ref.filter_ref = bf16[16,528,128]{2,1,0:T(8,128)(2,1)} async-done(((bf16[16,528,128]{2,1,0:T(8,128)(2,1)}), bf16[16,528,128]{2,1,0:T(8,128)(2,1)}, u32[]{:S(2)}, u32[]{:S(2)}) %all-to-all-start) | async-done | bytes 2162720 | tf_op jit(solution)/shard_map/all_to_all | solution.py:772
  73.7 6.1 %long_convs.2 = bf16[16,272,128]{2,1,0:T(8,128)(2,1)} custom-call(bf16[16,528,128]{2,1,0:T(8,128)(2,1)} %all-to-all-done.in_ref.filter_ref, bf16[16,528,128]{2,1,0:T(8,128)(2,1)} %all-to-all-done.in_ref.filter_ref), custom_call_target="tpu_custom_call" | custom-call | flops 2147483648 | bytes 2228224 | tf_op jit(solution)/shard_map/long_convs/pallas_call | solution.py:479
  79.8 4.7 %collective-permute-done.2.kp_ref.vp_ref = bf16[256,2048]{1,0:T(8,128)(2,1)} collective-permute-done((bf16[256,2048]{1,0:T(8,128)(2,1)}, bf16[256,2048]{1,0:T(8,128)(2,1)}, u32[]{:S(2)}, u32[]{:S(2)}) %collective-permute-start.2) | collective-permute-done | bytes 1048608 | tf_op jit(solution)/shard_map/ppermute | solution.py:27
  84.5 4.3 %all-to-all-start.2 = ((bf16[16,272,128]{2,1,0:T(8,128)(2,1)}), bf16[16,272,128]{2,1,0:T(8,128)(2,1)}, u32[]{:S(2)}, u32[]{:S(2)}) async-start(bf16[16,272,128]{2,1,0:T(8,128)(2,1)} %long_convs.2), calls=%async_computation.2 | async-start | bytes 2228224 | tf_op jit(solution)/shard_map/all_to_all | solution.py:791
  88.8 9.4 %filter_products.1 = (bf16[16,16,128]{2,1,0:T(8,128)(2,1)S(1)}, f32[1,1]{1,0:T(1,128)}) custom-call(bf16[16,528,128]{2,1,0:T(8,128)(2,1)} %all-to-all-done.in_ref.filter_ref), custom_call_target="tpu_custom_call" | custom-call | flops 2147483648 | bytes 2162688 | tf_op jit(solution)/shard_map/filter_products/pallas_call | solution.py:560
  98.2 1.5 collective-permute-start.4
  99.7 3.5 %attend_part.2 = bf16[128,2176]{1,0:T(8,128)(2,1)S(1)} custom-call(bf16[128,2048]{1,0:T(8,128)(2,1)} %collective-permute-done.1.q_ref, bf16[128,4096]{1,0:T(8,128)(2,1)S(1)} %copy-done.3, bf16[128,4096]{1,0:T(8,128)(2,1)S(1)} %copy-done.4), custom_call_target="tpu_custom_call" | custom-call | flops 134217728 | bytes 2621440 | tf_op jit(solution)/shard_map/attend_part/pallas_call | solution.py:183
  103.2 0.8 copy-done.9
  105.4 5.1 %long_convs.3 = bf16[16,288,128]{2,1,0:T(8,128)(2,1)S(1)} custom-call(bf16[16,528,128]{2,1,0:T(8,128)(2,1)} %all-to-all-done.in_ref.filter_ref, bf16[16,528,128]{2,1,0:T(8,128)(2,1)} %all-to-all-done.in_ref.filter_ref, bf16[16,16,128]{2,1,0:T(8,128)(2,1)S(1)} %get-tuple-element.53.refs_0_, f32[1,1]{1,0:T(1,128)S(6)} %add.3.refs_1_), custom_call_target="tpu_custom_call" | custom-call | flops 2147483648 | bytes 2359296 | tf_op jit(solution)/shard_map/long_convs/pallas_call | solution.py:479
  110.5 1.0 copy-done.8
  111.5 3.9 %all-to-all-done.2.in_ref = bf16[16,272,128]{2,1,0:T(8,128)(2,1)} async-done(((bf16[16,272,128]{2,1,0:T(8,128)(2,1)}), bf16[16,272,128]{2,1,0:T(8,128)(2,1)}, u32[]{:S(2)}, u32[]{:S(2)}) %all-to-all-start.2) | async-done | bytes 1114144 | tf_op jit(solution)/shard_map/all_to_all | solution.py:791
  115.4 4.6 %all-to-all-start.1 = ((bf16[16,288,128]{2,1,0:T(8,128)(2,1)}), bf16[16,288,128]{2,1,0:T(8,128)(2,1)}, u32[]{:S(2)}, u32[]{:S(2)}) async-start(bf16[16,288,128]{2,1,0:T(8,128)(2,1)} %copy-done.8), calls=%async_computation.1 | async-start | bytes 2359296 | tf_op jit(solution)/shard_map/all_to_all | solution.py:791
  120.0 2.0 %collective-permute-start.5 = (bf16[128,2176]{1,0:T(8,128)(2,1)}, bf16[128,2176]{1,0:T(8,128)(2,1)}, u32[]{:S(2)}, u32[]{:S(2)}) collective-permute-start(bf16[128,2176]{1,0:T(8,128)(2,1)} %copy-done.9), channel_id=1, source_target_pairs={{0,2},{2,4},{4,6},{6,8},{8,10},{10,12},{12,14},{14,16},{16,18},{18... | collective-permute-start | bytes 1671176 | tf_op jit(solution)/shard_map/ppermute | solution.py:27
  122.1 2.3 %attend_part.3.own_ref.own_log_ref = bf16[128,2176]{1,0:T(8,128)(2,1)S(1)} custom-call(bf16[128,4096]{1,0:T(8,128)(2,1)S(1)} %copy-done.6, bf16[128,4096]{1,0:T(8,128)(2,1)S(1)} %copy-done.3, bf16[128,4096]{1,0:T(8,128)(2,1)S(1)} %copy-done.4), custom_call_target="tpu_custom_call" | custom-call | flops 134217728 | bytes 2621440 | tf_op jit(solution)/shard_map/attend_part/pallas_call | solution.py:183
  124.5 0.8 copy-done.7
  125.3 4.7 %attend_whole.1._ = bf16[128,4096]{1,0:T(8,128)(2,1)} custom-call(s32[1]{0:T(128)} %bitcast.place_ref, bf16[128,4096]{1,0:T(8,128)(2,1)S(1)} %copy-done.6, bf16[128,4096]{1,0:T(8,128)(2,1)S(1)} %copy-done.3, bf16[128,4096]{1,0:T(8,128)(2,1)S(1)} %copy-done.4, bf16[256,2048]{1,0:T(8,128)(2,1)} %collective-permute-done.2.kp_ref.vp_ref, ...), custom_call_target="tpu_custom_call" | custom-call | flops 268435456 | bytes 5242880 | tf_op jit(solution)/shard_map/attend_whole/pallas_call | solution.py:203
  130.0 6.3 %after_exchange.2 = (bf16[128,4096]{1,0:T(8,128)(2,1)}, bf16[128,4096]{1,0:T(8,128)(2,1)}, bf16[128,4096]{1,0:T(8,128)(2,1)}) custom-call(bf16[16,272,128]{2,1,0:T(8,128)(2,1)} %all-to-all-done.2.in_ref, bf16[128,4096]{1,0:T(8,128)(2,1)} %og_ref.3, bf16[128,4096]{1,0:T(8,128)(2,1)} %k_ref.9, bf16[128,4096]{1,0:T(8,128)(2,1)} %v_ref.9, ...), custom_call_target="tpu_custom_call" | custom-call | flops 23592960 | bytes 4718592 | tf_op jit(solution)/shard_map/after_exchange/pallas_call | solution.py:719
  136.2 12.5 %all-to-all-done.1.in_ref = bf16[16,288,128]{2,1,0:T(8,128)(2,1)} async-done(((bf16[16,288,128]{2,1,0:T(8,128)(2,1)}), bf16[16,288,128]{2,1,0:T(8,128)(2,1)}, u32[]{:S(2)}, u32[]{:S(2)}) %all-to-all-start.1) | async-done | bytes 1179680 | tf_op jit(solution)/shard_map/all_to_all | solution.py:791
  148.7 6.6 %after_exchange.3 = (bf16[128,4096]{1,0:T(8,128)(2,1)}, bf16[128,4096]{1,0:T(8,128)(2,1)}, bf16[128,4096]{1,0:T(8,128)(2,1)}, f32[128,256]{1,0:T(8,128)}) custom-call(bf16[16,288,128]{2,1,0:T(8,128)(2,1)} %all-to-all-done.1.in_ref, bf16[128,4096]{1,0:T(8,128)(2,1)} %og_ref.3, ...), custom_call_target="tpu_custom_call", output_to_operand_aliasing={{0}: (7, {}), {1}: (8, {}), {2}: (9, {})} | custom-call | flops 23592960 | bytes 4718592 | tf_op jit(solution)/shard_map/after_exchange/pallas_call | solution.py:719
  155.3 2.8 %combine.1 = bf16[128,4096]{1,0:T(8,128)(2,1)} custom-call(s32[1]{0:T(128)} %bitcast.place_ref, bf16[128,2176]{1,0:T(8,128)(2,1)} %copy-done.7, bf16[128,2176]{1,0:T(8,128)(2,1)} %collective-permute-done.5.prev_ref.prev_log_ref, bf16[128,2176]{1,0:T(8,128)(2,1)} %copy-done.7, ...), custom_call_target="tpu_custom_call", output_to_operand_aliasing={{}: (5, {})} | custom-call | flops 33554432 | bytes 655360 | tf_op jit(solution)/shard_map/combine/pallas_call | solution.py:230
  (28 shorter events, 0.2 us)
Async XLA Ops:
  2.4 8.1 %collective-permute-start = (bf16[24,4096]{1,0:T(8,128)(2,1)}, bf16[24,4096]{1,0:T(8,128)(2,1)S(1)}, u32[]{:S(2)}, u32[]{:S(2)}) collective-permute-start(bf16[24,4096]{1,0:T(8,128)(2,1)} %edge_rows.2), channel_id=1, source_target_pairs={{0,2},{2,4},{4,6},{6,8},{8,10},{10,12},{12,14},{14,16},{16,18},{18... | collective-permute-start | bytes 589832 | tf_op jit(solution)/shard_map/ppermute | solution.py:27
  10.4 0.7 copy-start.10
  18.8 55.0 %all-to-all-start = ((bf16[16,528,128]{2,1,0:T(8,128)(2,1)}), bf16[16,528,128]{2,1,0:T(8,128)(2,1)}, u32[]{:S(2)}, u32[]{:S(2)}) async-start(bf16[16,528,128]{2,1,0:T(8,128)(2,1)} %before_exchange.1), calls=%async_computation | async-start | bytes 4325376 | tf_op jit(solution)/shard_map/all_to_all | solution.py:772
  24.1 1.0 slice-start
  24.1 1.2 slice-start.1
  24.1 4.3 %copy-start.5 = (bf16[128,4096]{1,0:T(8,128)(2,1)S(1)}, bf16[128,4096]{1,0:T(8,128)(2,1)}, u32[]{:S(2)}) copy-start(bf16[128,4096]{1,0:T(8,128)(2,1)} %q_ref.3) | copy-start | bytes 3145732
  24.1 9.6 %copy-start = (bf16[128,4096]{1,0:T(8,128)(2,1)S(1)}, bf16[128,4096]{1,0:T(8,128)(2,1)}, u32[]{:S(2)}) copy-start(bf16[128,4096]{1,0:T(8,128)(2,1)} %k_ref.9) | copy-start | bytes 3145732
  24.1 9.6 %copy-start.1 = (bf16[128,4096]{1,0:T(8,128)(2,1)S(1)}, bf16[128,4096]{1,0:T(8,128)(2,1)}, u32[]{:S(2)}) copy-start(bf16[128,4096]{1,0:T(8,128)(2,1)} %v_ref.9) | copy-start | bytes 3145732
  24.1 9.6 %copy-start.2 = (bf16[128,4096]{1,0:T(8,128)(2,1)S(1)}, bf16[128,4096]{1,0:T(8,128)(2,1)}, u32[]{:S(2)}) copy-start(bf16[128,4096]{1,0:T(8,128)(2,1)} %og_ref.3) | copy-start | bytes 3145732
  26.3 58.2 %collective-permute-start.2 = (bf16[256,2048]{1,0:T(8,128)(2,1)}, bf16[256,2048]{1,0:T(8,128)(2,1)}, u32[]{:S(2)}, u32[]{:S(2)}) collective-permute-start(bf16[256,2048]{1,0:T(8,128)(2,1)} %pad_maximum_fusion), channel_id=1, source_target_pairs={{0,2},{2,4},{4,6},{6,8},{8,10},{10,12},{12,14},{14,16},{16,18},{18... | collective-permute-start | bytes 3145736 | tf_op jit(solution)/shard_map/ppermute | solution.py:27
  29.2 50.6 %collective-permute-start.1 = (bf16[128,2048]{1,0:T(8,128)(2,1)}, bf16[128,2048]{1,0:T(8,128)(2,1)}, u32[]{:S(2)}, u32[]{:S(2)}) collective-permute-start(bf16[128,2048]{1,0:T(8,128)(2,1)} %slice.9), channel_id=1, source_target_pairs={{2,0},{4,2},{6,4},{8,6},{10,8},{12,10},{14,12},{16,14},{18,16},{20... | collective-permute-start | bytes 1572872 | tf_op jit(solution)/shard_map/ppermute | solution.py:27
  33.7 46.1 %collective-permute-start.3 = (bf16[24,4096]{1,0:T(8,128)(2,1)S(1)}, bf16[24,4096]{1,0:T(8,128)(2,1)S(1)}, u32[]{:S(2)}, u32[]{:S(2)}) collective-permute-start(bf16[24,4096]{1,0:T(8,128)(2,1)S(1)} %edge_rows.3), channel_id=1, source_target_pairs={{2,0},{4,2},{6,4},{8,6},{10,8},{12,10},{14,12},{16,14},{18,16},{20... | collective-permute-start | bytes 589832 | tf_op jit(solution)/shard_map/ppermute | solution.py:27
  79.8 18.4 %copy-start.11 = (bf16[24,4096]{1,0:T(8,128)(2,1)}, bf16[24,4096]{1,0:T(8,128)(2,1)S(1)}, u32[]{:S(2)}) copy-start(bf16[24,4096]{1,0:T(8,128)(2,1)S(1)} %collective-permute-done.3.next_ref) | copy-start | bytes 589828
  84.5 30.9 %all-to-all-start.2 = ((bf16[16,272,128]{2,1,0:T(8,128)(2,1)}), bf16[16,272,128]{2,1,0:T(8,128)(2,1)}, u32[]{:S(2)}, u32[]{:S(2)}) async-start(bf16[16,272,128]{2,1,0:T(8,128)(2,1)} %long_convs.2), calls=%async_computation.2 | async-start | bytes 2228224 | tf_op jit(solution)/shard_map/all_to_all | solution.py:791
  88.8 10.9 %copy-start.3 = (bf16[128,4096]{1,0:T(8,128)(2,1)S(1)}, bf16[128,4096]{1,0:T(8,128)(2,1)}, u32[]{:S(2)}) copy-start(bf16[128,4096]{1,0:T(8,128)(2,1)} %k_ref.7) | copy-start | bytes 3145732
  88.8 10.9 %copy-start.4 = (bf16[128,4096]{1,0:T(8,128)(2,1)S(1)}, bf16[128,4096]{1,0:T(8,128)(2,1)}, u32[]{:S(2)}) copy-start(bf16[128,4096]{1,0:T(8,128)(2,1)} %v_ref.7) | copy-start | bytes 3145732
  98.2 5.9 %collective-permute-start.4 = (f32[1,1]{1,0:T(1,128)}, f32[1,1]{1,0:T(1,128)}, u32[]{:S(2)}, u32[]{:S(2)}) collective-permute-start(f32[1,1]{1,0:T(1,128)} %get-tuple-element.54), channel_id=1, source_target_pairs={{0,1},{1,0},{2,3},{3,2},{4,5},{5,4},{6,7},{7,6},{8,9},{9,8},{10,11... | collective-permute-start | bytes 20 | tf_op jit(solution)/shard_map/ppermute | solution.py:34
  103.2 0.8 copy-start.9
  110.5 1.0 copy-start.8
  111.5 10.6 %copy-start.6 = (bf16[128,4096]{1,0:T(8,128)(2,1)S(1)}, bf16[128,4096]{1,0:T(8,128)(2,1)}, u32[]{:S(2)}) copy-start(bf16[128,4096]{1,0:T(8,128)(2,1)} %q_ref.3) | copy-start | bytes 3145732
  115.4 33.3 %all-to-all-start.1 = ((bf16[16,288,128]{2,1,0:T(8,128)(2,1)}), bf16[16,288,128]{2,1,0:T(8,128)(2,1)}, u32[]{:S(2)}, u32[]{:S(2)}) async-start(bf16[16,288,128]{2,1,0:T(8,128)(2,1)} %copy-done.8), calls=%async_computation.1 | async-start | bytes 2359296 | tf_op jit(solution)/shard_map/all_to_all | solution.py:791
  120.0 35.2 %collective-permute-start.5 = (bf16[128,2176]{1,0:T(8,128)(2,1)}, bf16[128,2176]{1,0:T(8,128)(2,1)}, u32[]{:S(2)}, u32[]{:S(2)}) collective-permute-start(bf16[128,2176]{1,0:T(8,128)(2,1)} %copy-done.9), channel_id=1, source_target_pairs={{0,2},{2,4},{4,6},{6,8},{8,10},{10,12},{12,14},{14,16},{16,18},{18... | collective-permute-start | bytes 1671176 | tf_op jit(solution)/shard_map/ppermute | solution.py:27
  124.5 0.8 copy-start.7

commit v17 on v16

--- a/solution.py
+++ b/solution.py
@@ -710,7 +710,7 @@
     channels = out_grad.shape[1] // chunks
     cpd, gpd = channels // n, groups // (n * chunks)
     last = chunk + 1 == chunks
-    tile = min(channels, max(512, cpd))
+    tile = min(channels, max(1024, cpd))
     per_tile = tile // cpd
     first = chunk * channels // tile
     block = pl.BlockSpec((rows, tile), lambda i: (0, first + i))

time: 160 us -> 160 us (level)
  no operation moved by 1% of the time
where the time goes in v17:
time: 160 us; the launch traced here: 158 us
  waiting for transfers between devices  65.3 us (41%)
  Pallas kernels  56.1 us (35%)
  starting transfers between devices  28 us (18%)
  local copies, waits for them, and re-layouts  5.35 us (3%)
  between operations  2.18 us (1%)
    all_to_all x1, waiting for transfers between devices, on_device(): lax.all_to_all(send, 'ctx', split_axis=0, concat_axis=0, tiled=True)  38.1 us
    all_to_all x2, waiting for transfers between devices, on_device(): lax.all_to_all(results, 'ctx', split_axis=0, concat_axis=0, tiled=True)  16.4 us
    pallas_call x2, Pallas kernels, after_exchange(): pl.pallas_call(functools.partial(after_kernel, cpd, gpd, chunks, last, bo...  12.8 us
    ppermute x5, starting transfers between devices, shifted(): return lax.ppermute(block, axis, route)  12.3 us
    pallas_call x2, Pallas kernels, long_convs(): pl.pallas_call(functools.partial(conv_kernel, cpd, gpd, chunk), grid=(pai...  11.2 us
    ppermute x5, waiting for transfers between devices, shifted(): return lax.ppermute(block, axis, route)  10.8 us
    pallas_call x1, Pallas kernels, filter_products(): pl.pallas_call(functools.partial(gram_kernel, cpd // gpd), grid=(pairs,),...  9.36 us
    all_to_all x2, starting transfers between devices, on_device(): lax.all_to_all(results, 'ctx', split_axis=0, concat_axis=0, tiled=True)  8.92 us
  transfers between devices with their start and end apart: 9, of which 5 were waited for; matrix products, arithmetic and copies ran while one was open for 1% of the time, Pallas kernels for 28%

profile of v17, /device:TPU:16, one launch (start us, length us, event | category | flops | bytes accessed | tf_op | source)
XLA Modules:
  0.0 158.1 jit_solution(7708664429033355419)
XLA Ops:
  0.6 1.7 %edge_rows.2 = bf16[24,4096]{1,0:T(8,128)(2,1)} custom-call(bf16[128,4096]{1,0:T(8,128)(2,1)} %refs_6_.1, bf16[128,4096]{1,0:T(8,128)(2,1)} %k_ref.9, bf16[128,4096]{1,0:T(8,128)(2,1)} %v_ref.9), custom_call_target="tpu_custom_call" | custom-call | tf_op jit(solution)/shard_map/edge_rows/pallas_call | solution.py:255
  2.4 1.9 %collective-permute-start = (bf16[24,4096]{1,0:T(8,128)(2,1)}, bf16[24,4096]{1,0:T(8,128)(2,1)S(1)}, u32[]{:S(2)}, u32[]{:S(2)}) collective-permute-start(bf16[24,4096]{1,0:T(8,128)(2,1)} %edge_rows.2), channel_id=1, source_target_pairs={{0,2},{2,4},{4,6},{6,8},{8,10},{10,12},{12,14},{14,16},{16,18},{18... | collective-permute-start | bytes 589832 | tf_op jit(solution)/shard_map/ppermute | solution.py:27
  4.3 6.2 %collective-permute-done.refs_4_.refs_10_.tail_ref = bf16[24,4096]{1,0:T(8,128)(2,1)S(1)} collective-permute-done((bf16[24,4096]{1,0:T(8,128)(2,1)}, bf16[24,4096]{1,0:T(8,128)(2,1)S(1)}, u32[]{:S(2)}, u32[]{:S(2)}) %collective-permute-start) | collective-permute-done | bytes 196640 | tf_op jit(solution)/shard_map/ppermute | solution.py:27
  10.4 0.7 copy-done.10
  11.1 7.6 %before_exchange.1 = bf16[16,528,128]{2,1,0:T(8,128)(2,1)} custom-call(bf16[128,4096]{1,0:T(8,128)(2,1)} %refs_6_.1, bf16[128,4096]{1,0:T(8,128)(2,1)} %k_ref.9, bf16[128,4096]{1,0:T(8,128)(2,1)} %v_ref.9, bf16[128,4096]{1,0:T(8,128)(2,1)} %og_ref.3, bf16[24,4096]{1,0:T(8,128)(2,1)} %copy-done.10, f32[3,7,4096]{2,1,0:T(8,128)} %taps_ref.3, ...), custom_call_target="tpu_custom_call" | custom-call | flops 26214400 | bytes 6291456 | tf_op jit(solution)/shard_map/before_exchange/pallas_call | solution.py:364
  18.8 5.3 %all-to-all-start = ((bf16[16,528,128]{2,1,0:T(8,128)(2,1)}), bf16[16,528,128]{2,1,0:T(8,128)(2,1)}, u32[]{:S(2)}, u32[]{:S(2)}) async-start(bf16[16,528,128]{2,1,0:T(8,128)(2,1)} %before_exchange.1), calls=%async_computation | async-start | bytes 4325376 | tf_op jit(solution)/shard_map/all_to_all | solution.py:772
  24.1 1.0 slice-done
  25.3 1.1 pad_maximum_fusion
  26.3 2.0 %collective-permute-start.2 = (bf16[256,2048]{1,0:T(8,128)(2,1)}, bf16[256,2048]{1,0:T(8,128)(2,1)}, u32[]{:S(2)}, u32[]{:S(2)}) collective-permute-start(bf16[256,2048]{1,0:T(8,128)(2,1)} %pad_maximum_fusion), channel_id=1, source_target_pairs={{0,2},{2,4},{4,6},{6,8},{8,10},{10,12},{12,14},{14,16},{16,18},{18... | collective-permute-start | bytes 3145736 | tf_op jit(solution)/shard_map/ppermute | solution.py:27
  28.4 0.8 slice.9
  29.2 4.4 %collective-permute-start.1 = (bf16[128,2048]{1,0:T(8,128)(2,1)}, bf16[128,2048]{1,0:T(8,128)(2,1)}, u32[]{:S(2)}, u32[]{:S(2)}) collective-permute-start(bf16[128,2048]{1,0:T(8,128)(2,1)} %slice.9), channel_id=1, source_target_pairs={{2,0},{4,2},{6,4},{8,6},{10,8},{12,10},{14,12},{16,14},{18,16},{20... | collective-permute-start | bytes 1572872 | tf_op jit(solution)/shard_map/ppermute | solution.py:27
  33.7 1.9 %collective-permute-start.3 = (bf16[24,4096]{1,0:T(8,128)(2,1)S(1)}, bf16[24,4096]{1,0:T(8,128)(2,1)S(1)}, u32[]{:S(2)}, u32[]{:S(2)}) collective-permute-start(bf16[24,4096]{1,0:T(8,128)(2,1)S(1)} %edge_rows.3), channel_id=1, source_target_pairs={{2,0},{4,2},{6,4},{8,6},{10,8},{12,10},{14,12},{16,14},{18,16},{20... | collective-permute-start | bytes 589832 | tf_op jit(solution)/shard_map/ppermute | solution.py:27
  35.6 38.1 %all-to-all-done.in_ref.filter_ref = bf16[16,528,128]{2,1,0:T(8,128)(2,1)} async-done(((bf16[16,528,128]{2,1,0:T(8,128)(2,1)}), bf16[16,528,128]{2,1,0:T(8,128)(2,1)}, u32[]{:S(2)}, u32[]{:S(2)}) %all-to-all-start) | async-done | bytes 2162720 | tf_op jit(solution)/shard_map/all_to_all | solution.py:772
  73.7 6.1 %long_convs.2 = bf16[16,272,128]{2,1,0:T(8,128)(2,1)} custom-call(bf16[16,528,128]{2,1,0:T(8,128)(2,1)} %all-to-all-done.in_ref.filter_ref, bf16[16,528,128]{2,1,0:T(8,128)(2,1)} %all-to-all-done.in_ref.filter_ref), custom_call_target="tpu_custom_call" | custom-call | flops 2147483648 | bytes 2228224 | tf_op jit(solution)/shard_map/long_convs/pallas_call | solution.py:479
  79.8 4.7 %collective-permute-done.2.kp_ref.vp_ref = bf16[256,2048]{1,0:T(8,128)(2,1)} collective-permute-done((bf16[256,2048]{1,0:T(8,128)(2,1)}, bf16[256,2048]{1,0:T(8,128)(2,1)}, u32[]{:S(2)}, u32[]{:S(2)}) %collective-permute-start.2) | collective-permute-done | bytes 1048608 | tf_op jit(solution)/shard_map/ppermute | solution.py:27
  84.5 4.3 %all-to-all-start.2 = ((bf16[16,272,128]{2,1,0:T(8,128)(2,1)}), bf16[16,272,128]{2,1,0:T(8,128)(2,1)}, u32[]{:S(2)}, u32[]{:S(2)}) async-start(bf16[16,272,128]{2,1,0:T(8,128)(2,1)} %long_convs.2), calls=%async_computation.2 | async-start | bytes 2228224 | tf_op jit(solution)/shard_map/all_to_all | solution.py:791
  88.8 9.4 %filter_products.1 = (bf16[16,16,128]{2,1,0:T(8,128)(2,1)S(1)}, f32[1,1]{1,0:T(1,128)}) custom-call(bf16[16,528,128]{2,1,0:T(8,128)(2,1)} %all-to-all-done.in_ref.filter_ref), custom_call_target="tpu_custom_call" | custom-call | flops 2147483648 | bytes 2162688 | tf_op jit(solution)/shard_map/filter_products/pallas_call | solution.py:560
  98.2 1.5 collective-permute-start.4
  99.7 3.5 %attend_part.2 = bf16[128,2176]{1,0:T(8,128)(2,1)S(1)} custom-call(bf16[128,2048]{1,0:T(8,128)(2,1)} %collective-permute-done.1.q_ref, bf16[128,4096]{1,0:T(8,128)(2,1)S(1)} %copy-done.3, bf16[128,4096]{1,0:T(8,128)(2,1)S(1)} %copy-done.4), custom_call_target="tpu_custom_call" | custom-call | flops 134217728 | bytes 2621440 | tf_op jit(solution)/shard_map/attend_part/pallas_call | solution.py:183
  103.2 0.8 copy-done.9
  105.4 5.1 %long_convs.3 = bf16[16,288,128]{2,1,0:T(8,128)(2,1)S(1)} custom-call(bf16[16,528,128]{2,1,0:T(8,128)(2,1)} %all-to-all-done.in_ref.filter_ref, bf16[16,528,128]{2,1,0:T(8,128)(2,1)} %all-to-all-done.in_ref.filter_ref, bf16[16,16,128]{2,1,0:T(8,128)(2,1)S(1)} %get-tuple-element.53.refs_0_, f32[1,1]{1,0:T(1,128)S(6)} %add.3.refs_1_), custom_call_target="tpu_custom_call" | custom-call | flops 2147483648 | bytes 2359296 | tf_op jit(solution)/shard_map/long_convs/pallas_call | solution.py:479
  110.5 1.0 copy-done.8
  111.5 3.9 %all-to-all-done.2.in_ref = bf16[16,272,128]{2,1,0:T(8,128)(2,1)} async-done(((bf16[16,272,128]{2,1,0:T(8,128)(2,1)}), bf16[16,272,128]{2,1,0:T(8,128)(2,1)}, u32[]{:S(2)}, u32[]{:S(2)}) %all-to-all-start.2) | async-done | bytes 1114144 | tf_op jit(solution)/shard_map/all_to_all | solution.py:791
  115.4 4.6 %all-to-all-start.1 = ((bf16[16,288,128]{2,1,0:T(8,128)(2,1)}), bf16[16,288,128]{2,1,0:T(8,128)(2,1)}, u32[]{:S(2)}, u32[]{:S(2)}) async-start(bf16[16,288,128]{2,1,0:T(8,128)(2,1)} %copy-done.8), calls=%async_computation.1 | async-start | bytes 2359296 | tf_op jit(solution)/shard_map/all_to_all | solution.py:791
  120.0 2.0 %collective-permute-start.5 = (bf16[128,2176]{1,0:T(8,128)(2,1)}, bf16[128,2176]{1,0:T(8,128)(2,1)}, u32[]{:S(2)}, u32[]{:S(2)}) collective-permute-start(bf16[128,2176]{1,0:T(8,128)(2,1)} %copy-done.9), channel_id=1, source_target_pairs={{0,2},{2,4},{4,6},{6,8},{8,10},{10,12},{12,14},{14,16},{16,18},{18... | collective-permute-start | bytes 1671176 | tf_op jit(solution)/shard_map/ppermute | solution.py:27
  122.1 2.3 %attend_part.3.own_ref.own_log_ref = bf16[128,2176]{1,0:T(8,128)(2,1)S(1)} custom-call(bf16[128,4096]{1,0:T(8,128)(2,1)S(1)} %copy-done.6, bf16[128,4096]{1,0:T(8,128)(2,1)S(1)} %copy-done.3, bf16[128,4096]{1,0:T(8,128)(2,1)S(1)} %copy-done.4), custom_call_target="tpu_custom_call" | custom-call | flops 134217728 | bytes 2621440 | tf_op jit(solution)/shard_map/attend_part/pallas_call | solution.py:183
  124.5 0.8 copy-done.7
  125.3 4.7 %attend_whole.1._ = bf16[128,4096]{1,0:T(8,128)(2,1)} custom-call(s32[1]{0:T(128)} %bitcast.place_ref, bf16[128,4096]{1,0:T(8,128)(2,1)S(1)} %copy-done.6, bf16[128,4096]{1,0:T(8,128)(2,1)S(1)} %copy-done.3, bf16[128,4096]{1,0:T(8,128)(2,1)S(1)} %copy-done.4, bf16[256,2048]{1,0:T(8,128)(2,1)} %collective-permute-done.2.kp_ref.vp_ref, ...), custom_call_target="tpu_custom_call" | custom-call | flops 268435456 | bytes 5242880 | tf_op jit(solution)/shard_map/attend_whole/pallas_call | solution.py:203
  130.0 6.2 %after_exchange.2 = (bf16[128,4096]{1,0:T(8,128)(2,1)}, bf16[128,4096]{1,0:T(8,128)(2,1)}, bf16[128,4096]{1,0:T(8,128)(2,1)}) custom-call(bf16[16,272,128]{2,1,0:T(8,128)(2,1)} %all-to-all-done.2.in_ref, bf16[128,4096]{1,0:T(8,128)(2,1)} %og_ref.3, bf16[128,4096]{1,0:T(8,128)(2,1)} %k_ref.9, bf16[128,4096]{1,0:T(8,128)(2,1)} %v_ref.9, ...), custom_call_target="tpu_custom_call" | custom-call | flops 23592960 | bytes 4718592 | tf_op jit(solution)/shard_map/after_exchange/pallas_call | solution.py:719
  136.2 12.5 %all-to-all-done.1.in_ref = bf16[16,288,128]{2,1,0:T(8,128)(2,1)} async-done(((bf16[16,288,128]{2,1,0:T(8,128)(2,1)}), bf16[16,288,128]{2,1,0:T(8,128)(2,1)}, u32[]{:S(2)}, u32[]{:S(2)}) %all-to-all-start.1) | async-done | bytes 1179680 | tf_op jit(solution)/shard_map/all_to_all | solution.py:791
  148.7 6.5 %after_exchange.3 = (bf16[128,4096]{1,0:T(8,128)(2,1)}, bf16[128,4096]{1,0:T(8,128)(2,1)}, bf16[128,4096]{1,0:T(8,128)(2,1)}, f32[128,256]{1,0:T(8,128)}) custom-call(bf16[16,288,128]{2,1,0:T(8,128)(2,1)} %all-to-all-done.1.in_ref, bf16[128,4096]{1,0:T(8,128)(2,1)} %og_ref.3, ...), custom_call_target="tpu_custom_call", output_to_operand_aliasing={{0}: (7, {}), {1}: (8, {}), {2}: (9, {})} | custom-call | flops 23592960 | bytes 4718592 | tf_op jit(solution)/shard_map/after_exchange/pallas_call | solution.py:719
  155.2 2.8 %combine.1 = bf16[128,4096]{1,0:T(8,128)(2,1)} custom-call(s32[1]{0:T(128)} %bitcast.place_ref, bf16[128,2176]{1,0:T(8,128)(2,1)} %copy-done.7, bf16[128,2176]{1,0:T(8,128)(2,1)} %collective-permute-done.5.prev_ref.prev_log_ref, bf16[128,2176]{1,0:T(8,128)(2,1)} %copy-done.7, ...), custom_call_target="tpu_custom_call", output_to_operand_aliasing={{}: (5, {})} | custom-call | flops 33554432 | bytes 655360 | tf_op jit(solution)/shard_map/combine/pallas_call | solution.py:230
  (28 shorter events, 0.2 us)
Async XLA Ops:
  2.4 8.1 %collective-permute-start = (bf16[24,4096]{1,0:T(8,128)(2,1)}, bf16[24,4096]{1,0:T(8,128)(2,1)S(1)}, u32[]{:S(2)}, u32[]{:S(2)}) collective-permute-start(bf16[24,4096]{1,0:T(8,128)(2,1)} %edge_rows.2), channel_id=1, source_target_pairs={{0,2},{2,4},{4,6},{6,8},{8,10},{10,12},{12,14},{14,16},{16,18},{18... | collective-permute-start | bytes 589832 | tf_op jit(solution)/shard_map/ppermute | solution.py:27
  10.4 0.7 copy-start.10
  18.8 55.0 %all-to-all-start = ((bf16[16,528,128]{2,1,0:T(8,128)(2,1)}), bf16[16,528,128]{2,1,0:T(8,128)(2,1)}, u32[]{:S(2)}, u32[]{:S(2)}) async-start(bf16[16,528,128]{2,1,0:T(8,128)(2,1)} %before_exchange.1), calls=%async_computation | async-start | bytes 4325376 | tf_op jit(solution)/shard_map/all_to_all | solution.py:772
  24.1 1.0 slice-start
  24.1 1.2 slice-start.1
  24.1 4.3 %copy-start.5 = (bf16[128,4096]{1,0:T(8,128)(2,1)S(1)}, bf16[128,4096]{1,0:T(8,128)(2,1)}, u32[]{:S(2)}) copy-start(bf16[128,4096]{1,0:T(8,128)(2,1)} %q_ref.3) | copy-start | bytes 3145732
  24.1 9.6 %copy-start = (bf16[128,4096]{1,0:T(8,128)(2,1)S(1)}, bf16[128,4096]{1,0:T(8,128)(2,1)}, u32[]{:S(2)}) copy-start(bf16[128,4096]{1,0:T(8,128)(2,1)} %k_ref.9) | copy-start | bytes 3145732
  24.1 9.6 %copy-start.1 = (bf16[128,4096]{1,0:T(8,128)(2,1)S(1)}, bf16[128,4096]{1,0:T(8,128)(2,1)}, u32[]{:S(2)}) copy-start(bf16[128,4096]{1,0:T(8,128)(2,1)} %v_ref.9) | copy-start | bytes 3145732
  24.1 9.6 %copy-start.2 = (bf16[128,4096]{1,0:T(8,128)(2,1)S(1)}, bf16[128,4096]{1,0:T(8,128)(2,1)}, u32[]{:S(2)}) copy-start(bf16[128,4096]{1,0:T(8,128)(2,1)} %og_ref.3) | copy-start | bytes 3145732
  26.3 58.2 %collective-permute-start.2 = (bf16[256,2048]{1,0:T(8,128)(2,1)}, bf16[256,2048]{1,0:T(8,128)(2,1)}, u32[]{:S(2)}, u32[]{:S(2)}) collective-permute-start(bf16[256,2048]{1,0:T(8,128)(2,1)} %pad_maximum_fusion), channel_id=1, source_target_pairs={{0,2},{2,4},{4,6},{6,8},{8,10},{10,12},{12,14},{14,16},{16,18},{18... | collective-permute-start | bytes 3145736 | tf_op jit(solution)/shard_map/ppermute | solution.py:27
  29.2 50.6 %collective-permute-start.1 = (bf16[128,2048]{1,0:T(8,128)(2,1)}, bf16[128,2048]{1,0:T(8,128)(2,1)}, u32[]{:S(2)}, u32[]{:S(2)}) collective-permute-start(bf16[128,2048]{1,0:T(8,128)(2,1)} %slice.9), channel_id=1, source_target_pairs={{2,0},{4,2},{6,4},{8,6},{10,8},{12,10},{14,12},{16,14},{18,16},{20... | collective-permute-start | bytes 1572872 | tf_op jit(solution)/shard_map/ppermute | solution.py:27
  33.7 46.1 %collective-permute-start.3 = (bf16[24,4096]{1,0:T(8,128)(2,1)S(1)}, bf16[24,4096]{1,0:T(8,128)(2,1)S(1)}, u32[]{:S(2)}, u32[]{:S(2)}) collective-permute-start(bf16[24,4096]{1,0:T(8,128)(2,1)S(1)} %edge_rows.3), channel_id=1, source_target_pairs={{2,0},{4,2},{6,4},{8,6},{10,8},{12,10},{14,12},{16,14},{18,16},{20... | collective-permute-start | bytes 589832 | tf_op jit(solution)/shard_map/ppermute | solution.py:27
  79.8 18.4 %copy-start.11 = (bf16[24,4096]{1,0:T(8,128)(2,1)}, bf16[24,4096]{1,0:T(8,128)(2,1)S(1)}, u32[]{:S(2)}) copy-start(bf16[24,4096]{1,0:T(8,128)(2,1)S(1)} %collective-permute-done.3.next_ref) | copy-start | bytes 589828
  84.5 30.9 %all-to-all-start.2 = ((bf16[16,272,128]{2,1,0:T(8,128)(2,1)}), bf16[16,272,128]{2,1,0:T(8,128)(2,1)}, u32[]{:S(2)}, u32[]{:S(2)}) async-start(bf16[16,272,128]{2,1,0:T(8,128)(2,1)} %long_convs.2), calls=%async_computation.2 | async-start | bytes 2228224 | tf_op jit(solution)/shard_map/all_to_all | solution.py:791
  88.8 10.9 %copy-start.3 = (bf16[128,4096]{1,0:T(8,128)(2,1)S(1)}, bf16[128,4096]{1,0:T(8,128)(2,1)}, u32[]{:S(2)}) copy-start(bf16[128,4096]{1,0:T(8,128)(2,1)} %k_ref.7) | copy-start | bytes 3145732
  88.8 10.9 %copy-start.4 = (bf16[128,4096]{1,0:T(8,128)(2,1)S(1)}, bf16[128,4096]{1,0:T(8,128)(2,1)}, u32[]{:S(2)}) copy-start(bf16[128,4096]{1,0:T(8,128)(2,1)} %v_ref.7) | copy-start | bytes 3145732
  98.2 5.9 %collective-permute-start.4 = (f32[1,1]{1,0:T(1,128)}, f32[1,1]{1,0:T(1,128)}, u32[]{:S(2)}, u32[]{:S(2)}) collective-permute-start(f32[1,1]{1,0:T(1,128)} %get-tuple-element.54), channel_id=1, source_target_pairs={{0,1},{1,0},{2,3},{3,2},{4,5},{5,4},{6,7},{7,6},{8,9},{9,8},{10,11... | collective-permute-start | bytes 20 | tf_op jit(solution)/shard_map/ppermute | solution.py:34
  103.2 0.8 copy-start.9
  110.5 1.0 copy-start.8
  111.5 10.6 %copy-start.6 = (bf16[128,4096]{1,0:T(8,128)(2,1)S(1)}, bf16[128,4096]{1,0:T(8,128)(2,1)}, u32[]{:S(2)}) copy-start(bf16[128,4096]{1,0:T(8,128)(2,1)} %q_ref.3) | copy-start | bytes 3145732
  115.4 33.3 %all-to-all-start.1 = ((bf16[16,288,128]{2,1,0:T(8,128)(2,1)}), bf16[16,288,128]{2,1,0:T(8,128)(2,1)}, u32[]{:S(2)}, u32[]{:S(2)}) async-start(bf16[16,288,128]{2,1,0:T(8,128)(2,1)} %copy-done.8), calls=%async_computation.1 | async-start | bytes 2359296 | tf_op jit(solution)/shard_map/all_to_all | solution.py:791
  120.0 35.2 %collective-permute-start.5 = (bf16[128,2176]{1,0:T(8,128)(2,1)}, bf16[128,2176]{1,0:T(8,128)(2,1)}, u32[]{:S(2)}, u32[]{:S(2)}) collective-permute-start(bf16[128,2176]{1,0:T(8,128)(2,1)} %copy-done.9), channel_id=1, source_target_pairs={{0,2},{2,4},{4,6},{6,8},{8,10},{10,12},{12,14},{14,16},{16,18},{18... | collective-permute-start | bytes 1671176 | tf_op jit(solution)/shard_map/ppermute | solution.py:27
  124.5 0.8 copy-start.7
